TPU v7x, 128 devices: a whole 4x4x4 slice. The times are simulated.
128 devices in a mesh: ctx: 32 (over z, y, core), head: 4 (over x).
Axes of the slice: x: 4, y: 4, z: 4, core: 2. Of those that a mesh axis runs over, the one named last changes fastest.
Arguments:
- tokens: bfloat16 [16384, 4096], P('ctx'), may hold values from -6 to 6
- x_weight: bfloat16 [4096, 8192], P('ctx', 'head'), may hold values from -0.09375 to 0.09375
- z_weight: bfloat16 [4096, 8192], P('ctx', 'head'), may hold values from -0.09375 to 0.09375
- bc_weight: bfloat16 [4096, 256], P('ctx'), may hold values from -0.09375 to 0.09375
- dt_weight: bfloat16 [4096, 128], P('ctx', 'head'), may hold values from -0.09375 to 0.09375
- conv_x: float32 [4, 8192], P(None, 'head'), may hold values from -3 to 3
- conv_bc: float32 [4, 256], replicated, may hold values from -3 to 3
- dt_bias: float32 [128], P('head'), may hold values from -1 to 1
- decay_rate: float32 [128], P('head'), may hold values from 3.0517578e-06 to 0.05
- skip: float32 [128], P('head'), may hold values from 0.5 to 1.5
- norm_gain: float32 [8192], P('head'), may hold values from 0.5 to 1.5
Outputs:
- mixed: bfloat16 [16384, 8192], P('ctx', 'head')
All inputs are finite; a program needn't handle non-finite values.
Results may differ from a plain program's by a relative error of at most 0.013.
Values may be sent and summed in bfloat16 or wider, within the bound.
No kernel may reach another device: no remote copies, remote signals or barrier semaphores. Data moves between devices by JAX's collectives and lax.ppermute only.
A program may use at most 192 MiB of HBM per device.

v0:
```python
import jax
import jax.numpy as jnp
from jax import lax
from jax.sharding import PartitionSpec as P

GROUP = 256


def entering(part, axis, combine, identity):
    place = lax.axis_index(axis)
    gathered = jax.tree.map(lambda a: lax.all_gather(a, axis), part)
    state = jax.tree.map(lambda a, e: jnp.zeros_like(a) + jnp.asarray(e, a.dtype), part, identity)

    def one(hop, state):
        return combine(
            state, jax.tree.map(lambda a: lax.dynamic_index_in_dim(a, hop, 0, False), gathered)
        )

    return lax.fori_loop(0, place, one, state)


def passed_along(block, axis, distance):
    devices = range(lax.axis_size(axis))
    route = [(i - distance, i) for i in devices if i - distance in devices]
    return lax.ppermute(block, axis, route)


def conv_rows(before, pre_rows, kernel):
    extended = jnp.concatenate([before, pre_rows], axis=0)
    accum = jnp.zeros(pre_rows.shape, jnp.float32)
    for offset in range(kernel.shape[0]):
        accum = accum + kernel[offset][None, :] * extended[
            offset : offset + pre_rows.shape[0]
        ].astype(jnp.float32)
    return jax.nn.silu(accum).astype(jnp.bfloat16)


def block_state(inputs, b_rows, step_size, log_decay):
    cumul = jnp.cumsum(log_decay, axis=0)
    weights_in = jnp.exp(cumul[-1][None, :] - cumul) * step_size
    weighted = (weights_in[:, :, None] * inputs.astype(jnp.float32)).astype(jnp.bfloat16)
    contrib = jnp.einsum("shp,sn->hpn", weighted, b_rows, preferred_element_type=jnp.float32)
    return (cumul, contrib)


def block_output(inputs, b_rows, c_rows, step_size, cumul, carried, skip):
    length = inputs.shape[0]
    scores = jnp.dot(c_rows, b_rows.T, preferred_element_type=jnp.float32)
    log_gaps = cumul.T[:, :, None] - cumul.T[:, None, :]
    causal = jnp.arange(length)[:, None] >= jnp.arange(length)[None, :]
    mixing = (
        scores[None] * jnp.exp(jnp.where(causal[None], log_gaps, -1e30)) * step_size.T[:, None, :]
    ).astype(jnp.bfloat16)
    output = jnp.einsum("hts,shp->thp", mixing, inputs, preferred_element_type=jnp.float32)
    output = output + jnp.exp(cumul)[:, :, None] * jnp.einsum(
        "tn,hpn->thp", c_rows.astype(jnp.float32), carried, precision=lax.Precision.HIGHEST
    )
    return output + skip[None, :, None] * inputs.astype(jnp.float32)


def cross_slabs(decay_total, final_state):

    def combine(earlier, later):
        return (earlier[0] * later[0], later[0][:, None, None] * earlier[1] + later[1])

    identity = (jnp.ones_like(decay_total), jnp.zeros_like(final_state))
    result = entering((decay_total, final_state), "ctx", combine, identity)
    return result[1]


def shards(
    tokens,
    x_weight,
    z_weight,
    bc_weight,
    dt_weight,
    conv_x,
    conv_bc,
    dt_bias,
    decay_rate,
    skip,
    norm_gain,
):
    row_count = tokens.shape[0]
    inner_local = x_weight.shape[1]
    heads_local = dt_weight.shape[1]
    head_size = inner_local // heads_local
    state_size = bc_weight.shape[1] // 2
    rim_rows = conv_x.shape[0] - 1

    def add_piece(piece):
        return jnp.dot(tokens, piece, preferred_element_type=jnp.float32)

    def add_pieces(pieces):
        return tuple((add_piece(piece) for piece in pieces))

    x_sum, z_sum = add_pieces(
        (
            lax.all_gather(x_weight, "ctx", axis=0, tiled=True),
            lax.all_gather(z_weight, "ctx", axis=0, tiled=True),
        )
    )
    bc_sum, dt_raw = add_pieces(
        (
            lax.all_gather(bc_weight, "ctx", axis=0, tiled=True),
            lax.all_gather(dt_weight, "ctx", axis=0, tiled=True),
        )
    )
    x_in = x_sum.astype(jnp.bfloat16)
    gate = z_sum.astype(jnp.bfloat16)
    bc_in = bc_sum.astype(jnp.bfloat16)
    x_before, bc_before = passed_along(
        (x_in[row_count - rim_rows :], bc_in[row_count - rim_rows :]), "ctx", 1
    )
    x_conv = conv_rows(x_before, x_in, conv_x)
    bc_conv = conv_rows(bc_before, bc_in, conv_bc)
    b_rows = bc_conv[:, :state_size]
    c_rows = bc_conv[:, state_size:]
    step_size = jax.nn.softplus(dt_raw + dt_bias[None, :])
    log_decay = -decay_rate[None, :] * step_size
    blocks = row_count // GROUP
    pieces = (
        x_conv.reshape(blocks, GROUP, heads_local, head_size),
        b_rows.reshape(blocks, GROUP, state_size),
        c_rows.reshape(blocks, GROUP, state_size),
        step_size.reshape(blocks, GROUP, heads_local),
        log_decay.reshape(blocks, GROUP, heads_local),
    )
    zero_state = jnp.zeros((heads_local, head_size, state_size), jnp.float32)
    zero_decay = jnp.zeros((heads_local,), jnp.float32)

    def run_outputs(carried, piece):
        inputs, b_block, c_block, step_block, decay_block = piece
        cumul, contrib = block_state(inputs, b_block, step_block, decay_block)
        output = block_output(inputs, b_block, c_block, step_block, cumul, carried, skip)
        return (jnp.exp(cumul[-1])[:, None, None] * carried + contrib, output)

    def run_states(carry, piece):
        carried, decay_sum = carry
        cumul, contrib = block_state(piece[0], piece[1], piece[3], piece[4])
        return (
            (jnp.exp(cumul[-1])[:, None, None] * carried + contrib, decay_sum + cumul[-1]),
            None,
        )

    (final_state, decay_sum), _ = lax.scan(run_states, (zero_state, zero_decay), pieces)
    incoming = cross_slabs(jnp.exp(decay_sum), final_state)
    _, outputs = lax.scan(run_outputs, incoming, pieces)
    ssm_out = outputs.reshape(row_count, heads_local, head_size)
    gated = ssm_out.reshape(row_count, inner_local) * jax.nn.silu(gate.astype(jnp.float32))
    squares = lax.psum(jnp.sum(gated * gated, axis=1), "head")
    scale = lax.rsqrt(squares / (inner_local * lax.axis_size("head")) + 1e-05)
    return (gated * scale[:, None] * norm_gain[None, :]).astype(jnp.bfloat16)


def solution(mesh):
    placed = (
        P("ctx", None),
        P("ctx", "head"),
        P("ctx", "head"),
        P("ctx", None),
        P("ctx", "head"),
        P(None, "head"),
        P(),
        P("head"),
        P("head"),
        P("head"),
        P("head"),
    )
    return jax.shard_map(
        shards, mesh=mesh, in_specs=placed, out_specs=P("ctx", "head"), check_vma=False
    )
```

profile of v0, /device:TPU:6, one launch (start us, length us, event | category | flops | bytes accessed | tf_op | source)
XLA Modules:
  0.0 390.5 jit_solution(12681157152801210353)
XLA Ops:
  8.7 26.1 %all_gather.24 = bf16[4096,32]{0,1:T(8,128)(2,1)S(1)} all-gather(bf16[128,32]{0,1:T(8,128)(2,1)} %param.21), channel_id=1, replica_groups=mesh['ctx'=32,'head'=4] {'ctx'}, dimensions={0}, use_global_device_ids=true | all-gather | bytes 270336 | tf_op jit(solution)/shard_map/all_gather | solution.py:106
  34.8 3.6 broadcast_multiply_fusion
  39.0 16.9 %all-gather.9.cloned.1.call-done = bf16[4096,256]{1,0:T(8,128)(2,1)} async-done(((bf16[128,256]{1,0:T(8,128)(2,1)}), bf16[4096,256]{1,0:T(8,128)(2,1)}) %all-gather.9.cloned.1.call-update) | async-done | bytes 2097168 | tf_op jit(solution)/shard_map/all_gather | solution.py:105
  56.0 4.1 %convolution_convert_fusion.2 = bf16[512,256]{1,0:T(8,128)(2,1)S(1)} fusion(bf16[512,4096]{1,0:T(8,128)(2,1)} %param.17, bf16[4096,256]{1,0:T(8,128)(2,1)} %all-gather.9.cloned.1.call-done), kind=kOutput, calls=%fused_computation.80 | convolution fusion | flops 1073872896 | bytes 6553600 | tf_op jit(solution)/shard_map/dot_general | solution.py:92
  60.1 2.2 collective-permute-start.1
  62.3 0.8 collective-permute-done.1
  63.4 66.7 %all-gather.7.cloned.1.call-done = bf16[4096,2048]{1,0:T(8,128)(2,1)} async-done(((bf16[128,2048]{1,0:T(8,128)(2,1)}), bf16[4096,2048]{1,0:T(8,128)(2,1)}) %all-gather.7.cloned.1.call-update) | async-done | bytes 16777232 | tf_op jit(solution)/shard_map/all_gather | solution.py:99
  130.1 13.6 %convolution_convert_fusion.1 = bf16[512,2048]{1,0:T(8,128)(2,1)S(1)} fusion(bf16[512,4096]{1,0:T(8,128)(2,1)} %param.17, bf16[4096,2048]{1,0:T(8,128)(2,1)} %all-gather.7.cloned.1.call-done), kind=kOutput, calls=%fused_computation.74 | convolution fusion | flops 8590983168 | bytes 23068672 | tf_op jit(solution)/shard_map/dot_general | solution.py:92
  143.7 2.2 collective-permute-start
  145.9 0.8 collective-permute-done
  146.7 2.9 multiply_convert_fusion.7
  149.6 5.3 %reshape.111 = bf16[2,256,32,64]{3,2,1,0:T(8,128)(2,1)} reshape(bf16[512,2048]{1,0:T(8,128)(2,1)S(1)} %multiply_convert_fusion.7) | data formatting | bytes 4194304 | tf_op jit(solution)/shard_map/reshape | solution.py:123
  154.9 4.9 %copy.58 = bf16[2,256,32,64]{1,3,2,0:T(8,128)(2,1)S(1)} copy(bf16[2,256,32,64]{3,2,1,0:T(8,128)(2,1)} %reshape.111) | data formatting | bytes 4194304
  159.8 5.0 %while.39 = (s32[]{:T(128)}, f32[32,64,128]{2,1,0:T(8,128)S(1)}, f32[32]{0:T(128)S(1)}, f32[2,256,32]{1,2,0:T(8,128)}, f32[2,256,32]{1,2,0:T(8,128)S(1)}, /*inde...) while((s32[]{:T(128)}, f32[32,64,128]{2,1,0:T(8,128)S(1)}, ...), condition=%wide.region_3.4_spmd.clone, body=%wide.region_0.3_spmd.clone.sunk | while | flops 137650336 | bytes 3544188 | solution.py:146
  159.8 0.8 copy_bitcast_fusion.10
  162.3 0.8 copy_bitcast_fusion.10
  164.9 1.0 copy-done
  167.8 66.7 %all-reduce = f32[1024]{0:T(1024)S(1)} all-reduce(f32[1024]{0:T(1024)S(1)} %exponential_dynamic-update-slice_fusion), channel_id=2, replica_groups=mesh['ctx'=32,'head'=4] {'ctx'}, use_global_device_ids=true, to_apply=%add | all-reduce | flops 1024 | bytes 8192
  234.6 48.0 %all-gather.13.cloned.1.call-done = f32[1024,64,128]{2,1,0:T(8,128)} async-done(((f32[32,64,128]{2,1,0:T(8,128)}), f32[1024,64,128]{2,1,0:T(8,128)}) %all-gather.13.cloned.1.call-update) | async-done | bytes 33554448 | tf_op jit(solution)/shard_map/all_gather | solution.py:11
  283.4 15.6 %while.38 = (s32[]{:T(128)}, f32[32,64,128]{2,1,0:T(8,128)S(1)}, f32[2,256,32,64]{1,3,2,0:T(8,128)}, f32[2,256,32]{1,2,0:T(8,128)}, f32[2,256,32]{1,2,0:T(8,128)...) while((s32[]{:T(128)}, f32[32,64,128]{2,1,0:T(8,128)S(1)}, ...), condition=%wide.region_9.10_spmd, body=%wide.region_6.9_spmd.sunk | while | flops 1241079936 | bytes 14097793 | solution.py:148
  283.4 0.8 copy_bitcast_fusion.8
  285.5 1.0 fusion.77
  286.6 4.0 %bitcast_dynamic-update-slice_fusion.2 = f32[2,256,32,64]{1,3,2,0:T(8,128)} fusion(f32[2,256,32,64]{1,3,2,0:T(8,128)} %get-tuple-element.499, s32[]{:T(128)} %get-tuple-element.497, f32[256,32,64]{0,2,1:T(8,128)S(1)} %fusion.77, f32[32,256]{1,0:T(8,128)S(1)} %dynamic-slice_bitcast_fusion.12, f32[32,256]{1,0:T(8,128)S(1)} %get-tuple-element.421, ...), kind=kOutput, calls=%fused_computation.10.clone.1 | convolution fusion | flops 281542656 | bytes 6751744 | tf_op jit(solution)/shard_map/while/body/eval_jaxpr/hts,shp->thp/dot_general | solution.py:54
  291.2 0.8 copy_bitcast_fusion.8
  293.3 1.0 fusion.77
  294.4 4.0 %bitcast_dynamic-update-slice_fusion.2 = f32[2,256,32,64]{1,3,2,0:T(8,128)} fusion(f32[2,256,32,64]{1,3,2,0:T(8,128)} %get-tuple-element.499, s32[]{:T(128)} %get-tuple-element.497, f32[256,32,64]{0,2,1:T(8,128)S(1)} %fusion.77, f32[32,256]{1,0:T(8,128)S(1)} %dynamic-slice_bitcast_fusion.12, f32[32,256]{1,0:T(8,128)S(1)} %get-tuple-element.421, ...), kind=kOutput, calls=%fused_computation.10.clone.1 | convolution fusion | flops 281542656 | bytes 6751744 | tf_op jit(solution)/shard_map/while/body/eval_jaxpr/hts,shp->thp/dot_general | solution.py:54
  299.0 9.1 %copy.64 = f32[2,256,32,64]{3,2,1,0:T(8,128)} copy(f32[2,256,32,64]{1,3,2,0:T(8,128)} %get-tuple-element.137) | data formatting | bytes 8388608 | tf_op jit(solution)/shard_map/reshape;reshape | solution.py:150
  308.2 7.8 %reshape.110 = f32[512,2048]{1,0:T(8,128)} reshape(f32[2,256,32,64]{3,2,1,0:T(8,128)} %copy.64) | data formatting | bytes 8388608 | tf_op jit(solution)/shard_map/reshape;reshape | solution.py:150
  316.0 40.4 %all-gather.11.cloned.1.call-done = bf16[4096,2048]{1,0:T(8,128)(2,1)} async-done(((bf16[128,2048]{1,0:T(8,128)(2,1)}), bf16[4096,2048]{1,0:T(8,128)(2,1)}) %all-gather.11.cloned.1.call-update) | async-done | bytes 16777232 | tf_op jit(solution)/shard_map/all_gather | solution.py:100
  356.4 16.2 %multiply_reduce_fusion = (f32[512]{0:T(512)S(1)}, f32[512,2048]{1,0:T(8,128)}) fusion(f32[512,2048]{1,0:T(8,128)} %reshape.110, bf16[512,4096]{1,0:T(8,128)(2,1)} %param.17, bf16[4096,2048]{1,0:T(8,128)(2,1)} %all-gather.11.cloned.1.call-done), kind=kOutput, calls=%fused_computation.71 | convolution fusion | flops 8599371776 | bytes 29362176 | tf_op jit(solution)/shard_map/dot_general | solution.py:92
  372.6 7.5 %psum.7 = f32[512]{0:T(512)S(1)} all-reduce(f32[512]{0:T(512)S(1)} %get-tuple-element.286), channel_id=1, replica_groups=mesh['ctx'=32,'head'=4] {'head'}, use_global_device_ids=true, to_apply=%region_11.12 | all-reduce | flops 512 | bytes 4096 | tf_op jit(solution)/shard_map/psum | solution.py:151
  380.1 3.9 %multiply_convert_fusion.6 = bf16[512,2048]{1,0:T(8,128)(2,1)} fusion(f32[512,2048]{1,0:T(8,128)} %get-tuple-element.287, f32[2048]{0:T(1024)S(1)} %copy-done.2, f32[512]{0:T(512)S(1)} %add_rsqrt_fusion), kind=kLoop, calls=%fused_computation.70 | loop fusion | flops 3145728 | bytes 6301696 | tf_op jit(solution)/shard_map/convert_element_type | solution.py:153
  (79 shorter events, 12.8 us)
Async XLA Ops:
  6.5 32.5 %copy-start.1 = (f32[4,2048]{1,0:T(4,128)S(1)}, f32[4,2048]{1,0:T(4,128)}, u32[]{:S(2)}) copy-start(f32[4,2048]{1,0:T(4,128)} %param.22) | copy-start | bytes 98308
  6.5 49.4 %all-gather.9.cloned.1.call-start = ((), (), s32[]{:S(2)}) async-start(), calls=%async_computation.1 | async-start | bytes 2162688 | tf_op jit(solution)/shard_map/all_gather | solution.py:105
  7.3 122.9 %all-gather.7.cloned.1.call-start = ((), (), s32[]{:S(2)}) async-start(), calls=%async_computation | async-start | bytes 17301504 | tf_op jit(solution)/shard_map/all_gather | solution.py:99
  8.0 274.6 %all-gather.13.cloned.1.call-start = ((), (), s32[]{:S(2)}) async-start(), calls=%async_computation.3 | async-start | bytes 34603008 | tf_op jit(solution)/shard_map/all_gather | solution.py:11
  38.4 23.9 %copy-start.3 = (f32[4,256]{1,0:T(4,128)S(1)}, f32[4,256]{1,0:T(4,128)}, u32[]{:S(2)}) copy-start(f32[4,256]{1,0:T(4,128)} %param.23) | copy-start | bytes 12292
  60.1 3.0 collective-permute-start.1
  143.7 3.0 collective-permute-start
  159.8 6.7 %copy-start.5 = (u32[128]{0:T(128)S(1)}, u32[128]{0:T(128)}, u32[]{:S(2)}) copy-start(u32[128]{0:T(128)} %constant.76) | copy-start | bytes 1540
  164.8 1.0 copy-start
  165.8 190.6 %all-gather.11.cloned.1.call-start = ((), (), s32[]{:S(2)}) async-start(), calls=%async_computation.2 | async-start | bytes 17301504 | tf_op jit(solution)/shard_map/all_gather | solution.py:100
  282.8 0.7 copy-start.4
  316.0 64.1 %copy-start.2 = (f32[2048]{0:T(1024)S(1)}, f32[2048]{0:T(1024)}, u32[]{:S(2)}) copy-start(f32[2048]{0:T(1024)} %param.27) | copy-start | bytes 24580
Sparse Core Ops, SparseCore 0:
  9.6 46.3 all-gather.8
  58.2 71.8 all-gather.6
  166.0 116.6 all-gather.12
  284.8 71.6 all-gather.10
where the time goes:
time: 396 us; the launch traced here: 391 us
  waiting for transfers between devices  176 us (44%)
  blocking collectives  100 us (25%)
  matrix products  50.2 us (13%)
  local copies, waits for them, and re-layouts  34.7 us (9%)
  between operations  14 us (4%)
  other arithmetic  11 us (3%)
  starting transfers between devices  4.45 us (1%)
    unnamed x1, blocking collectives  66.7 us
    all_gather x1, waiting for transfers between devices, shards(): lax.all_gather(x_weight, 'ctx', axis=0, tiled=True)  66.7 us
    all_gather x1, waiting for transfers between devices, entering(): gathered = jax.tree.map(lambda a: lax.all_gather(a, axis), part)  48 us
    all_gather x1, waiting for transfers between devices, shards(): lax.all_gather(z_weight, 'ctx', axis=0, tiled=True)  40.4 us
    dot_general x4, matrix products, add_piece(): return jnp.dot(tokens, piece, preferred_element_type=jnp.float32)  37.5 us
    all_gather x1, blocking collectives, shards(): lax.all_gather(dt_weight, 'ctx', axis=0, tiled=True)  26.1 us
    another operation x2, local copies, waits for them, and re-layouts, shards(): ssm_out.reshape(row_count, inner_local)  17 us
    all_gather x1, waiting for transfers between devices, shards(): lax.all_gather(bc_weight, 'ctx', axis=0, tiled=True)  16.9 us
  transfers between devices with their start and end apart: 6, of which 6 were waited for; matrix products, arithmetic and copies ran while one was open for 11% of the time, Pallas kernels for 0%

commit v1 on v0

v1 whole, which is shorter than its diff:
```python
import jax
import jax.numpy as jnp
from jax import lax
from jax.experimental import pallas as pl
from jax.experimental.pallas import tpu as pltpu
from jax.sharding import Mesh, PartitionSpec as P

GROUP = 256
HALO = 16
LANES = 128
HEAD = 64
F32 = jnp.float32
BF16 = jnp.bfloat16


def swap_cores(a):
    return lax.ppermute(a, "core", [(0, 1), (1, 0)])


def along_chips(a, distance):
    chips = lax.axis_size("z") * lax.axis_size("y")
    return lax.ppermute(a, ("z", "y"), [(i, i + distance) for i in range(chips - distance)])


def in_core_order(core, mine, other, axis):
    first = jnp.where(core == 0, mine, other)
    second = jnp.where(core == 0, other, mine)
    return jnp.concatenate([first, second], axis=axis)


def expand_heads(values, width):
    high = values.astype(BF16)
    rest = values - high.astype(F32)
    middle = rest.astype(BF16)
    low = (rest - middle.astype(F32)).astype(BF16)
    row = lax.broadcasted_iota(jnp.int32, (LANES, width), 0)
    col = lax.broadcasted_iota(jnp.int32, (LANES, width), 1)
    spread = ((col >= row * HEAD) & (col < row * HEAD + HEAD)).astype(BF16)
    dot = lambda part: jnp.dot(part, spread, preferred_element_type=F32)
    return dot(high) + dot(middle) + dot(low)


def silu(a):
    return a * (1.0 / (1.0 + jnp.exp(-a)))


def conv_block(ref, kernel_ref, start):
    taps = kernel_ref.shape[0]
    rows = ref[pl.ds(start, GROUP + HALO), :].astype(F32)
    first = HALO - (taps - 1)
    accum = kernel_ref[0:1, :] * rows[first : first + GROUP]
    for tap in range(1, taps):
        accum = accum + kernel_ref[tap : tap + 1, :] * rows[first + tap : first + tap + GROUP]
    return silu(accum).astype(BF16)


def states_kernel(
    x_ref, bc_ref, dt_ref, conv_x_ref, conv_bc_ref, bias_ref, rate_ref,
    xc_ref, bcc_ref, cum_ref, cum_slab_ref, cum_t_ref, step_t_ref, entering_ref, final_ref,
    state, total,
):
    block = pl.program_id(0)
    start = pl.multiple_of(block * GROUP, GROUP)
    width = x_ref.shape[1]
    heads = cum_t_ref.shape[0]

    @pl.when(block == 0)
    def _():
        state[...] = jnp.zeros_like(state)
        total[...] = jnp.zeros_like(total)

    xc = conv_block(x_ref, conv_x_ref, start)
    xc_ref[...] = xc
    bcc = conv_block(bc_ref, conv_bc_ref, start)
    bcc_ref[...] = bcc
    raw = dt_ref[pl.ds(start + HALO, GROUP), :] + bias_ref[...]
    step = jnp.maximum(raw, 0.0) + jnp.log1p(jnp.exp(-jnp.abs(raw)))
    log_decay = -rate_ref[...] * step
    row = lax.broadcasted_iota(jnp.int32, (GROUP, GROUP), 0)
    col = lax.broadcasted_iota(jnp.int32, (GROUP, GROUP), 1)
    lower = (row >= col).astype(F32)
    cum = jnp.dot(lower, log_decay, preferred_element_type=F32, precision=lax.Precision.HIGHEST)
    last = cum[GROUP - 1 : GROUP, :]
    cum_ref[...] = cum
    cum_slab_ref[...] = cum + total[0:1, :]
    cum_t_ref[...] = cum.T[:heads, :]
    step_t_ref[...] = step.T[:heads, :]
    entering_ref[0] = state[...].astype(BF16)
    weights_in = expand_heads(jnp.exp(last - cum) * step, width)
    weighted = (weights_in * xc.astype(F32)).astype(BF16)
    contrib = lax.dot_general(
        bcc[:, :LANES], weighted, (((0,), (0,)), ((), ())), preferred_element_type=F32
    )
    decay = expand_heads(jnp.broadcast_to(jnp.exp(last), (8, LANES)), width)
    state[...] = state[...] * decay[0:1] + contrib
    total[...] = total[...] + jnp.broadcast_to(last, total.shape)

    @pl.when(block == pl.num_programs(0) - 1)
    def _():
        final_ref[:LANES, :] = state[...]
        final_ref[LANES:, :] = expand_heads(jnp.exp(total[...]), width)


def outputs_kernel(xc_ref, bcc_ref, cum_ref, cum_t_ref, step_t_ref, entering_ref, skip_ref, out_ref):
    width = xc_ref.shape[1]
    b_rows, c_rows = bcc_ref[:, :LANES], bcc_ref[:, LANES:]
    scores = lax.dot_general(c_rows, b_rows, (((1,), (1,)), ((), ())), preferred_element_type=F32)
    row = lax.broadcasted_iota(jnp.int32, (GROUP, GROUP), 0)
    col = lax.broadcasted_iota(jnp.int32, (GROUP, GROUP), 1)
    scores = jnp.where(row >= col, scores, 0.0)
    cum = cum_ref[...]
    grown = expand_heads(jnp.exp(cum), width)
    out_ref[...] = grown * jnp.dot(c_rows, entering_ref[0], preferred_element_type=F32)
    lane = lax.broadcasted_iota(jnp.int32, (GROUP, LANES), 1)

    def mixing(head):
        gaps = cum[:, head : head + 1] - cum_t_ref[head : head + 1, :]
        return (
            scores * jnp.exp(jnp.minimum(gaps, 0.0)) * step_t_ref[head : head + 1, :]
        ).astype(BF16)

    for pair in range(width // LANES):
        lanes = slice(pair * LANES, (pair + 1) * LANES)
        inputs = xc_ref[:, lanes]
        zero = jnp.zeros_like(inputs)
        both = jnp.concatenate([mixing(2 * pair), mixing(2 * pair + 1)], axis=1)
        stacked = jnp.concatenate(
            [jnp.where(lane < HEAD, inputs, zero), jnp.where(lane < HEAD, zero, inputs)], axis=0
        )
        out_ref[:, lanes] = (
            out_ref[:, lanes]
            + jnp.dot(both, stacked, preferred_element_type=F32)
            + skip_ref[:, lanes] * inputs.astype(F32)
        )


def gate_kernel(
    tokens_ref, weight_ref, local_ref, bcc_ref, cum_ref, incoming_ref, gated_ref, squares_ref, accum
):
    step = pl.program_id(0)
    rows, width = accum.shape
    product = jnp.dot(tokens_ref[HALO:, :], weight_ref[...], preferred_element_type=F32)

    @pl.when(step == 0)
    def _():
        accum[...] = product

    @pl.when(step > 0)
    def _():
        accum[...] = accum[...] + product

    @pl.when(step == pl.num_programs(0) - 1)
    def _():
        for block in range(rows // GROUP):
            part = slice(block * GROUP, (block + 1) * GROUP)
            gate = accum[part, :].astype(BF16).astype(F32)
            grown = expand_heads(jnp.exp(cum_ref[part, :]), width)
            carried = jnp.dot(bcc_ref[part, LANES:], incoming_ref[...], preferred_element_type=F32)
            gated = (local_ref[part, :] + grown * carried) * silu(gate)
            gated_ref[part, :] = gated.astype(BF16)
            squares_ref[part, :] = jnp.sum(gated * gated, axis=1, keepdims=True)


def whole(shape):
    return pl.BlockSpec(shape, lambda i: (0,) * len(shape))


def rows_of(width):
    return pl.BlockSpec((GROUP, width), lambda i: (i, 0))


def local_states(x_in, bc_in, dt_raw, conv_x, conv_bc, bias, rate, heads):
    rows, width = x_in.shape[0] - HALO, x_in.shape[1]
    blocks = rows // GROUP
    shape = jax.ShapeDtypeStruct
    by_lane = pl.BlockSpec((heads, GROUP), lambda i: (0, i))
    return pl.pallas_call(
        states_kernel,
        grid=(blocks,),
        in_specs=[whole(a.shape) for a in (x_in, bc_in, dt_raw, conv_x, conv_bc, bias, rate)],
        out_specs=[
            rows_of(width), rows_of(2 * LANES), rows_of(LANES), rows_of(LANES), by_lane, by_lane,
            pl.BlockSpec((1, LANES, width), lambda i: (i, 0, 0)), whole((LANES + 8, width)),
        ],
        out_shape=[
            shape((rows, width), BF16), shape((rows, 2 * LANES), BF16),
            shape((rows, LANES), F32), shape((rows, LANES), F32),
            shape((heads, rows), F32), shape((heads, rows), F32),
            shape((blocks, LANES, width), BF16), shape((LANES + 8, width), F32),
        ],
        scratch_shapes=[pltpu.VMEM((LANES, width), F32), pltpu.VMEM((8, LANES), F32)],
        compiler_params=pltpu.CompilerParams(vmem_limit_bytes=40 * 2**20),
        cost_estimate=pl.CostEstimate(flops=4 * 10**9, bytes_accessed=10 * 2**20, transcendentals=0),
        name="states",
    )(x_in, bc_in, dt_raw, conv_x, conv_bc, bias, rate)


def local_outputs(xc, bcc, cum, cum_t, step_t, entering, skip):
    rows, width = xc.shape
    heads = cum_t.shape[0]
    by_lane = pl.BlockSpec((heads, GROUP), lambda i: (0, i))
    return pl.pallas_call(
        outputs_kernel,
        grid=(rows // GROUP,),
        in_specs=[
            rows_of(width), rows_of(2 * LANES), rows_of(LANES), by_lane, by_lane,
            pl.BlockSpec((1, LANES, width), lambda i: (i, 0, 0)), whole((1, width)),
        ],
        out_specs=rows_of(width),
        out_shape=jax.ShapeDtypeStruct((rows, width), F32),
        compiler_params=pltpu.CompilerParams(vmem_limit_bytes=40 * 2**20),
        cost_estimate=pl.CostEstimate(flops=10**10, bytes_accessed=10 * 2**20, transcendentals=4 * 2**20),
        name="outputs",
    )(xc, bcc, cum, cum_t, step_t, entering, skip)


def gate_outputs(tokens, weight, local, bcc, cum_slab, incoming):
    rows, width = local.shape
    depth = 512
    return pl.pallas_call(
        gate_kernel,
        grid=(weight.shape[0] // depth,),
        in_specs=[
            pl.BlockSpec((tokens.shape[0], depth), lambda i: (0, i)),
            pl.BlockSpec((depth, width), lambda i: (i, 0)),
            whole(local.shape), whole(bcc.shape), whole(cum_slab.shape), whole(incoming.shape),
        ],
        out_specs=[whole((rows, width)), whole((rows, 1))],
        out_shape=[
            jax.ShapeDtypeStruct((rows, width), BF16), jax.ShapeDtypeStruct((rows, 1), F32),
        ],
        scratch_shapes=[pltpu.VMEM((rows, width), F32)],
        compiler_params=pltpu.CompilerParams(vmem_limit_bytes=48 * 2**20),
        cost_estimate=pl.CostEstimate(flops=10**10, bytes_accessed=20 * 2**20, transcendentals=0),
        name="gate",
    )(tokens, weight, local, bcc, cum_slab, incoming)


def entering_state(final):
    window, decay = final[:LANES], final[LANES : LANES + 1]
    state, state_decay = None, None
    chips = lax.axis_size("z") * lax.axis_size("y")
    distance = 1
    while distance < chips:
        high = decay.astype(BF16)
        low = (decay - high.astype(F32)).astype(BF16)
        pad = jnp.zeros((HALO - 2, decay.shape[1]), BF16)
        sent = jnp.concatenate([window.astype(BF16), high, low, pad], axis=0)
        got = along_chips(sent, distance).astype(F32)
        got_decay = got[LANES : LANES + 1] + got[LANES + 1 : LANES + 2]
        got = got[:LANES]
        if state is None:
            state, state_decay = got, got_decay
        else:
            state, state_decay = got * state_decay + state, got_decay * state_decay
        window, decay = got * decay + window, got_decay * decay
        distance *= 2
    return state.astype(BF16)


def shards(
    tokens, x_weight, z_weight, bc_weight, dt_weight, conv_x, conv_bc, dt_bias, decay_rate, skip,
    norm_gain,
):
    core = lax.axis_index("core")
    width = x_weight.shape[1] // 2
    heads = dt_weight.shape[1] // 2

    def mine(a, axis):
        size = a.shape[axis] // 2
        return lax.dynamic_slice_in_dim(a, core * size, size, axis)

    def others(a, axis):
        size = a.shape[axis] // 2
        return lax.dynamic_slice_in_dim(a, (1 - core) * size, size, axis)

    def paired(a):
        return in_core_order(core, mine(a, 1), swap_cores(others(a, 1)), 0)

    gather = lambda a: lax.all_gather(a, ("z", "y"), axis=0, tiled=True)
    early = jnp.concatenate(
        [paired(x_weight), paired(bc_weight), jnp.pad(paired(dt_weight), ((0, 0), (0, LANES - heads)))],
        axis=1,
    )
    early = gather(early)
    z_whole = gather(paired(z_weight))
    slabs = in_core_order(core, tokens, swap_cores(tokens), 0)
    extended = jnp.concatenate([along_chips(slabs[-HALO:], 1), slabs], axis=0)

    x_in = jnp.dot(extended, early[:, :width], preferred_element_type=F32).astype(BF16)
    small = jnp.dot(extended, early[:, width:], preferred_element_type=F32)
    bc_half = small[:, :LANES].astype(BF16)
    bc_in = in_core_order(core, bc_half, swap_cores(bc_half), 1)
    dt_raw = small[:, LANES:]

    def per_lane(a):
        return jnp.pad(mine(a, 0), (0, LANES - heads))[None, :]

    xc, bcc, cum, cum_slab, cum_t, step_t, entering, final = local_states(
        x_in, bc_in, dt_raw, mine(conv_x, 1), conv_bc, per_lane(dt_bias), per_lane(decay_rate), heads
    )
    incoming = entering_state(final)
    skip_lanes = jnp.repeat(mine(skip, 0), HEAD)[None, :]
    local = local_outputs(xc, bcc, cum, cum_t, step_t, entering, skip_lanes)
    gated, squares = gate_outputs(extended, z_whole, local, bcc, cum_slab, incoming)

    summed = lax.psum(squares[:, 0], ("core", "x"))
    inner = 2 * width * lax.axis_size("x")
    scale = lax.rsqrt(mine(summed, 0) / inner + 1e-05)
    full = in_core_order(core, mine(gated, 0), swap_cores(others(gated, 0)), 1)
    return (full.astype(F32) * scale[:, None] * norm_gain[None, :]).astype(BF16)


def solution(mesh):
    fine = Mesh(mesh.devices.reshape(4, 4, 2, 4), ("z", "y", "core", "x"))
    ctx = ("z", "y", "core")
    placed = (
        P(ctx, None),
        P(ctx, "x"),
        P(ctx, "x"),
        P(ctx, None),
        P(ctx, "x"),
        P(None, "x"),
        P(),
        P("x"),
        P("x"),
        P("x"),
        P("x"),
    )
    return jax.shard_map(
        shards, mesh=fine, in_specs=placed, out_specs=P(ctx, "x"), check_vma=False
    )
```

time: 396 us -> 252 us (0.64)
  blocking collectives: 100 us -> 12.9 us
  waiting for transfers between devices: 176 us -> 99.9 us
  Pallas kernels: 0 us -> 38 us
  matrix products: 50.2 us -> 19.2 us
  local copies, waits for them, and re-layouts: 34.7 us -> 9.42 us
  starting transfers between devices: 4.45 us -> 28.7 us
  other arithmetic: 11 us -> 26 us
    all_gather x4 -> x2, waiting for transfers between devices: 172 us -> 60.7 us  [shards(): gather = lambda a: lax.all_gather(a, ('z', 'y'), axis=0, tiled=True)]
    unnamed x1 -> x0, blocking collectives: 66.7 us -> none
    pallas_call x0 -> x3, Pallas kernels: none -> 38 us  [the longest x1 19.5 us: gate_outputs(): pl.pallas_call(gate_kernel, grid=(weight.shape[0] // depth,), in_specs=[p...]
    ppermute x2 -> x12, waiting for transfers between devices: 1.55 us -> 39.2 us  [the longest x5 32.6 us: along_chips(): lax.ppermute(a, ('z', 'y'), [(i, i + distance) for i in range(chips - dis...]
    dot_general x14 -> x2, matrix products: 50.2 us -> 19.2 us  [the longest x1 12.4 us: shards(): jnp.dot(extended, early[:, :width], preferred_element_type=F32).astype(BF16)]
    all_gather x1 -> x0, blocking collectives: 26.1 us -> none  [shards(): lax.all_gather(dt_weight, 'ctx', axis=0, tiled=True)]
    ppermute x2 -> x12, starting transfers between devices: 4.33 us -> 28.7 us  [the longest x5 27.2 us: along_chips(): lax.ppermute(a, ('z', 'y'), [(i, i + distance) for i in range(chips - dis...]
    another operation x11 -> x2, local copies, waits for them, and re-layouts: 18.9 us -> 0.08 us  [the longest x1 0.08 us: shards(): skip_lanes = jnp.repeat(mine(skip, 0), HEAD)[None, :]]
  transfers between devices with their start and end apart: 6 -> 14, of which waited for: 6 -> 8; matrix products, arithmetic and copies ran while one was open for 11% -> 17% of each run, Pallas kernels for 0% -> 7%
where the time goes in v1:
time: 252 us; the launch traced here: 248 us
  waiting for transfers between devices  99.9 us (40%)
  Pallas kernels  38 us (15%)
  starting transfers between devices  28.7 us (11%)
  other arithmetic  26 us (10%)
  matrix products  19.2 us (8%)
  between operations  13.9 us (6%)
  blocking collectives  12.9 us (5%)
  local copies, waits for them, and re-layouts  9.42 us (4%)
    all_gather x2, waiting for transfers between devices, shards(): gather = lambda a: lax.all_gather(a, ('z', 'y'), axis=0, tiled=True)  60.7 us
    ppermute x5, waiting for transfers between devices, along_chips(): lax.ppermute(a, ('z', 'y'), [(i, i + distance) for i in range(chips - dis...  32.6 us
    ppermute x5, starting transfers between devices, along_chips(): lax.ppermute(a, ('z', 'y'), [(i, i + distance) for i in range(chips - dis...  27.2 us
    pallas_call x1, Pallas kernels, gate_outputs(): pl.pallas_call(gate_kernel, grid=(weight.shape[0] // depth,), in_specs=[p...  19.5 us
    psum x1, blocking collectives, shards(): summed = lax.psum(squares[:, 0], ('core', 'x'))  12.9 us
    dot_general x1, matrix products, shards(): jnp.dot(extended, early[:, :width], preferred_element_type=F32).astype(BF16)  12.4 us
    pallas_call x1, Pallas kernels, local_states(): pl.pallas_call(states_kernel, grid=(blocks,), in_specs=[whole(a.shape) fo...  11.7 us
    select_n x7, other arithmetic, in_core_order(): first = jnp.where(core == 0, mine, other)  10.1 us
  transfers between devices with their start and end apart: 14, of which 8 were waited for; matrix products, arithmetic and copies ran while one was open for 17% of the time, Pallas kernels for 7%

profile of v1, /device:TPU:6, one launch (start us, length us, event | category | flops | bytes accessed | tf_op | source)
XLA Modules:
  0.0 248.0 jit_solution(15551286000059989063)
XLA Ops:
  7.3 1.0 constant_dynamic-slice_fusion.4
  11.7 1.1 broadcast_select_fusion.7
  13.7 1.0 constant_dynamic-slice_fusion.5
  15.3 1.0 collective-permute-done.2
  17.5 5.2 %collective-permute-done = bf16[512,4096]{1,0:T(8,128)(2,1)} collective-permute-done((bf16[512,4096]{1,0:T(8,128)(2,1)}, bf16[512,4096]{1,0:T(8,128)(2,1)}, u32[]{:S(2)}, u32[]{:S(2)}) %collective-permute-start) | collective-permute-done | bytes 4194336 | tf_op jit(solution)/shard_map/ppermute | solution.py:17
  22.6 5.6 %broadcast_select_fusion = (bf16[512,4096]{1,0:T(8,128)(2,1)}, bf16[512,4096]{1,0:T(8,128)(2,1)S(1)}) fusion(bf16[512,4096]{1,0:T(8,128)(2,1)} %param.11, bf16[512,4096]{1,0:T(8,128)(2,1)} %collective-permute-done, pred[]{:T(512)S(6)} %eq.2), kind=kLoop, calls=%fused_computation.4 | loop fusion | flops 4194304 | bytes 16777216 | tf_op jit(solution)/shard_map/jit(_where)/select_n | solution.py:26
  28.2 3.6 %collective-permute-start.1 = (bf16[16,4096]{1,0:T(8,128)(2,1)S(1)}, bf16[16,4096]{1,0:T(8,128)(2,1)S(1)}, u32[]{:S(2)}, u32[]{:S(2)}) collective-permute-start(bf16[16,4096]{1,0:T(8,128)(2,1)S(1)} %slice.73), channel_id=1, source_target_pairs={{0,8},{8,16},{16,24},{24,32},{32,40},{40,48},{48,56},{56,64},{64,7... | collective-permute-start | bytes 393224 | tf_op jit(solution)/shard_map/ppermute | solution.py:22
  31.9 5.8 %collective-permute-done.1 = bf16[16,4096]{1,0:T(8,128)(2,1)S(1)} collective-permute-done((bf16[16,4096]{1,0:T(8,128)(2,1)S(1)}, bf16[16,4096]{1,0:T(8,128)(2,1)S(1)}, u32[]{:S(2)}, u32[]{:S(2)}) %collective-permute-start.1) | collective-permute-done | bytes 131104 | tf_op jit(solution)/shard_map/ppermute | solution.py:22
  37.7 60.7 %all-gather.5.cloned.1.call-done = bf16[4096,1280]{1,0:T(8,128)(2,1)} async-done(((bf16[256,1280]{1,0:T(8,128)(2,1)}), bf16[4096,1280]{1,0:T(8,128)(2,1)}) %all-gather.5.cloned.1.call-update) | async-done | bytes 10485776 | tf_op jit(solution)/shard_map/all_gather | solution.py:280
  98.4 6.8 %fusion.5 = f32[1040,256]{1,0:T(8,128)S(1)} fusion(bf16[4096,1280]{1,0:T(8,128)(2,1)} %all-gather.5.cloned.1.call-done, bf16[512,4096]{1,0:T(8,128)(2,1)} %copy-done.11, bf16[512,4096]{1,0:T(8,128)(2,1)} %get-tuple-element.34, bf16[16,4096]{1,0:T(8,128)(2,1)S(1)} %collective-permute-done.1), kind=kOutput, calls=%fused_computation.7 | convolution fusion | flops 2206597120 | bytes 11681792 | tf_op jit(solution)/shard_map/dot_general | solution.py:291
  105.5 12.4 %fusion.2.x_ref = bf16[1040,1024]{1,0:T(8,128)(2,1)S(1)} fusion(bf16[4096,1280]{1,0:T(8,128)(2,1)} %all-gather.5.cloned.1.call-done, bf16[512,4096]{1,0:T(8,128)(2,1)S(1)} %copy-done.12, bf16[512,4096]{1,0:T(8,128)(2,1)S(1)} %copy-done.13, bf16[16,4096]{1,0:T(8,128)(2,1)S(1)} %collective-permute-done.1), kind=kOutput, calls=%fused_computation.6 | convolution fusion | flops 8750776320 | bytes 19038208 | tf_op jit(solution)/shard_map/dot_general | solution.py:290
  118.1 11.7 %states.1 = (bf16[1024,1024]{1,0:T(8,128)(2,1)S(1)}, bf16[1024,256]{1,0:T(8,128)(2,1)S(1)}, f32[1024,128]{1,0:T(8,128)S(1)}, f32[1024,128]{1,0:T(8,128)S(1)}, f3...) custom-call(bf16[1040,1024]{1,0:T(8,128)(2,1)S(1)} %fusion.2.x_ref, ...), custom_call_target="tpu_custom_call" | custom-call | flops 4000000000 | bytes 10485760 | tf_op jit(solution)/shard_map/states/pallas_call | solution.py:177
  130.1 3.4 %collective-permute-start.7 = (bf16[144,1024]{1,0:T(8,128)(2,1)S(1)}, bf16[144,1024]{1,0:T(8,128)(2,1)S(1)}, u32[]{:S(2)}, u32[]{:S(2)}) collective-permute-start(bf16[144,1024]{1,0:T(8,128)(2,1)S(1)} %maximum_maximum_fusion), channel_id=1, source_target_pairs={{0,8},{8,16},{16,24},{24,32},{32,40},{40,48},{48,56},{56,64},{64,7... | collective-permute-start | bytes 884744 | tf_op jit(solution)/shard_map/ppermute | solution.py:22
  133.5 13.1 %collective-permute-done.7 = bf16[144,1024]{1,0:T(8,128)(2,1)S(1)} collective-permute-done((bf16[144,1024]{1,0:T(8,128)(2,1)S(1)}, bf16[144,1024]{1,0:T(8,128)(2,1)S(1)}, u32[]{:S(2)}, u32[]{:S(2)}) %collective-permute-start.7) | collective-permute-done | bytes 294944 | tf_op jit(solution)/shard_map/ppermute | solution.py:22
  146.8 1.0 fusion.16
  148.6 6.6 %collective-permute-start.8 = (bf16[144,1024]{1,0:T(8,128)(2,1)}, bf16[144,1024]{1,0:T(8,128)(2,1)}, u32[]{:S(2)}, u32[]{:S(2)}) collective-permute-start(bf16[144,1024]{1,0:T(8,128)(2,1)} %maximum_maximum_fusion.1), channel_id=1, source_target_pairs={{0,16},{8,24},{16,32},{24,40},{32,48},{40,56},{48,64},{56,72},{64,... | collective-permute-start | bytes 884744 | tf_op jit(solution)/shard_map/ppermute | solution.py:22
  155.4 12.6 %collective-permute-done.8 = bf16[144,1024]{1,0:T(8,128)(2,1)} collective-permute-done((bf16[144,1024]{1,0:T(8,128)(2,1)}, bf16[144,1024]{1,0:T(8,128)(2,1)}, u32[]{:S(2)}, u32[]{:S(2)}) %collective-permute-start.8) | collective-permute-done | bytes 294944 | tf_op jit(solution)/shard_map/ppermute | solution.py:22
  168.0 1.0 convert_element_type.86
  169.1 1.1 fusion.9
  170.3 7.5 %collective-permute-start.9 = (bf16[144,1024]{1,0:T(8,128)(2,1)S(1)}, bf16[144,1024]{1,0:T(8,128)(2,1)S(1)}, u32[]{:S(2)}, u32[]{:S(2)}) collective-permute-start(bf16[144,1024]{1,0:T(8,128)(2,1)S(1)} %maximum_maximum_fusion.2), channel_id=1, source_target_pairs={{0,32},{8,40},{16,48},{24,56},{32,64},{40,72},{48,80},{56,88},{64,... | collective-permute-start | bytes 884744 | tf_op jit(solution)/shard_map/ppermute | solution.py:22
  177.8 7.2 %pad_maximum_fusion.tokens_ref = bf16[1040,4096]{1,0:T(8,128)(2,1)} fusion(bf16[512,4096]{1,0:T(8,128)(2,1)} %copy-done.11, bf16[512,4096]{1,0:T(8,128)(2,1)} %get-tuple-element.34, bf16[16,4096]{1,0:T(8,128)(2,1)S(1)} %collective-permute-done.1), kind=kLoop, calls=%fused_computation | loop fusion | flops 25559040 | bytes 17039360 | tf_op jit(solution)/shard_map/concatenate | solution.py:288
  185.0 1.0 collective-permute-done.9
  186.4 6.2 %collective-permute-start.10 = (bf16[144,1024]{1,0:T(8,128)(2,1)S(1)}, bf16[144,1024]{1,0:T(8,128)(2,1)S(1)}, u32[]{:S(2)}, u32[]{:S(2)}) collective-permute-start(bf16[144,1024]{1,0:T(8,128)(2,1)S(1)} %maximum_maximum_fusion.3), channel_id=1, source_target_pairs={{0,64},{8,72},{16,80},{24,88},{32,96},{40,104},{48,112},{56,120},{... | collective-permute-start | bytes 884744 | tf_op jit(solution)/shard_map/ppermute | solution.py:22
  192.7 6.8 %outputs.1.local_ref = f32[1024,1024]{1,0:T(8,128)S(1)} custom-call(bf16[1024,1024]{1,0:T(8,128)(2,1)S(1)} %get-tuple-element.15.xc_ref, bf16[1024,256]{1,0:T(8,128)(2,1)S(1)} %copy-done.5, f32[1024,128]{1,0:T(8,128)S(1)} %copy-done.10, f32[16,1024]{1,0:T(8,128)S(1)} %get-tuple-element.18.cum_t_ref, f32[16,1024]{1,0:T(8,128)S(1)} %get-tuple-element.19.step_t_ref, ...), custom_call_target="tpu_custom_call" | custom-call | flops 10000000000 | bytes 10485760 | tf_op jit(solution)/shard_map/outputs/pallas_call | solution.py:202
  199.4 2.0 copy-done.3
  201.7 1.0 copy-done.6
  202.8 1.0 copy-done.8
  203.8 19.5 %gate.1 = (bf16[1024,1024]{1,0:T(8,128)(2,1)S(1)}, f32[1024,1]{1,0:T(8,128)S(1)}) custom-call(bf16[1040,4096]{1,0:T(8,128)(2,1)} %pad_maximum_fusion.tokens_ref, bf16[4096,1024]{1,0:T(8,128)(2,1)} %all-gather.3.cloned.1.call-done.weight_ref, f32[1024,1024]{1,0:T(8,128)} %copy-done.3, bf16[1024,256]{1,0:T(8,128)(2,1)S(1)} %copy-done.6, ...), custom_call_target="tpu_custom_call" | custom-call | flops 10000000000 | bytes 20971520 | tf_op jit(solution)/shard_map/gate/pallas_call | solution.py:220
  223.3 1.0 constant_dynamic-slice_fusion
  224.5 12.9 %psum.7 = f32[1024]{0:T(1024)S(1)} all-reduce(f32[1024]{0:T(1024)S(1)} %reduce), channel_id=1, replica_groups=mesh['z'=4,'y'=4,'core'=2,'x'=4] {'core','x'}, use_global_device_ids=true, to_apply=%region_0.1 | all-reduce | flops 1024 | bytes 8192 | tf_op jit(solution)/shard_map/psum | solution.py:307
  237.5 1.8 broadcast_select_fusion.3
  239.3 1.9 multiply_convert_fusion
  (100 shorter events, 9.7 us)
Async XLA Ops:
  6.5 25.4 %copy-start = (f32[4,2048]{1,0:T(4,128)S(1)}, f32[4,2048]{1,0:T(4,128)}, u32[]{:S(2)}) copy-start(f32[4,2048]{1,0:T(4,128)} %param.16) | copy-start | bytes 98308
  6.5 9.8 %copy-start.17 = (bf16[128,2048]{1,0:T(8,128)(2,1)S(1)}, bf16[128,2048]{1,0:T(8,128)(2,1)}, u32[]{:S(2)}) copy-start(bf16[128,2048]{1,0:T(8,128)(2,1)} %param.13) | copy-start | bytes 1572868
  6.5 10.7 %copy-start.19 = (f32[32]{0:T(128)S(1)}, f32[32]{0:T(128)}, u32[]{:S(2)}) copy-start(f32[32]{0:T(128)} %param.18) | copy-start | bytes 388
  6.5 10.8 %copy-start.20 = (f32[32]{0:T(128)S(1)}, f32[32]{0:T(128)}, u32[]{:S(2)}) copy-start(f32[32]{0:T(128)} %param.19) | copy-start | bytes 388
  6.5 91.8 %all-gather.5.cloned.1.call-start = ((), (), s32[]{:S(2)}) async-start(), calls=%async_computation.1 | async-start | bytes 11141120 | tf_op jit(solution)/shard_map/all_gather | solution.py:280
  7.3 2.3 collective-permute-start.5
  8.3 3.3 %collective-permute-start.3 = (bf16[128,1024]{1,0:T(8,128)(2,1)S(1)}, bf16[128,1024]{1,0:T(8,128)(2,1)S(1)}, u32[]{:S(2)}, u32[]{:S(2)}) collective-permute-start(bf16[128,1024]{1,0:T(8,128)(2,1)S(1)} %constant_dynamic-slice_fusion.4), channel_id=1, source_target_pairs={{0,4},{4,0},{1,5},{5,1},{2,6},{6,2},{3,7},{7,3},{8,12},{12,8},{9,1... | collective-permute-start | bytes 786440 | tf_op jit(solution)/shard_map/ppermute | solution.py:17
  9.7 1.2 collective-permute-start.4
  13.6 188.1 %all-gather.3.cloned.1.call-start = ((), (), s32[]{:S(2)}) async-start(), calls=%async_computation | async-start | bytes 8912896 | tf_op jit(solution)/shard_map/all_gather | solution.py:280
  14.7 1.6 collective-permute-start.2
  14.9 7.7 %collective-permute-start = (bf16[512,4096]{1,0:T(8,128)(2,1)}, bf16[512,4096]{1,0:T(8,128)(2,1)}, u32[]{:S(2)}, u32[]{:S(2)}) collective-permute-start(bf16[512,4096]{1,0:T(8,128)(2,1)} %param.11), channel_id=1, source_target_pairs={{0,4},{4,0},{1,5},{5,1},{2,6},{6,2},{3,7},{7,3},{8,12},{12,8},{9,1... | collective-permute-start | bytes 12582920 | tf_op jit(solution)/shard_map/ppermute | solution.py:17
  28.2 3.6 %copy-start.11 = (bf16[512,4096]{1,0:T(8,128)(2,1)}, bf16[512,4096]{1,0:T(8,128)(2,1)S(1)}, u32[]{:S(2)}) copy-start(bf16[512,4096]{1,0:T(8,128)(2,1)S(1)} %get-tuple-element.35) | copy-start | bytes 12582916
  28.2 9.5 %collective-permute-start.1 = (bf16[16,4096]{1,0:T(8,128)(2,1)S(1)}, bf16[16,4096]{1,0:T(8,128)(2,1)S(1)}, u32[]{:S(2)}, u32[]{:S(2)}) collective-permute-start(bf16[16,4096]{1,0:T(8,128)(2,1)S(1)} %slice.73), channel_id=1, source_target_pairs={{0,8},{8,16},{16,24},{24,32},{32,40},{40,48},{48,56},{56,64},{64,7... | collective-permute-start | bytes 393224 | tf_op jit(solution)/shard_map/ppermute | solution.py:22
  98.4 7.1 %copy-start.12 = (bf16[512,4096]{1,0:T(8,128)(2,1)S(1)}, bf16[512,4096]{1,0:T(8,128)(2,1)}, u32[]{:S(2)}) copy-start(bf16[512,4096]{1,0:T(8,128)(2,1)} %copy-done.11) | copy-start | bytes 12582916
  98.4 7.1 %copy-start.13 = (bf16[512,4096]{1,0:T(8,128)(2,1)S(1)}, bf16[512,4096]{1,0:T(8,128)(2,1)}, u32[]{:S(2)}) copy-start(bf16[512,4096]{1,0:T(8,128)(2,1)} %get-tuple-element.34) | copy-start | bytes 12582916
  105.2 12.9 %copy-start.2 = (f32[4,256]{1,0:T(4,128)S(1)}, f32[4,256]{1,0:T(4,128)}, u32[]{:S(2)}) copy-start(f32[4,256]{1,0:T(4,128)} %conv_bc_ref.1) | copy-start | bytes 12292
  105.2 12.7 %collective-permute-start.6 = (bf16[1040,128]{1,0:T(8,128)(2,1)S(1)}, bf16[1040,128]{1,0:T(8,128)(2,1)S(1)}, u32[]{:S(2)}, u32[]{:S(2)}) collective-permute-start(bf16[1040,128]{1,0:T(8,128)(2,1)S(1)} %slice.138), channel_id=1, source_target_pairs={{0,4},{4,0},{1,5},{5,1},{2,6},{6,2},{3,7},{7,3},{8,12},{12,8},{9,1... | collective-permute-start | bytes 798728 | tf_op jit(solution)/shard_map/ppermute | solution.py:17
  129.9 17.8 %copy-start.4 = (bf16[1024,256]{1,0:T(8,128)(2,1)}, bf16[1024,256]{1,0:T(8,128)(2,1)S(1)}, u32[]{:S(2)}) copy-start(bf16[1024,256]{1,0:T(8,128)(2,1)S(1)} %get-tuple-element.16.bcc_ref) | copy-start | bytes 1572868
  129.9 17.8 %copy-start.7 = (f32[1024,128]{1,0:T(8,128)}, f32[1024,128]{1,0:T(8,128)S(1)}, u32[]{:S(2)}) copy-start(f32[1024,128]{1,0:T(8,128)S(1)} %get-tuple-element.21.cum_ref) | copy-start | bytes 1572868
  129.9 17.8 %copy-start.9 = (f32[1024,128]{1,0:T(8,128)}, f32[1024,128]{1,0:T(8,128)S(1)}, u32[]{:S(2)}) copy-start(f32[1024,128]{1,0:T(8,128)S(1)} %get-tuple-element.17.cum_ref) | copy-start | bytes 1572868
  129.9 25.2 %copy-start.21 = (f32[32]{0:T(128)S(1)}, f32[32]{0:T(128)}, u32[]{:S(2)}) copy-start(f32[32]{0:T(128)} %param.20) | copy-start | bytes 388
  130.1 16.5 %collective-permute-start.7 = (bf16[144,1024]{1,0:T(8,128)(2,1)S(1)}, bf16[144,1024]{1,0:T(8,128)(2,1)S(1)}, u32[]{:S(2)}, u32[]{:S(2)}) collective-permute-start(bf16[144,1024]{1,0:T(8,128)(2,1)S(1)} %maximum_maximum_fusion), channel_id=1, source_target_pairs={{0,8},{8,16},{16,24},{24,32},{32,40},{40,48},{48,56},{56,64},{64,7... | collective-permute-start | bytes 884744 | tf_op jit(solution)/shard_map/ppermute | solution.py:22
  148.6 19.4 %collective-permute-start.8 = (bf16[144,1024]{1,0:T(8,128)(2,1)}, bf16[144,1024]{1,0:T(8,128)(2,1)}, u32[]{:S(2)}, u32[]{:S(2)}) collective-permute-start(bf16[144,1024]{1,0:T(8,128)(2,1)} %maximum_maximum_fusion.1), channel_id=1, source_target_pairs={{0,16},{8,24},{16,32},{24,40},{32,48},{40,56},{48,64},{56,72},{64,... | collective-permute-start | bytes 884744 | tf_op jit(solution)/shard_map/ppermute | solution.py:22
  170.3 15.8 %copy-start.14 = (f32[128,1024]{1,0:T(8,128)S(1)}, f32[128,1024]{1,0:T(8,128)}, u32[]{:S(2)}) copy-start(f32[128,1024]{1,0:T(8,128)} %get-tuple-element.30) | copy-start | bytes 1572868
  170.3 22.3 %copy-start.5 = (bf16[1024,256]{1,0:T(8,128)(2,1)S(1)}, bf16[1024,256]{1,0:T(8,128)(2,1)}, u32[]{:S(2)}) copy-start(bf16[1024,256]{1,0:T(8,128)(2,1)} %copy-done.4) | copy-start | bytes 1572868
  170.3 22.3 %copy-start.10 = (f32[1024,128]{1,0:T(8,128)S(1)}, f32[1024,128]{1,0:T(8,128)}, u32[]{:S(2)}) copy-start(f32[1024,128]{1,0:T(8,128)} %copy-done.9) | copy-start | bytes 1572868
  170.3 15.7 %collective-permute-start.9 = (bf16[144,1024]{1,0:T(8,128)(2,1)S(1)}, bf16[144,1024]{1,0:T(8,128)(2,1)S(1)}, u32[]{:S(2)}, u32[]{:S(2)}) collective-permute-start(bf16[144,1024]{1,0:T(8,128)(2,1)S(1)} %maximum_maximum_fusion.2), channel_id=1, source_target_pairs={{0,32},{8,40},{16,48},{24,56},{32,64},{40,72},{48,80},{56,88},{64,... | collective-permute-start | bytes 884744 | tf_op jit(solution)/shard_map/ppermute | solution.py:22
  186.4 15.1 %collective-permute-start.10 = (bf16[144,1024]{1,0:T(8,128)(2,1)S(1)}, bf16[144,1024]{1,0:T(8,128)(2,1)S(1)}, u32[]{:S(2)}, u32[]{:S(2)}) collective-permute-start(bf16[144,1024]{1,0:T(8,128)(2,1)S(1)} %maximum_maximum_fusion.3), channel_id=1, source_target_pairs={{0,64},{8,72},{16,80},{24,88},{32,96},{40,104},{48,112},{56,120},{... | collective-permute-start | bytes 884744 | tf_op jit(solution)/shard_map/ppermute | solution.py:22
  192.6 8.9 %copy-start.16 = (f32[144,1024]{1,0:T(8,128)S(1)}, f32[144,1024]{1,0:T(8,128)}, u32[]{:S(2)}) copy-start(f32[144,1024]{1,0:T(8,128)} %copy-done.15) | copy-start | bytes 1769476
  223.3 16.1 %copy-start.18 = (f32[2048]{0:T(1024)S(1)}, f32[2048]{0:T(1024)}, u32[]{:S(2)}) copy-start(f32[2048]{0:T(1024)} %param.21) | copy-start | bytes 24580
  224.3 13.2 %collective-permute-start.11 = (bf16[512,1024]{1,0:T(8,128)(2,1)}, bf16[512,1024]{1,0:T(8,128)(2,1)}, u32[]{:S(2)}, u32[]{:S(2)}) collective-permute-start(bf16[512,1024]{1,0:T(8,128)(2,1)} %constant_dynamic-slice_fusion), channel_id=1, source_target_pairs={{0,4},{4,0},{1,5},{5,1},{2,6},{6,2},{3,7},{7,3},{8,12},{12,8},{9,1... | collective-permute-start | bytes 3145736 | tf_op jit(solution)/shard_map/ppermute | solution.py:17
  237.4 3.8 %copy-start.1 = (f32[4,2048]{1,0:T(4,128)S(1)}, f32[4,2048]{1,0:T(4,128)}, u32[]{:S(2)}) copy-start(f32[4,2048]{1,0:T(4,128)} %param.16) | copy-start | bytes 98308
  (4 other events, 6.0 us)
Sparse Core Ops, SparseCore 0:
  13.8 84.5 all-gather.4
  100.5 82.8 all-gather.2

commit v2 on v1

--- a/solution.py
+++ b/solution.py
@@ -1,3 +1,5 @@
+import functools
+
 import jax
 import jax.numpy as jnp
 from jax import lax
@@ -15,6 +17,11 @@
 
 def swap_cores(a):
     return lax.ppermute(a, "core", [(0, 1), (1, 0)])
+
+
+def round_ring(a, axis, distance):
+    size = lax.axis_size(axis)
+    return lax.ppermute(a, axis, [(i, (i + distance) % size) for i in range(size)])
 
 
 def along_chips(a, distance):
@@ -41,7 +48,8 @@
 
 
 def silu(a):
-    return a * (1.0 / (1.0 + jnp.exp(-a)))
+    half = 0.5 * a
+    return half + half * jnp.tanh(half)
 
 
 def conv_block(ref, kernel_ref, start):
@@ -134,31 +142,68 @@
         )
 
 
-def gate_kernel(
-    tokens_ref, weight_ref, local_ref, bcc_ref, cum_ref, incoming_ref, gated_ref, squares_ref, accum
-):
+def staged_kernel(sources, count, order_ref, tokens_ref, *refs):
+    weights, before, accum = refs[:count], refs[count:-1], refs[-1]
     step = pl.program_id(0)
-    rows, width = accum.shape
+    for place, source in enumerate(sources):
+
+        @pl.when(step == place)
+        def _():
+            parts = [weights[ref][first : first + size, :] for ref, first, size in source]
+            block = parts[0] if len(parts) == 1 else jnp.concatenate(parts, axis=0)
+            product = jnp.dot(tokens_ref[...], block, preferred_element_type=F32)
+            if place == 0:
+                accum[...] = before[0][...] + product if before else product
+            else:
+                accum[...] = accum[...] + product
+
+
+def z_kernel(tokens_ref, weight_ref, gate_ref, accum):
+    step = pl.program_id(0)
     product = jnp.dot(tokens_ref[HALO:, :], weight_ref[...], preferred_element_type=F32)
 
     @pl.when(step == 0)
     def _():
         accum[...] = product
 
-    @pl.when(step > 0)
+    @pl.when((step > 0) & (step < pl.num_programs(0) - 1))
     def _():
         accum[...] = accum[...] + product
 
     @pl.when(step == pl.num_programs(0) - 1)
     def _():
-        for block in range(rows // GROUP):
-            part = slice(block * GROUP, (block + 1) * GROUP)
-            gate = accum[part, :].astype(BF16).astype(F32)
-            grown = expand_heads(jnp.exp(cum_ref[part, :]), width)
-            carried = jnp.dot(bcc_ref[part, LANES:], incoming_ref[...], preferred_element_type=F32)
-            gated = (local_ref[part, :] + grown * carried) * silu(gate)
-            gated_ref[part, :] = gated.astype(BF16)
-            squares_ref[part, :] = jnp.sum(gated * gated, axis=1, keepdims=True)
+        gate_ref[...] = (accum[...] + product).astype(BF16)
+
+
+def gate_kernel(gate_ref, local_ref, bcc_ref, cum_ref, incoming_ref, gated_ref, squares_ref):
+    width = local_ref.shape[1]
+    grown = expand_heads(jnp.exp(cum_ref[...]), width)
+    carried = jnp.dot(bcc_ref[:, LANES:], incoming_ref[...], preferred_element_type=F32)
+    gated = (local_ref[...] + grown * carried) * silu(gate_ref[...].astype(F32))
+    gated_ref[...] = gated.astype(BF16)
+    squares = gated * gated
+    high = squares.astype(BF16)
+    low = (squares - high.astype(F32)).astype(BF16)
+    ones = jnp.ones((8, width), BF16)
+    across = (((1,), (1,)), ((), ()))
+    summed = lax.dot_general(ones, high, across, preferred_element_type=F32) + lax.dot_general(
+        ones, low, across, preferred_element_type=F32
+    )
+    squares_ref[...] = summed[0:1, :]
+
+
+def norm_kernel(core_ref, mine_ref, other_ref, squares_ref, gain_ref, out_ref):
+    half = pl.program_id(0)
+    across = jnp.broadcast_to(squares_ref[...], (8, squares_ref.shape[1]))
+    scale = lax.rsqrt(across + 1e-05).T[:, 0:1]
+
+    @pl.when(half == core_ref[0])
+    def _():
+        out_ref[...] = (mine_ref[...].astype(F32) * scale * gain_ref[...]).astype(BF16)
+
+    @pl.when(half != core_ref[0])
+    def _():
+        out_ref[...] = (other_ref[...].astype(F32) * scale * gain_ref[...]).astype(BF16)
 
 
 def whole(shape):
@@ -214,48 +259,170 @@
     )(xc, bcc, cum, cum_t, step_t, entering, skip)
 
 
-def gate_outputs(tokens, weight, local, bcc, cum_slab, incoming):
-    rows, width = local.shape
-    depth = 512
-    return pl.pallas_call(
-        gate_kernel,
+def project(tokens, order, weights, sources, before=None):
+    rows, width, depth = tokens.shape[0], weights[0].shape[1], 256
+    fixed = lambda a: pl.BlockSpec(a.shape, lambda i, order: (0,) * a.ndim)
+    operands = list(weights) + ([] if before is None else [before])
+    accum = jax.ShapeDtypeStruct((rows, width), F32)
+    return pl.pallas_call(
+        functools.partial(staged_kernel, sources, len(weights)),
+        grid_spec=pltpu.PrefetchScalarGridSpec(
+            num_scalar_prefetch=1,
+            grid=(len(sources),),
+            in_specs=[pl.BlockSpec((rows, depth), lambda i, order: (0, order[i]))]
+            + [fixed(a) for a in operands],
+            out_specs=fixed(accum),
+        ),
+        out_shape=accum,
+        compiler_params=pltpu.CompilerParams(vmem_limit_bytes=48 * 2**20),
+        cost_estimate=pl.CostEstimate(
+            flops=2 * rows * width * depth * len(sources), bytes_accessed=12 * 2**20, transcendentals=0
+        ),
+        name="project",
+    )(order, tokens, *operands)
+
+
+def project_gate(tokens, weight):
+    rows, width, depth = tokens.shape[0] - HALO, weight.shape[1], 1024
+    return pl.pallas_call(
+        z_kernel,
         grid=(weight.shape[0] // depth,),
         in_specs=[
             pl.BlockSpec((tokens.shape[0], depth), lambda i: (0, i)),
             pl.BlockSpec((depth, width), lambda i: (i, 0)),
-            whole(local.shape), whole(bcc.shape), whole(cum_slab.shape), whole(incoming.shape),
-        ],
-        out_specs=[whole((rows, width)), whole((rows, 1))],
-        out_shape=[
-            jax.ShapeDtypeStruct((rows, width), BF16), jax.ShapeDtypeStruct((rows, 1), F32),
-        ],
+        ],
+        out_specs=whole((rows, width)),
+        out_shape=jax.ShapeDtypeStruct((rows, width), BF16),
         scratch_shapes=[pltpu.VMEM((rows, width), F32)],
         compiler_params=pltpu.CompilerParams(vmem_limit_bytes=48 * 2**20),
         cost_estimate=pl.CostEstimate(flops=10**10, bytes_accessed=20 * 2**20, transcendentals=0),
+        name="project_gate",
+    )(tokens, weight)
+
+
+def gate_outputs(gate, local, bcc, cum_slab, incoming):
+    rows, width = local.shape
+    return pl.pallas_call(
+        gate_kernel,
+        grid=(rows // GROUP,),
+        in_specs=[
+            rows_of(width), rows_of(width), rows_of(2 * LANES), rows_of(LANES), whole(incoming.shape),
+        ],
+        out_specs=[rows_of(width), pl.BlockSpec((1, GROUP), lambda i: (0, i))],
+        out_shape=[
+            jax.ShapeDtypeStruct((rows, width), BF16), jax.ShapeDtypeStruct((1, rows), F32),
+        ],
+        compiler_params=pltpu.CompilerParams(vmem_limit_bytes=40 * 2**20),
+        cost_estimate=pl.CostEstimate(flops=10**9, bytes_accessed=10 * 2**20, transcendentals=0),
         name="gate",
-    )(tokens, weight, local, bcc, cum_slab, incoming)
+    )(gate, local, bcc, cum_slab, incoming)
+
+
+def normalized(core, gated, other, mean_squares, gain):
+    rows, width = other.shape
+    return pl.pallas_call(
+        norm_kernel,
+        grid_spec=pltpu.PrefetchScalarGridSpec(
+            num_scalar_prefetch=1,
+            grid=(2,),
+            in_specs=[
+                pl.BlockSpec((rows, width), lambda j, core: (core[0], 0)),
+                pl.BlockSpec((rows, width), lambda j, core: (0, 0)),
+                pl.BlockSpec((1, rows), lambda j, core: (0, 0)),
+                pl.BlockSpec((1, width), lambda j, core: (0, j)),
+            ],
+            out_specs=pl.BlockSpec((rows, width), lambda j, core: (0, j)),
+        ),
+        out_shape=jax.ShapeDtypeStruct((rows, 2 * width), BF16),
+        compiler_params=pltpu.CompilerParams(vmem_limit_bytes=40 * 2**20),
+        cost_estimate=pl.CostEstimate(flops=10**7, bytes_accessed=4 * 2**20, transcendentals=0),
+        name="normalized",
+    )(core[None], gated, other, mean_squares, gain)
+
+
+def packed(state, decay):
+    high = decay.astype(BF16)
+    low = (decay - high.astype(F32)).astype(BF16)
+    pad = jnp.zeros((HALO - 2, decay.shape[1]), BF16)
+    return jnp.concatenate([state.astype(BF16), high, low, pad], axis=0)
+
+
+def unpacked(sent):
+    sent = sent.astype(F32)
+    return sent[:LANES], sent[LANES : LANES + 1] + sent[LANES + 1 : LANES + 2]
 
 
 def entering_state(final):
-    window, decay = final[:LANES], final[LANES : LANES + 1]
-    state, state_decay = None, None
-    chips = lax.axis_size("z") * lax.axis_size("y")
-    distance = 1
-    while distance < chips:
-        high = decay.astype(BF16)
-        low = (decay - high.astype(F32)).astype(BF16)
-        pad = jnp.zeros((HALO - 2, decay.shape[1]), BF16)
-        sent = jnp.concatenate([window.astype(BF16), high, low, pad], axis=0)
-        got = along_chips(sent, distance).astype(F32)
-        got_decay = got[LANES : LANES + 1] + got[LANES + 1 : LANES + 2]
-        got = got[:LANES]
-        if state is None:
-            state, state_decay = got, got_decay
-        else:
-            state, state_decay = got * state_decay + state, got_decay * state_decay
-        window, decay = got * decay + window, got_decay * decay
-        distance *= 2
-    return state.astype(BF16)
+    size = lax.axis_size("y")
+    place = lax.axis_index("y")
+    own = packed(final[:LANES], final[LANES : LANES + 1])
+    parts = [own] + [round_ring(own, "y", distance) for distance in range(1, size)]
+    total = jnp.zeros((LANES, final.shape[1]), F32)
+    decay = jnp.ones((1, final.shape[1]), F32)
+    before, before_decay = total, decay
+    for index in range(size):
+        chosen = parts[0]
+        for distance in range(1, size):
+            chosen = jnp.where((place - index) % size == distance, parts[distance], chosen)
+        state, state_decay = unpacked(chosen)
+        before = jnp.where(place == index, total, before)
+        before_decay = jnp.where(place == index, decay, before_decay)
+        total = total * state_decay + state
+        decay = decay * state_decay
+    sent = packed(total, decay)
+    rows = lax.axis_size("z")
+    earlier = jnp.zeros_like(total)
+    for distance in range(rows - 1, 0, -1):
+        got = lax.ppermute(sent, "z", [(i, i + distance) for i in range(rows - distance)])
+        state, state_decay = unpacked(got)
+        earlier = earlier * state_decay + state
+    return (earlier * before_decay + before).astype(BF16)
+
+
+def project_early(tokens, own):
+    y, z = lax.axis_index("y"), lax.axis_index("z")
+    block = own.shape[0]
+    half = block // 2
+
+    def order(*places):
+        return jnp.stack([(z + dz) % 4 * 4 + (y + dy) % 4 for dy, dz in places]).astype(jnp.int32)
+
+    y_less, y_more = round_ring(own, "y", 1), round_ring(own, "y", -1)
+    z_less, z_more = round_ring(own, "z", 1), round_ring(own, "z", -1)
+    join = lambda *parts: jnp.concatenate(parts, axis=0)
+    from_y_less = round_ring(join(z_less, y_less[:half]), "y", 1)
+    from_y_more = round_ring(join(z_more, y_more[half:]), "y", -1)
+    from_z_less = round_ring(join(y_more, z_less[:half]), "z", 1)
+    from_z_more = round_ring(join(y_less, z_more[half:]), "z", -1)
+    y_far = join(from_y_less[block:], from_y_more[block:])
+    z_far = join(from_z_less[block:], from_z_more[block:])
+    far_y_less, far_y_more = round_ring(z_far, "y", 1), round_ring(z_far, "y", -1)
+    far_z_less, far_z_more = round_ring(y_far, "z", 1), round_ring(y_far, "z", -1)
+    far_top = round_ring(far_y_less[:half], "y", 1)
+    far_low = round_ring(far_z_more[half:], "z", -1)
+
+    full = lambda count: [((i, 0, block),) for i in range(count)]
+    accum = project(
+        tokens,
+        order((0, 0), (-1, 0), (1, 0), (0, -1), (0, 1)),
+        [own, y_less, y_more, z_less, z_more],
+        full(5),
+    )
+    accum = project(
+        tokens,
+        order((-1, -1), (1, 1), (1, -1), (-1, 1), (2, 0), (0, 2)),
+        [from_y_less, from_y_more, from_z_less, from_z_more],
+        full(4) + [((0, block, half), (1, block, half)), ((2, block, half), (3, block, half))],
+        accum,
+    )
+    accum = project(
+        tokens,
+        order((-1, 2), (1, 2), (2, -1), (2, 1)),
+        [far_y_less, far_y_more, far_z_less, far_z_more],
+        full(4),
+        accum,
+    )
+    return project(tokens, order((2, 2)), [far_top, far_low], [((0, 0, half), (1, 0, half))], accum)
 
 
 def shards(
@@ -277,18 +444,17 @@
     def paired(a):
         return in_core_order(core, mine(a, 1), swap_cores(others(a, 1)), 0)
 
-    gather = lambda a: lax.all_gather(a, ("z", "y"), axis=0, tiled=True)
     early = jnp.concatenate(
         [paired(x_weight), paired(bc_weight), jnp.pad(paired(dt_weight), ((0, 0), (0, LANES - heads)))],
         axis=1,
     )
-    early = gather(early)
-    z_whole = gather(paired(z_weight))
+    z_whole = lax.all_gather(paired(z_weight), ("z", "y"), axis=0, tiled=True)
     slabs = in_core_order(core, tokens, swap_cores(tokens), 0)
     extended = jnp.concatenate([along_chips(slabs[-HALO:], 1), slabs], axis=0)
 
-    x_in = jnp.dot(extended, early[:, :width], preferred_element_type=F32).astype(BF16)
-    small = jnp.dot(extended, early[:, width:], preferred_element_type=F32)
+    projected = project_early(extended, early)
+    x_in = projected[:, :width].astype(BF16)
+    small = projected[:, width:]
     bc_half = small[:, :LANES].astype(BF16)
     bc_in = in_core_order(core, bc_half, swap_cores(bc_half), 1)
     dt_raw = small[:, LANES:]
@@ -302,13 +468,14 @@
     incoming = entering_state(final)
     skip_lanes = jnp.repeat(mine(skip, 0), HEAD)[None, :]
     local = local_outputs(xc, bcc, cum, cum_t, step_t, entering, skip_lanes)
-    gated, squares = gate_outputs(extended, z_whole, local, bcc, cum_slab, incoming)
-
-    summed = lax.psum(squares[:, 0], ("core", "x"))
-    inner = 2 * width * lax.axis_size("x")
-    scale = lax.rsqrt(mine(summed, 0) / inner + 1e-05)
-    full = in_core_order(core, mine(gated, 0), swap_cores(others(gated, 0)), 1)
-    return (full.astype(F32) * scale[:, None] * norm_gain[None, :]).astype(BF16)
+    gate = project_gate(extended, z_whole)
+    gated, squares = gate_outputs(gate, local, bcc, cum_slab, incoming)
+
+    other = swap_cores(others(gated, 0))
+    summed = mine(squares + swap_cores(squares), 1)
+    across = [round_ring(summed, "x", distance) for distance in range(1, lax.axis_size("x"))]
+    mean_squares = (summed + sum(across)) / (2 * width * lax.axis_size("x"))
+    return normalized(core, gated, other, mean_squares, norm_gain[None, :])
 
 
 def solution(mesh):

time: 252 us -> 265 us (1.052)
  Pallas kernels: 38 us -> 73.5 us
  matrix products: 19.2 us -> 0 us
  blocking collectives: 12.9 us -> 0 us
  waiting for transfers between devices: 99.9 us -> 108 us
  starting transfers between devices: 28.7 us -> 34.8 us
  other arithmetic: 26 us -> 22 us
    ppermute x0 -> x23, waiting for transfers between devices: none -> 97.9 us  [the longest x20 96.3 us: round_ring(): lax.ppermute(a, axis, [(i, (i + distance) % size) for i in range(size)])]
    all_gather x2 -> x1, waiting for transfers between devices: 60.7 us -> 0.02 us  [shards(): z_whole = lax.all_gather(paired(z_weight), ('z', 'y'), axis=0, tiled=True)]
    pallas_call x1 -> x7, Pallas kernels: 19.5 us -> 54.6 us  [the longest x4 33.7 us: project(): pl.pallas_call(functools.partial(staged_kernel, sources, len(weights)), g...]
    ppermute x5 -> x1, waiting for transfers between devices: 32.6 us -> 0.01 us  [along_chips(): lax.ppermute(a, ('z', 'y'), [(i, i + distance) for i in range(chips - dis...]
    ppermute x0 -> x23, starting transfers between devices: none -> 29.5 us  [the longest x20 23.2 us: round_ring(): lax.ppermute(a, axis, [(i, (i + distance) % size) for i in range(size)])]
    ppermute x5 -> x1, starting transfers between devices: 27.2 us -> 3.47 us  [along_chips(): lax.ppermute(a, ('z', 'y'), [(i, i + distance) for i in range(chips - dis...]
    dot_general x2 -> x0, matrix products: 19.2 us -> none  [the longest x1 12.4 us: shards(): jnp.dot(extended, early[:, :width], preferred_element_type=F32).astype(BF16)]
    psum x1 -> x0, blocking collectives: 12.9 us -> none  [shards(): summed = lax.psum(squares[:, 0], ('core', 'x'))]
  transfers between devices with their start and end apart: 14 -> 33, of which waited for: 8 -> 15; matrix products, arithmetic and copies ran while one was open for 17% -> 9% of each run, Pallas kernels for 7% -> 20%
where the time goes in v2:
time: 265 us; the launch traced here: 264 us
  waiting for transfers between devices  108 us (41%)
  Pallas kernels  73.5 us (28%)
  starting transfers between devices  34.8 us (13%)
  other arithmetic  22 us (8%)
  between operations  14.2 us (5%)
  local copies, waits for them, and re-layouts  11.6 us (4%)
    ppermute x20, waiting for transfers between devices, round_ring(): lax.ppermute(a, axis, [(i, (i + distance) % size) for i in range(size)])  96.3 us
    pallas_call x4, Pallas kernels, project(): pl.pallas_call(functools.partial(staged_kernel, sources, len(weights)), g...  33.7 us
    ppermute x20, starting transfers between devices, round_ring(): lax.ppermute(a, axis, [(i, (i + distance) % size) for i in range(size)])  23.2 us
    pallas_call x1, Pallas kernels, project_gate(): pl.pallas_call(z_kernel, grid=(weight.shape[0] // depth,), in_specs=[pl.B...  13.2 us
    pallas_call x1, Pallas kernels, local_states(): pl.pallas_call(states_kernel, grid=(blocks,), in_specs=[whole(a.shape) fo...  11.5 us
    ppermute x8, waiting for transfers between devices, swap_cores(): return lax.ppermute(a, 'core', [(0, 1), (1, 0)])  9.66 us
    pallas_call x1, Pallas kernels, local_outputs(): pl.pallas_call(outputs_kernel, grid=(rows // GROUP,), in_specs=[rows_of(w...  7.39 us
    concatenate x1, other arithmetic, shards(): extended = jnp.concatenate([along_chips(slabs[-HALO:], 1), slabs], axis=0)  7.16 us
  transfers between devices with their start and end apart: 33, of which 15 were waited for; matrix products, arithmetic and copies ran while one was open for 9% of the time, Pallas kernels for 20%

profile of v2, /device:TPU:6, one launch (start us, length us, event | category | flops | bytes accessed | tf_op | source)
XLA Modules:
  0.0 263.6 jit_solution(6122732947999418680)
XLA Ops:
  12.6 5.6 %collective-permute-done.4 = bf16[128,128]{1,0:T(8,128)(2,1)S(1)} collective-permute-done((bf16[128,128]{1,0:T(8,128)(2,1)S(1)}, bf16[128,128]{1,0:T(8,128)(2,1)S(1)}, u32[]{:S(2)}, u32[]{:S(2)}) %collective-permute-start.4) | collective-permute-done | bytes 32800 | tf_op jit(solution)/shard_map/ppermute | solution.py:19
  18.4 4.1 %collective-permute-start.10 = (bf16[256,1280]{1,0:T(8,128)(2,1)S(1)}, bf16[256,1280]{1,0:T(8,128)(2,1)S(1)}, u32[]{:S(2)}, u32[]{:S(2)}) collective-permute-start(bf16[256,1280]{1,0:T(8,128)(2,1)S(1)} %fusion.1.refs_0_), channel_id=1, source_target_pairs={{0,96},{32,0},{64,32},{96,64},{1,97},{33,1},{65,33},{97,65},{2,98}... | collective-permute-start | bytes 1966088 | tf_op jit(solution)/shard_map/ppermute | solution.py:24
  24.1 1.7 collective-permute-start.6
  25.8 19.5 %collective-permute-done.10.refs_4_ = bf16[256,1280]{1,0:T(8,128)(2,1)S(1)} collective-permute-done((bf16[256,1280]{1,0:T(8,128)(2,1)S(1)}, bf16[256,1280]{1,0:T(8,128)(2,1)S(1)}, u32[]{:S(2)}, u32[]{:S(2)}) %collective-permute-start.10) | collective-permute-done | bytes 655392 | tf_op jit(solution)/shard_map/ppermute | solution.py:24
  45.3 3.4 %collective-permute-done.9.refs_1_ = bf16[256,1280]{1,0:T(8,128)(2,1)S(1)} collective-permute-done((bf16[256,1280]{1,0:T(8,128)(2,1)S(1)}, bf16[256,1280]{1,0:T(8,128)(2,1)S(1)}, u32[]{:S(2)}, u32[]{:S(2)}) %collective-permute-start.9) | collective-permute-done | bytes 655392 | tf_op jit(solution)/shard_map/ppermute | solution.py:24
  50.0 1.6 collective-permute-start.14
  52.0 2.7 %collective-permute-start.15 = (bf16[384,1280]{1,0:T(8,128)(2,1)S(1)}, bf16[384,1280]{1,0:T(8,128)(2,1)S(1)}, u32[]{:S(2)}, u32[]{:S(2)}) collective-permute-start(bf16[384,1280]{1,0:T(8,128)(2,1)S(1)} %pad_maximum_fusion.4), channel_id=1, source_target_pairs={{0,24},{8,0},{16,8},{24,16},{1,25},{9,1},{17,9},{25,17},{2,26},{10... | collective-permute-start | bytes 2949128 | tf_op jit(solution)/shard_map/ppermute | solution.py:24
  54.7 42.4 %collective-permute-done.8.refs_2_ = bf16[384,1280]{1,0:T(8,128)(2,1)S(1)} collective-permute-done((bf16[384,1280]{1,0:T(8,128)(2,1)S(1)}, bf16[384,1280]{1,0:T(8,128)(2,1)S(1)}, u32[]{:S(2)}, u32[]{:S(2)}) %collective-permute-start.8) | collective-permute-done | bytes 983072 | tf_op jit(solution)/shard_map/ppermute | solution.py:24
  100.7 5.3 %broadcast_select_fusion = (bf16[512,4096]{1,0:T(8,128)(2,1)}, bf16[512,4096]{1,0:T(8,128)(2,1)}) fusion(bf16[512,4096]{1,0:T(8,128)(2,1)S(1)} %copy-done.18, bf16[512,4096]{1,0:T(8,128)(2,1)} %collective-permute-done, pred[]{:T(512)S(6)} %eq.109), kind=kLoop, calls=%fused_computation.1 | loop fusion | flops 4194304 | bytes 16777216 | tf_op jit(solution)/shard_map/jit(_where)/select_n | solution.py:33
  107.5 3.5 %collective-permute-start.1 = (bf16[16,4096]{1,0:T(8,128)(2,1)}, bf16[16,4096]{1,0:T(8,128)(2,1)S(1)}, u32[]{:S(2)}, u32[]{:S(2)}) collective-permute-start(bf16[16,4096]{1,0:T(8,128)(2,1)} %slice.154), channel_id=1, source_target_pairs={{0,8},{8,16},{16,24},{24,32},{32,40},{40,48},{48,56},{56,64},{64,7... | collective-permute-start | bytes 393224 | tf_op jit(solution)/shard_map/ppermute | solution.py:29
  111.3 2.5 collective-permute-start.18
  113.8 9.9 %collective-permute-done.12.refs_0_ = bf16[256,1280]{1,0:T(8,128)(2,1)} collective-permute-done((bf16[256,1280]{1,0:T(8,128)(2,1)}, bf16[256,1280]{1,0:T(8,128)(2,1)}, u32[]{:S(2)}, u32[]{:S(2)}) %collective-permute-start.12) | collective-permute-done | bytes 655392 | tf_op jit(solution)/shard_map/ppermute | solution.py:24
  126.5 7.2 %pad_maximum_fusion.tokens_ref = bf16[1040,4096]{1,0:T(8,128)(2,1)} fusion(bf16[512,4096]{1,0:T(8,128)(2,1)} %get-tuple-element.32, bf16[512,4096]{1,0:T(8,128)(2,1)} %get-tuple-element.31, bf16[16,4096]{1,0:T(8,128)(2,1)S(1)} %collective-permute-done.1), kind=kLoop, calls=%fused_computation | loop fusion | flops 25559040 | bytes 17039360 | tf_op jit(solution)/shard_map/concatenate | solution.py:453
  133.6 9.0 %project.4.refs_4_ = f32[1040,1280]{1,0:T(8,128)} custom-call(s32[5]{0:T(128)S(1)} %stack.75.order_ref, bf16[1040,4096]{1,0:T(8,128)(2,1)} %pad_maximum_fusion.tokens_ref, bf16[256,1280]{1,0:T(8,128)(2,1)S(1)} %fusion.1.refs_0_, bf16[256,1280]{1,0:T(8,128)(2,1)S(1)} %collective-permute-done.9.refs_1_, bf16[256,1280]{1,0:T(8,128)(2,1)S(1)} %collective-permute-done.6.refs_2_, ...), custom_call_target="tpu_custom_call" | custom-call | flops 3407872000 | bytes 12582912 | tf_op jit(solution)/shard_map/project/pallas_call | solution.py:267
  142.6 11.4 %project.5.refs_4_ = f32[1040,1280]{1,0:T(8,128)} custom-call(s32[6]{0:T(128)S(1)} %stack.69.order_ref, bf16[1040,4096]{1,0:T(8,128)(2,1)} %pad_maximum_fusion.tokens_ref, bf16[384,1280]{1,0:T(8,128)(2,1)S(1)} %copy-done.7, bf16[384,1280]{1,0:T(8,128)(2,1)S(1)} %copy-done.11, bf16[384,1280]{1,0:T(8,128)(2,1)S(1)} %copy-done.9, ...), custom_call_target="tpu_custom_call" | custom-call | flops 4089446400 | bytes 12582912 | tf_op jit(solution)/shard_map/project/pallas_call | solution.py:267
  154.0 9.8 %project.6.refs_2_ = f32[1040,1280]{1,0:T(8,128)} custom-call(s32[4]{0:T(128)S(1)} %pad_add_fusion.order_ref, bf16[1040,4096]{1,0:T(8,128)(2,1)} %pad_maximum_fusion.tokens_ref, bf16[256,1280]{1,0:T(8,128)(2,1)} %collective-permute-done.12.refs_0_, bf16[256,1280]{1,0:T(8,128)(2,1)S(1)} %collective-permute-done.18.refs_1_, ...), custom_call_target="tpu_custom_call" | custom-call | flops 2726297600 | bytes 12582912 | tf_op jit(solution)/shard_map/project/pallas_call | solution.py:267
  163.8 3.6 %project.7 = f32[1040,1280]{1,0:T(8,128)S(1)} custom-call(s32[1]{0:T(128)} %bitcast.1.order_ref, bf16[1040,4096]{1,0:T(8,128)(2,1)} %pad_maximum_fusion.tokens_ref, bf16[128,1280]{1,0:T(8,128)(2,1)S(1)} %collective-permute-done.13.refs_0_, bf16[128,1280]{1,0:T(8,128)(2,1)S(1)} %collective-permute-done.17.refs_1_, f32[1040,1280]{1,0:T(8,128)} %project.6.refs_2_), custom_call_target="tpu_custom_call" | custom-call | flops 681574400 | bytes 12582912 | tf_op jit(solution)/shard_map/project/pallas_call | solution.py:267
  169.5 11.5 %states.1 = (bf16[1024,1024]{1,0:T(8,128)(2,1)S(1)}, bf16[1024,256]{1,0:T(8,128)(2,1)S(1)}, f32[1024,128]{1,0:T(8,128)S(1)}, f32[1024,128]{1,0:T(8,128)S(1)}, f3...) custom-call(bf16[1040,1024]{1,0:T(8,128)(2,1)S(1)} %slice.165.x_ref,, ...), custom_call_target="tpu_custom_call" | custom-call | flops 4000000000 | bytes 10485760 | tf_op jit(solution)/shard_map/states/pallas_call | solution.py:222
  183.6 2.8 %collective-permute-start.21 = (bf16[144,1024]{1,0:T(8,128)(2,1)}, bf16[144,1024]{1,0:T(8,128)(2,1)}, u32[]{:S(2)}, u32[]{:S(2)}) collective-permute-start(bf16[144,1024]{1,0:T(8,128)(2,1)} %maximum_maximum_fusion), channel_id=1, source_target_pairs={{0,24},{8,0},{16,8},{24,16},{1,25},{9,1},{17,9},{25,17},{2,26},{10... | collective-permute-start | bytes 884744 | tf_op jit(solution)/shard_map/ppermute | solution.py:24
  187.5 12.1 %collective-permute-done.21 = bf16[144,1024]{1,0:T(8,128)(2,1)} collective-permute-done((bf16[144,1024]{1,0:T(8,128)(2,1)}, bf16[144,1024]{1,0:T(8,128)(2,1)}, u32[]{:S(2)}, u32[]{:S(2)}) %collective-permute-start.21) | collective-permute-done | bytes 294944 | tf_op jit(solution)/shard_map/ppermute | solution.py:24
  199.6 3.5 %collective-permute-done.23 = bf16[144,1024]{1,0:T(8,128)(2,1)} collective-permute-done((bf16[144,1024]{1,0:T(8,128)(2,1)}, bf16[144,1024]{1,0:T(8,128)(2,1)}, u32[]{:S(2)}, u32[]{:S(2)}) %collective-permute-start.23) | collective-permute-done | bytes 294944 | tf_op jit(solution)/shard_map/ppermute | solution.py:24
  203.2 1.6 select_convert_fusion
  208.4 3.3 %collective-permute-start.25 = (bf16[144,1024]{1,0:T(8,128)(2,1)S(1)}, bf16[144,1024]{1,0:T(8,128)(2,1)S(1)}, u32[]{:S(2)}, u32[]{:S(2)}) collective-permute-start(bf16[144,1024]{1,0:T(8,128)(2,1)S(1)} %maximum_maximum_fusion.1), channel_id=1, source_target_pairs={{0,64},{32,96},{1,65},{33,97},{2,66},{34,98},{3,67},{35,99},{4,68}... | collective-permute-start | bytes 884744 | tf_op jit(solution)/shard_map/ppermute | solution.py:376
  213.0 7.4 %outputs.1.local_ref = f32[1024,1024]{1,0:T(8,128)S(1)} custom-call(bf16[1024,1024]{1,0:T(8,128)(2,1)S(1)} %get-tuple-element.15.xc_ref, bf16[1024,256]{1,0:T(8,128)(2,1)S(1)} %get-tuple-element.16.bcc_ref, f32[1024,128]{1,0:T(8,128)S(1)} %copy-done.17, f32[16,1024]{1,0:T(8,128)S(1)} %get-tuple-element.18.cum_t_ref, ...), custom_call_target="tpu_custom_call" | custom-call | flops 10000000000 | bytes 10485760 | tf_op jit(solution)/shard_map/outputs/pallas_call | solution.py:247
  220.5 2.0 copy-done.2
  224.7 13.2 %project_gate.1.gate_ref = bf16[1024,1024]{1,0:T(8,128)(2,1)S(1)} custom-call(bf16[1040,4096]{1,0:T(8,128)(2,1)} %pad_maximum_fusion.tokens_ref, bf16[4096,1024]{1,0:T(8,128)(2,1)} %all-gather.2.cloned.1.call-done.weight_ref), custom_call_target="tpu_custom_call" | custom-call | flops 10000000000 | bytes 20971520 | tf_op jit(solution)/shard_map/project_gate/pallas_call | solution.py:287
  237.9 5.8 %gate.1 = (bf16[1024,1024]{1,0:T(8,128)(2,1)S(1)}, f32[1,1024]{1,0:T(1,128)S(1)}) custom-call(bf16[1024,1024]{1,0:T(8,128)(2,1)S(1)} %project_gate.1.gate_ref, f32[1024,1024]{1,0:T(8,128)S(1)} %copy-done.3, bf16[1024,256]{1,0:T(8,128)(2,1)S(1)} %get-tuple-element.16.bcc_ref, f32[1024,128]{1,0:T(8,128)S(1)} %get-tuple-element.21.cum_ref, ...), custom_call_target="tpu_custom_call" | custom-call | flops 1000000000 | bytes 10485760 | tf_op jit(solution)/shard_map/gate/pallas_call | solution.py:305
  245.3 1.8 collective-permute-done.28
  247.6 2.4 collective-permute-start.30
  250.7 2.0 collective-permute-done.30
  252.6 2.1 collective-permute-done.31
  254.8 1.9 normalized.1
  (168 shorter events, 33.0 us)
Async XLA Ops:
  6.5 218.1 %all-gather.2.cloned.1.call-start = ((), (), s32[]{:S(2)}) async-start(), calls=%async_computation | async-start | bytes 8912896 | tf_op jit(solution)/shard_map/all_gather | solution.py:451
  7.6 1.6 collective-permute-start.2
  11.4 89.1 %collective-permute-start = (bf16[512,4096]{1,0:T(8,128)(2,1)}, bf16[512,4096]{1,0:T(8,128)(2,1)}, u32[]{:S(2)}, u32[]{:S(2)}) collective-permute-start(bf16[512,4096]{1,0:T(8,128)(2,1)} %param.11), channel_id=1, source_target_pairs={{0,4},{4,0},{1,5},{5,1},{2,6},{6,2},{3,7},{7,3},{8,12},{12,8},{9,1... | collective-permute-start | bytes 12582920 | tf_op jit(solution)/shard_map/ppermute | solution.py:19
  11.8 6.4 %collective-permute-start.3 = (bf16[128,1024]{1,0:T(8,128)(2,1)S(1)}, bf16[128,1024]{1,0:T(8,128)(2,1)S(1)}, u32[]{:S(2)}, u32[]{:S(2)}) collective-permute-start(bf16[128,1024]{1,0:T(8,128)(2,1)S(1)} %constant_dynamic-slice_fusion.6), channel_id=1, source_target_pairs={{0,4},{4,0},{1,5},{5,1},{2,6},{6,2},{3,7},{7,3},{8,12},{12,8},{9,1... | collective-permute-start | bytes 786440 | tf_op jit(solution)/shard_map/ppermute | solution.py:19
  12.1 6.2 %collective-permute-start.4 = (bf16[128,128]{1,0:T(8,128)(2,1)S(1)}, bf16[128,128]{1,0:T(8,128)(2,1)S(1)}, u32[]{:S(2)}, u32[]{:S(2)}) collective-permute-start(bf16[128,128]{1,0:T(8,128)(2,1)S(1)} %constant_dynamic-slice_fusion.5), channel_id=1, source_target_pairs={{0,4},{4,0},{1,5},{5,1},{2,6},{6,2},{3,7},{7,3},{8,12},{12,8},{9,1... | collective-permute-start | bytes 98312 | tf_op jit(solution)/shard_map/ppermute | solution.py:19
  18.4 26.8 %collective-permute-start.10 = (bf16[256,1280]{1,0:T(8,128)(2,1)S(1)}, bf16[256,1280]{1,0:T(8,128)(2,1)S(1)}, u32[]{:S(2)}, u32[]{:S(2)}) collective-permute-start(bf16[256,1280]{1,0:T(8,128)(2,1)S(1)} %fusion.1.refs_0_), channel_id=1, source_target_pairs={{0,96},{32,0},{64,32},{96,64},{1,97},{33,1},{65,33},{97,65},{2,98}... | collective-permute-start | bytes 1966088 | tf_op jit(solution)/shard_map/ppermute | solution.py:24
  22.5 26.2 %collective-permute-start.9 = (bf16[256,1280]{1,0:T(8,128)(2,1)S(1)}, bf16[256,1280]{1,0:T(8,128)(2,1)S(1)}, u32[]{:S(2)}, u32[]{:S(2)}) collective-permute-start(bf16[256,1280]{1,0:T(8,128)(2,1)S(1)} %fusion.1.refs_0_), channel_id=1, source_target_pairs={{0,8},{8,16},{16,24},{24,0},{1,9},{9,17},{17,25},{25,1},{2,10},{10... | collective-permute-start | bytes 1966088 | tf_op jit(solution)/shard_map/ppermute | solution.py:24
  24.1 25.9 %collective-permute-start.7 = (bf16[256,1280]{1,0:T(8,128)(2,1)S(1)}, bf16[256,1280]{1,0:T(8,128)(2,1)S(1)}, u32[]{:S(2)}, u32[]{:S(2)}) collective-permute-start(bf16[256,1280]{1,0:T(8,128)(2,1)S(1)} %fusion.1.refs_0_), channel_id=1, source_target_pairs={{0,32},{32,64},{64,96},{96,0},{1,33},{33,65},{65,97},{97,1},{2,34}... | collective-permute-start | bytes 1966088 | tf_op jit(solution)/shard_map/ppermute | solution.py:24
  24.1 27.6 %collective-permute-start.6 = (bf16[256,1280]{1,0:T(8,128)(2,1)S(1)}, bf16[256,1280]{1,0:T(8,128)(2,1)S(1)}, u32[]{:S(2)}, u32[]{:S(2)}) collective-permute-start(bf16[256,1280]{1,0:T(8,128)(2,1)S(1)} %fusion.1.refs_0_), channel_id=1, source_target_pairs={{0,24},{8,0},{16,8},{24,16},{1,25},{9,1},{17,9},{25,17},{2,26},{10... | collective-permute-start | bytes 1966088 | tf_op jit(solution)/shard_map/ppermute | solution.py:24
  48.8 48.2 %collective-permute-start.11 = (bf16[384,1280]{1,0:T(8,128)(2,1)S(1)}, bf16[384,1280]{1,0:T(8,128)(2,1)S(1)}, u32[]{:S(2)}, u32[]{:S(2)}) collective-permute-start(bf16[384,1280]{1,0:T(8,128)(2,1)S(1)} %pad_maximum_fusion.2), channel_id=1, source_target_pairs={{0,96},{32,0},{64,32},{96,64},{1,97},{33,1},{65,33},{97,65},{2,98}... | collective-permute-start | bytes 2949128 | tf_op jit(solution)/shard_map/ppermute | solution.py:24
  50.0 49.0 %collective-permute-start.14 = (bf16[384,1280]{1,0:T(8,128)(2,1)S(1)}, bf16[384,1280]{1,0:T(8,128)(2,1)S(1)}, u32[]{:S(2)}, u32[]{:S(2)}) collective-permute-start(bf16[384,1280]{1,0:T(8,128)(2,1)S(1)} %pad_maximum_fusion.3), channel_id=1, source_target_pairs={{0,8},{8,16},{16,24},{24,0},{1,9},{9,17},{17,25},{25,1},{2,10},{10... | collective-permute-start | bytes 2949128 | tf_op jit(solution)/shard_map/ppermute | solution.py:24
  51.8 45.2 %collective-permute-start.8 = (bf16[384,1280]{1,0:T(8,128)(2,1)S(1)}, bf16[384,1280]{1,0:T(8,128)(2,1)S(1)}, u32[]{:S(2)}, u32[]{:S(2)}) collective-permute-start(bf16[384,1280]{1,0:T(8,128)(2,1)S(1)} %pad_maximum_fusion.1), channel_id=1, source_target_pairs={{0,32},{32,64},{64,96},{96,0},{1,33},{33,65},{65,97},{97,1},{2,34}... | collective-permute-start | bytes 2949128 | tf_op jit(solution)/shard_map/ppermute | solution.py:24
  52.0 47.1 %collective-permute-start.15 = (bf16[384,1280]{1,0:T(8,128)(2,1)S(1)}, bf16[384,1280]{1,0:T(8,128)(2,1)S(1)}, u32[]{:S(2)}, u32[]{:S(2)}) collective-permute-start(bf16[384,1280]{1,0:T(8,128)(2,1)S(1)} %pad_maximum_fusion.4), channel_id=1, source_target_pairs={{0,24},{8,0},{16,8},{24,16},{1,25},{9,1},{17,9},{25,17},{2,26},{10... | collective-permute-start | bytes 2949128 | tf_op jit(solution)/shard_map/ppermute | solution.py:24
  98.0 25.7 %collective-permute-start.12 = (bf16[256,1280]{1,0:T(8,128)(2,1)}, bf16[256,1280]{1,0:T(8,128)(2,1)}, u32[]{:S(2)}, u32[]{:S(2)}) collective-permute-start(bf16[256,1280]{1,0:T(8,128)(2,1)} %pad_maximum_fusion.5), channel_id=1, source_target_pairs={{0,8},{8,16},{16,24},{24,0},{1,9},{9,17},{17,25},{25,1},{2,10},{10... | collective-permute-start | bytes 1966088 | tf_op jit(solution)/shard_map/ppermute | solution.py:24
  100.0 25.2 %collective-permute-start.16 = (bf16[256,1280]{1,0:T(8,128)(2,1)}, bf16[256,1280]{1,0:T(8,128)(2,1)}, u32[]{:S(2)}, u32[]{:S(2)}) collective-permute-start(bf16[256,1280]{1,0:T(8,128)(2,1)} %pad_maximum_fusion.6), channel_id=1, source_target_pairs={{0,96},{32,0},{64,32},{96,64},{1,97},{33,1},{65,33},{97,65},{2,98}... | collective-permute-start | bytes 1966088 | tf_op jit(solution)/shard_map/ppermute | solution.py:24
  107.5 19.0 %collective-permute-start.1 = (bf16[16,4096]{1,0:T(8,128)(2,1)}, bf16[16,4096]{1,0:T(8,128)(2,1)S(1)}, u32[]{:S(2)}, u32[]{:S(2)}) collective-permute-start(bf16[16,4096]{1,0:T(8,128)(2,1)} %slice.154), channel_id=1, source_target_pairs={{0,8},{8,16},{16,24},{24,32},{32,40},{40,48},{48,56},{56,64},{64,7... | collective-permute-start | bytes 393224 | tf_op jit(solution)/shard_map/ppermute | solution.py:29
  111.3 42.7 %collective-permute-start.18 = (bf16[256,1280]{1,0:T(8,128)(2,1)}, bf16[256,1280]{1,0:T(8,128)(2,1)S(1)}, u32[]{:S(2)}, u32[]{:S(2)}) collective-permute-start(bf16[256,1280]{1,0:T(8,128)(2,1)} %pad_maximum_fusion.5), channel_id=1, source_target_pairs={{0,24},{8,0},{16,8},{24,16},{1,25},{9,1},{17,9},{25,17},{2,26},{10... | collective-permute-start | bytes 1966088 | tf_op jit(solution)/shard_map/ppermute | solution.py:24
  113.8 40.2 %collective-permute-start.19 = (bf16[256,1280]{1,0:T(8,128)(2,1)}, bf16[256,1280]{1,0:T(8,128)(2,1)S(1)}, u32[]{:S(2)}, u32[]{:S(2)}) collective-permute-start(bf16[256,1280]{1,0:T(8,128)(2,1)} %pad_maximum_fusion.6), channel_id=1, source_target_pairs={{0,32},{32,64},{64,96},{96,0},{1,33},{33,65},{65,97},{97,1},{2,34}... | collective-permute-start | bytes 1966088 | tf_op jit(solution)/shard_map/ppermute | solution.py:24
  124.7 39.1 %collective-permute-start.13 = (bf16[128,1280]{1,0:T(8,128)(2,1)S(1)}, bf16[128,1280]{1,0:T(8,128)(2,1)S(1)}, u32[]{:S(2)}, u32[]{:S(2)}) collective-permute-start(bf16[128,1280]{1,0:T(8,128)(2,1)S(1)} %slice.159), channel_id=1, source_target_pairs={{0,8},{8,16},{16,24},{24,0},{1,9},{9,17},{17,25},{25,1},{2,10},{10... | collective-permute-start | bytes 983048 | tf_op jit(solution)/shard_map/ppermute | solution.py:24
  126.2 37.6 %collective-permute-start.17 = (bf16[128,1280]{1,0:T(8,128)(2,1)S(1)}, bf16[128,1280]{1,0:T(8,128)(2,1)S(1)}, u32[]{:S(2)}, u32[]{:S(2)}) collective-permute-start(bf16[128,1280]{1,0:T(8,128)(2,1)S(1)} %slice.164), channel_id=1, source_target_pairs={{0,96},{32,0},{64,32},{96,64},{1,97},{33,1},{65,33},{97,65},{2,98}... | collective-permute-start | bytes 983048 | tf_op jit(solution)/shard_map/ppermute | solution.py:24
  167.7 1.6 collective-permute-start.20
  183.6 16.0 %collective-permute-start.21 = (bf16[144,1024]{1,0:T(8,128)(2,1)}, bf16[144,1024]{1,0:T(8,128)(2,1)}, u32[]{:S(2)}, u32[]{:S(2)}) collective-permute-start(bf16[144,1024]{1,0:T(8,128)(2,1)} %maximum_maximum_fusion), channel_id=1, source_target_pairs={{0,24},{8,0},{16,8},{24,16},{1,25},{9,1},{17,9},{25,17},{2,26},{10... | collective-permute-start | bytes 884744 | tf_op jit(solution)/shard_map/ppermute | solution.py:24
  186.4 13.2 %collective-permute-start.22 = (bf16[144,1024]{1,0:T(8,128)(2,1)}, bf16[144,1024]{1,0:T(8,128)(2,1)}, u32[]{:S(2)}, u32[]{:S(2)}) collective-permute-start(bf16[144,1024]{1,0:T(8,128)(2,1)} %maximum_maximum_fusion), channel_id=1, source_target_pairs={{0,16},{8,24},{16,0},{24,8},{1,17},{9,25},{17,1},{25,9},{2,18},{10... | collective-permute-start | bytes 884744 | tf_op jit(solution)/shard_map/ppermute | solution.py:24
  186.8 16.3 %collective-permute-start.23 = (bf16[144,1024]{1,0:T(8,128)(2,1)}, bf16[144,1024]{1,0:T(8,128)(2,1)}, u32[]{:S(2)}, u32[]{:S(2)}) collective-permute-start(bf16[144,1024]{1,0:T(8,128)(2,1)} %maximum_maximum_fusion), channel_id=1, source_target_pairs={{0,8},{8,16},{16,24},{24,0},{1,9},{9,17},{17,25},{25,1},{2,10},{10... | collective-permute-start | bytes 884744 | tf_op jit(solution)/shard_map/ppermute | solution.py:24
  206.8 15.7 %collective-permute-start.24 = (bf16[144,1024]{1,0:T(8,128)(2,1)S(1)}, bf16[144,1024]{1,0:T(8,128)(2,1)S(1)}, u32[]{:S(2)}, u32[]{:S(2)}) collective-permute-start(bf16[144,1024]{1,0:T(8,128)(2,1)S(1)} %maximum_maximum_fusion.1), channel_id=1, source_target_pairs={{0,96},{1,97},{2,98},{3,99},{4,100},{5,101},{6,102},{7,103},{8,104... | collective-permute-start | bytes 884744 | tf_op jit(solution)/shard_map/ppermute | solution.py:376
  208.4 14.1 %collective-permute-start.25 = (bf16[144,1024]{1,0:T(8,128)(2,1)S(1)}, bf16[144,1024]{1,0:T(8,128)(2,1)S(1)}, u32[]{:S(2)}, u32[]{:S(2)}) collective-permute-start(bf16[144,1024]{1,0:T(8,128)(2,1)S(1)} %maximum_maximum_fusion.1), channel_id=1, source_target_pairs={{0,64},{32,96},{1,65},{33,97},{2,66},{34,98},{3,67},{35,99},{4,68}... | collective-permute-start | bytes 884744 | tf_op jit(solution)/shard_map/ppermute | solution.py:376
  211.7 12.4 %collective-permute-start.26 = (bf16[144,1024]{1,0:T(8,128)(2,1)S(1)}, bf16[144,1024]{1,0:T(8,128)(2,1)S(1)}, u32[]{:S(2)}, u32[]{:S(2)}) collective-permute-start(bf16[144,1024]{1,0:T(8,128)(2,1)S(1)} %maximum_maximum_fusion.1), channel_id=1, source_target_pairs={{0,32},{32,64},{64,96},{1,33},{33,65},{65,97},{2,34},{34,66},{66,9... | collective-permute-start | bytes 884744 | tf_op jit(solution)/shard_map/ppermute | solution.py:376
  244.8 10.0 %collective-permute-start.27 = (bf16[512,1024]{1,0:T(8,128)(2,1)}, bf16[512,1024]{1,0:T(8,128)(2,1)S(1)}, u32[]{:S(2)}, u32[]{:S(2)}) collective-permute-start(bf16[512,1024]{1,0:T(8,128)(2,1)} %constant_dynamic-slice_fusion.2), channel_id=1, source_target_pairs={{0,4},{4,0},{1,5},{5,1},{2,6},{6,2},{3,7},{7,3},{8,12},{12,8},{9,1... | collective-permute-start | bytes 3145736 | tf_op jit(solution)/shard_map/ppermute | solution.py:19
  244.8 2.3 collective-permute-start.28
  247.1 3.6 %collective-permute-start.29 = (f32[1,512]{1,0:T(1,128)S(1)}, f32[1,512]{1,0:T(1,128)S(1)}, u32[]{:S(2)}, u32[]{:S(2)}) collective-permute-start(f32[1,512]{1,0:T(1,128)S(1)} %fusion.9), channel_id=1, source_target_pairs={{0,1},{1,2},{2,3},{3,0},{4,5},{5,6},{6,7},{7,4},{8,9},{9,10},{10,1... | collective-permute-start | bytes 6152 | tf_op jit(solution)/shard_map/ppermute | solution.py:24
  247.6 5.1 %collective-permute-start.30 = (f32[1,512]{1,0:T(1,128)S(1)}, f32[1,512]{1,0:T(1,128)S(1)}, u32[]{:S(2)}, u32[]{:S(2)}) collective-permute-start(f32[1,512]{1,0:T(1,128)S(1)} %fusion.9), channel_id=1, source_target_pairs={{0,2},{1,3},{2,0},{3,1},{4,6},{5,7},{6,4},{7,5},{8,10},{9,11},{10,... | collective-permute-start | bytes 6152 | tf_op jit(solution)/shard_map/ppermute | solution.py:24
  250.0 4.8 %collective-permute-start.31 = (f32[1,512]{1,0:T(1,128)S(1)}, f32[1,512]{1,0:T(1,128)S(1)}, u32[]{:S(2)}, u32[]{:S(2)}) collective-permute-start(f32[1,512]{1,0:T(1,128)S(1)} %fusion.9), channel_id=1, source_target_pairs={{0,3},{1,0},{2,1},{3,2},{4,7},{5,4},{6,5},{7,6},{8,11},{9,8},{10,9... | collective-permute-start | bytes 6152 | tf_op jit(solution)/shard_map/ppermute | solution.py:24
  (28 other events, 309.0 us)
Sparse Core Ops, SparseCore 0:
  11.3 106.5 all-gather.1

commit v3 on v2

v3 whole, which is shorter than its diff:
```python
import functools

import jax
import jax.numpy as jnp
from jax import lax
from jax.experimental import pallas as pl
from jax.experimental.pallas import tpu as pltpu
from jax.sharding import Mesh, PartitionSpec as P

GROUP = 256
HALO = 16
LANES = 128
HEAD = 64
F32 = jnp.float32
BF16 = jnp.bfloat16


def swap_cores(a):
    return lax.ppermute(a, "core", [(0, 1), (1, 0)])


def round_ring(a, axis, distance):
    size = lax.axis_size(axis)
    return lax.ppermute(a, axis, [(i, (i + distance) % size) for i in range(size)])


def along_chips(a, distance):
    chips = lax.axis_size("z") * lax.axis_size("y")
    return lax.ppermute(a, ("z", "y"), [(i, i + distance) for i in range(chips - distance)])


def in_core_order(core, mine, other, axis):
    first = jnp.where(core == 0, mine, other)
    second = jnp.where(core == 0, other, mine)
    return jnp.concatenate([first, second], axis=axis)


def expand_heads(values, width):
    high = values.astype(BF16)
    rest = values - high.astype(F32)
    middle = rest.astype(BF16)
    low = (rest - middle.astype(F32)).astype(BF16)
    row = lax.broadcasted_iota(jnp.int32, (LANES, width), 0)
    col = lax.broadcasted_iota(jnp.int32, (LANES, width), 1)
    spread = ((col >= row * HEAD) & (col < row * HEAD + HEAD)).astype(BF16)
    dot = lambda part: jnp.dot(part, spread, preferred_element_type=F32)
    return dot(high) + dot(middle) + dot(low)


def silu(a):
    half = 0.5 * a
    return half + half * jnp.tanh(half)


def conv_rows(rows, kernel_ref):
    taps, count = kernel_ref.shape[0], rows.shape[0] - HALO
    first = HALO - (taps - 1)
    accum = kernel_ref[0:1, :] * rows[first : first + count]
    for tap in range(1, taps):
        accum = accum + kernel_ref[tap : tap + 1, :] * rows[first + tap : first + tap + count]
    return silu(accum).astype(BF16)


def prepare_kernel(
    place_ref, own_ref, other_ref, before_ref, weight_ref, conv_ref, bias_ref, rate_ref,
    bcc_ref, cum_ref, cum_slab_ref, cum_t_ref, step_t_ref, weights_in_ref, decays_ref,
    accum,
):
    step = pl.program_id(0)
    core = place_ref[0]
    slab = own_ref.shape[0]
    heads = cum_t_ref.shape[0]
    rows_own = pl.ds(pl.multiple_of(HALO + slab * core, HALO), slab)
    rows_other = pl.ds(pl.multiple_of(HALO + slab * (1 - core), HALO), slab)

    @pl.when(step == 0)
    def _():
        accum[...] = jnp.zeros_like(accum)

    weight = weight_ref[...]
    for rows, ref in ((slice(0, HALO), before_ref), (rows_own, own_ref), (rows_other, other_ref)):
        accum[rows, :] = accum[rows, :] + jnp.dot(ref[...], weight, preferred_element_type=F32)

    @pl.when(step == pl.num_programs(0) - 1)
    def _():
        total = jnp.zeros((1, LANES), F32)
        row = lax.broadcasted_iota(jnp.int32, (GROUP, GROUP), 0)
        col = lax.broadcasted_iota(jnp.int32, (GROUP, GROUP), 1)
        lower = (row >= col).astype(F32)
        for block in range(2 * slab // GROUP):
            part = slice(block * GROUP, (block + 1) * GROUP)
            narrow = accum[block * GROUP : (block + 1) * GROUP + HALO, : 2 * LANES]
            bcc_ref[part, :] = conv_rows(narrow.astype(BF16).astype(F32), conv_ref)
            raw = accum[block * GROUP + HALO : (block + 1) * GROUP + HALO, 2 * LANES :]
            raw = jnp.where(core == 0, raw, pltpu.roll(raw, LANES - heads, axis=1))
            raw = raw + bias_ref[...]
            step_size = jnp.maximum(raw, 0.0) + jnp.log1p(jnp.exp(-jnp.abs(raw)))
            log_decay = -rate_ref[...] * step_size
            cum = jnp.dot(
                lower, log_decay, preferred_element_type=F32, precision=lax.Precision.HIGHEST
            )
            last = cum[GROUP - 1 : GROUP, :]
            cum_ref[part, :] = cum
            cum_slab_ref[part, :] = cum + total
            cum_t_ref[:, part] = cum.T[:heads, :]
            step_t_ref[:, part] = step_size.T[:heads, :]
            weights_in_ref[part, :] = jnp.exp(last - cum) * step_size
            decays_ref[block * 8 : block * 8 + 8, :] = jnp.broadcast_to(jnp.exp(last), (8, LANES))
            total = total + last
        end = decays_ref.shape[0] - 8
        decays_ref[end:, :] = jnp.broadcast_to(jnp.exp(total), (8, LANES))


def block_columns(ref, place_ref, first, count):
    core = place_ref[0]
    parts = []
    for index in range(first, first + count):
        base = place_ref[1 + index] * (2 * LANES)
        for start in (base + LANES * core, base + LANES * (1 - core)):
            parts.append(ref[:, pl.ds(pl.multiple_of(start, LANES), LANES)])
    return jnp.concatenate(parts, axis=1)


def stacked(sources, refs):
    return jnp.concatenate([refs[ref][first : first + size, :] for ref, first, size in sources], axis=0)


def first_kernel(sources, count, place_ref, own_ref, other_ref, before_ref, *refs):
    weights, (out_ref, out_before_ref) = refs[:-2], refs[-2:]
    block = pl.program_id(0)
    is_own = block // 2 == place_ref[0]

    def product(ref):
        columns = block_columns(ref, place_ref, 0, count)
        return jnp.dot(columns, stacked(sources, weights), preferred_element_type=F32)

    @pl.when(block == 0)
    def _():
        out_before_ref[...] = product(before_ref)

    @pl.when(is_own)
    def _():
        out_ref[...] = product(own_ref)

    @pl.when(jnp.logical_not(is_own))
    def _():
        out_ref[...] = product(other_ref)


def states_kernel(
    sources, done, count, place_ref, own_ref, other_ref, before_ref, *refs
):
    weights = refs[:-12]
    (
        sum_ref, sum_before_ref, bcc_ref, weights_in_ref, decays_ref, conv_ref,
        xc_ref, entering_ref, final_ref,
        state, x_in, tail,
    ) = refs[-12:]
    block = pl.program_id(0)
    width = x_in.shape[1]
    is_own = block // 2 == place_ref[0]

    def product(ref):
        columns = block_columns(ref, place_ref, done, count)
        return jnp.dot(columns, stacked(sources, weights), preferred_element_type=F32)

    @pl.when(block == 0)
    def _():
        state[...] = jnp.zeros_like(state)
        tail[...] = (sum_before_ref[...] + product(before_ref)).astype(BF16).astype(F32)

    @pl.when(is_own)
    def _():
        x_in[...] = (sum_ref[...] + product(own_ref)).astype(BF16).astype(F32)

    @pl.when(jnp.logical_not(is_own))
    def _():
        x_in[...] = (sum_ref[...] + product(other_ref)).astype(BF16).astype(F32)

    rows = jnp.concatenate([tail[...], x_in[...]], axis=0)
    tail[...] = rows[GROUP:]
    xc = conv_rows(rows, conv_ref)
    xc_ref[...] = xc
    entering_ref[0] = state[...].astype(BF16)
    weighted = (expand_heads(weights_in_ref[...], width) * xc.astype(F32)).astype(BF16)
    contrib = lax.dot_general(
        bcc_ref[:, :LANES], weighted, (((0,), (0,)), ((), ())), preferred_element_type=F32
    )
    decay = expand_heads(decays_ref[pl.ds(pl.multiple_of(block * 8, 8), 8), :], width)
    state[...] = state[...] * decay[0:1] + contrib

    @pl.when(block == pl.num_programs(0) - 1)
    def _():
        end = decays_ref.shape[0] - 8
        final_ref[:LANES, :] = state[...].astype(BF16)
        final_ref[LANES:, :] = split_decay(expand_heads(decays_ref[end:, :], width)[0:1])


def split_decay(decay):
    high = decay.astype(BF16)
    low = decay - high.astype(F32)
    row = lax.broadcasted_iota(jnp.int32, (HALO, decay.shape[1]), 0)
    return jnp.where(row == 0, high.astype(F32), jnp.where(row == 1, low, 0.0)).astype(BF16)


def unpacked(sent):
    sent = sent.astype(F32)
    return sent[:LANES], sent[LANES : LANES + 1] + sent[LANES + 1 : LANES + 2]


def row_kernel(place_ref, *refs):
    size = len(refs) - 3
    parts, (total_ref, before_ref, before_decay_ref) = refs[:size], refs[size:]
    place = place_ref[0]
    width = total_ref.shape[1]
    total, decay = jnp.zeros((LANES, width), F32), jnp.ones((1, width), F32)
    before_ref[...] = total
    before_decay_ref[...] = jnp.broadcast_to(decay, before_decay_ref.shape)
    for index in range(size):
        if index > 0:

            @pl.when(place == index)
            def _():
                before_ref[...] = total
                before_decay_ref[...] = jnp.broadcast_to(decay, before_decay_ref.shape)

        distance = (place - index + size) % size
        chosen = parts[0][...]
        for other in range(1, size):
            chosen = jnp.where(distance == other, parts[other][...], chosen)
        state, state_decay = unpacked(chosen)
        total = total * state_decay + state
        decay = decay * state_decay
    total_ref[:LANES, :] = total.astype(BF16)
    total_ref[LANES:, :] = split_decay(decay)


def outputs_kernel(xc_ref, bcc_ref, cum_ref, cum_t_ref, step_t_ref, entering_ref, skip_ref, out_ref):
    width = xc_ref.shape[1]
    b_rows, c_rows = bcc_ref[:, :LANES], bcc_ref[:, LANES:]
    scores = lax.dot_general(c_rows, b_rows, (((1,), (1,)), ((), ())), preferred_element_type=F32)
    row = lax.broadcasted_iota(jnp.int32, (GROUP, GROUP), 0)
    col = lax.broadcasted_iota(jnp.int32, (GROUP, GROUP), 1)
    scores = jnp.where(row >= col, scores, 0.0)
    cum = cum_ref[...]
    grown = expand_heads(jnp.exp(cum), width)
    out_ref[...] = grown * jnp.dot(c_rows, entering_ref[0], preferred_element_type=F32)
    lane = lax.broadcasted_iota(jnp.int32, (GROUP, LANES), 1)

    def mixing(head):
        gaps = cum[:, head : head + 1] - cum_t_ref[head : head + 1, :]
        return (
            scores * jnp.exp(jnp.minimum(gaps, 0.0)) * step_t_ref[head : head + 1, :]
        ).astype(BF16)

    for pair in range(width // LANES):
        lanes = slice(pair * LANES, (pair + 1) * LANES)
        inputs = xc_ref[:, lanes]
        zero = jnp.zeros_like(inputs)
        both = jnp.concatenate([mixing(2 * pair), mixing(2 * pair + 1)], axis=1)
        stacked = jnp.concatenate(
            [jnp.where(lane < HEAD, inputs, zero), jnp.where(lane < HEAD, zero, inputs)], axis=0
        )
        out_ref[:, lanes] = (
            out_ref[:, lanes]
            + jnp.dot(both, stacked, preferred_element_type=F32)
            + skip_ref[:, lanes] * inputs.astype(F32)
        )


def z_kernel(place_ref, own_ref, other_ref, weight_ref, gate_ref, accum):
    step = pl.program_id(0)
    slab = own_ref.shape[0]
    core = place_ref[0]

    def product(ref):
        return jnp.dot(ref[...], weight_ref[...], preferred_element_type=F32)

    for index, ref in enumerate((own_ref, other_ref)):
        rows = slice(index * slab, (index + 1) * slab)
        target = pl.ds(pl.multiple_of(slab * (core if index == 0 else 1 - core), slab), slab)

        @pl.when(step == 0)
        def _():
            accum[rows, :] = product(ref)

        @pl.when((step > 0) & (step < pl.num_programs(0) - 1))
        def _():
            accum[rows, :] = accum[rows, :] + product(ref)

        @pl.when(step == pl.num_programs(0) - 1)
        def _():
            gate_ref[target, :] = (accum[rows, :] + product(ref)).astype(BF16)


def gate_kernel(
    gate_ref, local_ref, bcc_ref, cum_ref, before_ref, before_decay_ref, *refs
):
    earlier, (gated_ref, squares_ref, incoming) = refs[:-3], refs[-3:]
    width = local_ref.shape[1]

    @pl.when(pl.program_id(0) == 0)
    def _():
        carried = jnp.zeros((LANES, width), F32)
        for part in earlier:
            state, decay = unpacked(part[...])
            carried = carried * decay + state
        incoming[...] = (carried * before_decay_ref[0:1, :] + before_ref[...]).astype(BF16)

    grown = expand_heads(jnp.exp(cum_ref[...]), width)
    carried = jnp.dot(bcc_ref[:, LANES:], incoming[...], preferred_element_type=F32)
    gated = (local_ref[...] + grown * carried) * silu(gate_ref[...].astype(F32))
    gated_ref[...] = gated.astype(BF16)
    squares = gated * gated
    high = squares.astype(BF16)
    low = (squares - high.astype(F32)).astype(BF16)
    ones = jnp.ones((8, width), BF16)
    across = (((1,), (1,)), ((), ()))
    summed = lax.dot_general(ones, high, across, preferred_element_type=F32) + lax.dot_general(
        ones, low, across, preferred_element_type=F32
    )
    squares_ref[...] = summed[0:1, :]


def norm_kernel(core_ref, mine_ref, other_ref, squares_ref, gain_ref, out_ref):
    half = pl.program_id(0)
    across = jnp.broadcast_to(squares_ref[...], (8, squares_ref.shape[1]))
    scale = lax.rsqrt(across + 1e-05).T[:, 0:1]

    @pl.when(half == core_ref[0])
    def _():
        out_ref[...] = (mine_ref[...].astype(F32) * scale * gain_ref[...]).astype(BF16)

    @pl.when(half != core_ref[0])
    def _():
        out_ref[...] = (other_ref[...].astype(F32) * scale * gain_ref[...]).astype(BF16)


def whole(shape):
    return pl.BlockSpec(shape, lambda i: (0,) * len(shape))


def rows_of(width):
    return pl.BlockSpec((GROUP, width), lambda i: (i, 0))


def params(flops, megabytes):
    return dict(
        compiler_params=pltpu.CompilerParams(vmem_limit_bytes=48 * 2**20),
        cost_estimate=pl.CostEstimate(
            flops=int(flops), bytes_accessed=megabytes * 2**20, transcendentals=0
        ),
    )


def fixed(a):
    return pl.BlockSpec(a.shape, lambda i, place: (0,) * len(a.shape))


def row_block(width):
    return pl.BlockSpec((GROUP, width), lambda i, place: (i, 0))


def slab_blocks(depth):
    own = pl.BlockSpec((GROUP, depth), lambda i, place: (jnp.clip(i - 2 * place[0], 0, 1), 0))
    other = pl.BlockSpec((GROUP, depth), lambda i, place: (jnp.clip(i - 2 + 2 * place[0], 0, 1), 0))
    return [own, other]


def prepared(place, slabs, weight, conv_bc, bias, rate, heads):
    own, other, before = slabs
    slab, rows, depth = own.shape[0], 2 * own.shape[0], 512
    shape = jax.ShapeDtypeStruct
    outs = [
        shape((rows, 2 * LANES), BF16), shape((rows, LANES), F32), shape((rows, LANES), F32),
        shape((heads, rows), F32), shape((heads, rows), F32), shape((rows, LANES), F32),
        shape((rows // GROUP * 8 + 8, LANES), F32),
    ]
    columns = lambda a: pl.BlockSpec((a.shape[0], depth), lambda i, place: (0, i))
    return pl.pallas_call(
        prepare_kernel,
        grid_spec=pltpu.PrefetchScalarGridSpec(
            num_scalar_prefetch=1,
            grid=(own.shape[1] // depth,),
            in_specs=[columns(a) for a in slabs]
            + [pl.BlockSpec((depth, weight.shape[1]), lambda i, place: (i, 0))]
            + [fixed(a) for a in (conv_bc, bias, rate)],
            out_specs=[fixed(a) for a in outs],
            scratch_shapes=[pltpu.VMEM((HALO + rows, weight.shape[1]), F32)],
        ),
        out_shape=outs,
        name="prepared",
        **params(4e9, 14),
    )(place, *slabs, weight, conv_bc, bias, rate)


def first_products(place, slabs, weights, sources, count):
    own, other, before = slabs
    width = weights[0].shape[1]
    outs = [
        jax.ShapeDtypeStruct((2 * own.shape[0], width), F32), jax.ShapeDtypeStruct((HALO, width), F32),
    ]
    return pl.pallas_call(
        functools.partial(first_kernel, sources, count),
        grid_spec=pltpu.PrefetchScalarGridSpec(
            num_scalar_prefetch=1,
            grid=(2 * own.shape[0] // GROUP,),
            in_specs=slab_blocks(own.shape[1]) + [fixed(a) for a in (before, *weights)],
            out_specs=[row_block(width), fixed(outs[1])],
        ),
        out_shape=outs,
        name="first_products",
        **params(6e9, 18),
    )(place, *slabs, *weights)


def local_states(place, slabs, weights, sources, done, count, sums, bcc, weights_in, decays, conv_x):
    own, other, before = slabs
    rows, width = sums[0].shape
    blocks = rows // GROUP
    outs = [
        jax.ShapeDtypeStruct((rows, width), BF16),
        jax.ShapeDtypeStruct((blocks, LANES, width), BF16),
        jax.ShapeDtypeStruct((LANES + HALO, width), BF16),
    ]
    return pl.pallas_call(
        functools.partial(states_kernel, sources, done, count),
        grid_spec=pltpu.PrefetchScalarGridSpec(
            num_scalar_prefetch=1,
            grid=(blocks,),
            in_specs=slab_blocks(own.shape[1])
            + [fixed(a) for a in (before, *weights)]
            + [
                row_block(width), fixed(sums[1]), row_block(2 * LANES), row_block(LANES),
                fixed(decays), fixed(conv_x),
            ],
            out_specs=[
                row_block(width),
                pl.BlockSpec((1, LANES, width), lambda i, place: (i, 0, 0)),
                fixed(outs[2]),
            ],
            scratch_shapes=[
                pltpu.VMEM((LANES, width), F32), pltpu.VMEM((GROUP, width), F32),
                pltpu.VMEM((HALO, width), F32),
            ],
        ),
        out_shape=outs,
        name="states",
        **params(8e9, 16),
    )(place, *slabs, *weights, *sums, bcc, weights_in, decays, conv_x)


def local_outputs(xc, bcc, cum, cum_t, step_t, entering, skip):
    rows, width = xc.shape
    heads = cum_t.shape[0]
    by_lane = pl.BlockSpec((heads, GROUP), lambda i: (0, i))
    return pl.pallas_call(
        outputs_kernel,
        grid=(rows // GROUP,),
        in_specs=[
            rows_of(width), rows_of(2 * LANES), rows_of(LANES), by_lane, by_lane,
            pl.BlockSpec((1, LANES, width), lambda i: (i, 0, 0)), whole((1, width)),
        ],
        out_specs=rows_of(width),
        out_shape=jax.ShapeDtypeStruct((rows, width), F32),
        compiler_params=pltpu.CompilerParams(vmem_limit_bytes=40 * 2**20),
        cost_estimate=pl.CostEstimate(flops=10**10, bytes_accessed=10 * 2**20, transcendentals=4 * 2**20),
        name="outputs",
    )(xc, bcc, cum, cum_t, step_t, entering, skip)


def project_gate(place, slabs, weight):
    own, other, _ = slabs
    rows, width, depth = 2 * own.shape[0], weight.shape[1], 1024
    columns = pl.BlockSpec((own.shape[0], depth), lambda i, place: (0, i))
    out = jax.ShapeDtypeStruct((rows, width), BF16)
    return pl.pallas_call(
        z_kernel,
        grid_spec=pltpu.PrefetchScalarGridSpec(
            num_scalar_prefetch=1,
            grid=(weight.shape[0] // depth,),
            in_specs=[columns, columns, pl.BlockSpec((depth, width), lambda i, place: (i, 0))],
            out_specs=fixed(out),
            scratch_shapes=[pltpu.VMEM((rows, width), F32)],
        ),
        out_shape=out,
        name="project_gate",
        **params(9e9, 20),
    )(place, own, other, weight)


def gate_outputs(gate, local, bcc, cum_slab, before, before_decay, earlier):
    rows, width = local.shape
    return pl.pallas_call(
        gate_kernel,
        grid=(rows // GROUP,),
        in_specs=[rows_of(width), rows_of(width), rows_of(2 * LANES), rows_of(LANES)]
        + [whole(a.shape) for a in (before, before_decay, *earlier)],
        out_specs=[rows_of(width), pl.BlockSpec((1, GROUP), lambda i: (0, i))],
        out_shape=[
            jax.ShapeDtypeStruct((rows, width), BF16), jax.ShapeDtypeStruct((1, rows), F32),
        ],
        scratch_shapes=[pltpu.VMEM((LANES, width), BF16)],
        name="gate",
        **params(1e9, 10),
    )(gate, local, bcc, cum_slab, before, before_decay, *earlier)


def normalized(core, gated, other, mean_squares, gain):
    rows, width = other.shape
    return pl.pallas_call(
        norm_kernel,
        grid_spec=pltpu.PrefetchScalarGridSpec(
            num_scalar_prefetch=1,
            grid=(2,),
            in_specs=[
                pl.BlockSpec((rows, width), lambda j, core: (core[0], 0)),
                pl.BlockSpec((rows, width), lambda j, core: (0, 0)),
                pl.BlockSpec((1, rows), lambda j, core: (0, 0)),
                pl.BlockSpec((1, width), lambda j, core: (0, j)),
            ],
            out_specs=pl.BlockSpec((rows, width), lambda j, core: (0, j)),
        ),
        out_shape=jax.ShapeDtypeStruct((rows, 2 * width), BF16),
        compiler_params=pltpu.CompilerParams(vmem_limit_bytes=40 * 2**20),
        cost_estimate=pl.CostEstimate(flops=10**7, bytes_accessed=4 * 2**20, transcendentals=0),
        name="normalized",
    )(core.astype(jnp.int32)[None], gated, other, mean_squares, gain)


def earlier_states(final):
    size = lax.axis_size("y")
    parts = [final] + [round_ring(final, "y", distance) for distance in range(1, size)]
    width = final.shape[1]
    outs = [
        jax.ShapeDtypeStruct(final.shape, BF16),
        jax.ShapeDtypeStruct((LANES, width), F32),
        jax.ShapeDtypeStruct((8, width), F32),
    ]
    total, before, before_decay = pl.pallas_call(
        row_kernel,
        grid_spec=pltpu.PrefetchScalarGridSpec(
            num_scalar_prefetch=1,
            grid=(1,),
            in_specs=[fixed(a) for a in parts],
            out_specs=[fixed(a) for a in outs],
        ),
        out_shape=outs,
        name="row_states",
        **params(1e7, 2),
    )(lax.axis_index("y").astype(jnp.int32)[None], *parts)
    rows = lax.axis_size("z")
    earlier = [
        lax.ppermute(total, "z", [(i, i + distance) for i in range(rows - distance)])
        for distance in range(rows - 1, 0, -1)
    ]
    return before, before_decay, earlier


def travelling(own):
    block = own.shape[0]
    half = block // 2
    y_less, y_more = round_ring(own, "y", 1), round_ring(own, "y", -1)
    z_less, z_more = round_ring(own, "z", 1), round_ring(own, "z", -1)
    join = lambda *parts: jnp.concatenate(parts, axis=0)
    from_y_less = round_ring(join(z_less, y_less[:half]), "y", 1)
    from_y_more = round_ring(join(z_more, y_more[half:]), "y", -1)
    from_z_less = round_ring(join(y_more, z_less[:half]), "z", 1)
    from_z_more = round_ring(join(y_less, z_more[half:]), "z", -1)
    y_far = join(from_y_less[block:], from_y_more[block:])
    z_far = join(from_z_less[block:], from_z_more[block:])
    far_y_less, far_y_more = round_ring(z_far, "y", 1), round_ring(z_far, "y", -1)
    far_z_less, far_z_more = round_ring(y_far, "z", 1), round_ring(y_far, "z", -1)
    far_top = round_ring(far_y_less[:half], "y", 1)
    far_low = round_ring(far_z_more[half:], "z", -1)

    full = lambda indices: [(i, 0, block) for i in indices]
    near = [own, y_less, y_more, z_less, z_more, from_y_less, from_y_more, from_z_less, from_z_more]
    near_sources = full(range(9)) + [(i, block, half) for i in (5, 6, 7, 8)]
    far = [far_y_less, far_y_more, far_z_less, far_z_more, far_top, far_low]
    far_sources = full(range(4)) + [(4, 0, half), (5, 0, half)]
    places = (
        ((0, 0), (-1, 0), (1, 0), (0, -1), (0, 1), (-1, -1), (1, 1), (1, -1), (-1, 1), (2, 0), (0, 2))
        + ((-1, 2), (1, 2), (2, -1), (2, 1), (2, 2))
    )
    y, z = lax.axis_index("y"), lax.axis_index("z")
    order = [(z + dz) % 4 * 4 + (y + dy) % 4 for dy, dz in places]
    return near, near_sources, far, far_sources, order


def shards(
    tokens, x_weight, z_weight, bc_weight, dt_weight, conv_x, conv_bc, dt_bias, decay_rate, skip,
    norm_gain,
):
    core = lax.axis_index("core")
    width = x_weight.shape[1] // 2
    heads = dt_weight.shape[1] // 2

    def mine(a, axis):
        size = a.shape[axis] // 2
        return lax.dynamic_slice_in_dim(a, core * size, size, axis)

    def others(a, axis):
        size = a.shape[axis] // 2
        return lax.dynamic_slice_in_dim(a, (1 - core) * size, size, axis)

    def per_lane(a):
        return jnp.pad(mine(a, 0), (0, LANES - heads))[None, :]

    narrow = jnp.concatenate(
        [bc_weight, dt_weight, jnp.zeros((bc_weight.shape[0], LANES - 2 * heads), BF16)], axis=1
    )
    narrow = lax.all_gather(narrow, ("z", "y", "core"), axis=0, tiled=True)
    own_block = jnp.concatenate([mine(x_weight, 1), swap_cores(others(x_weight, 1))], axis=0)
    near, near_sources, far, far_sources, order = travelling(own_block)
    place = jnp.stack([core, *order]).astype(jnp.int32)

    tokens, z_weight, _ = lax.optimization_barrier((tokens, z_weight, own_block))
    other = swap_cores(tokens)
    last = jnp.where(core == 0, other[-HALO:], tokens[-HALO:])
    slabs = (tokens, other, along_chips(last, 1))
    z_block = in_core_order(core, mine(z_weight, 1), swap_cores(others(z_weight, 1)), 0)
    z_block, _ = lax.optimization_barrier((z_block, near[1]))
    z_whole = lax.all_gather(z_block, ("z", "y"), axis=0, tiled=True)

    bcc, cum, cum_slab, cum_t, step_t, weights_in, decays = prepared(
        place, slabs, narrow, conv_bc, per_lane(dt_bias), per_lane(decay_rate), heads
    )
    sums = first_products(place, slabs, near, near_sources, 11)
    xc, entering, final = local_states(
        place, slabs, far, far_sources, 11, 5, sums, bcc, weights_in, decays, mine(conv_x, 1)
    )
    before, before_decay, earlier = earlier_states(final)
    skip_lanes = jnp.repeat(mine(skip, 0), HEAD)[None, :]
    local = local_outputs(xc, bcc, cum, cum_t, step_t, entering, skip_lanes)
    gate = project_gate(place, slabs, z_whole)
    gated, squares = gate_outputs(gate, local, bcc, cum_slab, before, before_decay, earlier)

    other = swap_cores(others(gated, 0))
    summed = mine(squares + swap_cores(squares), 1)
    across = [round_ring(summed, "x", distance) for distance in range(1, lax.axis_size("x"))]
    mean_squares = (summed + sum(across)) / (2 * width * lax.axis_size("x"))
    return normalized(core, gated, other, mean_squares, norm_gain[None, :])


def solution(mesh):
    fine = Mesh(mesh.devices.reshape(4, 4, 2, 4), ("z", "y", "core", "x"))
    ctx = ("z", "y", "core")
    placed = (
        P(ctx, None),
        P(ctx, "x"),
        P(ctx, "x"),
        P(ctx, None),
        P(ctx, "x"),
        P(None, "x"),
        P(),
        P("x"),
        P("x"),
        P("x"),
        P("x"),
    )
    return jax.shard_map(
        shards, mesh=fine, in_specs=placed, out_specs=P(ctx, "x"), check_vma=False
    )
```

time: 265 us -> 217 us (0.82)
  waiting for transfers between devices: 108 us -> 57.3 us
  other arithmetic: 22 us -> 9.64 us
  local copies, waits for them, and re-layouts: 11.6 us -> 21.8 us
  starting transfers between devices: 34.8 us -> 43.7 us
  Pallas kernels: 73.5 us -> 70.4 us
    ppermute x20, waiting for transfers between devices: 96.3 us -> 53.9 us  [round_ring(): lax.ppermute(a, axis, [(i, (i + distance) % size) for i in range(size)])]
    unnamed x54 -> x47, local copies, waits for them, and re-layouts: 4.62 us -> 13.6 us
    ppermute x20, starting transfers between devices: 23.2 us -> 31.3 us  [round_ring(): lax.ppermute(a, axis, [(i, (i + distance) % size) for i in range(size)])]
    select_n x6 -> x1, other arithmetic: 6.52 us -> 0.12 us  [in_core_order(): first = jnp.where(core == 0, mine, other)]
    ppermute x8 -> x5, waiting for transfers between devices: 9.66 us -> 3.31 us  [swap_cores(): return lax.ppermute(a, 'core', [(0, 1), (1, 0)])]
    pallas_call x6 -> x5, Pallas kernels: 58.4 us -> 54.3 us  [the longest x1 16 us: local_states(): pl.pallas_call(functools.partial(states_kernel, sources, done, count), gr...]
    convert_element_type x9 -> x0, other arithmetic: 3.9 us -> none  [the longest x5 3.29 us: unpacked(): sent = sent.astype(F32)]
    concatenate x10 -> x8, other arithmetic: 10.2 us -> 7.05 us  [the longest x6 5.51 us: travelling(): join = lambda *parts: jnp.concatenate(parts, axis=0)]
  transfers between devices with their start and end apart: 33 -> 31, of which waited for: 15 -> 10; matrix products, arithmetic and copies ran while one was open for 9% -> 7% of each run, Pallas kernels for 20% -> 28%
where the time goes in v3:
time: 217 us
  Pallas kernels  70.4 us (32%)
  waiting for transfers between devices  57.3 us (26%)
  starting transfers between devices  43.7 us (20%)
  local copies, waits for them, and re-layouts  21.8 us (10%)
  between operations  13.8 us (6%)
  other arithmetic  9.64 us (4%)
    ppermute x20, waiting for transfers between devices, round_ring(): lax.ppermute(a, axis, [(i, (i + distance) % size) for i in range(size)])  53.9 us
    ppermute x20, starting transfers between devices, round_ring(): lax.ppermute(a, axis, [(i, (i + distance) % size) for i in range(size)])  31.3 us
    pallas_call x1, Pallas kernels, local_states(): pl.pallas_call(functools.partial(states_kernel, sources, done, count), gr...  16 us
    unnamed x47, local copies, waits for them, and re-layouts  13.6 us
    pallas_call x1, Pallas kernels, project_gate(): pl.pallas_call(z_kernel, grid_spec=pltpu.PrefetchScalarGridSpec(num_scala...  13 us
    pallas_call x1, Pallas kernels, first_products(): pl.pallas_call(functools.partial(first_kernel, sources, count), grid_spec...  12.4 us
    pallas_call x1, Pallas kernels, prepared(): pl.pallas_call(prepare_kernel, grid_spec=pltpu.PrefetchScalarGridSpec(num...  12.2 us
    pallas_call x1, Pallas kernels, gate_outputs(): pl.pallas_call(gate_kernel, grid=(rows // GROUP,), in_specs=[rows_of(widt...  7.31 us
  transfers between devices with their start and end apart: 31, of which 10 were waited for; matrix products, arithmetic and copies ran while one was open for 7% of the time, Pallas kernels for 28%

profile of v3, /device:TPU:6, one launch (start us, length us, event | category | flops | bytes accessed | tf_op | source)
XLA Modules:
  0.0 216.7 jit_solution(9000640871222296598)
XLA Ops:
  12.1 1.6 collective-permute-start.3
  14.6 13.4 %collective-permute-done.3.refs_1_ = bf16[256,1024]{1,0:T(8,128)(2,1)S(1)} collective-permute-done((bf16[256,1024]{1,0:T(8,128)(2,1)S(1)}, bf16[256,1024]{1,0:T(8,128)(2,1)S(1)}, u32[]{:S(2)}, u32[]{:S(2)}) %collective-permute-start.3) | collective-permute-done | bytes 524320 | tf_op jit(solution)/shard_map/ppermute | solution.py:24
  28.2 4.6 %collective-permute-start.8 = (bf16[256,1024]{1,0:T(8,128)(2,1)S(1)}, bf16[256,1024]{1,0:T(8,128)(2,1)S(1)}, u32[]{:S(2)}, u32[]{:S(2)}) collective-permute-start(bf16[256,1024]{1,0:T(8,128)(2,1)S(1)} %pad_maximum_fusion.4.refs_0_), channel_id=1, source_target_pairs={{0,96},{32,0},{64,32},{96,64},{1,97},{33,1},{65,33},{97,65},{2,98}... | collective-permute-start | bytes 1572872 | tf_op jit(solution)/shard_map/ppermute | solution.py:24
  32.8 1.8 collective-permute-start.5
  34.6 12.1 %collective-permute-done.8.refs_4_ = bf16[256,1024]{1,0:T(8,128)(2,1)S(1)} collective-permute-done((bf16[256,1024]{1,0:T(8,128)(2,1)S(1)}, bf16[256,1024]{1,0:T(8,128)(2,1)S(1)}, u32[]{:S(2)}, u32[]{:S(2)}) %collective-permute-start.8) | collective-permute-done | bytes 524320 | tf_op jit(solution)/shard_map/ppermute | solution.py:24
  47.7 3.7 %collective-permute-start.9 = (bf16[384,1024]{1,0:T(8,128)(2,1)}, bf16[384,1024]{1,0:T(8,128)(2,1)S(1)}, u32[]{:S(2)}, u32[]{:S(2)}) collective-permute-start(bf16[384,1024]{1,0:T(8,128)(2,1)} %pad_maximum_fusion.1), channel_id=1, source_target_pairs={{0,96},{32,0},{64,32},{96,64},{1,97},{33,1},{65,33},{97,65},{2,98}... | collective-permute-start | bytes 2359304 | tf_op jit(solution)/shard_map/ppermute | solution.py:24
  53.3 1.8 collective-permute-start.13
  56.5 13.8 %collective-permute-done.9.refs_8_ = bf16[384,1024]{1,0:T(8,128)(2,1)S(1)} collective-permute-done((bf16[384,1024]{1,0:T(8,128)(2,1)}, bf16[384,1024]{1,0:T(8,128)(2,1)S(1)}, u32[]{:S(2)}, u32[]{:S(2)}) %collective-permute-start.9) | collective-permute-done | bytes 786464 | tf_op jit(solution)/shard_map/ppermute | solution.py:24
  70.3 2.8 %collective-permute-done.7.refs_7_ = bf16[384,1024]{1,0:T(8,128)(2,1)} collective-permute-done((bf16[384,1024]{1,0:T(8,128)(2,1)}, bf16[384,1024]{1,0:T(8,128)(2,1)}, u32[]{:S(2)}, u32[]{:S(2)}) %collective-permute-start.7) | collective-permute-done | bytes 786464 | tf_op jit(solution)/shard_map/ppermute | solution.py:24
  77.7 2.9 %collective-permute-start.15 = (bf16[256,1024]{1,0:T(8,128)(2,1)}, bf16[256,1024]{1,0:T(8,128)(2,1)}, u32[]{:S(2)}, u32[]{:S(2)}) collective-permute-start(bf16[256,1024]{1,0:T(8,128)(2,1)} %pad_maximum_fusion.7), channel_id=1, source_target_pairs={{0,96},{32,0},{64,32},{96,64},{1,97},{33,1},{65,33},{97,65},{2,98}... | collective-permute-start | bytes 1572872 | tf_op jit(solution)/shard_map/ppermute | solution.py:24
  80.6 1.6 slice_select_fusion
  82.2 4.4 %collective-permute-start.4 = (bf16[16,4096]{1,0:T(8,128)(2,1)}, bf16[16,4096]{1,0:T(8,128)(2,1)}, u32[]{:S(2)}, u32[]{:S(2)}) collective-permute-start(bf16[16,4096]{1,0:T(8,128)(2,1)} %slice_select_fusion), channel_id=1, source_target_pairs={{0,8},{8,16},{16,24},{24,32},{32,40},{40,48},{48,56},{56,64},{64,7... | collective-permute-start | bytes 393224 | tf_op jit(solution)/shard_map/ppermute | solution.py:29
  87.0 4.0 %collective-permute-start.14 = (bf16[256,1024]{1,0:T(8,128)(2,1)}, bf16[256,1024]{1,0:T(8,128)(2,1)}, u32[]{:S(2)}, u32[]{:S(2)}) collective-permute-start(bf16[256,1024]{1,0:T(8,128)(2,1)} %pad_maximum_fusion.7), channel_id=1, source_target_pairs={{0,32},{32,64},{64,96},{96,0},{1,33},{33,65},{65,97},{97,1},{2,34}... | collective-permute-start | bytes 1572872 | tf_op jit(solution)/shard_map/ppermute | solution.py:24
  91.0 5.0 %collective-permute-done.10.refs_0_ = bf16[256,1024]{1,0:T(8,128)(2,1)S(1)} collective-permute-done((bf16[256,1024]{1,0:T(8,128)(2,1)}, bf16[256,1024]{1,0:T(8,128)(2,1)S(1)}, u32[]{:S(2)}, u32[]{:S(2)}) %collective-permute-start.10) | collective-permute-done | bytes 524320 | tf_op jit(solution)/shard_map/ppermute | solution.py:24
  96.9 1.7 slice.58
  98.6 2.3 %collective-permute-start.17 = (bf16[128,1024]{1,0:T(8,128)(2,1)}, bf16[128,1024]{1,0:T(8,128)(2,1)}, u32[]{:S(2)}, u32[]{:S(2)}) collective-permute-start(bf16[128,1024]{1,0:T(8,128)(2,1)} %slice.58), channel_id=1, source_target_pairs={{0,96},{32,0},{64,32},{96,64},{1,97},{33,1},{65,33},{97,65},{2,98}... | collective-permute-start | bytes 786440 | tf_op jit(solution)/shard_map/ppermute | solution.py:24
  102.0 12.4 %first_products.1 = (f32[1024,1024]{1,0:T(8,128)}, f32[16,1024]{1,0:T(8,128)S(1)}) custom-call(s32[17]{0:T(128)S(1)} %stack.68.place_ref, bf16[512,4096]{1,0:T(8,128)(2,1)} %own_ref.3, bf16[512,4096]{1,0:T(8,128)(2,1)} %collective-permute-done.1.other_ref, bf16[16,4096]{1,0:T(8,128)(2,1)} %collective-permute-done.4.before_ref, ...), custom_call_target="tpu_custom_call" | custom-call | flops 6000000000 | bytes 18874368 | tf_op jit(solution)/shard_map/first_products/pallas_call | solution.py:403
  115.0 2.0 copy-done.14
  117.0 12.2 %prepared.1 = (bf16[1024,256]{1,0:T(8,128)(2,1)S(1)}, f32[1024,128]{1,0:T(8,128)S(1)}, f32[1024,128]{1,0:T(8,128)S(1)}, f32[16,1024]{1,0:T(8,128)S(1)}, f32[16,1...) custom-call(s32[17]{0:T(128)S(1)} %stack.68.place_ref, bf16[512,4096]{1,0:T(8,128)(2,1)} %own_ref.3, ...), custom_call_target="tpu_custom_call" | custom-call | flops 4000000000 | bytes 14680064 | tf_op jit(solution)/shard_map/prepared/pallas_call | solution.py:380
  129.3 16.0 %states.1 = (bf16[1024,1024]{1,0:T(8,128)(2,1)}, bf16[4,128,1024]{2,1,0:T(8,128)(2,1)S(1)}, bf16[144,1024]{1,0:T(8,128)(2,1)S(1)}) custom-call(s32[17]{0:T(128)S(1)} %stack.68.place_ref, bf16[512,4096]{1,0:T(8,128)(2,1)} %own_ref.3, bf16[512,4096]{1,0:T(8,128)(2,1)} %collective-permute-done.1.other_ref, bf16[16,4096]{1,0:T(8,128)(2,1)} %collective-permute-done.4.before_ref, ...), custom_call_target="tpu_custom_call" | custom-call | flops 8000000000 | bytes 16777216 | tf_op jit(solution)/shard_map/states/pallas_call | solution.py:426
  145.9 3.5 %collective-permute-start.19 = (bf16[144,1024]{1,0:T(8,128)(2,1)S(1)}, bf16[144,1024]{1,0:T(8,128)(2,1)S(1)}, u32[]{:S(2)}, u32[]{:S(2)}) collective-permute-start(bf16[144,1024]{1,0:T(8,128)(2,1)S(1)} %get-tuple-element.39.refs_0_), channel_id=1, source_target_pairs={{0,16},{8,24},{16,0},{24,8},{1,17},{9,25},{17,1},{25,9},{2,18},{10... | collective-permute-start | bytes 884744 | tf_op jit(solution)/shard_map/ppermute | solution.py:24
  151.7 7.0 %outputs.1.local_ref = f32[1024,1024]{1,0:T(8,128)S(1)} custom-call(bf16[1024,1024]{1,0:T(8,128)(2,1)S(1)} %copy-done.16, bf16[1024,256]{1,0:T(8,128)(2,1)S(1)} %get-tuple-element.30.refs_8_.bcc_ref, f32[1024,128]{1,0:T(8,128)S(1)} %get-tuple-element.34.cum_ref, f32[16,1024]{1,0:T(8,128)S(1)} %get-tuple-element.35.cum_t_ref, ...), custom_call_target="tpu_custom_call" | custom-call | flops 10000000000 | bytes 10485760 | tf_op jit(solution)/shard_map/outputs/pallas_call | solution.py:457
  158.7 1.9 copy-done.1
  160.6 2.0 collective-permute-done.19.refs_2_
  164.1 3.0 %collective-permute-start.21 = (bf16[144,1024]{1,0:T(8,128)(2,1)S(1)}, bf16[144,1024]{1,0:T(8,128)(2,1)S(1)}, u32[]{:S(2)}, u32[]{:S(2)}) collective-permute-start(bf16[144,1024]{1,0:T(8,128)(2,1)S(1)} %get-tuple-element.42), channel_id=1, source_target_pairs={{0,96},{1,97},{2,98},{3,99},{4,100},{5,101},{6,102},{7,103},{8,104... | collective-permute-start | bytes 884744 | tf_op jit(solution)/shard_map/ppermute | solution.py:554
  168.4 2.8 %collective-permute-start.23 = (bf16[144,1024]{1,0:T(8,128)(2,1)S(1)}, bf16[144,1024]{1,0:T(8,128)(2,1)S(1)}, u32[]{:S(2)}, u32[]{:S(2)}) collective-permute-start(bf16[144,1024]{1,0:T(8,128)(2,1)S(1)} %get-tuple-element.42), channel_id=1, source_target_pairs={{0,32},{32,64},{64,96},{1,33},{33,65},{65,97},{2,34},{34,66},{66,9... | collective-permute-start | bytes 884744 | tf_op jit(solution)/shard_map/ppermute | solution.py:554
  171.2 13.0 %project_gate.1.gate_ref = bf16[1024,1024]{1,0:T(8,128)(2,1)S(1)} custom-call(s32[17]{0:T(128)S(1)} %stack.68.place_ref, bf16[512,4096]{1,0:T(8,128)(2,1)} %own_ref.3, bf16[512,4096]{1,0:T(8,128)(2,1)} %collective-permute-done.1.other_ref, bf16[4096,1024]{1,0:T(8,128)(2,1)} %all-gather.3.cloned.1.call-done.weight_ref), custom_call_target="tpu_custom_call" | custom-call | flops 8999999488 | bytes 20971520 | tf_op jit(solution)/shard_map/project_gate/pallas_call | solution.py:477
  188.9 7.3 %gate.1 = (bf16[1024,1024]{1,0:T(8,128)(2,1)S(1)}, f32[1,1024]{1,0:T(1,128)S(1)}) custom-call(bf16[1024,1024]{1,0:T(8,128)(2,1)} %copy-done.2, f32[1024,1024]{1,0:T(8,128)} %copy-done.1, bf16[1024,256]{1,0:T(8,128)(2,1)S(1)} %get-tuple-element.30.refs_8_.bcc_ref, f32[1024,128]{1,0:T(8,128)S(1)} %get-tuple-element.38.cum_ref, f32[128,1024]{1,0:T(8,128)S(1)} %copy-done.4, ...), custom_call_target="tpu_custom_call" | custom-call | flops 1000000000 | bytes 10485760 | tf_op jit(solution)/shard_map/gate/pallas_call | solution.py:494
  197.8 1.8 collective-permute-done.25
  200.4 2.4 %collective-permute-start.26 = (f32[1,512]{1,0:T(1,128)S(1)}, f32[1,512]{1,0:T(1,128)S(1)}, u32[]{:S(2)}, u32[]{:S(2)}) collective-permute-start(f32[1,512]{1,0:T(1,128)S(1)} %dynamic-slice_add_fusion), channel_id=1, source_target_pairs={{0,1},{1,2},{2,3},{3,0},{4,5},{5,6},{6,7},{7,4},{8,9},{9,10},{10,1... | collective-permute-start | bytes 6152 | tf_op jit(solution)/shard_map/ppermute | solution.py:24
  204.4 3.5 %collective-permute-done.27 = f32[1,512]{1,0:T(1,128)S(1)} collective-permute-done((f32[1,512]{1,0:T(1,128)S(1)}, f32[1,512]{1,0:T(1,128)S(1)}, u32[]{:S(2)}, u32[]{:S(2)}) %collective-permute-start.27) | collective-permute-done | bytes 2080 | tf_op jit(solution)/shard_map/ppermute | solution.py:24
  207.9 1.9 normalized.1
  (123 shorter events, 32.9 us)
Async XLA Ops:
  6.5 80.4 %copy-start = (f32[4,2048]{1,0:T(4,128)S(1)}, f32[4,2048]{1,0:T(4,128)}, u32[]{:S(2)}) copy-start(f32[4,2048]{1,0:T(4,128)} %param.16) | copy-start | bytes 98308
  6.5 108.5 %all-gather.5.cloned.1.call-start = ((), (), s32[]{:S(2)}) async-start(), calls=%async_computation.1 | async-start | bytes 3244032 | tf_op jit(solution)/shard_map/all_gather | solution.py:613
  9.0 162.2 %all-gather.3.cloned.1.call-start = ((), (), s32[]{:S(2)}) async-start(), calls=%async_computation | async-start | bytes 8912896 | tf_op jit(solution)/shard_map/all_gather | solution.py:624
  10.2 1.6 collective-permute-start
  11.9 1.8 collective-permute-start.2
  12.1 16.0 %collective-permute-start.3 = (bf16[256,1024]{1,0:T(8,128)(2,1)S(1)}, bf16[256,1024]{1,0:T(8,128)(2,1)S(1)}, u32[]{:S(2)}, u32[]{:S(2)}) collective-permute-start(bf16[256,1024]{1,0:T(8,128)(2,1)S(1)} %pad_maximum_fusion.4.refs_0_), channel_id=1, source_target_pairs={{0,8},{8,16},{16,24},{24,0},{1,9},{9,17},{17,25},{25,1},{2,10},{10... | collective-permute-start | bytes 1572872 | tf_op jit(solution)/shard_map/ppermute | solution.py:24
  28.1 52.5 %collective-permute-start.1 = (bf16[512,4096]{1,0:T(8,128)(2,1)}, bf16[512,4096]{1,0:T(8,128)(2,1)}, u32[]{:S(2)}, u32[]{:S(2)}) collective-permute-start(bf16[512,4096]{1,0:T(8,128)(2,1)} %own_ref.3), channel_id=1, source_target_pairs={{0,4},{4,0},{1,5},{5,1},{2,6},{6,2},{3,7},{7,3},{8,12},{12,8},{9,1... | collective-permute-start | bytes 12582920 | tf_op jit(solution)/shard_map/ppermute | solution.py:19
  28.2 18.5 %collective-permute-start.8 = (bf16[256,1024]{1,0:T(8,128)(2,1)S(1)}, bf16[256,1024]{1,0:T(8,128)(2,1)S(1)}, u32[]{:S(2)}, u32[]{:S(2)}) collective-permute-start(bf16[256,1024]{1,0:T(8,128)(2,1)S(1)} %pad_maximum_fusion.4.refs_0_), channel_id=1, source_target_pairs={{0,96},{32,0},{64,32},{96,64},{1,97},{33,1},{65,33},{97,65},{2,98}... | collective-permute-start | bytes 1572872 | tf_op jit(solution)/shard_map/ppermute | solution.py:24
  32.8 18.5 %collective-permute-start.6 = (bf16[256,1024]{1,0:T(8,128)(2,1)S(1)}, bf16[256,1024]{1,0:T(8,128)(2,1)S(1)}, u32[]{:S(2)}, u32[]{:S(2)}) collective-permute-start(bf16[256,1024]{1,0:T(8,128)(2,1)S(1)} %pad_maximum_fusion.4.refs_0_), channel_id=1, source_target_pairs={{0,32},{32,64},{64,96},{96,0},{1,33},{33,65},{65,97},{97,1},{2,34}... | collective-permute-start | bytes 1572872 | tf_op jit(solution)/shard_map/ppermute | solution.py:24
  32.8 18.6 %collective-permute-start.5 = (bf16[256,1024]{1,0:T(8,128)(2,1)S(1)}, bf16[256,1024]{1,0:T(8,128)(2,1)S(1)}, u32[]{:S(2)}, u32[]{:S(2)}) collective-permute-start(bf16[256,1024]{1,0:T(8,128)(2,1)S(1)} %pad_maximum_fusion.4.refs_0_), channel_id=1, source_target_pairs={{0,24},{8,0},{16,8},{24,16},{1,25},{9,1},{17,9},{25,17},{2,26},{10... | collective-permute-start | bytes 1572872 | tf_op jit(solution)/shard_map/ppermute | solution.py:24
  47.7 22.6 %collective-permute-start.9 = (bf16[384,1024]{1,0:T(8,128)(2,1)}, bf16[384,1024]{1,0:T(8,128)(2,1)S(1)}, u32[]{:S(2)}, u32[]{:S(2)}) collective-permute-start(bf16[384,1024]{1,0:T(8,128)(2,1)} %pad_maximum_fusion.1), channel_id=1, source_target_pairs={{0,96},{32,0},{64,32},{96,64},{1,97},{33,1},{65,33},{97,65},{2,98}... | collective-permute-start | bytes 2359304 | tf_op jit(solution)/shard_map/ppermute | solution.py:24
  52.4 20.7 %collective-permute-start.7 = (bf16[384,1024]{1,0:T(8,128)(2,1)}, bf16[384,1024]{1,0:T(8,128)(2,1)}, u32[]{:S(2)}, u32[]{:S(2)}) collective-permute-start(bf16[384,1024]{1,0:T(8,128)(2,1)} %pad_maximum_fusion), channel_id=1, source_target_pairs={{0,32},{32,64},{64,96},{96,0},{1,33},{33,65},{65,97},{97,1},{2,34}... | collective-permute-start | bytes 2359304 | tf_op jit(solution)/shard_map/ppermute | solution.py:24
  53.3 21.5 %collective-permute-start.13 = (bf16[384,1024]{1,0:T(8,128)(2,1)}, bf16[384,1024]{1,0:T(8,128)(2,1)}, u32[]{:S(2)}, u32[]{:S(2)}) collective-permute-start(bf16[384,1024]{1,0:T(8,128)(2,1)} %pad_maximum_fusion.3), channel_id=1, source_target_pairs={{0,24},{8,0},{16,8},{24,16},{1,25},{9,1},{17,9},{25,17},{2,26},{10... | collective-permute-start | bytes 2359304 | tf_op jit(solution)/shard_map/ppermute | solution.py:24
  56.1 19.7 %collective-permute-start.12 = (bf16[384,1024]{1,0:T(8,128)(2,1)}, bf16[384,1024]{1,0:T(8,128)(2,1)}, u32[]{:S(2)}, u32[]{:S(2)}) collective-permute-start(bf16[384,1024]{1,0:T(8,128)(2,1)} %pad_maximum_fusion.2), channel_id=1, source_target_pairs={{0,8},{8,16},{16,24},{24,0},{1,9},{9,17},{17,25},{25,1},{2,10},{10... | collective-permute-start | bytes 2359304 | tf_op jit(solution)/shard_map/ppermute | solution.py:24
  74.9 21.2 %collective-permute-start.10 = (bf16[256,1024]{1,0:T(8,128)(2,1)}, bf16[256,1024]{1,0:T(8,128)(2,1)S(1)}, u32[]{:S(2)}, u32[]{:S(2)}) collective-permute-start(bf16[256,1024]{1,0:T(8,128)(2,1)} %pad_maximum_fusion.6), channel_id=1, source_target_pairs={{0,8},{8,16},{16,24},{24,0},{1,9},{9,17},{17,25},{25,1},{2,10},{10... | collective-permute-start | bytes 1572872 | tf_op jit(solution)/shard_map/ppermute | solution.py:24
  77.7 19.2 %collective-permute-start.15 = (bf16[256,1024]{1,0:T(8,128)(2,1)}, bf16[256,1024]{1,0:T(8,128)(2,1)}, u32[]{:S(2)}, u32[]{:S(2)}) collective-permute-start(bf16[256,1024]{1,0:T(8,128)(2,1)} %pad_maximum_fusion.7), channel_id=1, source_target_pairs={{0,96},{32,0},{64,32},{96,64},{1,97},{33,1},{65,33},{97,65},{2,98}... | collective-permute-start | bytes 1572872 | tf_op jit(solution)/shard_map/ppermute | solution.py:24
  82.2 18.6 %collective-permute-start.4 = (bf16[16,4096]{1,0:T(8,128)(2,1)}, bf16[16,4096]{1,0:T(8,128)(2,1)}, u32[]{:S(2)}, u32[]{:S(2)}) collective-permute-start(bf16[16,4096]{1,0:T(8,128)(2,1)} %slice_select_fusion), channel_id=1, source_target_pairs={{0,8},{8,16},{16,24},{24,32},{32,40},{40,48},{48,56},{56,64},{64,7... | collective-permute-start | bytes 393224 | tf_op jit(solution)/shard_map/ppermute | solution.py:29
  87.0 42.3 %collective-permute-start.11 = (bf16[256,1024]{1,0:T(8,128)(2,1)}, bf16[256,1024]{1,0:T(8,128)(2,1)}, u32[]{:S(2)}, u32[]{:S(2)}) collective-permute-start(bf16[256,1024]{1,0:T(8,128)(2,1)} %pad_maximum_fusion.6), channel_id=1, source_target_pairs={{0,24},{8,0},{16,8},{24,16},{1,25},{9,1},{17,9},{25,17},{2,26},{10... | collective-permute-start | bytes 1572872 | tf_op jit(solution)/shard_map/ppermute | solution.py:24
  87.0 42.2 %collective-permute-start.14 = (bf16[256,1024]{1,0:T(8,128)(2,1)}, bf16[256,1024]{1,0:T(8,128)(2,1)}, u32[]{:S(2)}, u32[]{:S(2)}) collective-permute-start(bf16[256,1024]{1,0:T(8,128)(2,1)} %pad_maximum_fusion.7), channel_id=1, source_target_pairs={{0,32},{32,64},{64,96},{96,0},{1,33},{33,65},{65,97},{97,1},{2,34}... | collective-permute-start | bytes 1572872 | tf_op jit(solution)/shard_map/ppermute | solution.py:24
  96.9 32.4 %collective-permute-start.16 = (bf16[128,1024]{1,0:T(8,128)(2,1)}, bf16[128,1024]{1,0:T(8,128)(2,1)S(1)}, u32[]{:S(2)}, u32[]{:S(2)}) collective-permute-start(bf16[128,1024]{1,0:T(8,128)(2,1)} %slice.57), channel_id=1, source_target_pairs={{0,8},{8,16},{16,24},{24,0},{1,9},{9,17},{17,25},{25,1},{2,10},{10... | collective-permute-start | bytes 786440 | tf_op jit(solution)/shard_map/ppermute | solution.py:24
  98.6 30.7 %collective-permute-start.17 = (bf16[128,1024]{1,0:T(8,128)(2,1)}, bf16[128,1024]{1,0:T(8,128)(2,1)}, u32[]{:S(2)}, u32[]{:S(2)}) collective-permute-start(bf16[128,1024]{1,0:T(8,128)(2,1)} %slice.58), channel_id=1, source_target_pairs={{0,96},{32,0},{64,32},{96,64},{1,97},{33,1},{65,33},{97,65},{2,98}... | collective-permute-start | bytes 786440 | tf_op jit(solution)/shard_map/ppermute | solution.py:24
  145.3 15.3 %collective-permute-start.18 = (bf16[144,1024]{1,0:T(8,128)(2,1)S(1)}, bf16[144,1024]{1,0:T(8,128)(2,1)S(1)}, u32[]{:S(2)}, u32[]{:S(2)}) collective-permute-start(bf16[144,1024]{1,0:T(8,128)(2,1)S(1)} %get-tuple-element.39.refs_0_), channel_id=1, source_target_pairs={{0,8},{8,16},{16,24},{24,0},{1,9},{9,17},{17,25},{25,1},{2,10},{10... | collective-permute-start | bytes 884744 | tf_op jit(solution)/shard_map/ppermute | solution.py:24
  145.9 16.6 %collective-permute-start.19 = (bf16[144,1024]{1,0:T(8,128)(2,1)S(1)}, bf16[144,1024]{1,0:T(8,128)(2,1)S(1)}, u32[]{:S(2)}, u32[]{:S(2)}) collective-permute-start(bf16[144,1024]{1,0:T(8,128)(2,1)S(1)} %get-tuple-element.39.refs_0_), channel_id=1, source_target_pairs={{0,16},{8,24},{16,0},{24,8},{1,17},{9,25},{17,1},{25,9},{2,18},{10... | collective-permute-start | bytes 884744 | tf_op jit(solution)/shard_map/ppermute | solution.py:24
  149.4 13.1 %collective-permute-start.20 = (bf16[144,1024]{1,0:T(8,128)(2,1)S(1)}, bf16[144,1024]{1,0:T(8,128)(2,1)S(1)}, u32[]{:S(2)}, u32[]{:S(2)}) collective-permute-start(bf16[144,1024]{1,0:T(8,128)(2,1)S(1)} %get-tuple-element.39.refs_0_), channel_id=1, source_target_pairs={{0,24},{8,0},{16,8},{24,16},{1,25},{9,1},{17,9},{25,17},{2,26},{10... | collective-permute-start | bytes 884744 | tf_op jit(solution)/shard_map/ppermute | solution.py:24
  164.1 21.4 %collective-permute-start.21 = (bf16[144,1024]{1,0:T(8,128)(2,1)S(1)}, bf16[144,1024]{1,0:T(8,128)(2,1)S(1)}, u32[]{:S(2)}, u32[]{:S(2)}) collective-permute-start(bf16[144,1024]{1,0:T(8,128)(2,1)S(1)} %get-tuple-element.42), channel_id=1, source_target_pairs={{0,96},{1,97},{2,98},{3,99},{4,100},{5,101},{6,102},{7,103},{8,104... | collective-permute-start | bytes 884744 | tf_op jit(solution)/shard_map/ppermute | solution.py:554
  167.1 18.4 %collective-permute-start.22 = (bf16[144,1024]{1,0:T(8,128)(2,1)S(1)}, bf16[144,1024]{1,0:T(8,128)(2,1)S(1)}, u32[]{:S(2)}, u32[]{:S(2)}) collective-permute-start(bf16[144,1024]{1,0:T(8,128)(2,1)S(1)} %get-tuple-element.42), channel_id=1, source_target_pairs={{0,64},{32,96},{1,65},{33,97},{2,66},{34,98},{3,67},{35,99},{4,68}... | collective-permute-start | bytes 884744 | tf_op jit(solution)/shard_map/ppermute | solution.py:554
  168.4 17.8 %collective-permute-start.23 = (bf16[144,1024]{1,0:T(8,128)(2,1)S(1)}, bf16[144,1024]{1,0:T(8,128)(2,1)S(1)}, u32[]{:S(2)}, u32[]{:S(2)}) collective-permute-start(bf16[144,1024]{1,0:T(8,128)(2,1)S(1)} %get-tuple-element.42), channel_id=1, source_target_pairs={{0,32},{32,64},{64,96},{1,33},{33,65},{65,97},{2,34},{34,66},{66,9... | collective-permute-start | bytes 884744 | tf_op jit(solution)/shard_map/ppermute | solution.py:554
  197.2 10.7 %collective-permute-start.24 = (bf16[512,1024]{1,0:T(8,128)(2,1)}, bf16[512,1024]{1,0:T(8,128)(2,1)S(1)}, u32[]{:S(2)}, u32[]{:S(2)}) collective-permute-start(bf16[512,1024]{1,0:T(8,128)(2,1)} %constant_dynamic-slice_fusion), channel_id=1, source_target_pairs={{0,4},{4,0},{1,5},{5,1},{2,6},{6,2},{3,7},{7,3},{8,12},{12,8},{9,1... | collective-permute-start | bytes 3145736 | tf_op jit(solution)/shard_map/ppermute | solution.py:19
  197.2 2.3 %collective-permute-start.25 = (f32[1,1024]{1,0:T(1,128)S(1)}, f32[1,1024]{1,0:T(1,128)S(1)}, u32[]{:S(2)}, u32[]{:S(2)}) collective-permute-start(f32[1,1024]{1,0:T(1,128)S(1)} %get-tuple-element.44), channel_id=1, source_target_pairs={{0,4},{4,0},{1,5},{5,1},{2,6},{6,2},{3,7},{7,3},{8,12},{12,8},{9,1... | collective-permute-start | bytes 12296 | tf_op jit(solution)/shard_map/ppermute | solution.py:19
  199.5 4.8 %collective-permute-start.28 = (f32[1,512]{1,0:T(1,128)S(1)}, f32[1,512]{1,0:T(1,128)S(1)}, u32[]{:S(2)}, u32[]{:S(2)}) collective-permute-start(f32[1,512]{1,0:T(1,128)S(1)} %dynamic-slice_add_fusion), channel_id=1, source_target_pairs={{0,3},{1,0},{2,1},{3,2},{4,7},{5,4},{6,5},{7,6},{8,11},{9,8},{10,9... | collective-permute-start | bytes 6152 | tf_op jit(solution)/shard_map/ppermute | solution.py:24
  200.4 3.9 %collective-permute-start.26 = (f32[1,512]{1,0:T(1,128)S(1)}, f32[1,512]{1,0:T(1,128)S(1)}, u32[]{:S(2)}, u32[]{:S(2)}) collective-permute-start(f32[1,512]{1,0:T(1,128)S(1)} %dynamic-slice_add_fusion), channel_id=1, source_target_pairs={{0,1},{1,2},{2,3},{3,0},{4,5},{5,6},{6,7},{7,4},{8,9},{9,10},{10,1... | collective-permute-start | bytes 6152 | tf_op jit(solution)/shard_map/ppermute | solution.py:24
  202.8 5.1 %collective-permute-start.27 = (f32[1,512]{1,0:T(1,128)S(1)}, f32[1,512]{1,0:T(1,128)S(1)}, u32[]{:S(2)}, u32[]{:S(2)}) collective-permute-start(f32[1,512]{1,0:T(1,128)S(1)} %dynamic-slice_add_fusion), channel_id=1, source_target_pairs={{0,2},{1,3},{2,0},{3,1},{4,6},{5,7},{6,4},{7,5},{8,10},{9,11},{10,... | collective-permute-start | bytes 6152 | tf_op jit(solution)/shard_map/ppermute | solution.py:24
  (22 other events, 134.7 us)
Sparse Core Ops, SparseCore 0:
  9.6 49.0 all-gather.4
  60.8 78.5 all-gather.2

commit v4 on v3

--- a/solution.py
+++ b/solution.py
@@ -11,6 +11,7 @@
 HALO = 16
 LANES = 128
 HEAD = 64
+VMEM = 60 * 2**20
 F32 = jnp.float32
 BF16 = jnp.bfloat16
 
@@ -61,54 +62,16 @@
     return silu(accum).astype(BF16)
 
 
-def prepare_kernel(
-    place_ref, own_ref, other_ref, before_ref, weight_ref, conv_ref, bias_ref, rate_ref,
-    bcc_ref, cum_ref, cum_slab_ref, cum_t_ref, step_t_ref, weights_in_ref, decays_ref,
-    accum,
-):
-    step = pl.program_id(0)
-    core = place_ref[0]
-    slab = own_ref.shape[0]
-    heads = cum_t_ref.shape[0]
-    rows_own = pl.ds(pl.multiple_of(HALO + slab * core, HALO), slab)
-    rows_other = pl.ds(pl.multiple_of(HALO + slab * (1 - core), HALO), slab)
-
-    @pl.when(step == 0)
-    def _():
-        accum[...] = jnp.zeros_like(accum)
-
-    weight = weight_ref[...]
-    for rows, ref in ((slice(0, HALO), before_ref), (rows_own, own_ref), (rows_other, other_ref)):
-        accum[rows, :] = accum[rows, :] + jnp.dot(ref[...], weight, preferred_element_type=F32)
-
-    @pl.when(step == pl.num_programs(0) - 1)
-    def _():
-        total = jnp.zeros((1, LANES), F32)
-        row = lax.broadcasted_iota(jnp.int32, (GROUP, GROUP), 0)
-        col = lax.broadcasted_iota(jnp.int32, (GROUP, GROUP), 1)
-        lower = (row >= col).astype(F32)
-        for block in range(2 * slab // GROUP):
-            part = slice(block * GROUP, (block + 1) * GROUP)
-            narrow = accum[block * GROUP : (block + 1) * GROUP + HALO, : 2 * LANES]
-            bcc_ref[part, :] = conv_rows(narrow.astype(BF16).astype(F32), conv_ref)
-            raw = accum[block * GROUP + HALO : (block + 1) * GROUP + HALO, 2 * LANES :]
-            raw = jnp.where(core == 0, raw, pltpu.roll(raw, LANES - heads, axis=1))
-            raw = raw + bias_ref[...]
-            step_size = jnp.maximum(raw, 0.0) + jnp.log1p(jnp.exp(-jnp.abs(raw)))
-            log_decay = -rate_ref[...] * step_size
-            cum = jnp.dot(
-                lower, log_decay, preferred_element_type=F32, precision=lax.Precision.HIGHEST
-            )
-            last = cum[GROUP - 1 : GROUP, :]
-            cum_ref[part, :] = cum
-            cum_slab_ref[part, :] = cum + total
-            cum_t_ref[:, part] = cum.T[:heads, :]
-            step_t_ref[:, part] = step_size.T[:heads, :]
-            weights_in_ref[part, :] = jnp.exp(last - cum) * step_size
-            decays_ref[block * 8 : block * 8 + 8, :] = jnp.broadcast_to(jnp.exp(last), (8, LANES))
-            total = total + last
-        end = decays_ref.shape[0] - 8
-        decays_ref[end:, :] = jnp.broadcast_to(jnp.exp(total), (8, LANES))
+def pack_kernel(core_ref, x_ref, bc_ref, dt_ref, mine_ref, send_ref):
+    width, heads = x_ref.shape[1] // 2, dt_ref.shape[0] // 2
+    rows = x_ref.shape[0]
+    for ref, core in ((mine_ref, core_ref[0]), (send_ref, 1 - core_ref[0])):
+        for panel in range(width // LANES):
+            lanes = pl.ds(pl.multiple_of(core * width + panel * LANES, LANES), LANES)
+            ref[panel * rows : (panel + 1) * rows, :] = x_ref[:, lanes]
+        lanes = pl.ds(pl.multiple_of(core * LANES, LANES), LANES)
+        ref[width // LANES * rows : width // LANES * rows + rows, :] = bc_ref[:, lanes]
+        ref[width // LANES * rows + rows :, :] = dt_ref[pl.ds(pl.multiple_of(core * heads, heads), heads), :]
 
 
 def block_columns(ref, place_ref, first, count):
@@ -121,52 +84,98 @@
     return jnp.concatenate(parts, axis=1)
 
 
-def stacked(sources, refs):
-    return jnp.concatenate([refs[ref][first : first + size, :] for ref, first, size in sources], axis=0)
-
-
-def first_kernel(sources, count, place_ref, own_ref, other_ref, before_ref, *refs):
-    weights, (out_ref, out_before_ref) = refs[:-2], refs[-2:]
+def unpack_wide(chunks, refs, target):
+    for index, (ref, base) in enumerate(chunks):
+        for panel in range(target.shape[1] // LANES):
+            start = base + panel * LANES
+            target[index * LANES : (index + 1) * LANES, panel * LANES : (panel + 1) * LANES] = refs[
+                ref
+            ][start : start + LANES, :]
+
+
+def unpack_narrow(chunks, refs, width, bc, dt):
+    for index, (ref, base) in enumerate(chunks):
+        rows = slice(index * LANES, (index + 1) * LANES)
+        bc[rows, :] = refs[ref][base + width : base + width + LANES, :]
+        dt[:, rows] = refs[ref][base + width + LANES : base + width + LANES + dt.shape[0], :]
+
+
+def narrow_products(columns, bc, dt):
+    turned = (((1,), (1,)), ((), ()))
+    return (
+        jnp.dot(columns, bc[...], preferred_element_type=F32),
+        lax.dot_general(columns, dt[...], turned, preferred_element_type=F32),
+    )
+
+
+def first_kernel(chunks, count, place_ref, own_ref, other_ref, before_ref, *refs):
+    weights = refs[:-8]
+    x_ref, x_before_ref, bc_ref, bc_before_ref, dt_ref, wide, bc, dt = refs[-8:]
     block = pl.program_id(0)
     is_own = block // 2 == place_ref[0]
 
-    def product(ref):
+    @pl.when(block == 0)
+    def _():
+        unpack_wide(chunks, weights, wide)
+        unpack_narrow(chunks, weights, wide.shape[1], bc, dt)
+        columns = block_columns(before_ref, place_ref, 0, count)
+        x_before_ref[...] = jnp.dot(columns, wide[...], preferred_element_type=F32)
+        bc_before_ref[...] = narrow_products(columns, bc, dt)[0]
+
+    def products(ref):
         columns = block_columns(ref, place_ref, 0, count)
-        return jnp.dot(columns, stacked(sources, weights), preferred_element_type=F32)
+        x_ref[...] = jnp.dot(columns, wide[...], preferred_element_type=F32)
+        bc_ref[...], dt_ref[...] = narrow_products(columns, bc, dt)
+
+    @pl.when(is_own)
+    def _():
+        products(own_ref)
+
+    @pl.when(jnp.logical_not(is_own))
+    def _():
+        products(other_ref)
+
+
+def narrow_kernel(chunks, width, done, count, place_ref, own_ref, other_ref, before_ref, *refs):
+    weights = refs[:-7]
+    sum_ref, sum_before_ref, sum_dt_ref, out_ref, raw_ref, bc, dt = refs[-7:]
+    block = pl.program_id(0)
+    is_own = block // 2 == place_ref[0]
+    rows = pl.ds(pl.multiple_of(HALO + block * GROUP, HALO), GROUP)
 
     @pl.when(block == 0)
     def _():
-        out_before_ref[...] = product(before_ref)
+        unpack_narrow(chunks, weights, width, bc, dt)
+        columns = block_columns(before_ref, place_ref, done, count)
+        out_ref[:HALO, :] = (sum_before_ref[...] + narrow_products(columns, bc, dt)[0]).astype(BF16)
+
+    def products(ref):
+        added, raw = narrow_products(block_columns(ref, place_ref, done, count), bc, dt)
+        out_ref[rows, :] = (sum_ref[...] + added).astype(BF16)
+        raw_ref[...] = sum_dt_ref[...] + raw
 
     @pl.when(is_own)
     def _():
-        out_ref[...] = product(own_ref)
+        products(own_ref)
 
     @pl.when(jnp.logical_not(is_own))
     def _():
-        out_ref[...] = product(other_ref)
-
-
-def states_kernel(
-    sources, done, count, place_ref, own_ref, other_ref, before_ref, *refs
-):
-    weights = refs[:-12]
-    (
-        sum_ref, sum_before_ref, bcc_ref, weights_in_ref, decays_ref, conv_ref,
-        xc_ref, entering_ref, final_ref,
-        state, x_in, tail,
-    ) = refs[-12:]
+        products(other_ref)
+
+
+def inputs_kernel(chunks, done, count, place_ref, own_ref, other_ref, before_ref, *refs):
+    weights = refs[:-7]
+    sum_ref, sum_before_ref, conv_ref, xc_ref, wide, x_in, tail = refs[-7:]
     block = pl.program_id(0)
-    width = x_in.shape[1]
     is_own = block // 2 == place_ref[0]
 
     def product(ref):
         columns = block_columns(ref, place_ref, done, count)
-        return jnp.dot(columns, stacked(sources, weights), preferred_element_type=F32)
+        return jnp.dot(columns, wide[...], preferred_element_type=F32)
 
     @pl.when(block == 0)
     def _():
-        state[...] = jnp.zeros_like(state)
+        unpack_wide(chunks, weights, wide)
         tail[...] = (sum_before_ref[...] + product(before_ref)).astype(BF16).astype(F32)
 
     @pl.when(is_own)
@@ -179,21 +188,57 @@
 
     rows = jnp.concatenate([tail[...], x_in[...]], axis=0)
     tail[...] = rows[GROUP:]
-    xc = conv_rows(rows, conv_ref)
-    xc_ref[...] = xc
+    xc_ref[...] = conv_rows(rows, conv_ref)
+
+
+def states_kernel(
+    core_ref, xc_ref, bc_mine_ref, bc_other_ref, raw_ref, conv_ref, bias_ref, rate_ref,
+    bcc_ref, cum_ref, cum_slab_ref, cum_t_ref, step_t_ref, entering_ref, final_ref,
+    state, total,
+):
+    block = pl.program_id(0)
+    width, heads = xc_ref.shape[1], cum_t_ref.shape[0]
+    start = pl.multiple_of(block * GROUP, GROUP)
+
+    @pl.when(block == 0)
+    def _():
+        state[...] = jnp.zeros_like(state)
+        total[...] = jnp.zeros_like(total)
+
+    mine = bc_mine_ref[pl.ds(start, GROUP + HALO), :].astype(F32)
+    other = bc_other_ref[pl.ds(start, GROUP + HALO), :].astype(F32)
+    first = core_ref[0] == 0
+    b_rows = conv_rows(jnp.where(first, mine, other), conv_ref.at[:, :LANES])
+    c_rows = conv_rows(jnp.where(first, other, mine), conv_ref.at[:, LANES:])
+    bcc_ref[:, :LANES] = b_rows
+    bcc_ref[:, LANES:] = c_rows
+    raw = jnp.concatenate([raw_ref[...], jnp.zeros((GROUP, LANES - heads), F32)], axis=1)
+    raw = raw + bias_ref[...]
+    step_size = jnp.maximum(raw, 0.0) + jnp.log1p(jnp.exp(-jnp.abs(raw)))
+    log_decay = -rate_ref[...] * step_size
+    row = lax.broadcasted_iota(jnp.int32, (GROUP, GROUP), 0)
+    col = lax.broadcasted_iota(jnp.int32, (GROUP, GROUP), 1)
+    lower = (row >= col).astype(F32)
+    cum = jnp.dot(lower, log_decay, preferred_element_type=F32, precision=lax.Precision.HIGHEST)
+    last = cum[GROUP - 1 : GROUP, :]
+    cum_ref[...] = cum
+    cum_slab_ref[...] = cum + total[0:1, :]
+    cum_t_ref[...] = cum.T[:heads, :]
+    step_t_ref[...] = step_size.T[:heads, :]
     entering_ref[0] = state[...].astype(BF16)
-    weighted = (expand_heads(weights_in_ref[...], width) * xc.astype(F32)).astype(BF16)
+    weights_in = expand_heads(jnp.exp(last - cum) * step_size, width)
+    weighted = (weights_in * xc_ref[...].astype(F32)).astype(BF16)
     contrib = lax.dot_general(
-        bcc_ref[:, :LANES], weighted, (((0,), (0,)), ((), ())), preferred_element_type=F32
-    )
-    decay = expand_heads(decays_ref[pl.ds(pl.multiple_of(block * 8, 8), 8), :], width)
+        b_rows, weighted, (((0,), (0,)), ((), ())), preferred_element_type=F32
+    )
+    decay = expand_heads(jnp.broadcast_to(jnp.exp(last), (8, LANES)), width)
     state[...] = state[...] * decay[0:1] + contrib
+    total[...] = total[...] + jnp.broadcast_to(last, total.shape)
 
     @pl.when(block == pl.num_programs(0) - 1)
     def _():
-        end = decays_ref.shape[0] - 8
         final_ref[:LANES, :] = state[...].astype(BF16)
-        final_ref[LANES:, :] = split_decay(expand_heads(decays_ref[end:, :], width)[0:1])
+        final_ref[LANES:, :] = split_decay(expand_heads(jnp.exp(total[...]), width)[0:1])
 
 
 def split_decay(decay):
@@ -346,7 +391,7 @@
 
 def params(flops, megabytes):
     return dict(
-        compiler_params=pltpu.CompilerParams(vmem_limit_bytes=48 * 2**20),
+        compiler_params=pltpu.CompilerParams(vmem_limit_bytes=VMEM),
         cost_estimate=pl.CostEstimate(
             flops=int(flops), bytes_accessed=megabytes * 2**20, transcendentals=0
         ),
@@ -367,87 +412,115 @@
     return [own, other]
 
 
-def prepared(place, slabs, weight, conv_bc, bias, rate, heads):
-    own, other, before = slabs
-    slab, rows, depth = own.shape[0], 2 * own.shape[0], 512
-    shape = jax.ShapeDtypeStruct
-    outs = [
-        shape((rows, 2 * LANES), BF16), shape((rows, LANES), F32), shape((rows, LANES), F32),
-        shape((heads, rows), F32), shape((heads, rows), F32), shape((rows, LANES), F32),
-        shape((rows // GROUP * 8 + 8, LANES), F32),
-    ]
-    columns = lambda a: pl.BlockSpec((a.shape[0], depth), lambda i, place: (0, i))
+def packed_weights(core, x_weight, bc_weight, dt_turned):
+    out = jax.ShapeDtypeStruct(
+        (x_weight.shape[1] // 2 + bc_weight.shape[0] + dt_turned.shape[0] // 2, LANES), BF16
+    )
     return pl.pallas_call(
-        prepare_kernel,
+        pack_kernel,
         grid_spec=pltpu.PrefetchScalarGridSpec(
             num_scalar_prefetch=1,
-            grid=(own.shape[1] // depth,),
-            in_specs=[columns(a) for a in slabs]
-            + [pl.BlockSpec((depth, weight.shape[1]), lambda i, place: (i, 0))]
-            + [fixed(a) for a in (conv_bc, bias, rate)],
-            out_specs=[fixed(a) for a in outs],
-            scratch_shapes=[pltpu.VMEM((HALO + rows, weight.shape[1]), F32)],
+            grid=(1,),
+            in_specs=[fixed(a) for a in (x_weight, bc_weight, dt_turned)],
+            out_specs=[fixed(out), fixed(out)],
         ),
-        out_shape=outs,
-        name="prepared",
-        **params(4e9, 14),
-    )(place, *slabs, weight, conv_bc, bias, rate)
-
-
-def first_products(place, slabs, weights, sources, count):
+        out_shape=[out, out],
+        name="packed_weights",
+        **params(1e6, 1),
+    )(core, x_weight, bc_weight, dt_turned)
+
+
+def by_blocks(kernel, name, cost, place, slabs, weights, extras, extra_specs, outs, out_specs, scratch):
     own, other, before = slabs
-    width = weights[0].shape[1]
-    outs = [
-        jax.ShapeDtypeStruct((2 * own.shape[0], width), F32), jax.ShapeDtypeStruct((HALO, width), F32),
-    ]
     return pl.pallas_call(
-        functools.partial(first_kernel, sources, count),
+        kernel,
         grid_spec=pltpu.PrefetchScalarGridSpec(
             num_scalar_prefetch=1,
             grid=(2 * own.shape[0] // GROUP,),
-            in_specs=slab_blocks(own.shape[1]) + [fixed(a) for a in (before, *weights)],
-            out_specs=[row_block(width), fixed(outs[1])],
+            in_specs=slab_blocks(own.shape[1]) + [fixed(a) for a in (before, *weights)] + extra_specs,
+            out_specs=out_specs,
+            scratch_shapes=scratch,
         ),
         out_shape=outs,
-        name="first_products",
-        **params(6e9, 18),
-    )(place, *slabs, *weights)
-
-
-def local_states(place, slabs, weights, sources, done, count, sums, bcc, weights_in, decays, conv_x):
-    own, other, before = slabs
-    rows, width = sums[0].shape
-    blocks = rows // GROUP
+        name=name,
+        **cost,
+    )(place, *slabs, *weights, *extras)
+
+
+def first_products(place, slabs, weights, chunks, width, heads):
+    shape, rows = jax.ShapeDtypeStruct, 2 * slabs[0].shape[0]
     outs = [
-        jax.ShapeDtypeStruct((rows, width), BF16),
-        jax.ShapeDtypeStruct((blocks, LANES, width), BF16),
-        jax.ShapeDtypeStruct((LANES + HALO, width), BF16),
+        shape((rows, width), F32), shape((HALO, width), F32),
+        shape((rows, LANES), F32), shape((HALO, LANES), F32), shape((rows, heads), F32),
+    ]
+    specs = [row_block(width), fixed(outs[1]), row_block(LANES), fixed(outs[3]), row_block(heads)]
+    depth = len(chunks) * LANES
+    scratch = [
+        pltpu.VMEM((depth, width), BF16), pltpu.VMEM((depth, LANES), BF16), pltpu.VMEM((heads, depth), BF16),
+    ]
+    kernel = functools.partial(first_kernel, chunks, len(chunks) // 2)
+    return by_blocks(
+        kernel, "first_products", params(9e9, 20), place, slabs, weights, [], [], outs, specs, scratch
+    )
+
+
+def narrow_inputs(place, slabs, weights, chunks, done, sums):
+    sum_bc, sum_before, sum_dt = sums
+    rows, heads = sum_dt.shape
+    width = weights[0].shape[0] // 2 - LANES - heads
+    outs = [jax.ShapeDtypeStruct((HALO + rows, LANES), BF16), jax.ShapeDtypeStruct((rows, heads), F32)]
+    depth = len(chunks) * LANES
+    return by_blocks(
+        functools.partial(narrow_kernel, chunks, width, done, len(chunks) // 2),
+        "narrow_inputs", params(2e9, 12), place, slabs, weights,
+        [sum_bc, sum_before, sum_dt], [row_block(LANES), fixed(sum_before), row_block(heads)],
+        outs, [fixed(outs[0]), row_block(heads)],
+        [pltpu.VMEM((depth, LANES), BF16), pltpu.VMEM((heads, depth), BF16)],
+    )
+
+
+def head_inputs(place, slabs, weights, chunks, done, sums, conv_x):
+    sum_x, sum_before = sums
+    rows, width = sum_x.shape
+    return by_blocks(
+        functools.partial(inputs_kernel, chunks, done, len(chunks) // 2),
+        "head_inputs", params(5e9, 18), place, slabs, weights,
+        [sum_x, sum_before, conv_x], [row_block(width), fixed(sum_before), fixed(conv_x)],
+        jax.ShapeDtypeStruct((rows, width), BF16), row_block(width),
+        [
+            pltpu.VMEM((len(chunks) * LANES, width), BF16), pltpu.VMEM((GROUP, width), F32),
+            pltpu.VMEM((HALO, width), F32),
+        ],
+    )
+
+
+def local_states(core, xc, bc_mine, bc_other, raw, conv_bc, bias, rate):
+    rows, width = xc.shape
+    heads, blocks = raw.shape[1], rows // GROUP
+    shape = jax.ShapeDtypeStruct
+    by_lane = pl.BlockSpec((heads, GROUP), lambda i, core: (0, i))
+    outs = [
+        shape((rows, 2 * LANES), BF16), shape((rows, LANES), F32), shape((rows, LANES), F32),
+        shape((heads, rows), F32), shape((heads, rows), F32),
+        shape((blocks, LANES, width), BF16), shape((LANES + HALO, width), BF16),
     ]
     return pl.pallas_call(
-        functools.partial(states_kernel, sources, done, count),
+        states_kernel,
         grid_spec=pltpu.PrefetchScalarGridSpec(
             num_scalar_prefetch=1,
             grid=(blocks,),
-            in_specs=slab_blocks(own.shape[1])
-            + [fixed(a) for a in (before, *weights)]
-            + [
-                row_block(width), fixed(sums[1]), row_block(2 * LANES), row_block(LANES),
-                fixed(decays), fixed(conv_x),
+            in_specs=[row_block(width), fixed(bc_mine), fixed(bc_other), row_block(heads)]
+            + [fixed(a) for a in (conv_bc, bias, rate)],
+            out_specs=[
+                row_block(2 * LANES), row_block(LANES), row_block(LANES), by_lane, by_lane,
+                pl.BlockSpec((1, LANES, width), lambda i, core: (i, 0, 0)), fixed(outs[6]),
             ],
-            out_specs=[
-                row_block(width),
-                pl.BlockSpec((1, LANES, width), lambda i, place: (i, 0, 0)),
-                fixed(outs[2]),
-            ],
-            scratch_shapes=[
-                pltpu.VMEM((LANES, width), F32), pltpu.VMEM((GROUP, width), F32),
-                pltpu.VMEM((HALO, width), F32),
-            ],
+            scratch_shapes=[pltpu.VMEM((LANES, width), F32), pltpu.VMEM((8, LANES), F32)],
         ),
         out_shape=outs,
         name="states",
-        **params(8e9, 16),
-    )(place, *slabs, *weights, *sums, bcc, weights_in, decays, conv_x)
+        **params(5e9, 8),
+    )(core, xc, bc_mine, bc_other, raw, conv_bc, bias, rate)
 
 
 def local_outputs(xc, bcc, cum, cum_t, step_t, entering, skip):
@@ -463,7 +536,7 @@
         ],
         out_specs=rows_of(width),
         out_shape=jax.ShapeDtypeStruct((rows, width), F32),
-        compiler_params=pltpu.CompilerParams(vmem_limit_bytes=40 * 2**20),
+        compiler_params=pltpu.CompilerParams(vmem_limit_bytes=VMEM),
         cost_estimate=pl.CostEstimate(flops=10**10, bytes_accessed=10 * 2**20, transcendentals=4 * 2**20),
         name="outputs",
     )(xc, bcc, cum, cum_t, step_t, entering, skip)
@@ -522,7 +595,7 @@
             out_specs=pl.BlockSpec((rows, width), lambda j, core: (0, j)),
         ),
         out_shape=jax.ShapeDtypeStruct((rows, 2 * width), BF16),
-        compiler_params=pltpu.CompilerParams(vmem_limit_bytes=40 * 2**20),
+        compiler_params=pltpu.CompilerParams(vmem_limit_bytes=VMEM),
         cost_estimate=pl.CostEstimate(flops=10**7, bytes_accessed=4 * 2**20, transcendentals=0),
         name="normalized",
     )(core.astype(jnp.int32)[None], gated, other, mean_squares, gain)
@@ -557,7 +630,7 @@
     return before, before_decay, earlier
 
 
-def travelling(own):
+def near_blocks(own):
     block = own.shape[0]
     half = block // 2
     y_less, y_more = round_ring(own, "y", 1), round_ring(own, "y", -1)
@@ -569,23 +642,29 @@
     from_z_more = round_ring(join(y_less, z_more[half:]), "z", -1)
     y_far = join(from_y_less[block:], from_y_more[block:])
     z_far = join(from_z_less[block:], from_z_more[block:])
+    near = [own, y_less, y_more, z_less, z_more, from_y_less, from_y_more, from_z_less, from_z_more]
+    chunks = [(i, base) for i in range(9) for base in (0, half)] + [(i, block) for i in (5, 6, 7, 8)]
+    return near, chunks, y_far, z_far
+
+
+def far_blocks(y_far, z_far, hold):
+    half = y_far.shape[0] // 2
     far_y_less, far_y_more = round_ring(z_far, "y", 1), round_ring(z_far, "y", -1)
     far_z_less, far_z_more = round_ring(y_far, "z", 1), round_ring(y_far, "z", -1)
-    far_top = round_ring(far_y_less[:half], "y", 1)
-    far_low = round_ring(far_z_more[half:], "z", -1)
-
-    full = lambda indices: [(i, 0, block) for i in indices]
-    near = [own, y_less, y_more, z_less, z_more, from_y_less, from_y_more, from_z_less, from_z_more]
-    near_sources = full(range(9)) + [(i, block, half) for i in (5, 6, 7, 8)]
+    top, low = hold(far_y_less[:half], far_z_more[half:])
+    far_top, far_low = round_ring(top, "y", 1), round_ring(low, "z", -1)
     far = [far_y_less, far_y_more, far_z_less, far_z_more, far_top, far_low]
-    far_sources = full(range(4)) + [(4, 0, half), (5, 0, half)]
+    chunks = [(i, base) for i in range(4) for base in (0, half)] + [(4, 0), (5, 0)]
+    return far, chunks
+
+
+def block_order():
     places = (
         ((0, 0), (-1, 0), (1, 0), (0, -1), (0, 1), (-1, -1), (1, 1), (1, -1), (-1, 1), (2, 0), (0, 2))
         + ((-1, 2), (1, 2), (2, -1), (2, 1), (2, 2))
     )
     y, z = lax.axis_index("y"), lax.axis_index("z")
-    order = [(z + dz) % 4 * 4 + (y + dy) % 4 for dy, dz in places]
-    return near, near_sources, far, far_sources, order
+    return [(z + dz) % 4 * 4 + (y + dy) % 4 for dy, dz in places]
 
 
 def shards(
@@ -607,28 +686,29 @@
     def per_lane(a):
         return jnp.pad(mine(a, 0), (0, LANES - heads))[None, :]
 
-    narrow = jnp.concatenate(
-        [bc_weight, dt_weight, jnp.zeros((bc_weight.shape[0], LANES - 2 * heads), BF16)], axis=1
-    )
-    narrow = lax.all_gather(narrow, ("z", "y", "core"), axis=0, tiled=True)
-    own_block = jnp.concatenate([mine(x_weight, 1), swap_cores(others(x_weight, 1))], axis=0)
-    near, near_sources, far, far_sources, order = travelling(own_block)
-    place = jnp.stack([core, *order]).astype(jnp.int32)
+    place = jnp.stack([core, *block_order()]).astype(jnp.int32)
+    this_core = place[:1]
+    packed, send = packed_weights(this_core, x_weight, bc_weight, dt_weight.T)
+    own_block = jnp.concatenate([packed, swap_cores(send)], axis=0)
+    near, near_chunks, y_far, z_far = near_blocks(own_block)
 
     tokens, z_weight, _ = lax.optimization_barrier((tokens, z_weight, own_block))
     other = swap_cores(tokens)
     last = jnp.where(core == 0, other[-HALO:], tokens[-HALO:])
     slabs = (tokens, other, along_chips(last, 1))
     z_block = in_core_order(core, mine(z_weight, 1), swap_cores(others(z_weight, 1)), 0)
-    z_block, _ = lax.optimization_barrier((z_block, near[1]))
+    z_block, *_ = lax.optimization_barrier((z_block, *near[1:5]))
     z_whole = lax.all_gather(z_block, ("z", "y"), axis=0, tiled=True)
 
-    bcc, cum, cum_slab, cum_t, step_t, weights_in, decays = prepared(
-        place, slabs, narrow, conv_bc, per_lane(dt_bias), per_lane(decay_rate), heads
-    )
-    sums = first_products(place, slabs, near, near_sources, 11)
-    xc, entering, final = local_states(
-        place, slabs, far, far_sources, 11, 5, sums, bcc, weights_in, decays, mine(conv_x, 1)
+    y_far, z_far, _ = lax.optimization_barrier((y_far, z_far, slabs[2]))
+    sum_x, sum_x_before, *narrow_sums = first_products(place, slabs, near, near_chunks, width, heads)
+    hold = lambda top, low: lax.optimization_barrier((top, low, sum_x))[:2]
+    far, far_chunks = far_blocks(y_far, z_far, hold)
+    bc_mine, raw = narrow_inputs(place, slabs, far, far_chunks, 11, narrow_sums)
+    bc_other = swap_cores(bc_mine)
+    xc = head_inputs(place, slabs, far, far_chunks, 11, (sum_x, sum_x_before), mine(conv_x, 1))
+    bcc, cum, cum_slab, cum_t, step_t, entering, final = local_states(
+        this_core, xc, bc_mine, bc_other, raw, conv_bc, per_lane(dt_bias), per_lane(decay_rate)
     )
     before, before_decay, earlier = earlier_states(final)
     skip_lanes = jnp.repeat(mine(skip, 0), HEAD)[None, :]

time: 217 us -> 243 us (1.12)
  Pallas kernels: 70.4 us -> 90.8 us
  waiting for transfers between devices: 57.3 us -> 75.2 us
  local copies, waits for them, and re-layouts: 21.8 us -> 15 us
  starting transfers between devices: 43.7 us -> 40.4 us
    ppermute x20, waiting for transfers between devices: 53.9 us -> 67.9 us  [round_ring(): lax.ppermute(a, axis, [(i, (i + distance) % size) for i in range(size)])]
    pallas_call x3 -> x5, Pallas kernels: 40.6 us -> 52.5 us  [the longest x3 39.4 us: by_blocks(): pl.pallas_call(kernel, grid_spec=pltpu.PrefetchScalarGridSpec(num_scalar_...]
    unnamed x47 -> x53, local copies, waits for them, and re-layouts: 13.6 us -> 6.6 us
    ppermute x1, waiting for transfers between devices: 0.01 us -> 4.98 us  [along_chips(): lax.ppermute(a, ('z', 'y'), [(i, i + distance) for i in range(chips - dis...]
    concatenate x8 -> x6, other arithmetic: 7.05 us -> 4.08 us  [near_blocks(): join = lambda *parts: jnp.concatenate(parts, axis=0)]
  transfers between devices with their start and end apart: 31 -> 31, of which waited for: 10 -> 15; matrix products, arithmetic and copies ran while one was open for 7% -> 6% of each run, Pallas kernels for 28% -> 32%
where the time goes in v4:
time: 243 us
  Pallas kernels  90.8 us (37%)
  waiting for transfers between devices  75.2 us (31%)
  starting transfers between devices  40.4 us (17%)
  local copies, waits for them, and re-layouts  15 us (6%)
  between operations  13.8 us (6%)
  other arithmetic  7.58 us (3%)
    ppermute x20, waiting for transfers between devices, round_ring(): lax.ppermute(a, axis, [(i, (i + distance) % size) for i in range(size)])  67.9 us
    pallas_call x3, Pallas kernels, by_blocks(): pl.pallas_call(kernel, grid_spec=pltpu.PrefetchScalarGridSpec(num_scalar_...  39.4 us
    ppermute x20, starting transfers between devices, round_ring(): lax.ppermute(a, axis, [(i, (i + distance) % size) for i in range(size)])  29.1 us
    pallas_call x1, Pallas kernels, project_gate(): pl.pallas_call(z_kernel, grid_spec=pltpu.PrefetchScalarGridSpec(num_scala...  14.4 us
    pallas_call x1, Pallas kernels, local_states(): pl.pallas_call(states_kernel, grid_spec=pltpu.PrefetchScalarGridSpec(num_...  11.1 us
    pallas_call x1, Pallas kernels, local_outputs(): pl.pallas_call(outputs_kernel, grid=(rows // GROUP,), in_specs=[rows_of(w...  9.03 us
    pallas_call x1, Pallas kernels, gate_outputs(): pl.pallas_call(gate_kernel, grid=(rows // GROUP,), in_specs=[rows_of(widt...  8.76 us
    ppermute x3, starting transfers between devices, earlier_states(): lax.ppermute(total, 'z', [(i, i + distance) for i in range(rows - distanc...  7.55 us
  transfers between devices with their start and end apart: 31, of which 15 were waited for; matrix products, arithmetic and copies ran while one was open for 6% of the time, Pallas kernels for 32%

profile of v4, /device:TPU:6, one launch (start us, length us, event | category | flops | bytes accessed | tf_op | source)
XLA Modules:
  0.0 242.8 jit_solution(13793518332314324662)
XLA Ops:
  6.5 2.1 packed_weights.1
  16.9 2.1 collective-permute-start.6
  20.9 7.8 %collective-permute-done.3.refs_1_ = bf16[2336,128]{1,0:T(8,128)(2,1)S(1)} collective-permute-done((bf16[2336,128]{1,0:T(8,128)(2,1)}, bf16[2336,128]{1,0:T(8,128)(2,1)S(1)}, u32[]{:S(2)}, u32[]{:S(2)}) %collective-permute-start.3) | collective-permute-done | bytes 598048 | tf_op jit(solution)/shard_map/ppermute | solution.py:25
  28.7 3.8 %collective-permute-done.5.refs_3_ = bf16[2336,128]{1,0:T(8,128)(2,1)S(1)} collective-permute-done((bf16[2336,128]{1,0:T(8,128)(2,1)}, bf16[2336,128]{1,0:T(8,128)(2,1)S(1)}, u32[]{:S(2)}, u32[]{:S(2)}) %collective-permute-start.5) | collective-permute-done | bytes 598048 | tf_op jit(solution)/shard_map/ppermute | solution.py:25
  37.9 2.8 %collective-permute-start.11 = (bf16[3504,128]{1,0:T(8,128)(2,1)}, bf16[3504,128]{1,0:T(8,128)(2,1)S(1)}, u32[]{:S(2)}, u32[]{:S(2)}) collective-permute-start(bf16[3504,128]{1,0:T(8,128)(2,1)} %pad_maximum_fusion.3), channel_id=1, source_target_pairs={{0,96},{32,0},{64,32},{96,64},{1,97},{33,1},{65,33},{97,65},{2,98}... | collective-permute-start | bytes 2691080 | tf_op jit(solution)/shard_map/ppermute | solution.py:25
  41.6 23.2 %collective-permute-done.9.refs_6_ = bf16[3504,128]{1,0:T(8,128)(2,1)} collective-permute-done((bf16[3504,128]{1,0:T(8,128)(2,1)}, bf16[3504,128]{1,0:T(8,128)(2,1)}, u32[]{:S(2)}, u32[]{:S(2)}) %collective-permute-start.9) | collective-permute-done | bytes 897056 | tf_op jit(solution)/shard_map/ppermute | solution.py:25
  65.7 2.6 %collective-permute-done.8.refs_5_ = bf16[3504,128]{1,0:T(8,128)(2,1)} collective-permute-done((bf16[3504,128]{1,0:T(8,128)(2,1)}, bf16[3504,128]{1,0:T(8,128)(2,1)}, u32[]{:S(2)}, u32[]{:S(2)}) %collective-permute-start.8) | collective-permute-done | bytes 897056 | tf_op jit(solution)/shard_map/ppermute | solution.py:25
  69.4 2.6 %collective-permute-done.10.refs_7_ = bf16[3504,128]{1,0:T(8,128)(2,1)S(1)} collective-permute-done((bf16[3504,128]{1,0:T(8,128)(2,1)S(1)}, bf16[3504,128]{1,0:T(8,128)(2,1)S(1)}, u32[]{:S(2)}, u32[]{:S(2)}) %collective-permute-start.10) | collective-permute-done | bytes 897056 | tf_op jit(solution)/shard_map/ppermute | solution.py:25
  74.0 2.3 collective-permute-start.7
  77.2 5.0 %collective-permute-done.7.before_ref = bf16[16,4096]{1,0:T(8,128)(2,1)S(1)} collective-permute-done((bf16[16,4096]{1,0:T(8,128)(2,1)S(1)}, bf16[16,4096]{1,0:T(8,128)(2,1)S(1)}, u32[]{:S(2)}, u32[]{:S(2)}) %collective-permute-start.7) | collective-permute-done | bytes 131104 | tf_op jit(solution)/shard_map/ppermute | solution.py:30
  82.1 2.5 %collective-permute-start.12 = (bf16[2336,128]{1,0:T(8,128)(2,1)}, bf16[2336,128]{1,0:T(8,128)(2,1)S(1)}, u32[]{:S(2)}, u32[]{:S(2)}) collective-permute-start(bf16[2336,128]{1,0:T(8,128)(2,1)} %pad_maximum_fusion.5), channel_id=1, source_target_pairs={{0,8},{8,16},{16,24},{24,0},{1,9},{9,17},{17,25},{25,1},{2,10},{10... | collective-permute-start | bytes 1794056 | tf_op jit(solution)/shard_map/ppermute | solution.py:25
  84.6 2.5 %collective-permute-start.13 = (bf16[2336,128]{1,0:T(8,128)(2,1)}, bf16[2336,128]{1,0:T(8,128)(2,1)S(1)}, u32[]{:S(2)}, u32[]{:S(2)}) collective-permute-start(bf16[2336,128]{1,0:T(8,128)(2,1)} %pad_maximum_fusion.5), channel_id=1, source_target_pairs={{0,24},{8,0},{16,8},{24,16},{1,25},{9,1},{17,9},{25,17},{2,26},{10... | collective-permute-start | bytes 1794056 | tf_op jit(solution)/shard_map/ppermute | solution.py:25
  87.2 2.8 %collective-permute-start.14 = (bf16[2336,128]{1,0:T(8,128)(2,1)S(1)}, bf16[2336,128]{1,0:T(8,128)(2,1)S(1)}, u32[]{:S(2)}, u32[]{:S(2)}) collective-permute-start(bf16[2336,128]{1,0:T(8,128)(2,1)S(1)} %pad_maximum_fusion.4), channel_id=1, source_target_pairs={{0,32},{32,64},{64,96},{96,0},{1,33},{33,65},{65,97},{97,1},{2,34}... | collective-permute-start | bytes 1794056 | tf_op jit(solution)/shard_map/ppermute | solution.py:25
  90.4 18.1 %first_products.1 = (f32[1024,1024]{1,0:T(8,128)}, f32[16,1024]{1,0:T(8,128)}, f32[1024,128]{1,0:T(8,128)}, f32[16,128]{1,0:T(8,128)}, f32[1024,16]{1,0:T(8,128)}) custom-call(s32[17]{0:T(128)} %stack.68.place_ref, bf16[512,4096]{1,0:T(8,128)(2,1)} %own_ref.3, bf16[512,4096]{1,0:T(8,128)(2,1)} %collective-permute-done.1.other_ref, ...), custom_call_target="tpu_custom_call" | custom-call | flops 8999999488 | bytes 20971520 | tf_op jit(solution)/shard_map/first_products/pallas_call | solution.py:435
  108.5 5.1 %collective-permute-done.12.refs_0_ = bf16[2336,128]{1,0:T(8,128)(2,1)S(1)} collective-permute-done((bf16[2336,128]{1,0:T(8,128)(2,1)}, bf16[2336,128]{1,0:T(8,128)(2,1)S(1)}, u32[]{:S(2)}, u32[]{:S(2)}) %collective-permute-start.12) | collective-permute-done | bytes 598048 | tf_op jit(solution)/shard_map/ppermute | solution.py:25
  114.4 3.5 %collective-permute-done.15.refs_3_ = bf16[2336,128]{1,0:T(8,128)(2,1)S(1)} collective-permute-done((bf16[2336,128]{1,0:T(8,128)(2,1)S(1)}, bf16[2336,128]{1,0:T(8,128)(2,1)S(1)}, u32[]{:S(2)}, u32[]{:S(2)}) %collective-permute-start.15) | collective-permute-done | bytes 598048 | tf_op jit(solution)/shard_map/ppermute | solution.py:25
  122.6 8.5 %collective-permute-done.16.refs_4_ = bf16[1168,128]{1,0:T(8,128)(2,1)S(1)} collective-permute-done((bf16[1168,128]{1,0:T(8,128)(2,1)}, bf16[1168,128]{1,0:T(8,128)(2,1)S(1)}, u32[]{:S(2)}, u32[]{:S(2)}) %collective-permute-start.16) | collective-permute-done | bytes 299040 | tf_op jit(solution)/shard_map/ppermute | solution.py:25
  131.8 8.1 %narrow_inputs.1 = (bf16[1040,128]{1,0:T(8,128)(2,1)}, f32[1024,16]{1,0:T(8,128)}) custom-call(s32[17]{0:T(128)} %stack.68.place_ref, bf16[512,4096]{1,0:T(8,128)(2,1)} %own_ref.3, bf16[512,4096]{1,0:T(8,128)(2,1)} %collective-permute-done.1.other_ref, bf16[16,4096]{1,0:T(8,128)(2,1)} %copy-done.18, bf16[2336,128]{1,0:T(8,128)(2,1)} %copy-done.1, ...), custom_call_target="tpu_custom_call" | custom-call | flops 2000000000 | bytes 12582912 | tf_op jit(solution)/shard_map/narrow_inputs/pallas_call | solution.py:435
  140.2 13.1 %head_inputs.1.xc_ref = bf16[1024,1024]{1,0:T(8,128)(2,1)} custom-call(s32[17]{0:T(128)} %stack.68.place_ref, bf16[512,4096]{1,0:T(8,128)(2,1)} %own_ref.3, bf16[512,4096]{1,0:T(8,128)(2,1)} %collective-permute-done.1.other_ref, bf16[16,4096]{1,0:T(8,128)(2,1)} %copy-done.18, bf16[2336,128]{1,0:T(8,128)(2,1)} %copy-done.1, bf16[2336,128]{1,0:T(8,128)(2,1)} %copy-done.8, ...), custom_call_target="tpu_custom_call" | custom-call | flops 5000000000 | bytes 18874368 | tf_op jit(solution)/shard_map/head_inputs/pallas_call | solution.py:435
  154.0 11.1 %states.1 = (bf16[1024,256]{1,0:T(8,128)(2,1)}, f32[1024,128]{1,0:T(8,128)}, f32[1024,128]{1,0:T(8,128)}, f32[16,1024]{1,0:T(8,128)}, f32[16,1024]{1,0:T(8,128)}...) custom-call(s32[1]{0:T(128)} %bitcast.core_ref, bf16[1024,1024]{1,0:T(8,128)(2,1)} %head_inputs.1.xc_ref, ...), custom_call_target="tpu_custom_call" | custom-call | flops 5000000000 | bytes 8388608 | tf_op jit(solution)/shard_map/states/pallas_call | solution.py:507
  165.2 2.3 collective-permute-start.20
  168.6 9.0 %outputs.1.local_ref = f32[1024,1024]{1,0:T(8,128)} custom-call(bf16[1024,1024]{1,0:T(8,128)(2,1)} %head_inputs.1.xc_ref, bf16[1024,256]{1,0:T(8,128)(2,1)} %get-tuple-element.49.bcc_ref, f32[1024,128]{1,0:T(8,128)} %get-tuple-element.50.cum_ref, f32[16,1024]{1,0:T(8,128)} %get-tuple-element.51.cum_t_ref, f32[16,1024]{1,0:T(8,128)} %get-tuple-element.52.step_t_ref, ...), custom_call_target="tpu_custom_call" | custom-call | flops 10000000000 | bytes 10485760 | tf_op jit(solution)/shard_map/outputs/pallas_call | solution.py:530
  177.7 5.1 %collective-permute-done.19.refs_1_ = bf16[144,1024]{1,0:T(8,128)(2,1)S(1)} collective-permute-done((bf16[144,1024]{1,0:T(8,128)(2,1)}, bf16[144,1024]{1,0:T(8,128)(2,1)S(1)}, u32[]{:S(2)}, u32[]{:S(2)}) %collective-permute-start.19) | collective-permute-done | bytes 294944 | tf_op jit(solution)/shard_map/ppermute | solution.py:25
  184.3 2.7 %row_states.1 = (bf16[144,1024]{1,0:T(8,128)(2,1)}, f32[128,1024]{1,0:T(8,128)}, f32[8,1024]{1,0:T(8,128)}) custom-call(s32[1]{0:T(128)} %bitcast.20.place_ref, bf16[144,1024]{1,0:T(8,128)(2,1)} %get-tuple-element.55.refs_0_, bf16[144,1024]{1,0:T(8,128)(2,1)} %copy-done.15, bf16[144,1024]{1,0:T(8,128)(2,1)} %copy-done.16, bf16[144,1024]{1,0:T(8,128)(2,1)} %copy-done.17), custom_call_target="tpu_custom_call" | custom-call | flops 10000000 | bytes 2097152 | tf_op jit(solution)/shard_map/row_states/pallas_call | solution.py:613
  186.9 3.2 %collective-permute-start.22 = (bf16[144,1024]{1,0:T(8,128)(2,1)}, bf16[144,1024]{1,0:T(8,128)(2,1)S(1)}, u32[]{:S(2)}, u32[]{:S(2)}) collective-permute-start(bf16[144,1024]{1,0:T(8,128)(2,1)} %get-tuple-element.58), channel_id=1, source_target_pairs={{0,96},{1,97},{2,98},{3,99},{4,100},{5,101},{6,102},{7,103},{8,104... | collective-permute-start | bytes 884744 | tf_op jit(solution)/shard_map/ppermute | solution.py:627
  190.1 2.5 %collective-permute-start.23 = (bf16[144,1024]{1,0:T(8,128)(2,1)}, bf16[144,1024]{1,0:T(8,128)(2,1)S(1)}, u32[]{:S(2)}, u32[]{:S(2)}) collective-permute-start(bf16[144,1024]{1,0:T(8,128)(2,1)} %get-tuple-element.58), channel_id=1, source_target_pairs={{0,64},{32,96},{1,65},{33,97},{2,66},{34,98},{3,67},{35,99},{4,68}... | collective-permute-start | bytes 884744 | tf_op jit(solution)/shard_map/ppermute | solution.py:627
  194.5 14.4 %project_gate.1.gate_ref = bf16[1024,1024]{1,0:T(8,128)(2,1)} custom-call(s32[17]{0:T(128)} %stack.68.place_ref, bf16[512,4096]{1,0:T(8,128)(2,1)} %own_ref.3, bf16[512,4096]{1,0:T(8,128)(2,1)} %collective-permute-done.1.other_ref, bf16[4096,1024]{1,0:T(8,128)(2,1)} %all-gather.2.cloned.1.call-done.weight_ref), custom_call_target="tpu_custom_call" | custom-call | flops 8999999488 | bytes 20971520 | tf_op jit(solution)/shard_map/project_gate/pallas_call | solution.py:550
  209.8 8.8 %gate.1 = (bf16[1024,1024]{1,0:T(8,128)(2,1)}, f32[1,1024]{1,0:T(1,128)}) custom-call(bf16[1024,1024]{1,0:T(8,128)(2,1)} %project_gate.1.gate_ref, f32[1024,1024]{1,0:T(8,128)} %outputs.1.local_ref, bf16[1024,256]{1,0:T(8,128)(2,1)} %get-tuple-element.49.bcc_ref, f32[1024,128]{1,0:T(8,128)} %get-tuple-element.54.cum_ref, ...), custom_call_target="tpu_custom_call" | custom-call | flops 1000000000 | bytes 10485760 | tf_op jit(solution)/shard_map/gate/pallas_call | solution.py:567
  220.5 2.2 collective-permute-done.26
  223.5 2.4 collective-permute-start.27
  227.4 3.5 %collective-permute-done.28 = f32[1,512]{1,0:T(1,128)S(1)} collective-permute-done((f32[1,512]{1,0:T(1,128)S(1)}, f32[1,512]{1,0:T(1,128)S(1)}, u32[]{:S(2)}, u32[]{:S(2)}) %collective-permute-start.28) | collective-permute-done | bytes 2080 | tf_op jit(solution)/shard_map/ppermute | solution.py:25
  232.5 3.5 %normalized.1 = bf16[512,2048]{1,0:T(8,128)(2,1)} custom-call(s32[1]{0:T(128)} %bitcast.core_ref, bf16[1024,1024]{1,0:T(8,128)(2,1)} %get-tuple-element.59.mine_ref, bf16[512,1024]{1,0:T(8,128)(2,1)} %copy-done.7, f32[1,512]{1,0:T(1,128)} %add_multiply_fusion.squares_ref, f32[1,2048]{1,0:T(1,128)} %bitcast.25), custom_call_target="tpu_custom_call" | custom-call | flops 10000000 | bytes 4194304 | tf_op jit(solution)/shard_map/normalized/pallas_call | solution.py:584
  (126 shorter events, 39.9 us)
Async XLA Ops:
  6.5 115.5 %copy-start = (f32[4,2048]{1,0:T(4,128)S(1)}, f32[4,2048]{1,0:T(4,128)}, u32[]{:S(2)}) copy-start(f32[4,2048]{1,0:T(4,128)} %param.16) | copy-start | bytes 98308
  6.5 188.0 %all-gather.2.cloned.1.call-start = ((), (), s32[]{:S(2)}) async-start(), calls=%async_computation | async-start | bytes 8912896 | tf_op jit(solution)/shard_map/all_gather | solution.py:701
  8.6 1.8 collective-permute-start
  11.2 7.8 %collective-permute-start.2 = (bf16[128,1024]{1,0:T(8,128)(2,1)S(1)}, bf16[128,1024]{1,0:T(8,128)(2,1)}, u32[]{:S(2)}, u32[]{:S(2)}) collective-permute-start(bf16[128,1024]{1,0:T(8,128)(2,1)S(1)} %constant_dynamic-slice_fusion.2), channel_id=1, source_target_pairs={{0,4},{4,0},{1,5},{5,1},{2,6},{6,2},{3,7},{7,3},{8,12},{12,8},{9,1... | collective-permute-start | bytes 786440 | tf_op jit(solution)/shard_map/ppermute | solution.py:20
  11.7 17.0 %collective-permute-start.3 = (bf16[2336,128]{1,0:T(8,128)(2,1)}, bf16[2336,128]{1,0:T(8,128)(2,1)S(1)}, u32[]{:S(2)}, u32[]{:S(2)}) collective-permute-start(bf16[2336,128]{1,0:T(8,128)(2,1)} %constant_dynamic-update-slice_fusion.refs_0_), channel_id=1, source_target_pairs={{0,8},{8,16},{16,24},{24,0},{1,9},{9,17},{17,25},{25,1},{2,10},{10... | collective-permute-start | bytes 1794056 | tf_op jit(solution)/shard_map/ppermute | solution.py:25
  13.3 15.4 %collective-permute-start.4 = (bf16[2336,128]{1,0:T(8,128)(2,1)}, bf16[2336,128]{1,0:T(8,128)(2,1)S(1)}, u32[]{:S(2)}, u32[]{:S(2)}) collective-permute-start(bf16[2336,128]{1,0:T(8,128)(2,1)} %constant_dynamic-update-slice_fusion.refs_0_), channel_id=1, source_target_pairs={{0,24},{8,0},{16,8},{24,16},{1,25},{9,1},{17,9},{25,17},{2,26},{10... | collective-permute-start | bytes 1794056 | tf_op jit(solution)/shard_map/ppermute | solution.py:25
  15.0 17.6 %collective-permute-start.5 = (bf16[2336,128]{1,0:T(8,128)(2,1)}, bf16[2336,128]{1,0:T(8,128)(2,1)S(1)}, u32[]{:S(2)}, u32[]{:S(2)}) collective-permute-start(bf16[2336,128]{1,0:T(8,128)(2,1)} %constant_dynamic-update-slice_fusion.refs_0_), channel_id=1, source_target_pairs={{0,32},{32,64},{64,96},{96,0},{1,33},{33,65},{65,97},{97,1},{2,34}... | collective-permute-start | bytes 1794056 | tf_op jit(solution)/shard_map/ppermute | solution.py:25
  16.9 15.7 %collective-permute-start.6 = (bf16[2336,128]{1,0:T(8,128)(2,1)}, bf16[2336,128]{1,0:T(8,128)(2,1)S(1)}, u32[]{:S(2)}, u32[]{:S(2)}) collective-permute-start(bf16[2336,128]{1,0:T(8,128)(2,1)} %constant_dynamic-update-slice_fusion.refs_0_), channel_id=1, source_target_pairs={{0,96},{32,0},{64,32},{96,64},{1,97},{33,1},{65,33},{97,65},{2,98}... | collective-permute-start | bytes 1794056 | tf_op jit(solution)/shard_map/ppermute | solution.py:25
  32.6 40.3 %collective-permute-start.1 = (bf16[512,4096]{1,0:T(8,128)(2,1)}, bf16[512,4096]{1,0:T(8,128)(2,1)}, u32[]{:S(2)}, u32[]{:S(2)}) collective-permute-start(bf16[512,4096]{1,0:T(8,128)(2,1)} %own_ref.3), channel_id=1, source_target_pairs={{0,4},{4,0},{1,5},{5,1},{2,6},{6,2},{3,7},{7,3},{8,12},{12,8},{9,1... | collective-permute-start | bytes 12582920 | tf_op jit(solution)/shard_map/ppermute | solution.py:20
  33.9 30.9 %collective-permute-start.9 = (bf16[3504,128]{1,0:T(8,128)(2,1)}, bf16[3504,128]{1,0:T(8,128)(2,1)}, u32[]{:S(2)}, u32[]{:S(2)}) collective-permute-start(bf16[3504,128]{1,0:T(8,128)(2,1)} %pad_maximum_fusion.1), channel_id=1, source_target_pairs={{0,24},{8,0},{16,8},{24,16},{1,25},{9,1},{17,9},{25,17},{2,26},{10... | collective-permute-start | bytes 2691080 | tf_op jit(solution)/shard_map/ppermute | solution.py:25
  36.5 31.8 %collective-permute-start.8 = (bf16[3504,128]{1,0:T(8,128)(2,1)}, bf16[3504,128]{1,0:T(8,128)(2,1)}, u32[]{:S(2)}, u32[]{:S(2)}) collective-permute-start(bf16[3504,128]{1,0:T(8,128)(2,1)} %pad_maximum_fusion), channel_id=1, source_target_pairs={{0,8},{8,16},{16,24},{24,0},{1,9},{9,17},{17,25},{25,1},{2,10},{10... | collective-permute-start | bytes 2691080 | tf_op jit(solution)/shard_map/ppermute | solution.py:25
  37.9 31.4 %collective-permute-start.11 = (bf16[3504,128]{1,0:T(8,128)(2,1)}, bf16[3504,128]{1,0:T(8,128)(2,1)S(1)}, u32[]{:S(2)}, u32[]{:S(2)}) collective-permute-start(bf16[3504,128]{1,0:T(8,128)(2,1)} %pad_maximum_fusion.3), channel_id=1, source_target_pairs={{0,96},{32,0},{64,32},{96,64},{1,97},{33,1},{65,33},{97,65},{2,98}... | collective-permute-start | bytes 2691080 | tf_op jit(solution)/shard_map/ppermute | solution.py:25
  40.8 31.2 %collective-permute-start.10 = (bf16[3504,128]{1,0:T(8,128)(2,1)S(1)}, bf16[3504,128]{1,0:T(8,128)(2,1)S(1)}, u32[]{:S(2)}, u32[]{:S(2)}) collective-permute-start(bf16[3504,128]{1,0:T(8,128)(2,1)S(1)} %pad_maximum_fusion.2), channel_id=1, source_target_pairs={{0,32},{32,64},{64,96},{96,0},{1,33},{33,65},{65,97},{97,1},{2,34}... | collective-permute-start | bytes 2691080 | tf_op jit(solution)/shard_map/ppermute | solution.py:25
  74.0 8.2 %collective-permute-start.7 = (bf16[16,4096]{1,0:T(8,128)(2,1)S(1)}, bf16[16,4096]{1,0:T(8,128)(2,1)S(1)}, u32[]{:S(2)}, u32[]{:S(2)}) collective-permute-start(bf16[16,4096]{1,0:T(8,128)(2,1)S(1)} %slice_select_fusion), channel_id=1, source_target_pairs={{0,8},{8,16},{16,24},{24,32},{32,40},{40,48},{48,56},{56,64},{64,7... | collective-permute-start | bytes 393224 | tf_op jit(solution)/shard_map/ppermute | solution.py:30
  82.1 31.5 %collective-permute-start.12 = (bf16[2336,128]{1,0:T(8,128)(2,1)}, bf16[2336,128]{1,0:T(8,128)(2,1)S(1)}, u32[]{:S(2)}, u32[]{:S(2)}) collective-permute-start(bf16[2336,128]{1,0:T(8,128)(2,1)} %pad_maximum_fusion.5), channel_id=1, source_target_pairs={{0,8},{8,16},{16,24},{24,0},{1,9},{9,17},{17,25},{25,1},{2,10},{10... | collective-permute-start | bytes 1794056 | tf_op jit(solution)/shard_map/ppermute | solution.py:25
  84.6 38.0 %collective-permute-start.13 = (bf16[2336,128]{1,0:T(8,128)(2,1)}, bf16[2336,128]{1,0:T(8,128)(2,1)S(1)}, u32[]{:S(2)}, u32[]{:S(2)}) collective-permute-start(bf16[2336,128]{1,0:T(8,128)(2,1)} %pad_maximum_fusion.5), channel_id=1, source_target_pairs={{0,24},{8,0},{16,8},{24,16},{1,25},{9,1},{17,9},{25,17},{2,26},{10... | collective-permute-start | bytes 1794056 | tf_op jit(solution)/shard_map/ppermute | solution.py:25
  87.2 35.4 %collective-permute-start.14 = (bf16[2336,128]{1,0:T(8,128)(2,1)S(1)}, bf16[2336,128]{1,0:T(8,128)(2,1)S(1)}, u32[]{:S(2)}, u32[]{:S(2)}) collective-permute-start(bf16[2336,128]{1,0:T(8,128)(2,1)S(1)} %pad_maximum_fusion.4), channel_id=1, source_target_pairs={{0,32},{32,64},{64,96},{96,0},{1,33},{33,65},{65,97},{97,1},{2,34}... | collective-permute-start | bytes 1794056 | tf_op jit(solution)/shard_map/ppermute | solution.py:25
  89.9 28.0 %collective-permute-start.15 = (bf16[2336,128]{1,0:T(8,128)(2,1)S(1)}, bf16[2336,128]{1,0:T(8,128)(2,1)S(1)}, u32[]{:S(2)}, u32[]{:S(2)}) collective-permute-start(bf16[2336,128]{1,0:T(8,128)(2,1)S(1)} %pad_maximum_fusion.4), channel_id=1, source_target_pairs={{0,96},{32,0},{64,32},{96,64},{1,97},{33,1},{65,33},{97,65},{2,98}... | collective-permute-start | bytes 1794056 | tf_op jit(solution)/shard_map/ppermute | solution.py:25
  118.7 12.4 %collective-permute-start.16 = (bf16[1168,128]{1,0:T(8,128)(2,1)}, bf16[1168,128]{1,0:T(8,128)(2,1)S(1)}, u32[]{:S(2)}, u32[]{:S(2)}) collective-permute-start(bf16[1168,128]{1,0:T(8,128)(2,1)} %slice.57), channel_id=1, source_target_pairs={{0,8},{8,16},{16,24},{24,0},{1,9},{9,17},{17,25},{25,1},{2,10},{10... | collective-permute-start | bytes 897032 | tf_op jit(solution)/shard_map/ppermute | solution.py:25
  118.7 12.4 %collective-permute-start.17 = (bf16[1168,128]{1,0:T(8,128)(2,1)}, bf16[1168,128]{1,0:T(8,128)(2,1)}, u32[]{:S(2)}, u32[]{:S(2)}) collective-permute-start(bf16[1168,128]{1,0:T(8,128)(2,1)} %slice.58), channel_id=1, source_target_pairs={{0,96},{32,0},{64,32},{96,64},{1,97},{33,1},{65,33},{97,65},{2,98}... | collective-permute-start | bytes 897032 | tf_op jit(solution)/shard_map/ppermute | solution.py:25
  139.9 13.4 %collective-permute-start.18 = (bf16[1040,128]{1,0:T(8,128)(2,1)}, bf16[1040,128]{1,0:T(8,128)(2,1)S(1)}, u32[]{:S(2)}, u32[]{:S(2)}) collective-permute-start(bf16[1040,128]{1,0:T(8,128)(2,1)} %get-tuple-element.47.bc_mine_ref), channel_id=1, source_target_pairs={{0,4},{4,0},{1,5},{5,1},{2,6},{6,2},{3,7},{7,3},{8,12},{12,8},{9,1... | collective-permute-start | bytes 798728 | tf_op jit(solution)/shard_map/ppermute | solution.py:20
  165.1 17.6 %collective-permute-start.19 = (bf16[144,1024]{1,0:T(8,128)(2,1)}, bf16[144,1024]{1,0:T(8,128)(2,1)S(1)}, u32[]{:S(2)}, u32[]{:S(2)}) collective-permute-start(bf16[144,1024]{1,0:T(8,128)(2,1)} %get-tuple-element.55.refs_0_), channel_id=1, source_target_pairs={{0,8},{8,16},{16,24},{24,0},{1,9},{9,17},{17,25},{25,1},{2,10},{10... | collective-permute-start | bytes 884744 | tf_op jit(solution)/shard_map/ppermute | solution.py:25
  165.2 17.5 %collective-permute-start.20 = (bf16[144,1024]{1,0:T(8,128)(2,1)}, bf16[144,1024]{1,0:T(8,128)(2,1)S(1)}, u32[]{:S(2)}, u32[]{:S(2)}) collective-permute-start(bf16[144,1024]{1,0:T(8,128)(2,1)} %get-tuple-element.55.refs_0_), channel_id=1, source_target_pairs={{0,16},{8,24},{16,0},{24,8},{1,17},{9,25},{17,1},{25,9},{2,18},{10... | collective-permute-start | bytes 884744 | tf_op jit(solution)/shard_map/ppermute | solution.py:25
  167.5 16.0 %collective-permute-start.21 = (bf16[144,1024]{1,0:T(8,128)(2,1)}, bf16[144,1024]{1,0:T(8,128)(2,1)S(1)}, u32[]{:S(2)}, u32[]{:S(2)}) collective-permute-start(bf16[144,1024]{1,0:T(8,128)(2,1)} %get-tuple-element.55.refs_0_), channel_id=1, source_target_pairs={{0,24},{8,0},{16,8},{24,16},{1,25},{9,1},{17,9},{25,17},{2,26},{10... | collective-permute-start | bytes 884744 | tf_op jit(solution)/shard_map/ppermute | solution.py:25
  186.9 22.0 %collective-permute-start.22 = (bf16[144,1024]{1,0:T(8,128)(2,1)}, bf16[144,1024]{1,0:T(8,128)(2,1)S(1)}, u32[]{:S(2)}, u32[]{:S(2)}) collective-permute-start(bf16[144,1024]{1,0:T(8,128)(2,1)} %get-tuple-element.58), channel_id=1, source_target_pairs={{0,96},{1,97},{2,98},{3,99},{4,100},{5,101},{6,102},{7,103},{8,104... | collective-permute-start | bytes 884744 | tf_op jit(solution)/shard_map/ppermute | solution.py:627
  190.1 18.8 %collective-permute-start.23 = (bf16[144,1024]{1,0:T(8,128)(2,1)}, bf16[144,1024]{1,0:T(8,128)(2,1)S(1)}, u32[]{:S(2)}, u32[]{:S(2)}) collective-permute-start(bf16[144,1024]{1,0:T(8,128)(2,1)} %get-tuple-element.58), channel_id=1, source_target_pairs={{0,64},{32,96},{1,65},{33,97},{2,66},{34,98},{3,67},{35,99},{4,68}... | collective-permute-start | bytes 884744 | tf_op jit(solution)/shard_map/ppermute | solution.py:627
  192.7 16.2 %collective-permute-start.24 = (bf16[144,1024]{1,0:T(8,128)(2,1)}, bf16[144,1024]{1,0:T(8,128)(2,1)S(1)}, u32[]{:S(2)}, u32[]{:S(2)}) collective-permute-start(bf16[144,1024]{1,0:T(8,128)(2,1)} %get-tuple-element.58), channel_id=1, source_target_pairs={{0,32},{32,64},{64,96},{1,33},{33,65},{65,97},{2,34},{34,66},{66,9... | collective-permute-start | bytes 884744 | tf_op jit(solution)/shard_map/ppermute | solution.py:627
  219.9 11.7 %collective-permute-start.25 = (bf16[512,1024]{1,0:T(8,128)(2,1)S(1)}, bf16[512,1024]{1,0:T(8,128)(2,1)S(1)}, u32[]{:S(2)}, u32[]{:S(2)}) collective-permute-start(bf16[512,1024]{1,0:T(8,128)(2,1)S(1)} %constant_dynamic-slice_fusion), channel_id=1, source_target_pairs={{0,4},{4,0},{1,5},{5,1},{2,6},{6,2},{3,7},{7,3},{8,12},{12,8},{9,1... | collective-permute-start | bytes 3145736 | tf_op jit(solution)/shard_map/ppermute | solution.py:20
  220.0 2.6 %collective-permute-start.26 = (f32[1,1024]{1,0:T(1,128)S(1)}, f32[1,1024]{1,0:T(1,128)S(1)}, u32[]{:S(2)}, u32[]{:S(2)}) collective-permute-start(f32[1,1024]{1,0:T(1,128)S(1)} %copy-done.21), channel_id=1, source_target_pairs={{0,4},{4,0},{1,5},{5,1},{2,6},{6,2},{3,7},{7,3},{8,12},{12,8},{9,1... | collective-permute-start | bytes 12296 | tf_op jit(solution)/shard_map/ppermute | solution.py:20
  222.6 4.8 %collective-permute-start.29 = (f32[1,512]{1,0:T(1,128)S(1)}, f32[1,512]{1,0:T(1,128)S(1)}, u32[]{:S(2)}, u32[]{:S(2)}) collective-permute-start(f32[1,512]{1,0:T(1,128)S(1)} %dynamic-slice_add_fusion), channel_id=1, source_target_pairs={{0,3},{1,0},{2,1},{3,2},{4,7},{5,4},{6,5},{7,6},{8,11},{9,8},{10,9... | collective-permute-start | bytes 6152 | tf_op jit(solution)/shard_map/ppermute | solution.py:25
  223.5 4.0 %collective-permute-start.27 = (f32[1,512]{1,0:T(1,128)S(1)}, f32[1,512]{1,0:T(1,128)S(1)}, u32[]{:S(2)}, u32[]{:S(2)}) collective-permute-start(f32[1,512]{1,0:T(1,128)S(1)} %dynamic-slice_add_fusion), channel_id=1, source_target_pairs={{0,1},{1,2},{2,3},{3,0},{4,5},{5,6},{6,7},{7,4},{8,9},{9,10},{10,1... | collective-permute-start | bytes 6152 | tf_op jit(solution)/shard_map/ppermute | solution.py:25
  225.9 5.1 %collective-permute-start.28 = (f32[1,512]{1,0:T(1,128)S(1)}, f32[1,512]{1,0:T(1,128)S(1)}, u32[]{:S(2)}, u32[]{:S(2)}) collective-permute-start(f32[1,512]{1,0:T(1,128)S(1)} %dynamic-slice_add_fusion), channel_id=1, source_target_pairs={{0,2},{1,3},{2,0},{3,1},{4,6},{5,7},{6,4},{7,5},{8,10},{9,11},{10,... | collective-permute-start | bytes 6152 | tf_op jit(solution)/shard_map/ppermute | solution.py:25
  (25 other events, 240.8 us)
Sparse Core Ops, SparseCore 0:
  32.7 96.4 all-gather.1

commit v5 on v3

--- a/solution.py
+++ b/solution.py
@@ -344,9 +344,9 @@
     return pl.BlockSpec((GROUP, width), lambda i: (i, 0))
 
 
-def params(flops, megabytes):
+def params(flops, megabytes, vmem=48):
     return dict(
-        compiler_params=pltpu.CompilerParams(vmem_limit_bytes=48 * 2**20),
+        compiler_params=pltpu.CompilerParams(vmem_limit_bytes=vmem * 2**20),
         cost_estimate=pl.CostEstimate(
             flops=int(flops), bytes_accessed=megabytes * 2**20, transcendentals=0
         ),
@@ -502,7 +502,7 @@
         ],
         scratch_shapes=[pltpu.VMEM((LANES, width), BF16)],
         name="gate",
-        **params(1e9, 10),
+        **params(1e9, 10, 60),
     )(gate, local, bcc, cum_slab, before, before_decay, *earlier)
 
 
@@ -557,7 +557,11 @@
     return before, before_decay, earlier
 
 
-def travelling(own):
+def tied(values, *to):
+    return lax.optimization_barrier((*values, *to))[: len(values)]
+
+
+def near_blocks(own):
     block = own.shape[0]
     half = block // 2
     y_less, y_more = round_ring(own, "y", 1), round_ring(own, "y", -1)
@@ -569,23 +573,29 @@
     from_z_more = round_ring(join(y_less, z_more[half:]), "z", -1)
     y_far = join(from_y_less[block:], from_y_more[block:])
     z_far = join(from_z_less[block:], from_z_more[block:])
+    near = [own, y_less, y_more, z_less, z_more, from_y_less, from_y_more, from_z_less, from_z_more]
+    sources = [(i, 0, block) for i in range(9)] + [(i, block, half) for i in (5, 6, 7, 8)]
+    return near, sources, y_far, z_far
+
+
+def far_blocks(y_far, z_far, before_last):
+    block = y_far.shape[0]
+    half = block // 2
     far_y_less, far_y_more = round_ring(z_far, "y", 1), round_ring(z_far, "y", -1)
     far_z_less, far_z_more = round_ring(y_far, "z", 1), round_ring(y_far, "z", -1)
-    far_top = round_ring(far_y_less[:half], "y", 1)
-    far_low = round_ring(far_z_more[half:], "z", -1)
-
-    full = lambda indices: [(i, 0, block) for i in indices]
-    near = [own, y_less, y_more, z_less, z_more, from_y_less, from_y_more, from_z_less, from_z_more]
-    near_sources = full(range(9)) + [(i, block, half) for i in (5, 6, 7, 8)]
-    far = [far_y_less, far_y_more, far_z_less, far_z_more, far_top, far_low]
-    far_sources = full(range(4)) + [(4, 0, half), (5, 0, half)]
+    top, low = tied((far_y_less[:half], far_z_more[half:]), before_last)
+    far = [far_y_less, far_y_more, far_z_less, far_z_more, round_ring(top, "y", 1), round_ring(low, "z", -1)]
+    sources = [(i, 0, block) for i in range(4)] + [(4, 0, half), (5, 0, half)]
+    return far, sources
+
+
+def block_order():
     places = (
         ((0, 0), (-1, 0), (1, 0), (0, -1), (0, 1), (-1, -1), (1, 1), (1, -1), (-1, 1), (2, 0), (0, 2))
         + ((-1, 2), (1, 2), (2, -1), (2, 1), (2, 2))
     )
     y, z = lax.axis_index("y"), lax.axis_index("z")
-    order = [(z + dz) % 4 * 4 + (y + dy) % 4 for dy, dz in places]
-    return near, near_sources, far, far_sources, order
+    return [(z + dz) % 4 * 4 + (y + dy) % 4 for dy, dz in places]
 
 
 def shards(
@@ -612,21 +622,26 @@
     )
     narrow = lax.all_gather(narrow, ("z", "y", "core"), axis=0, tiled=True)
     own_block = jnp.concatenate([mine(x_weight, 1), swap_cores(others(x_weight, 1))], axis=0)
-    near, near_sources, far, far_sources, order = travelling(own_block)
-    place = jnp.stack([core, *order]).astype(jnp.int32)
-
-    tokens, z_weight, _ = lax.optimization_barrier((tokens, z_weight, own_block))
-    other = swap_cores(tokens)
-    last = jnp.where(core == 0, other[-HALO:], tokens[-HALO:])
-    slabs = (tokens, other, along_chips(last, 1))
+    near, near_sources, y_far, z_far = near_blocks(own_block)
+    place = jnp.stack([core, *block_order()]).astype(jnp.int32)
+
+    (z_weight,) = tied((z_weight,), own_block)
     z_block = in_core_order(core, mine(z_weight, 1), swap_cores(others(z_weight, 1)), 0)
-    z_block, _ = lax.optimization_barrier((z_block, near[1]))
     z_whole = lax.all_gather(z_block, ("z", "y"), axis=0, tiled=True)
-
+    (tokens,) = tied((tokens,), *near[1:5])
+    chips = lax.axis_size("z") * lax.axis_size("y")
+    to_next = lambda target: lax.ppermute(
+        tokens[-HALO:], ("z", "y", "core"),
+        [(2 * i + 1, 2 * i + 2 + target) for i in range(chips - 1)],
+    )
+    slabs = (tokens, swap_cores(tokens), to_next(0) + to_next(1))
+
+    y_far, z_far = tied((y_far, z_far), *slabs[1:])
+    sums = first_products(place, slabs, near, near_sources, 11)
+    far, far_sources = far_blocks(y_far, z_far, sums[0])
     bcc, cum, cum_slab, cum_t, step_t, weights_in, decays = prepared(
         place, slabs, narrow, conv_bc, per_lane(dt_bias), per_lane(decay_rate), heads
     )
-    sums = first_products(place, slabs, near, near_sources, 11)
     xc, entering, final = local_states(
         place, slabs, far, far_sources, 11, 5, sums, bcc, weights_in, decays, mine(conv_x, 1)
     )

time: 217 us -> 213 us (0.982)
  waiting for transfers between devices: 57.3 us -> 51.9 us
    ppermute x20, waiting for transfers between devices: 53.9 us -> 46.6 us  [round_ring(): lax.ppermute(a, axis, [(i, (i + distance) % size) for i in range(size)])]
    ppermute x1 -> x2, starting transfers between devices: 4.36 us -> 2.65 us  [shards(): lax.ppermute(tokens[-HALO:], ('z', 'y', 'core'), [(2 * i + 1, 2 * i + 2 +...]
    unnamed x47 -> x51, local copies, waits for them, and re-layouts: 13.6 us -> 12.7 us
    slice x10 -> x12, local copies, waits for them, and re-layouts: 5.48 us -> 4.92 us  [the longest x2 2.01 us: near_blocks(): z_far = join(from_z_less[block:], from_z_more[block:])]
  transfers between devices with their start and end apart: 31 -> 32, of which waited for: 10 -> 13; matrix products, arithmetic and copies ran while one was open for 7% -> 7% of each run, Pallas kernels for 28% -> 29%
where the time goes in v5:
time: 213 us; the launch traced here: 212 us
  Pallas kernels  71.5 us (34%)
  waiting for transfers between devices  51.9 us (24%)
  starting transfers between devices  43.3 us (20%)
  local copies, waits for them, and re-layouts  21.7 us (10%)
  between operations  13.8 us (6%)
  other arithmetic  9.69 us (5%)
    ppermute x20, waiting for transfers between devices, round_ring(): lax.ppermute(a, axis, [(i, (i + distance) % size) for i in range(size)])  46.6 us
    ppermute x20, starting transfers between devices, round_ring(): lax.ppermute(a, axis, [(i, (i + distance) % size) for i in range(size)])  31 us
    pallas_call x1, Pallas kernels, local_states(): pl.pallas_call(functools.partial(states_kernel, sources, done, count), gr...  15.8 us
    pallas_call x1, Pallas kernels, project_gate(): pl.pallas_call(z_kernel, grid_spec=pltpu.PrefetchScalarGridSpec(num_scala...  13 us
    unnamed x51, local copies, waits for them, and re-layouts  12.7 us
    pallas_call x1, Pallas kernels, first_products(): pl.pallas_call(functools.partial(first_kernel, sources, count), grid_spec...  12.4 us
    pallas_call x1, Pallas kernels, prepared(): pl.pallas_call(prepare_kernel, grid_spec=pltpu.PrefetchScalarGridSpec(num...  12.1 us
    ppermute x3, starting transfers between devices, earlier_states(): lax.ppermute(total, 'z', [(i, i + distance) for i in range(rows - distanc...  8.83 us
  transfers between devices with their start and end apart: 32, of which 13 were waited for; matrix products, arithmetic and copies ran while one was open for 7% of the time, Pallas kernels for 29%

profile of v5, /device:TPU:6, one launch (start us, length us, event | category | flops | bytes accessed | tf_op | source)
XLA Modules:
  0.0 211.9 jit_solution(474633670637137030)
XLA Ops:
  14.5 1.6 collective-permute-start.1
  16.1 1.7 collective-permute-start.2
  17.8 1.9 collective-permute-start.3
  19.7 2.1 %collective-permute-start.4 = (bf16[256,1024]{1,0:T(8,128)(2,1)S(1)}, bf16[256,1024]{1,0:T(8,128)(2,1)S(1)}, u32[]{:S(2)}, u32[]{:S(2)}) collective-permute-start(bf16[256,1024]{1,0:T(8,128)(2,1)S(1)} %pad_maximum_fusion.4.refs_0_), channel_id=1, source_target_pairs={{0,96},{32,0},{64,32},{96,64},{1,97},{33,1},{65,33},{97,65},{2,98}... | collective-permute-start | bytes 1572872 | tf_op jit(solution)/shard_map/ppermute | solution.py:24
  21.8 8.7 %collective-permute-done.1.refs_1_ = bf16[256,1024]{1,0:T(8,128)(2,1)S(1)} collective-permute-done((bf16[256,1024]{1,0:T(8,128)(2,1)S(1)}, bf16[256,1024]{1,0:T(8,128)(2,1)S(1)}, u32[]{:S(2)}, u32[]{:S(2)}) %collective-permute-start.1) | collective-permute-done | bytes 524320 | tf_op jit(solution)/shard_map/ppermute | solution.py:24
  30.9 4.3 %collective-permute-done.3.refs_3_ = bf16[256,1024]{1,0:T(8,128)(2,1)S(1)} collective-permute-done((bf16[256,1024]{1,0:T(8,128)(2,1)S(1)}, bf16[256,1024]{1,0:T(8,128)(2,1)S(1)}, u32[]{:S(2)}, u32[]{:S(2)}) %collective-permute-start.3) | collective-permute-done | bytes 524320 | tf_op jit(solution)/shard_map/ppermute | solution.py:24
  44.9 2.8 %collective-permute-start.12 = (bf16[384,1024]{1,0:T(8,128)(2,1)}, bf16[384,1024]{1,0:T(8,128)(2,1)}, u32[]{:S(2)}, u32[]{:S(2)}) collective-permute-start(bf16[384,1024]{1,0:T(8,128)(2,1)} %pad_maximum_fusion.3), channel_id=1, source_target_pairs={{0,96},{32,0},{64,32},{96,64},{1,97},{33,1},{65,33},{97,65},{2,98}... | collective-permute-start | bytes 2359304 | tf_op jit(solution)/shard_map/ppermute | solution.py:24
  49.2 16.1 %collective-permute-done.10.refs_6_ = bf16[384,1024]{1,0:T(8,128)(2,1)S(1)} collective-permute-done((bf16[384,1024]{1,0:T(8,128)(2,1)}, bf16[384,1024]{1,0:T(8,128)(2,1)S(1)}, u32[]{:S(2)}, u32[]{:S(2)}) %collective-permute-start.10) | collective-permute-done | bytes 786464 | tf_op jit(solution)/shard_map/ppermute | solution.py:24
  65.4 3.5 %collective-permute-done.9.refs_5_ = bf16[384,1024]{1,0:T(8,128)(2,1)} collective-permute-done((bf16[384,1024]{1,0:T(8,128)(2,1)}, bf16[384,1024]{1,0:T(8,128)(2,1)}, u32[]{:S(2)}, u32[]{:S(2)}) %collective-permute-start.9) | collective-permute-done | bytes 786464 | tf_op jit(solution)/shard_map/ppermute | solution.py:24
  73.9 3.0 %collective-permute-start.14 = (bf16[256,1024]{1,0:T(8,128)(2,1)}, bf16[256,1024]{1,0:T(8,128)(2,1)}, u32[]{:S(2)}, u32[]{:S(2)}) collective-permute-start(bf16[256,1024]{1,0:T(8,128)(2,1)} %pad_maximum_fusion.7), channel_id=1, source_target_pairs={{0,24},{8,0},{16,8},{24,16},{1,25},{9,1},{17,9},{25,17},{2,26},{10... | collective-permute-start | bytes 1572872 | tf_op jit(solution)/shard_map/ppermute | solution.py:24
  76.9 1.9 collective-permute-start.15
  81.3 12.4 %first_products.1 = (f32[1024,1024]{1,0:T(8,128)}, f32[16,1024]{1,0:T(8,128)S(1)}) custom-call(s32[17]{0:T(128)S(1)} %stack.68.place_ref, bf16[512,4096]{1,0:T(8,128)(2,1)} %own_ref.3, bf16[512,4096]{1,0:T(8,128)(2,1)} %collective-permute-done.5.other_ref, bf16[16,4096]{1,0:T(8,128)(2,1)S(1)} %add.204.before_ref, ...), custom_call_target="tpu_custom_call" | custom-call | flops 6000000000 | bytes 18874368 | tf_op jit(solution)/shard_map/first_products/pallas_call | solution.py:403
  93.7 1.9 collective-permute-done.13.refs_0_
  98.7 3.1 %collective-permute-start.18 = (bf16[128,1024]{1,0:T(8,128)(2,1)}, bf16[128,1024]{1,0:T(8,128)(2,1)S(1)}, u32[]{:S(2)}, u32[]{:S(2)}) collective-permute-start(bf16[128,1024]{1,0:T(8,128)(2,1)} %slice.54), channel_id=1, source_target_pairs={{0,96},{32,0},{64,32},{96,64},{1,97},{33,1},{65,33},{97,65},{2,98}... | collective-permute-start | bytes 786440 | tf_op jit(solution)/shard_map/ppermute | solution.py:24
  101.8 1.9 copy-done.15
  103.7 12.1 %prepared.1 = (bf16[1024,256]{1,0:T(8,128)(2,1)S(1)}, f32[1024,128]{1,0:T(8,128)S(1)}, f32[1024,128]{1,0:T(8,128)S(1)}, f32[16,1024]{1,0:T(8,128)S(1)}, f32[16,1...) custom-call(s32[17]{0:T(128)S(1)} %stack.68.place_ref, bf16[512,4096]{1,0:T(8,128)(2,1)} %own_ref.3, ...), custom_call_target="tpu_custom_call" | custom-call | flops 4000000000 | bytes 14680064 | tf_op jit(solution)/shard_map/prepared/pallas_call | solution.py:380
  116.7 15.8 %states.1 = (bf16[1024,1024]{1,0:T(8,128)(2,1)}, bf16[4,128,1024]{2,1,0:T(8,128)(2,1)S(1)}, bf16[144,1024]{1,0:T(8,128)(2,1)S(1)}) custom-call(s32[17]{0:T(128)S(1)} %stack.68.place_ref, bf16[512,4096]{1,0:T(8,128)(2,1)} %own_ref.3, bf16[512,4096]{1,0:T(8,128)(2,1)} %collective-permute-done.5.other_ref, bf16[16,4096]{1,0:T(8,128)(2,1)S(1)} %add.204.before_ref, ...), custom_call_target="tpu_custom_call" | custom-call | flops 8000000000 | bytes 16777216 | tf_op jit(solution)/shard_map/states/pallas_call | solution.py:426
  133.7 2.2 %collective-permute-start.20 = (bf16[144,1024]{1,0:T(8,128)(2,1)S(1)}, bf16[144,1024]{1,0:T(8,128)(2,1)S(1)}, u32[]{:S(2)}, u32[]{:S(2)}) collective-permute-start(bf16[144,1024]{1,0:T(8,128)(2,1)S(1)} %get-tuple-element.45.refs_0_), channel_id=1, source_target_pairs={{0,16},{8,24},{16,0},{24,8},{1,17},{9,25},{17,1},{25,9},{2,18},{10... | collective-permute-start | bytes 884744 | tf_op jit(solution)/shard_map/ppermute | solution.py:24
  135.9 1.9 collective-permute-start.21
  137.8 1.6 copy-done.17
  139.4 6.9 %outputs.1.local_ref = f32[1024,1024]{1,0:T(8,128)S(1)} custom-call(bf16[1024,1024]{1,0:T(8,128)(2,1)S(1)} %copy-done.17, bf16[1024,256]{1,0:T(8,128)(2,1)S(1)} %get-tuple-element.36.refs_8_.bcc_ref, f32[1024,128]{1,0:T(8,128)S(1)} %get-tuple-element.40.cum_ref, f32[16,1024]{1,0:T(8,128)S(1)} %get-tuple-element.41.cum_t_ref, ...), custom_call_target="tpu_custom_call" | custom-call | flops 10000000000 | bytes 10485760 | tf_op jit(solution)/shard_map/outputs/pallas_call | solution.py:457
  146.3 1.9 copy-done.2
  148.3 5.6 %collective-permute-done.20.refs_2_ = bf16[144,1024]{1,0:T(8,128)(2,1)S(1)} collective-permute-done((bf16[144,1024]{1,0:T(8,128)(2,1)S(1)}, bf16[144,1024]{1,0:T(8,128)(2,1)S(1)}, u32[]{:S(2)}, u32[]{:S(2)}) %collective-permute-start.20) | collective-permute-done | bytes 294944 | tf_op jit(solution)/shard_map/ppermute | solution.py:24
  156.0 4.5 %collective-permute-start.22 = (bf16[144,1024]{1,0:T(8,128)(2,1)S(1)}, bf16[144,1024]{1,0:T(8,128)(2,1)S(1)}, u32[]{:S(2)}, u32[]{:S(2)}) collective-permute-start(bf16[144,1024]{1,0:T(8,128)(2,1)S(1)} %get-tuple-element.48), channel_id=1, source_target_pairs={{0,96},{1,97},{2,98},{3,99},{4,100},{5,101},{6,102},{7,103},{8,104... | collective-permute-start | bytes 884744 | tf_op jit(solution)/shard_map/ppermute | solution.py:554
  161.9 3.0 %collective-permute-start.24 = (bf16[144,1024]{1,0:T(8,128)(2,1)S(1)}, bf16[144,1024]{1,0:T(8,128)(2,1)S(1)}, u32[]{:S(2)}, u32[]{:S(2)}) collective-permute-start(bf16[144,1024]{1,0:T(8,128)(2,1)S(1)} %get-tuple-element.48), channel_id=1, source_target_pairs={{0,32},{32,64},{64,96},{1,33},{33,65},{65,97},{2,34},{34,66},{66,9... | collective-permute-start | bytes 884744 | tf_op jit(solution)/shard_map/ppermute | solution.py:554
  164.9 13.0 %project_gate.1.gate_ref = bf16[1024,1024]{1,0:T(8,128)(2,1)S(1)} custom-call(s32[17]{0:T(128)S(1)} %stack.68.place_ref, bf16[512,4096]{1,0:T(8,128)(2,1)} %own_ref.3, bf16[512,4096]{1,0:T(8,128)(2,1)} %collective-permute-done.5.other_ref, bf16[4096,1024]{1,0:T(8,128)(2,1)} %all-gather.3.cloned.1.call-done.weight_ref), custom_call_target="tpu_custom_call" | custom-call | flops 8999999488 | bytes 20971520 | tf_op jit(solution)/shard_map/project_gate/pallas_call | solution.py:477
  180.1 8.7 %gate.1 = (bf16[1024,1024]{1,0:T(8,128)(2,1)}, f32[1,1024]{1,0:T(1,128)}) custom-call(bf16[1024,1024]{1,0:T(8,128)(2,1)} %copy-done.3, f32[1024,1024]{1,0:T(8,128)} %copy-done.2, bf16[1024,256]{1,0:T(8,128)(2,1)} %copy-done.6, f32[1024,128]{1,0:T(8,128)} %copy-done.7, f32[128,1024]{1,0:T(8,128)} %copy-done.8, f32[8,1024]{1,0:T(8,128)} %copy-done.13, ...), custom_call_target="tpu_custom_call" | custom-call | flops 1000000000 | bytes 10485760 | tf_op jit(solution)/shard_map/gate/pallas_call | solution.py:494
  188.8 2.4 %constant_dynamic-slice_fusion = bf16[512,1024]{1,0:T(8,128)(2,1)} fusion(bf16[1024,1024]{1,0:T(8,128)(2,1)} %get-tuple-element.49.mine_ref, s32[]{:T(128)S(6)} %select_n.129), kind=kLoop, calls=%fused_computation.13 | loop fusion | bytes 2097156 | tf_op jit(solution)/shard_map/dynamic_slice | solution.py:615
  191.8 2.4 %collective-permute-done.26 = f32[1,1024]{1,0:T(1,128)S(1)} collective-permute-done((f32[1,1024]{1,0:T(1,128)}, f32[1,1024]{1,0:T(1,128)S(1)}, u32[]{:S(2)}, u32[]{:S(2)}) %collective-permute-start.26) | collective-permute-done | bytes 4128 | tf_op jit(solution)/shard_map/ppermute | solution.py:19
  195.7 2.4 %collective-permute-start.27 = (f32[1,512]{1,0:T(1,128)S(1)}, f32[1,512]{1,0:T(1,128)S(1)}, u32[]{:S(2)}, u32[]{:S(2)}) collective-permute-start(f32[1,512]{1,0:T(1,128)S(1)} %dynamic-slice_add_fusion), channel_id=1, source_target_pairs={{0,1},{1,2},{2,3},{3,0},{4,5},{5,6},{6,7},{7,4},{8,9},{9,10},{10,1... | collective-permute-start | bytes 6152 | tf_op jit(solution)/shard_map/ppermute | solution.py:24
  199.6 3.5 %collective-permute-done.28 = f32[1,512]{1,0:T(1,128)S(1)} collective-permute-done((f32[1,512]{1,0:T(1,128)S(1)}, f32[1,512]{1,0:T(1,128)S(1)}, u32[]{:S(2)}, u32[]{:S(2)}) %collective-permute-start.28) | collective-permute-done | bytes 2080 | tf_op jit(solution)/shard_map/ppermute | solution.py:24
  203.2 1.9 normalized.1
  (131 shorter events, 41.3 us)
Async XLA Ops:
  6.5 95.3 %all-gather.5.cloned.1.call-start = ((), (), s32[]{:S(2)}) async-start(), calls=%async_computation.1 | async-start | bytes 3244032 | tf_op jit(solution)/shard_map/all_gather | solution.py:623
  9.0 155.9 %all-gather.3.cloned.1.call-start = ((), (), s32[]{:S(2)}) async-start(), calls=%async_computation | async-start | bytes 8912896 | tf_op jit(solution)/shard_map/all_gather | solution.py:630
  10.2 1.6 collective-permute-start
  11.9 1.6 collective-permute-start.6
  14.5 16.0 %collective-permute-start.1 = (bf16[256,1024]{1,0:T(8,128)(2,1)S(1)}, bf16[256,1024]{1,0:T(8,128)(2,1)S(1)}, u32[]{:S(2)}, u32[]{:S(2)}) collective-permute-start(bf16[256,1024]{1,0:T(8,128)(2,1)S(1)} %pad_maximum_fusion.4.refs_0_), channel_id=1, source_target_pairs={{0,8},{8,16},{16,24},{24,0},{1,9},{9,17},{17,25},{25,1},{2,10},{10... | collective-permute-start | bytes 1572872 | tf_op jit(solution)/shard_map/ppermute | solution.py:24
  16.1 14.8 %collective-permute-start.2 = (bf16[256,1024]{1,0:T(8,128)(2,1)S(1)}, bf16[256,1024]{1,0:T(8,128)(2,1)S(1)}, u32[]{:S(2)}, u32[]{:S(2)}) collective-permute-start(bf16[256,1024]{1,0:T(8,128)(2,1)S(1)} %pad_maximum_fusion.4.refs_0_), channel_id=1, source_target_pairs={{0,24},{8,0},{16,8},{24,16},{1,25},{9,1},{17,9},{25,17},{2,26},{10... | collective-permute-start | bytes 1572872 | tf_op jit(solution)/shard_map/ppermute | solution.py:24
  17.8 17.4 %collective-permute-start.3 = (bf16[256,1024]{1,0:T(8,128)(2,1)S(1)}, bf16[256,1024]{1,0:T(8,128)(2,1)S(1)}, u32[]{:S(2)}, u32[]{:S(2)}) collective-permute-start(bf16[256,1024]{1,0:T(8,128)(2,1)S(1)} %pad_maximum_fusion.4.refs_0_), channel_id=1, source_target_pairs={{0,32},{32,64},{64,96},{96,0},{1,33},{33,65},{65,97},{97,1},{2,34}... | collective-permute-start | bytes 1572872 | tf_op jit(solution)/shard_map/ppermute | solution.py:24
  19.7 15.5 %collective-permute-start.4 = (bf16[256,1024]{1,0:T(8,128)(2,1)S(1)}, bf16[256,1024]{1,0:T(8,128)(2,1)S(1)}, u32[]{:S(2)}, u32[]{:S(2)}) collective-permute-start(bf16[256,1024]{1,0:T(8,128)(2,1)S(1)} %pad_maximum_fusion.4.refs_0_), channel_id=1, source_target_pairs={{0,96},{32,0},{64,32},{96,64},{1,97},{33,1},{65,33},{97,65},{2,98}... | collective-permute-start | bytes 1572872 | tf_op jit(solution)/shard_map/ppermute | solution.py:24
  35.2 38.5 %collective-permute-start.5 = (bf16[512,4096]{1,0:T(8,128)(2,1)}, bf16[512,4096]{1,0:T(8,128)(2,1)}, u32[]{:S(2)}, u32[]{:S(2)}) collective-permute-start(bf16[512,4096]{1,0:T(8,128)(2,1)} %own_ref.3), channel_id=1, source_target_pairs={{0,4},{4,0},{1,5},{5,1},{2,6},{6,2},{3,7},{7,3},{8,12},{12,8},{9,1... | collective-permute-start | bytes 12582920 | tf_op jit(solution)/shard_map/ppermute | solution.py:19
  36.3 8.6 %collective-permute-start.7 = (bf16[16,4096]{1,0:T(8,128)(2,1)S(1)}, bf16[16,4096]{1,0:T(8,128)(2,1)}, u32[]{:S(2)}, u32[]{:S(2)}) collective-permute-start(bf16[16,4096]{1,0:T(8,128)(2,1)S(1)} %slice.34), channel_id=1, source_target_pairs={{4,8},{12,16},{20,24},{28,32},{36,40},{44,48},{52,56},{60,64},{68,... | collective-permute-start | bytes 393224 | tf_op jit(solution)/shard_map/ppermute | solution.py:633
  37.6 10.1 %collective-permute-start.8 = (bf16[16,4096]{1,0:T(8,128)(2,1)S(1)}, bf16[16,4096]{1,0:T(8,128)(2,1)}, u32[]{:S(2)}, u32[]{:S(2)}) collective-permute-start(bf16[16,4096]{1,0:T(8,128)(2,1)S(1)} %slice.34), channel_id=1, source_target_pairs={{4,12},{12,20},{20,28},{28,36},{36,44},{44,52},{52,60},{60,68},{68... | collective-permute-start | bytes 393224 | tf_op jit(solution)/shard_map/ppermute | solution.py:633
  39.9 25.5 %collective-permute-start.10 = (bf16[384,1024]{1,0:T(8,128)(2,1)}, bf16[384,1024]{1,0:T(8,128)(2,1)S(1)}, u32[]{:S(2)}, u32[]{:S(2)}) collective-permute-start(bf16[384,1024]{1,0:T(8,128)(2,1)} %pad_maximum_fusion.1), channel_id=1, source_target_pairs={{0,24},{8,0},{16,8},{24,16},{1,25},{9,1},{17,9},{25,17},{2,26},{10... | collective-permute-start | bytes 2359304 | tf_op jit(solution)/shard_map/ppermute | solution.py:24
  42.3 26.6 %collective-permute-start.9 = (bf16[384,1024]{1,0:T(8,128)(2,1)}, bf16[384,1024]{1,0:T(8,128)(2,1)}, u32[]{:S(2)}, u32[]{:S(2)}) collective-permute-start(bf16[384,1024]{1,0:T(8,128)(2,1)} %pad_maximum_fusion), channel_id=1, source_target_pairs={{0,8},{8,16},{16,24},{24,0},{1,9},{9,17},{17,25},{25,1},{2,10},{10... | collective-permute-start | bytes 2359304 | tf_op jit(solution)/shard_map/ppermute | solution.py:24
  44.9 25.0 %collective-permute-start.12 = (bf16[384,1024]{1,0:T(8,128)(2,1)}, bf16[384,1024]{1,0:T(8,128)(2,1)}, u32[]{:S(2)}, u32[]{:S(2)}) collective-permute-start(bf16[384,1024]{1,0:T(8,128)(2,1)} %pad_maximum_fusion.3), channel_id=1, source_target_pairs={{0,96},{32,0},{64,32},{96,64},{1,97},{33,1},{65,33},{97,65},{2,98}... | collective-permute-start | bytes 2359304 | tf_op jit(solution)/shard_map/ppermute | solution.py:24
  47.7 23.3 %collective-permute-start.11 = (bf16[384,1024]{1,0:T(8,128)(2,1)}, bf16[384,1024]{1,0:T(8,128)(2,1)}, u32[]{:S(2)}, u32[]{:S(2)}) collective-permute-start(bf16[384,1024]{1,0:T(8,128)(2,1)} %pad_maximum_fusion.2), channel_id=1, source_target_pairs={{0,32},{32,64},{64,96},{96,0},{1,33},{33,65},{65,97},{97,1},{2,34}... | collective-permute-start | bytes 2359304 | tf_op jit(solution)/shard_map/ppermute | solution.py:24
  73.7 21.9 %collective-permute-start.13 = (bf16[256,1024]{1,0:T(8,128)(2,1)}, bf16[256,1024]{1,0:T(8,128)(2,1)S(1)}, u32[]{:S(2)}, u32[]{:S(2)}) collective-permute-start(bf16[256,1024]{1,0:T(8,128)(2,1)} %pad_maximum_fusion.7), channel_id=1, source_target_pairs={{0,8},{8,16},{16,24},{24,0},{1,9},{9,17},{17,25},{25,1},{2,10},{10... | collective-permute-start | bytes 1572872 | tf_op jit(solution)/shard_map/ppermute | solution.py:24
  73.9 42.8 %collective-permute-start.14 = (bf16[256,1024]{1,0:T(8,128)(2,1)}, bf16[256,1024]{1,0:T(8,128)(2,1)}, u32[]{:S(2)}, u32[]{:S(2)}) collective-permute-start(bf16[256,1024]{1,0:T(8,128)(2,1)} %pad_maximum_fusion.7), channel_id=1, source_target_pairs={{0,24},{8,0},{16,8},{24,16},{1,25},{9,1},{17,9},{25,17},{2,26},{10... | collective-permute-start | bytes 1572872 | tf_op jit(solution)/shard_map/ppermute | solution.py:24
  76.9 39.7 %collective-permute-start.15 = (bf16[256,1024]{1,0:T(8,128)(2,1)}, bf16[256,1024]{1,0:T(8,128)(2,1)}, u32[]{:S(2)}, u32[]{:S(2)}) collective-permute-start(bf16[256,1024]{1,0:T(8,128)(2,1)} %pad_maximum_fusion.6), channel_id=1, source_target_pairs={{0,32},{32,64},{64,96},{96,0},{1,33},{33,65},{65,97},{97,1},{2,34}... | collective-permute-start | bytes 1572872 | tf_op jit(solution)/shard_map/ppermute | solution.py:24
  78.8 17.9 %collective-permute-start.16 = (bf16[256,1024]{1,0:T(8,128)(2,1)}, bf16[256,1024]{1,0:T(8,128)(2,1)S(1)}, u32[]{:S(2)}, u32[]{:S(2)}) collective-permute-start(bf16[256,1024]{1,0:T(8,128)(2,1)} %pad_maximum_fusion.6), channel_id=1, source_target_pairs={{0,96},{32,0},{64,32},{96,64},{1,97},{33,1},{65,33},{97,65},{2,98}... | collective-permute-start | bytes 1572872 | tf_op jit(solution)/shard_map/ppermute | solution.py:24
  98.3 18.4 %collective-permute-start.17 = (bf16[128,1024]{1,0:T(8,128)(2,1)S(1)}, bf16[128,1024]{1,0:T(8,128)(2,1)S(1)}, u32[]{:S(2)}, u32[]{:S(2)}) collective-permute-start(bf16[128,1024]{1,0:T(8,128)(2,1)S(1)} %slice.53), channel_id=1, source_target_pairs={{0,8},{8,16},{16,24},{24,0},{1,9},{9,17},{17,25},{25,1},{2,10},{10... | collective-permute-start | bytes 786440 | tf_op jit(solution)/shard_map/ppermute | solution.py:24
  98.7 18.0 %collective-permute-start.18 = (bf16[128,1024]{1,0:T(8,128)(2,1)}, bf16[128,1024]{1,0:T(8,128)(2,1)S(1)}, u32[]{:S(2)}, u32[]{:S(2)}) collective-permute-start(bf16[128,1024]{1,0:T(8,128)(2,1)} %slice.54), channel_id=1, source_target_pairs={{0,96},{32,0},{64,32},{96,64},{1,97},{33,1},{65,33},{97,65},{2,98}... | collective-permute-start | bytes 786440 | tf_op jit(solution)/shard_map/ppermute | solution.py:24
  132.4 15.8 %collective-permute-start.19 = (bf16[144,1024]{1,0:T(8,128)(2,1)S(1)}, bf16[144,1024]{1,0:T(8,128)(2,1)S(1)}, u32[]{:S(2)}, u32[]{:S(2)}) collective-permute-start(bf16[144,1024]{1,0:T(8,128)(2,1)S(1)} %get-tuple-element.45.refs_0_), channel_id=1, source_target_pairs={{0,8},{8,16},{16,24},{24,0},{1,9},{9,17},{17,25},{25,1},{2,10},{10... | collective-permute-start | bytes 884744 | tf_op jit(solution)/shard_map/ppermute | solution.py:24
  133.7 20.2 %collective-permute-start.20 = (bf16[144,1024]{1,0:T(8,128)(2,1)S(1)}, bf16[144,1024]{1,0:T(8,128)(2,1)S(1)}, u32[]{:S(2)}, u32[]{:S(2)}) collective-permute-start(bf16[144,1024]{1,0:T(8,128)(2,1)S(1)} %get-tuple-element.45.refs_0_), channel_id=1, source_target_pairs={{0,16},{8,24},{16,0},{24,8},{1,17},{9,25},{17,1},{25,9},{2,18},{10... | collective-permute-start | bytes 884744 | tf_op jit(solution)/shard_map/ppermute | solution.py:24
  135.9 18.0 %collective-permute-start.21 = (bf16[144,1024]{1,0:T(8,128)(2,1)S(1)}, bf16[144,1024]{1,0:T(8,128)(2,1)S(1)}, u32[]{:S(2)}, u32[]{:S(2)}) collective-permute-start(bf16[144,1024]{1,0:T(8,128)(2,1)S(1)} %get-tuple-element.45.refs_0_), channel_id=1, source_target_pairs={{0,24},{8,0},{16,8},{24,16},{1,25},{9,1},{17,9},{25,17},{2,26},{10... | collective-permute-start | bytes 884744 | tf_op jit(solution)/shard_map/ppermute | solution.py:24
  156.0 23.2 %collective-permute-start.22 = (bf16[144,1024]{1,0:T(8,128)(2,1)S(1)}, bf16[144,1024]{1,0:T(8,128)(2,1)S(1)}, u32[]{:S(2)}, u32[]{:S(2)}) collective-permute-start(bf16[144,1024]{1,0:T(8,128)(2,1)S(1)} %get-tuple-element.48), channel_id=1, source_target_pairs={{0,96},{1,97},{2,98},{3,99},{4,100},{5,101},{6,102},{7,103},{8,104... | collective-permute-start | bytes 884744 | tf_op jit(solution)/shard_map/ppermute | solution.py:554
  160.6 18.6 %collective-permute-start.23 = (bf16[144,1024]{1,0:T(8,128)(2,1)S(1)}, bf16[144,1024]{1,0:T(8,128)(2,1)S(1)}, u32[]{:S(2)}, u32[]{:S(2)}) collective-permute-start(bf16[144,1024]{1,0:T(8,128)(2,1)S(1)} %get-tuple-element.48), channel_id=1, source_target_pairs={{0,64},{32,96},{1,65},{33,97},{2,66},{34,98},{3,67},{35,99},{4,68}... | collective-permute-start | bytes 884744 | tf_op jit(solution)/shard_map/ppermute | solution.py:554
  161.9 17.3 %collective-permute-start.24 = (bf16[144,1024]{1,0:T(8,128)(2,1)S(1)}, bf16[144,1024]{1,0:T(8,128)(2,1)S(1)}, u32[]{:S(2)}, u32[]{:S(2)}) collective-permute-start(bf16[144,1024]{1,0:T(8,128)(2,1)S(1)} %get-tuple-element.48), channel_id=1, source_target_pairs={{0,32},{32,64},{64,96},{1,33},{33,65},{65,97},{2,34},{34,66},{66,9... | collective-permute-start | bytes 884744 | tf_op jit(solution)/shard_map/ppermute | solution.py:554
  191.3 11.9 %collective-permute-start.25 = (bf16[512,1024]{1,0:T(8,128)(2,1)}, bf16[512,1024]{1,0:T(8,128)(2,1)S(1)}, u32[]{:S(2)}, u32[]{:S(2)}) collective-permute-start(bf16[512,1024]{1,0:T(8,128)(2,1)} %constant_dynamic-slice_fusion), channel_id=1, source_target_pairs={{0,4},{4,0},{1,5},{5,1},{2,6},{6,2},{3,7},{7,3},{8,12},{12,8},{9,1... | collective-permute-start | bytes 3145736 | tf_op jit(solution)/shard_map/ppermute | solution.py:19
  191.3 2.9 %collective-permute-start.26 = (f32[1,1024]{1,0:T(1,128)}, f32[1,1024]{1,0:T(1,128)S(1)}, u32[]{:S(2)}, u32[]{:S(2)}) collective-permute-start(f32[1,1024]{1,0:T(1,128)} %get-tuple-element.50), channel_id=1, source_target_pairs={{0,4},{4,0},{1,5},{5,1},{2,6},{6,2},{3,7},{7,3},{8,12},{12,8},{9,1... | collective-permute-start | bytes 12296 | tf_op jit(solution)/shard_map/ppermute | solution.py:19
  194.8 4.8 %collective-permute-start.29 = (f32[1,512]{1,0:T(1,128)S(1)}, f32[1,512]{1,0:T(1,128)S(1)}, u32[]{:S(2)}, u32[]{:S(2)}) collective-permute-start(f32[1,512]{1,0:T(1,128)S(1)} %dynamic-slice_add_fusion), channel_id=1, source_target_pairs={{0,3},{1,0},{2,1},{3,2},{4,7},{5,4},{6,5},{7,6},{8,11},{9,8},{10,9... | collective-permute-start | bytes 6152 | tf_op jit(solution)/shard_map/ppermute | solution.py:24
  195.7 3.9 %collective-permute-start.27 = (f32[1,512]{1,0:T(1,128)S(1)}, f32[1,512]{1,0:T(1,128)S(1)}, u32[]{:S(2)}, u32[]{:S(2)}) collective-permute-start(f32[1,512]{1,0:T(1,128)S(1)} %dynamic-slice_add_fusion), channel_id=1, source_target_pairs={{0,1},{1,2},{2,3},{3,0},{4,5},{5,6},{6,7},{7,4},{8,9},{9,10},{10,1... | collective-permute-start | bytes 6152 | tf_op jit(solution)/shard_map/ppermute | solution.py:24
  198.0 5.1 %collective-permute-start.28 = (f32[1,512]{1,0:T(1,128)S(1)}, f32[1,512]{1,0:T(1,128)S(1)}, u32[]{:S(2)}, u32[]{:S(2)}) collective-permute-start(f32[1,512]{1,0:T(1,128)S(1)} %dynamic-slice_add_fusion), channel_id=1, source_target_pairs={{0,2},{1,3},{2,0},{3,1},{4,6},{5,7},{6,4},{7,5},{8,10},{9,11},{10,... | collective-permute-start | bytes 6152 | tf_op jit(solution)/shard_map/ppermute | solution.py:24
  (26 other events, 193.0 us)
Sparse Core Ops, SparseCore 0:
  9.6 51.0 all-gather.4
  62.8 83.4 all-gather.2

commit v6 on v5

--- a/solution.py
+++ b/solution.py
@@ -235,7 +235,7 @@
     total_ref[LANES:, :] = split_decay(decay)
 
 
-def outputs_kernel(xc_ref, bcc_ref, cum_ref, cum_t_ref, step_t_ref, entering_ref, skip_ref, out_ref):
+def outputs_kernel(xc_ref, bcc_ref, cum_ref, cum_t_ref, step_t_ref, entering_ref, skip_ref, out_ref, carried):
     width = xc_ref.shape[1]
     b_rows, c_rows = bcc_ref[:, :LANES], bcc_ref[:, LANES:]
     scores = lax.dot_general(c_rows, b_rows, (((1,), (1,)), ((), ())), preferred_element_type=F32)
@@ -244,7 +244,7 @@
     scores = jnp.where(row >= col, scores, 0.0)
     cum = cum_ref[...]
     grown = expand_heads(jnp.exp(cum), width)
-    out_ref[...] = grown * jnp.dot(c_rows, entering_ref[0], preferred_element_type=F32)
+    carried[...] = grown * jnp.dot(c_rows, entering_ref[0], preferred_element_type=F32)
     lane = lax.broadcasted_iota(jnp.int32, (GROUP, LANES), 1)
 
     def mixing(head):
@@ -262,10 +262,10 @@
             [jnp.where(lane < HEAD, inputs, zero), jnp.where(lane < HEAD, zero, inputs)], axis=0
         )
         out_ref[:, lanes] = (
-            out_ref[:, lanes]
+            carried[:, lanes]
             + jnp.dot(both, stacked, preferred_element_type=F32)
             + skip_ref[:, lanes] * inputs.astype(F32)
-        )
+        ).astype(BF16)
 
 
 def z_kernel(place_ref, own_ref, other_ref, weight_ref, gate_ref, accum):
@@ -294,9 +294,9 @@
 
 
 def gate_kernel(
-    gate_ref, local_ref, bcc_ref, cum_ref, before_ref, before_decay_ref, *refs
+    core_ref, gate_ref, local_ref, bcc_ref, cum_ref, before_ref, before_decay_ref, *refs
 ):
-    earlier, (gated_ref, squares_ref, incoming) = refs[:-3], refs[-3:]
+    earlier, (mine_ref, send_ref, squares_ref, incoming) = refs[:-4], refs[-4:]
     width = local_ref.shape[1]
 
     @pl.when(pl.program_id(0) == 0)
@@ -309,8 +309,17 @@
 
     grown = expand_heads(jnp.exp(cum_ref[...]), width)
     carried = jnp.dot(bcc_ref[:, LANES:], incoming[...], preferred_element_type=F32)
-    gated = (local_ref[...] + grown * carried) * silu(gate_ref[...].astype(F32))
-    gated_ref[...] = gated.astype(BF16)
+    gated = (local_ref[...].astype(F32) + grown * carried) * silu(gate_ref[...].astype(F32))
+    is_own = pl.program_id(0) // 2 == core_ref[0]
+
+    @pl.when(is_own)
+    def _():
+        mine_ref[...] = gated.astype(BF16)
+
+    @pl.when(jnp.logical_not(is_own))
+    def _():
+        send_ref[...] = gated.astype(BF16)
+
     squares = gated * gated
     high = squares.astype(BF16)
     low = (squares - high.astype(F32)).astype(BF16)
@@ -344,7 +353,7 @@
     return pl.BlockSpec((GROUP, width), lambda i: (i, 0))
 
 
-def params(flops, megabytes, vmem=48):
+def params(flops, megabytes, vmem=32):
     return dict(
         compiler_params=pltpu.CompilerParams(vmem_limit_bytes=vmem * 2**20),
         cost_estimate=pl.CostEstimate(
@@ -462,8 +471,9 @@
             pl.BlockSpec((1, LANES, width), lambda i: (i, 0, 0)), whole((1, width)),
         ],
         out_specs=rows_of(width),
-        out_shape=jax.ShapeDtypeStruct((rows, width), F32),
-        compiler_params=pltpu.CompilerParams(vmem_limit_bytes=40 * 2**20),
+        out_shape=jax.ShapeDtypeStruct((rows, width), BF16),
+        scratch_shapes=[pltpu.VMEM((GROUP, width), F32)],
+        compiler_params=pltpu.CompilerParams(vmem_limit_bytes=32 * 2**20),
         cost_estimate=pl.CostEstimate(flops=10**10, bytes_accessed=10 * 2**20, transcendentals=4 * 2**20),
         name="outputs",
     )(xc, bcc, cum, cum_t, step_t, entering, skip)
@@ -489,21 +499,23 @@
     )(place, own, other, weight)
 
 
-def gate_outputs(gate, local, bcc, cum_slab, before, before_decay, earlier):
+def gate_outputs(core, gate, local, bcc, cum_slab, before, before_decay, earlier):
     rows, width = local.shape
+    half = jax.ShapeDtypeStruct((rows // 2, width), BF16)
     return pl.pallas_call(
         gate_kernel,
-        grid=(rows // GROUP,),
-        in_specs=[rows_of(width), rows_of(width), rows_of(2 * LANES), rows_of(LANES)]
-        + [whole(a.shape) for a in (before, before_decay, *earlier)],
-        out_specs=[rows_of(width), pl.BlockSpec((1, GROUP), lambda i: (0, i))],
-        out_shape=[
-            jax.ShapeDtypeStruct((rows, width), BF16), jax.ShapeDtypeStruct((1, rows), F32),
-        ],
-        scratch_shapes=[pltpu.VMEM((LANES, width), BF16)],
+        grid_spec=pltpu.PrefetchScalarGridSpec(
+            num_scalar_prefetch=1,
+            grid=(rows // GROUP,),
+            in_specs=[row_block(width), row_block(width), row_block(2 * LANES), row_block(LANES)]
+            + [fixed(a) for a in (before, before_decay, *earlier)],
+            out_specs=slab_blocks(width) + [pl.BlockSpec((1, GROUP), lambda i, place: (0, i))],
+            scratch_shapes=[pltpu.VMEM((LANES, width), BF16)],
+        ),
+        out_shape=[half, half, jax.ShapeDtypeStruct((1, rows), F32)],
         name="gate",
-        **params(1e9, 10, 60),
-    )(gate, local, bcc, cum_slab, before, before_decay, *earlier)
+        **params(1e9, 10),
+    )(core, gate, local, bcc, cum_slab, before, before_decay, *earlier)
 
 
 def normalized(core, gated, other, mean_squares, gain):
@@ -514,7 +526,7 @@
             num_scalar_prefetch=1,
             grid=(2,),
             in_specs=[
-                pl.BlockSpec((rows, width), lambda j, core: (core[0], 0)),
+                pl.BlockSpec((rows, width), lambda j, core: (0, 0)),
                 pl.BlockSpec((rows, width), lambda j, core: (0, 0)),
                 pl.BlockSpec((1, rows), lambda j, core: (0, 0)),
                 pl.BlockSpec((1, width), lambda j, core: (0, j)),
@@ -522,7 +534,7 @@
             out_specs=pl.BlockSpec((rows, width), lambda j, core: (0, j)),
         ),
         out_shape=jax.ShapeDtypeStruct((rows, 2 * width), BF16),
-        compiler_params=pltpu.CompilerParams(vmem_limit_bytes=40 * 2**20),
+        compiler_params=pltpu.CompilerParams(vmem_limit_bytes=32 * 2**20),
         cost_estimate=pl.CostEstimate(flops=10**7, bytes_accessed=4 * 2**20, transcendentals=0),
         name="normalized",
     )(core.astype(jnp.int32)[None], gated, other, mean_squares, gain)
@@ -649,9 +661,9 @@
     skip_lanes = jnp.repeat(mine(skip, 0), HEAD)[None, :]
     local = local_outputs(xc, bcc, cum, cum_t, step_t, entering, skip_lanes)
     gate = project_gate(place, slabs, z_whole)
-    gated, squares = gate_outputs(gate, local, bcc, cum_slab, before, before_decay, earlier)
-
-    other = swap_cores(others(gated, 0))
+    gated, send, squares = gate_outputs(place[:1], gate, local, bcc, cum_slab, before, before_decay, earlier)
+
+    other = swap_cores(send)
     summed = mine(squares + swap_cores(squares), 1)
     across = [round_ring(summed, "x", distance) for distance in range(1, lax.axis_size("x"))]
     mean_squares = (summed + sum(across)) / (2 * width * lax.axis_size("x"))

time: 213 us -> 214 us (level)
  local copies, waits for them, and re-layouts: 21.7 us -> 29.5 us
  Pallas kernels: 71.5 us -> 65.3 us
    unnamed x51 -> x61, local copies, waits for them, and re-layouts: 12.7 us -> 23.7 us
    dynamic_slice x2 -> x1, local copies, waits for them, and re-layouts: 2.44 us -> 0.03 us  [others(): return lax.dynamic_slice_in_dim(a, (1 - core) * size, size, axis)]
  transfers between devices with their start and end apart: 32 -> 32, of which waited for: 13 -> 13; matrix products, arithmetic and copies ran while one was open for 7% -> 6% of each run, Pallas kernels for 29% -> 27%
where the time goes in v6:
time: 214 us; the launch traced here: 213 us
  Pallas kernels  65.3 us (31%)
  waiting for transfers between devices  52.1 us (24%)
  starting transfers between devices  43.3 us (20%)
  local copies, waits for them, and re-layouts  29.5 us (14%)
  between operations  13.8 us (6%)
  other arithmetic  8.9 us (4%)
    ppermute x20, waiting for transfers between devices, round_ring(): lax.ppermute(a, axis, [(i, (i + distance) % size) for i in range(size)])  47.3 us
    ppermute x20, starting transfers between devices, round_ring(): lax.ppermute(a, axis, [(i, (i + distance) % size) for i in range(size)])  31.1 us
    unnamed x61, local copies, waits for them, and re-layouts  23.7 us
    pallas_call x1, Pallas kernels, local_states(): pl.pallas_call(functools.partial(states_kernel, sources, done, count), gr...  14 us
    pallas_call x1, Pallas kernels, project_gate(): pl.pallas_call(z_kernel, grid_spec=pltpu.PrefetchScalarGridSpec(num_scala...  12.2 us
    pallas_call x1, Pallas kernels, prepared(): pl.pallas_call(prepare_kernel, grid_spec=pltpu.PrefetchScalarGridSpec(num...  11.9 us
    pallas_call x1, Pallas kernels, first_products(): pl.pallas_call(functools.partial(first_kernel, sources, count), grid_spec...  10.6 us
    ppermute x3, starting transfers between devices, earlier_states(): lax.ppermute(total, 'z', [(i, i + distance) for i in range(rows - distanc...  8.77 us
  transfers between devices with their start and end apart: 32, of which 13 were waited for; matrix products, arithmetic and copies ran while one was open for 6% of the time, Pallas kernels for 27%

profile of v6, /device:TPU:6, one launch (start us, length us, event | category | flops | bytes accessed | tf_op | source)
XLA Modules:
  0.0 213.0 jit_solution(11614549725672337256)
XLA Ops:
  17.8 1.9 collective-permute-start.3
  19.7 2.1 collective-permute-start.4
  21.8 8.7 %collective-permute-done.1.refs_1_ = bf16[256,1024]{1,0:T(8,128)(2,1)S(1)} collective-permute-done((bf16[256,1024]{1,0:T(8,128)(2,1)S(1)}, bf16[256,1024]{1,0:T(8,128)(2,1)S(1)}, u32[]{:S(2)}, u32[]{:S(2)}) %collective-permute-start.1) | collective-permute-done | bytes 524320 | tf_op jit(solution)/shard_map/ppermute | solution.py:24
  30.9 4.3 %collective-permute-done.3.refs_3_ = bf16[256,1024]{1,0:T(8,128)(2,1)S(1)} collective-permute-done((bf16[256,1024]{1,0:T(8,128)(2,1)S(1)}, bf16[256,1024]{1,0:T(8,128)(2,1)S(1)}, u32[]{:S(2)}, u32[]{:S(2)}) %collective-permute-start.3) | collective-permute-done | bytes 524320 | tf_op jit(solution)/shard_map/ppermute | solution.py:24
  44.8 2.8 %collective-permute-start.12 = (bf16[384,1024]{1,0:T(8,128)(2,1)}, bf16[384,1024]{1,0:T(8,128)(2,1)}, u32[]{:S(2)}, u32[]{:S(2)}) collective-permute-start(bf16[384,1024]{1,0:T(8,128)(2,1)} %pad_maximum_fusion.3), channel_id=1, source_target_pairs={{0,96},{32,0},{64,32},{96,64},{1,97},{33,1},{65,33},{97,65},{2,98}... | collective-permute-start | bytes 2359304 | tf_op jit(solution)/shard_map/ppermute | solution.py:24
  49.2 16.1 %collective-permute-done.10.refs_6_ = bf16[384,1024]{1,0:T(8,128)(2,1)S(1)} collective-permute-done((bf16[384,1024]{1,0:T(8,128)(2,1)}, bf16[384,1024]{1,0:T(8,128)(2,1)S(1)}, u32[]{:S(2)}, u32[]{:S(2)}) %collective-permute-start.10) | collective-permute-done | bytes 786464 | tf_op jit(solution)/shard_map/ppermute | solution.py:24
  65.3 3.6 %collective-permute-done.9.refs_5_ = bf16[384,1024]{1,0:T(8,128)(2,1)} collective-permute-done((bf16[384,1024]{1,0:T(8,128)(2,1)}, bf16[384,1024]{1,0:T(8,128)(2,1)}, u32[]{:S(2)}, u32[]{:S(2)}) %collective-permute-start.9) | collective-permute-done | bytes 786464 | tf_op jit(solution)/shard_map/ppermute | solution.py:24
  73.8 3.0 %collective-permute-start.14 = (bf16[256,1024]{1,0:T(8,128)(2,1)}, bf16[256,1024]{1,0:T(8,128)(2,1)}, u32[]{:S(2)}, u32[]{:S(2)}) collective-permute-start(bf16[256,1024]{1,0:T(8,128)(2,1)} %pad_maximum_fusion.7), channel_id=1, source_target_pairs={{0,24},{8,0},{16,8},{24,16},{1,25},{9,1},{17,9},{25,17},{2,26},{10... | collective-permute-start | bytes 1572872 | tf_op jit(solution)/shard_map/ppermute | solution.py:24
  76.8 2.1 collective-permute-start.15
  81.2 2.2 %copy-done.18 = bf16[512,4096]{1,0:T(8,128)(2,1)S(1)} copy-done((bf16[512,4096]{1,0:T(8,128)(2,1)S(1)}, bf16[512,4096]{1,0:T(8,128)(2,1)}, u32[]{:S(2)}) %copy-start.18) | copy-done | bytes 4194328
  83.4 10.6 %first_products.1 = (f32[1024,1024]{1,0:T(8,128)S(1)}, f32[16,1024]{1,0:T(8,128)S(1)}) custom-call(s32[17]{0:T(128)S(1)} %stack.68.place_ref, bf16[512,4096]{1,0:T(8,128)(2,1)S(1)} %copy-done.18, bf16[512,4096]{1,0:T(8,128)(2,1)} %collective-permute-done.5.other_ref, bf16[16,4096]{1,0:T(8,128)(2,1)S(1)} %add.201.before_ref, ...), custom_call_target="tpu_custom_call" | custom-call | flops 6000000000 | bytes 18874368 | tf_op jit(solution)/shard_map/first_products/pallas_call | solution.py:412
  94.0 1.9 copy-done.24
  97.9 3.0 %collective-permute-start.18 = (bf16[128,1024]{1,0:T(8,128)(2,1)S(1)}, bf16[128,1024]{1,0:T(8,128)(2,1)S(1)}, u32[]{:S(2)}, u32[]{:S(2)}) collective-permute-start(bf16[128,1024]{1,0:T(8,128)(2,1)S(1)} %slice.54), channel_id=1, source_target_pairs={{0,96},{32,0},{64,32},{96,64},{1,97},{33,1},{65,33},{97,65},{2,98}... | collective-permute-start | bytes 786440 | tf_op jit(solution)/shard_map/ppermute | solution.py:24
  100.9 2.2 %copy-done.19 = bf16[512,4096]{1,0:T(8,128)(2,1)S(1)} copy-done((bf16[512,4096]{1,0:T(8,128)(2,1)S(1)}, bf16[512,4096]{1,0:T(8,128)(2,1)}, u32[]{:S(2)}) %copy-start.19) | copy-done | bytes 4194328
  103.1 1.9 copy-done.22
  105.0 11.9 %prepared.1 = (bf16[1024,256]{1,0:T(8,128)(2,1)S(1)}, f32[1024,128]{1,0:T(8,128)S(1)}, f32[1024,128]{1,0:T(8,128)S(1)}, f32[16,1024]{1,0:T(8,128)S(1)}, f32[16,1...) custom-call(s32[17]{0:T(128)S(1)} %stack.68.place_ref, bf16[512,4096]{1,0:T(8,128)(2,1)S(1)} %copy-done.19, ...), custom_call_target="tpu_custom_call" | custom-call | flops 4000000000 | bytes 14680064 | tf_op jit(solution)/shard_map/prepared/pallas_call | solution.py:389
  117.7 14.0 %states.1 = (bf16[1024,1024]{1,0:T(8,128)(2,1)S(1)}, bf16[4,128,1024]{2,1,0:T(8,128)(2,1)S(1)}, bf16[144,1024]{1,0:T(8,128)(2,1)S(1)}) custom-call(s32[17]{0:T(128)S(1)} %stack.68.place_ref, bf16[512,4096]{1,0:T(8,128)(2,1)S(1)} %copy-done.19, bf16[512,4096]{1,0:T(8,128)(2,1)} %collective-permute-done.5.other_ref, bf16[16,4096]{1,0:T(8,128)(2,1)S(1)} %add.201.before_ref, ...), custom_call_target="tpu_custom_call" | custom-call | flops 8000000000 | bytes 16777216 | tf_op jit(solution)/shard_map/states/pallas_call | solution.py:435
  133.1 2.4 %collective-permute-start.20 = (bf16[144,1024]{1,0:T(8,128)(2,1)S(1)}, bf16[144,1024]{1,0:T(8,128)(2,1)S(1)}, u32[]{:S(2)}, u32[]{:S(2)}) collective-permute-start(bf16[144,1024]{1,0:T(8,128)(2,1)S(1)} %get-tuple-element.46.refs_0_), channel_id=1, source_target_pairs={{0,16},{8,24},{16,0},{24,8},{1,17},{9,25},{17,1},{25,9},{2,18},{10... | collective-permute-start | bytes 884744 | tf_op jit(solution)/shard_map/ppermute | solution.py:24
  135.5 1.7 collective-permute-start.21
  137.1 7.1 %outputs.1.local_ref = bf16[1024,1024]{1,0:T(8,128)(2,1)S(1)} custom-call(bf16[1024,1024]{1,0:T(8,128)(2,1)S(1)} %get-tuple-element.40.xc_ref, bf16[1024,256]{1,0:T(8,128)(2,1)S(1)} %get-tuple-element.37.refs_8_.bcc_ref, f32[1024,128]{1,0:T(8,128)S(1)} %get-tuple-element.41.cum_ref, f32[16,1024]{1,0:T(8,128)S(1)} %get-tuple-element.42.cum_t_ref, ...), custom_call_target="tpu_custom_call" | custom-call | flops 10000000000 | bytes 10485760 | tf_op jit(solution)/shard_map/outputs/pallas_call | solution.py:466
  144.3 2.8 %collective-permute-done.19.refs_1_ = bf16[144,1024]{1,0:T(8,128)(2,1)S(1)} collective-permute-done((bf16[144,1024]{1,0:T(8,128)(2,1)S(1)}, bf16[144,1024]{1,0:T(8,128)(2,1)S(1)}, u32[]{:S(2)}, u32[]{:S(2)}) %collective-permute-start.19) | collective-permute-done | bytes 294944 | tf_op jit(solution)/shard_map/ppermute | solution.py:24
  147.1 5.9 %collective-permute-done.20.refs_2_ = bf16[144,1024]{1,0:T(8,128)(2,1)S(1)} collective-permute-done((bf16[144,1024]{1,0:T(8,128)(2,1)S(1)}, bf16[144,1024]{1,0:T(8,128)(2,1)S(1)}, u32[]{:S(2)}, u32[]{:S(2)}) %collective-permute-start.20) | collective-permute-done | bytes 294944 | tf_op jit(solution)/shard_map/ppermute | solution.py:24
  154.6 4.5 %collective-permute-start.22 = (bf16[144,1024]{1,0:T(8,128)(2,1)S(1)}, bf16[144,1024]{1,0:T(8,128)(2,1)S(1)}, u32[]{:S(2)}, u32[]{:S(2)}) collective-permute-start(bf16[144,1024]{1,0:T(8,128)(2,1)S(1)} %get-tuple-element.49), channel_id=1, source_target_pairs={{0,96},{1,97},{2,98},{3,99},{4,100},{5,101},{6,102},{7,103},{8,104... | collective-permute-start | bytes 884744 | tf_op jit(solution)/shard_map/ppermute | solution.py:566
  160.4 3.0 %collective-permute-start.24 = (bf16[144,1024]{1,0:T(8,128)(2,1)S(1)}, bf16[144,1024]{1,0:T(8,128)(2,1)S(1)}, u32[]{:S(2)}, u32[]{:S(2)}) collective-permute-start(bf16[144,1024]{1,0:T(8,128)(2,1)S(1)} %get-tuple-element.49), channel_id=1, source_target_pairs={{0,32},{32,64},{64,96},{1,33},{33,65},{65,97},{2,34},{34,66},{66,9... | collective-permute-start | bytes 884744 | tf_op jit(solution)/shard_map/ppermute | solution.py:566
  163.4 2.2 %copy-done.20 = bf16[512,4096]{1,0:T(8,128)(2,1)S(1)} copy-done((bf16[512,4096]{1,0:T(8,128)(2,1)S(1)}, bf16[512,4096]{1,0:T(8,128)(2,1)}, u32[]{:S(2)}) %copy-start.20) | copy-done | bytes 4194328
  165.6 3.4 %copy-done.21 = bf16[4096,1024]{1,0:T(8,128)(2,1)S(1)} copy-done((bf16[4096,1024]{1,0:T(8,128)(2,1)S(1)}, bf16[4096,1024]{1,0:T(8,128)(2,1)}, u32[]{:S(2)}) %copy-start.21) | copy-done | bytes 8388632
  169.0 12.2 %project_gate.1.gate_ref = bf16[1024,1024]{1,0:T(8,128)(2,1)S(1)} custom-call(s32[17]{0:T(128)S(1)} %stack.68.place_ref, bf16[512,4096]{1,0:T(8,128)(2,1)S(1)} %copy-done.20, bf16[512,4096]{1,0:T(8,128)(2,1)} %collective-permute-done.5.other_ref, bf16[4096,1024]{1,0:T(8,128)(2,1)S(1)} %copy-done.21), custom_call_target="tpu_custom_call" | custom-call | flops 8999999488 | bytes 20971520 | tf_op jit(solution)/shard_map/project_gate/pallas_call | solution.py:487
  186.7 6.8 %gate.1 = (bf16[512,1024]{1,0:T(8,128)(2,1)S(1)}, bf16[512,1024]{1,0:T(8,128)(2,1)}, f32[1,1024]{1,0:T(1,128)S(1)}) custom-call(s32[1]{0:T(128)} %bitcast.core_ref, bf16[1024,1024]{1,0:T(8,128)(2,1)S(1)} %project_gate.1.gate_ref, bf16[1024,1024]{1,0:T(8,128)(2,1)S(1)} %outputs.1.local_ref, bf16[1024,256]{1,0:T(8,128)(2,1)S(1)} %copy-done.4, ...), custom_call_target="tpu_custom_call" | custom-call | flops 1000000000 | bytes 10485760 | tf_op jit(solution)/shard_map/gate/pallas_call | solution.py:505
  194.1 1.8 collective-permute-done.26
  196.7 2.4 %collective-permute-start.27 = (f32[1,512]{1,0:T(1,128)S(1)}, f32[1,512]{1,0:T(1,128)S(1)}, u32[]{:S(2)}, u32[]{:S(2)}) collective-permute-start(f32[1,512]{1,0:T(1,128)S(1)} %dynamic-slice_add_fusion), channel_id=1, source_target_pairs={{0,1},{1,2},{2,3},{3,0},{4,5},{5,6},{6,7},{7,4},{8,9},{9,10},{10,1... | collective-permute-start | bytes 6152 | tf_op jit(solution)/shard_map/ppermute | solution.py:24
  200.7 3.5 %collective-permute-done.28 = f32[1,512]{1,0:T(1,128)S(1)} collective-permute-done((f32[1,512]{1,0:T(1,128)S(1)}, f32[1,512]{1,0:T(1,128)S(1)}, u32[]{:S(2)}, u32[]{:S(2)}) %collective-permute-start.28) | collective-permute-done | bytes 2080 | tf_op jit(solution)/shard_map/ppermute | solution.py:24
  204.2 1.9 normalized.1
  (140 shorter events, 45.2 us)
Async XLA Ops:
  6.5 94.4 %all-gather.5.cloned.1.call-start = ((), (), s32[]{:S(2)}) async-start(), calls=%async_computation.1 | async-start | bytes 3244032 | tf_op jit(solution)/shard_map/all_gather | solution.py:635
  9.0 154.4 %all-gather.3.cloned.1.call-start = ((), (), s32[]{:S(2)}) async-start(), calls=%async_computation | async-start | bytes 8912896 | tf_op jit(solution)/shard_map/all_gather | solution.py:642
  10.1 1.6 collective-permute-start
  11.8 1.6 collective-permute-start.6
  14.4 16.0 %collective-permute-start.1 = (bf16[256,1024]{1,0:T(8,128)(2,1)S(1)}, bf16[256,1024]{1,0:T(8,128)(2,1)S(1)}, u32[]{:S(2)}, u32[]{:S(2)}) collective-permute-start(bf16[256,1024]{1,0:T(8,128)(2,1)S(1)} %pad_maximum_fusion.4.refs_0_), channel_id=1, source_target_pairs={{0,8},{8,16},{16,24},{24,0},{1,9},{9,17},{17,25},{25,1},{2,10},{10... | collective-permute-start | bytes 1572872 | tf_op jit(solution)/shard_map/ppermute | solution.py:24
  16.1 14.8 %collective-permute-start.2 = (bf16[256,1024]{1,0:T(8,128)(2,1)S(1)}, bf16[256,1024]{1,0:T(8,128)(2,1)S(1)}, u32[]{:S(2)}, u32[]{:S(2)}) collective-permute-start(bf16[256,1024]{1,0:T(8,128)(2,1)S(1)} %pad_maximum_fusion.4.refs_0_), channel_id=1, source_target_pairs={{0,24},{8,0},{16,8},{24,16},{1,25},{9,1},{17,9},{25,17},{2,26},{10... | collective-permute-start | bytes 1572872 | tf_op jit(solution)/shard_map/ppermute | solution.py:24
  17.8 17.4 %collective-permute-start.3 = (bf16[256,1024]{1,0:T(8,128)(2,1)S(1)}, bf16[256,1024]{1,0:T(8,128)(2,1)S(1)}, u32[]{:S(2)}, u32[]{:S(2)}) collective-permute-start(bf16[256,1024]{1,0:T(8,128)(2,1)S(1)} %pad_maximum_fusion.4.refs_0_), channel_id=1, source_target_pairs={{0,32},{32,64},{64,96},{96,0},{1,33},{33,65},{65,97},{97,1},{2,34}... | collective-permute-start | bytes 1572872 | tf_op jit(solution)/shard_map/ppermute | solution.py:24
  19.7 15.5 %collective-permute-start.4 = (bf16[256,1024]{1,0:T(8,128)(2,1)S(1)}, bf16[256,1024]{1,0:T(8,128)(2,1)S(1)}, u32[]{:S(2)}, u32[]{:S(2)}) collective-permute-start(bf16[256,1024]{1,0:T(8,128)(2,1)S(1)} %pad_maximum_fusion.4.refs_0_), channel_id=1, source_target_pairs={{0,96},{32,0},{64,32},{96,64},{1,97},{33,1},{65,33},{97,65},{2,98}... | collective-permute-start | bytes 1572872 | tf_op jit(solution)/shard_map/ppermute | solution.py:24
  35.2 38.4 %collective-permute-start.5 = (bf16[512,4096]{1,0:T(8,128)(2,1)}, bf16[512,4096]{1,0:T(8,128)(2,1)}, u32[]{:S(2)}, u32[]{:S(2)}) collective-permute-start(bf16[512,4096]{1,0:T(8,128)(2,1)} %own_ref.3), channel_id=1, source_target_pairs={{0,4},{4,0},{1,5},{5,1},{2,6},{6,2},{3,7},{7,3},{8,12},{12,8},{9,1... | collective-permute-start | bytes 12582920 | tf_op jit(solution)/shard_map/ppermute | solution.py:19
  36.2 8.6 %collective-permute-start.7 = (bf16[16,4096]{1,0:T(8,128)(2,1)S(1)}, bf16[16,4096]{1,0:T(8,128)(2,1)}, u32[]{:S(2)}, u32[]{:S(2)}) collective-permute-start(bf16[16,4096]{1,0:T(8,128)(2,1)S(1)} %slice.34), channel_id=1, source_target_pairs={{4,8},{12,16},{20,24},{28,32},{36,40},{44,48},{52,56},{60,64},{68,... | collective-permute-start | bytes 393224 | tf_op jit(solution)/shard_map/ppermute | solution.py:645
  37.6 10.1 %collective-permute-start.8 = (bf16[16,4096]{1,0:T(8,128)(2,1)S(1)}, bf16[16,4096]{1,0:T(8,128)(2,1)}, u32[]{:S(2)}, u32[]{:S(2)}) collective-permute-start(bf16[16,4096]{1,0:T(8,128)(2,1)S(1)} %slice.34), channel_id=1, source_target_pairs={{4,12},{12,20},{20,28},{28,36},{36,44},{44,52},{52,60},{60,68},{68... | collective-permute-start | bytes 393224 | tf_op jit(solution)/shard_map/ppermute | solution.py:645
  39.8 25.4 %collective-permute-start.10 = (bf16[384,1024]{1,0:T(8,128)(2,1)}, bf16[384,1024]{1,0:T(8,128)(2,1)S(1)}, u32[]{:S(2)}, u32[]{:S(2)}) collective-permute-start(bf16[384,1024]{1,0:T(8,128)(2,1)} %pad_maximum_fusion.1), channel_id=1, source_target_pairs={{0,24},{8,0},{16,8},{24,16},{1,25},{9,1},{17,9},{25,17},{2,26},{10... | collective-permute-start | bytes 2359304 | tf_op jit(solution)/shard_map/ppermute | solution.py:24
  42.3 26.5 %collective-permute-start.9 = (bf16[384,1024]{1,0:T(8,128)(2,1)}, bf16[384,1024]{1,0:T(8,128)(2,1)}, u32[]{:S(2)}, u32[]{:S(2)}) collective-permute-start(bf16[384,1024]{1,0:T(8,128)(2,1)} %pad_maximum_fusion), channel_id=1, source_target_pairs={{0,8},{8,16},{16,24},{24,0},{1,9},{9,17},{17,25},{25,1},{2,10},{10... | collective-permute-start | bytes 2359304 | tf_op jit(solution)/shard_map/ppermute | solution.py:24
  44.8 25.0 %collective-permute-start.12 = (bf16[384,1024]{1,0:T(8,128)(2,1)}, bf16[384,1024]{1,0:T(8,128)(2,1)}, u32[]{:S(2)}, u32[]{:S(2)}) collective-permute-start(bf16[384,1024]{1,0:T(8,128)(2,1)} %pad_maximum_fusion.3), channel_id=1, source_target_pairs={{0,96},{32,0},{64,32},{96,64},{1,97},{33,1},{65,33},{97,65},{2,98}... | collective-permute-start | bytes 2359304 | tf_op jit(solution)/shard_map/ppermute | solution.py:24
  47.6 23.2 %collective-permute-start.11 = (bf16[384,1024]{1,0:T(8,128)(2,1)}, bf16[384,1024]{1,0:T(8,128)(2,1)}, u32[]{:S(2)}, u32[]{:S(2)}) collective-permute-start(bf16[384,1024]{1,0:T(8,128)(2,1)} %pad_maximum_fusion.2), channel_id=1, source_target_pairs={{0,32},{32,64},{64,96},{96,0},{1,33},{33,65},{65,97},{97,1},{2,34}... | collective-permute-start | bytes 2359304 | tf_op jit(solution)/shard_map/ppermute | solution.py:24
  73.5 22.4 %collective-permute-start.13 = (bf16[256,1024]{1,0:T(8,128)(2,1)}, bf16[256,1024]{1,0:T(8,128)(2,1)S(1)}, u32[]{:S(2)}, u32[]{:S(2)}) collective-permute-start(bf16[256,1024]{1,0:T(8,128)(2,1)} %pad_maximum_fusion.7), channel_id=1, source_target_pairs={{0,8},{8,16},{16,24},{24,0},{1,9},{9,17},{17,25},{25,1},{2,10},{10... | collective-permute-start | bytes 1572872 | tf_op jit(solution)/shard_map/ppermute | solution.py:24
  73.8 43.9 %collective-permute-start.14 = (bf16[256,1024]{1,0:T(8,128)(2,1)}, bf16[256,1024]{1,0:T(8,128)(2,1)}, u32[]{:S(2)}, u32[]{:S(2)}) collective-permute-start(bf16[256,1024]{1,0:T(8,128)(2,1)} %pad_maximum_fusion.7), channel_id=1, source_target_pairs={{0,24},{8,0},{16,8},{24,16},{1,25},{9,1},{17,9},{25,17},{2,26},{10... | collective-permute-start | bytes 1572872 | tf_op jit(solution)/shard_map/ppermute | solution.py:24
  76.8 40.9 %collective-permute-start.15 = (bf16[256,1024]{1,0:T(8,128)(2,1)}, bf16[256,1024]{1,0:T(8,128)(2,1)}, u32[]{:S(2)}, u32[]{:S(2)}) collective-permute-start(bf16[256,1024]{1,0:T(8,128)(2,1)} %pad_maximum_fusion.6), channel_id=1, source_target_pairs={{0,32},{32,64},{64,96},{96,0},{1,33},{33,65},{65,97},{97,1},{2,34}... | collective-permute-start | bytes 1572872 | tf_op jit(solution)/shard_map/ppermute | solution.py:24
  78.9 17.7 %collective-permute-start.16 = (bf16[256,1024]{1,0:T(8,128)(2,1)}, bf16[256,1024]{1,0:T(8,128)(2,1)S(1)}, u32[]{:S(2)}, u32[]{:S(2)}) collective-permute-start(bf16[256,1024]{1,0:T(8,128)(2,1)} %pad_maximum_fusion.6), channel_id=1, source_target_pairs={{0,96},{32,0},{64,32},{96,64},{1,97},{33,1},{65,33},{97,65},{2,98}... | collective-permute-start | bytes 1572872 | tf_op jit(solution)/shard_map/ppermute | solution.py:24
  97.4 20.3 %collective-permute-start.17 = (bf16[128,1024]{1,0:T(8,128)(2,1)S(1)}, bf16[128,1024]{1,0:T(8,128)(2,1)S(1)}, u32[]{:S(2)}, u32[]{:S(2)}) collective-permute-start(bf16[128,1024]{1,0:T(8,128)(2,1)S(1)} %slice.53), channel_id=1, source_target_pairs={{0,8},{8,16},{16,24},{24,0},{1,9},{9,17},{17,25},{25,1},{2,10},{10... | collective-permute-start | bytes 786440 | tf_op jit(solution)/shard_map/ppermute | solution.py:24
  97.9 19.8 %collective-permute-start.18 = (bf16[128,1024]{1,0:T(8,128)(2,1)S(1)}, bf16[128,1024]{1,0:T(8,128)(2,1)S(1)}, u32[]{:S(2)}, u32[]{:S(2)}) collective-permute-start(bf16[128,1024]{1,0:T(8,128)(2,1)S(1)} %slice.54), channel_id=1, source_target_pairs={{0,96},{32,0},{64,32},{96,64},{1,97},{33,1},{65,33},{97,65},{2,98}... | collective-permute-start | bytes 786440 | tf_op jit(solution)/shard_map/ppermute | solution.py:24
  131.8 15.4 %collective-permute-start.19 = (bf16[144,1024]{1,0:T(8,128)(2,1)S(1)}, bf16[144,1024]{1,0:T(8,128)(2,1)S(1)}, u32[]{:S(2)}, u32[]{:S(2)}) collective-permute-start(bf16[144,1024]{1,0:T(8,128)(2,1)S(1)} %get-tuple-element.46.refs_0_), channel_id=1, source_target_pairs={{0,8},{8,16},{16,24},{24,0},{1,9},{9,17},{17,25},{25,1},{2,10},{10... | collective-permute-start | bytes 884744 | tf_op jit(solution)/shard_map/ppermute | solution.py:24
  133.1 20.0 %collective-permute-start.20 = (bf16[144,1024]{1,0:T(8,128)(2,1)S(1)}, bf16[144,1024]{1,0:T(8,128)(2,1)S(1)}, u32[]{:S(2)}, u32[]{:S(2)}) collective-permute-start(bf16[144,1024]{1,0:T(8,128)(2,1)S(1)} %get-tuple-element.46.refs_0_), channel_id=1, source_target_pairs={{0,16},{8,24},{16,0},{24,8},{1,17},{9,25},{17,1},{25,9},{2,18},{10... | collective-permute-start | bytes 884744 | tf_op jit(solution)/shard_map/ppermute | solution.py:24
  135.5 17.6 %collective-permute-start.21 = (bf16[144,1024]{1,0:T(8,128)(2,1)S(1)}, bf16[144,1024]{1,0:T(8,128)(2,1)S(1)}, u32[]{:S(2)}, u32[]{:S(2)}) collective-permute-start(bf16[144,1024]{1,0:T(8,128)(2,1)S(1)} %get-tuple-element.46.refs_0_), channel_id=1, source_target_pairs={{0,24},{8,0},{16,8},{24,16},{1,25},{9,1},{17,9},{25,17},{2,26},{10... | collective-permute-start | bytes 884744 | tf_op jit(solution)/shard_map/ppermute | solution.py:24
  154.6 26.6 %collective-permute-start.22 = (bf16[144,1024]{1,0:T(8,128)(2,1)S(1)}, bf16[144,1024]{1,0:T(8,128)(2,1)S(1)}, u32[]{:S(2)}, u32[]{:S(2)}) collective-permute-start(bf16[144,1024]{1,0:T(8,128)(2,1)S(1)} %get-tuple-element.49), channel_id=1, source_target_pairs={{0,96},{1,97},{2,98},{3,99},{4,100},{5,101},{6,102},{7,103},{8,104... | collective-permute-start | bytes 884744 | tf_op jit(solution)/shard_map/ppermute | solution.py:566
  159.1 22.2 %collective-permute-start.23 = (bf16[144,1024]{1,0:T(8,128)(2,1)S(1)}, bf16[144,1024]{1,0:T(8,128)(2,1)S(1)}, u32[]{:S(2)}, u32[]{:S(2)}) collective-permute-start(bf16[144,1024]{1,0:T(8,128)(2,1)S(1)} %get-tuple-element.49), channel_id=1, source_target_pairs={{0,64},{32,96},{1,65},{33,97},{2,66},{34,98},{3,67},{35,99},{4,68}... | collective-permute-start | bytes 884744 | tf_op jit(solution)/shard_map/ppermute | solution.py:566
  160.4 21.6 %collective-permute-start.24 = (bf16[144,1024]{1,0:T(8,128)(2,1)S(1)}, bf16[144,1024]{1,0:T(8,128)(2,1)S(1)}, u32[]{:S(2)}, u32[]{:S(2)}) collective-permute-start(bf16[144,1024]{1,0:T(8,128)(2,1)S(1)} %get-tuple-element.49), channel_id=1, source_target_pairs={{0,32},{32,64},{64,96},{1,33},{33,65},{65,97},{2,34},{34,66},{66,9... | collective-permute-start | bytes 884744 | tf_op jit(solution)/shard_map/ppermute | solution.py:566
  193.6 10.7 %collective-permute-start.25 = (bf16[512,1024]{1,0:T(8,128)(2,1)}, bf16[512,1024]{1,0:T(8,128)(2,1)S(1)}, u32[]{:S(2)}, u32[]{:S(2)}) collective-permute-start(bf16[512,1024]{1,0:T(8,128)(2,1)} %get-tuple-element.51), channel_id=1, source_target_pairs={{0,4},{4,0},{1,5},{5,1},{2,6},{6,2},{3,7},{7,3},{8,12},{12,8},{9,1... | collective-permute-start | bytes 3145736 | tf_op jit(solution)/shard_map/ppermute | solution.py:19
  193.6 2.3 %collective-permute-start.26 = (f32[1,1024]{1,0:T(1,128)S(1)}, f32[1,1024]{1,0:T(1,128)S(1)}, u32[]{:S(2)}, u32[]{:S(2)}) collective-permute-start(f32[1,1024]{1,0:T(1,128)S(1)} %get-tuple-element.52), channel_id=1, source_target_pairs={{0,4},{4,0},{1,5},{5,1},{2,6},{6,2},{3,7},{7,3},{8,12},{12,8},{9,1... | collective-permute-start | bytes 12296 | tf_op jit(solution)/shard_map/ppermute | solution.py:19
  195.9 4.8 %collective-permute-start.29 = (f32[1,512]{1,0:T(1,128)S(1)}, f32[1,512]{1,0:T(1,128)S(1)}, u32[]{:S(2)}, u32[]{:S(2)}) collective-permute-start(f32[1,512]{1,0:T(1,128)S(1)} %dynamic-slice_add_fusion), channel_id=1, source_target_pairs={{0,3},{1,0},{2,1},{3,2},{4,7},{5,4},{6,5},{7,6},{8,11},{9,8},{10,9... | collective-permute-start | bytes 6152 | tf_op jit(solution)/shard_map/ppermute | solution.py:24
  196.7 3.9 %collective-permute-start.27 = (f32[1,512]{1,0:T(1,128)S(1)}, f32[1,512]{1,0:T(1,128)S(1)}, u32[]{:S(2)}, u32[]{:S(2)}) collective-permute-start(f32[1,512]{1,0:T(1,128)S(1)} %dynamic-slice_add_fusion), channel_id=1, source_target_pairs={{0,1},{1,2},{2,3},{3,0},{4,5},{5,6},{6,7},{7,4},{8,9},{9,10},{10,1... | collective-permute-start | bytes 6152 | tf_op jit(solution)/shard_map/ppermute | solution.py:24
  199.1 5.1 %collective-permute-start.28 = (f32[1,512]{1,0:T(1,128)S(1)}, f32[1,512]{1,0:T(1,128)S(1)}, u32[]{:S(2)}, u32[]{:S(2)}) collective-permute-start(f32[1,512]{1,0:T(1,128)S(1)} %dynamic-slice_add_fusion), channel_id=1, source_target_pairs={{0,2},{1,3},{2,0},{3,1},{4,6},{5,7},{6,4},{7,5},{8,10},{9,11},{10,... | collective-permute-start | bytes 6152 | tf_op jit(solution)/shard_map/ppermute | solution.py:24
  (31 other events, 215.0 us)
Sparse Core Ops, SparseCore 0:
  9.6 51.0 all-gather.4
  62.8 82.8 all-gather.2

commit v7 on v6

--- a/solution.py
+++ b/solution.py
@@ -150,23 +150,27 @@
 def states_kernel(
     sources, done, count, place_ref, own_ref, other_ref, before_ref, *refs
 ):
-    weights = refs[:-12]
+    weights = refs[:-13]
     (
         sum_ref, sum_before_ref, bcc_ref, weights_in_ref, decays_ref, conv_ref,
         xc_ref, entering_ref, final_ref,
-        state, x_in, tail,
-    ) = refs[-12:]
+        state, x_in, tail, wide,
+    ) = refs[-13:]
     block = pl.program_id(0)
     width = x_in.shape[1]
     is_own = block // 2 == place_ref[0]
 
     def product(ref):
         columns = block_columns(ref, place_ref, done, count)
-        return jnp.dot(columns, stacked(sources, weights), preferred_element_type=F32)
+        return jnp.dot(columns, wide[...], preferred_element_type=F32)
 
     @pl.when(block == 0)
     def _():
         state[...] = jnp.zeros_like(state)
+        row = 0
+        for ref, first, size in sources:
+            wide[row : row + size, :] = weights[ref][first : first + size, :]
+            row += size
         tail[...] = (sum_before_ref[...] + product(before_ref)).astype(BF16).astype(F32)
 
     @pl.when(is_own)
@@ -353,7 +357,7 @@
     return pl.BlockSpec((GROUP, width), lambda i: (i, 0))
 
 
-def params(flops, megabytes, vmem=32):
+def params(flops, megabytes, vmem=60):
     return dict(
         compiler_params=pltpu.CompilerParams(vmem_limit_bytes=vmem * 2**20),
         cost_estimate=pl.CostEstimate(
@@ -451,11 +455,12 @@
             scratch_shapes=[
                 pltpu.VMEM((LANES, width), F32), pltpu.VMEM((GROUP, width), F32),
                 pltpu.VMEM((HALO, width), F32),
+                pltpu.VMEM((sum(size for _, _, size in sources), width), BF16),
             ],
         ),
         out_shape=outs,
         name="states",
-        **params(8e9, 16),
+        **params(11e9, 18, 48),
     )(place, *slabs, *weights, *sums, bcc, weights_in, decays, conv_x)
 
 
@@ -473,7 +478,7 @@
         out_specs=rows_of(width),
         out_shape=jax.ShapeDtypeStruct((rows, width), BF16),
         scratch_shapes=[pltpu.VMEM((GROUP, width), F32)],
-        compiler_params=pltpu.CompilerParams(vmem_limit_bytes=32 * 2**20),
+        compiler_params=pltpu.CompilerParams(vmem_limit_bytes=60 * 2**20),
         cost_estimate=pl.CostEstimate(flops=10**10, bytes_accessed=10 * 2**20, transcendentals=4 * 2**20),
         name="outputs",
     )(xc, bcc, cum, cum_t, step_t, entering, skip)
@@ -534,7 +539,7 @@
             out_specs=pl.BlockSpec((rows, width), lambda j, core: (0, j)),
         ),
         out_shape=jax.ShapeDtypeStruct((rows, 2 * width), BF16),
-        compiler_params=pltpu.CompilerParams(vmem_limit_bytes=32 * 2**20),
+        compiler_params=pltpu.CompilerParams(vmem_limit_bytes=60 * 2**20),
         cost_estimate=pl.CostEstimate(flops=10**7, bytes_accessed=4 * 2**20, transcendentals=0),
         name="normalized",
     )(core.astype(jnp.int32)[None], gated, other, mean_squares, gain)
@@ -573,32 +578,31 @@
     return lax.optimization_barrier((*values, *to))[: len(values)]
 
 
-def near_blocks(own):
+def travelling(own, after_first, before_third, before_last):
     block = own.shape[0]
     half = block // 2
     y_less, y_more = round_ring(own, "y", 1), round_ring(own, "y", -1)
     z_less, z_more = round_ring(own, "z", 1), round_ring(own, "z", -1)
+    after_first([own, y_less, y_more, z_less, z_more])
     join = lambda *parts: jnp.concatenate(parts, axis=0)
     from_y_less = round_ring(join(z_less, y_less[:half]), "y", 1)
     from_y_more = round_ring(join(z_more, y_more[half:]), "y", -1)
     from_z_less = round_ring(join(y_more, z_less[:half]), "z", 1)
     from_z_more = round_ring(join(y_less, z_more[half:]), "z", -1)
-    y_far = join(from_y_less[block:], from_y_more[block:])
-    z_far = join(from_z_less[block:], from_z_more[block:])
-    near = [own, y_less, y_more, z_less, z_more, from_y_less, from_y_more, from_z_less, from_z_more]
-    sources = [(i, 0, block) for i in range(9)] + [(i, block, half) for i in (5, 6, 7, 8)]
-    return near, sources, y_far, z_far
-
-
-def far_blocks(y_far, z_far, before_last):
-    block = y_far.shape[0]
-    half = block // 2
+    halves = tied((from_y_less, from_y_more, from_z_less, from_z_more), *before_third())
+    y_far = join(halves[0][block:], halves[1][block:])
+    z_far = join(halves[2][block:], halves[3][block:])
     far_y_less, far_y_more = round_ring(z_far, "y", 1), round_ring(z_far, "y", -1)
     far_z_less, far_z_more = round_ring(y_far, "z", 1), round_ring(y_far, "z", -1)
-    top, low = tied((far_y_less[:half], far_z_more[half:]), before_last)
-    far = [far_y_less, far_y_more, far_z_less, far_z_more, round_ring(top, "y", 1), round_ring(low, "z", -1)]
-    sources = [(i, 0, block) for i in range(4)] + [(4, 0, half), (5, 0, half)]
-    return far, sources
+    top, low = tied((far_y_less, far_z_more), *before_last(halves))
+    blocks = [
+        from_y_less, from_y_more, from_z_less, from_z_more,
+        far_y_less, far_y_more, far_z_less, far_z_more,
+        round_ring(top[:half], "y", 1), round_ring(low[half:], "z", -1),
+    ]
+    sources = [(i, 0, block) for i in range(4)] + [(i, block, half) for i in range(4)]
+    sources += [(i, 0, block) for i in range(4, 8)] + [(8, 0, half), (9, 0, half)]
+    return blocks, sources
 
 
 def block_order():
@@ -634,28 +638,36 @@
     )
     narrow = lax.all_gather(narrow, ("z", "y", "core"), axis=0, tiled=True)
     own_block = jnp.concatenate([mine(x_weight, 1), swap_cores(others(x_weight, 1))], axis=0)
-    near, near_sources, y_far, z_far = near_blocks(own_block)
     place = jnp.stack([core, *block_order()]).astype(jnp.int32)
-
-    (z_weight,) = tied((z_weight,), own_block)
-    z_block = in_core_order(core, mine(z_weight, 1), swap_cores(others(z_weight, 1)), 0)
-    z_whole = lax.all_gather(z_block, ("z", "y"), axis=0, tiled=True)
-    (tokens,) = tied((tokens,), *near[1:5])
-    chips = lax.axis_size("z") * lax.axis_size("y")
-    to_next = lambda target: lax.ppermute(
-        tokens[-HALO:], ("z", "y", "core"),
-        [(2 * i + 1, 2 * i + 2 + target) for i in range(chips - 1)],
-    )
-    slabs = (tokens, swap_cores(tokens), to_next(0) + to_next(1))
-
-    y_far, z_far = tied((y_far, z_far), *slabs[1:])
-    sums = first_products(place, slabs, near, near_sources, 11)
-    far, far_sources = far_blocks(y_far, z_far, sums[0])
-    bcc, cum, cum_slab, cum_t, step_t, weights_in, decays = prepared(
-        place, slabs, narrow, conv_bc, per_lane(dt_bias), per_lane(decay_rate), heads
-    )
+    slabs, sums, early, z_blocks, z_wholes = [], [], [], [], []
+
+    def after_first(blocks):
+        rows, z_rows = tied((tokens, z_weight), *blocks[1:])
+        chips = lax.axis_size("z") * lax.axis_size("y")
+        to_next = lambda target: lax.ppermute(
+            rows[-HALO:], ("z", "y", "core"),
+            [(2 * i + 1, 2 * i + 2 + target) for i in range(chips - 1)],
+        )
+        slabs.extend((rows, swap_cores(rows), to_next(0) + to_next(1)))
+        z_blocks.append(
+            in_core_order(core, mine(z_rows, 1), swap_cores(others(z_rows, 1)), 0)
+        )
+        sources = [(i, 0, blocks[0].shape[0]) for i in range(5)]
+        sums.extend(first_products(place, slabs, blocks, sources, 5))
+
+    def before_last(second):
+        (z_block,) = tied((z_blocks[0],), *second)
+        z_wholes.append(lax.all_gather(z_block, ("z", "y"), axis=0, tiled=True))
+        early.extend(
+            prepared(place, slabs, narrow, conv_bc, per_lane(dt_bias), per_lane(decay_rate), heads)
+        )
+        return early[:1]
+
+    blocks, sources = travelling(own_block, after_first, lambda: sums[:1], before_last)
+    bcc, cum, cum_slab, cum_t, step_t, weights_in, decays = early
+    (z_whole,) = z_wholes
     xc, entering, final = local_states(
-        place, slabs, far, far_sources, 11, 5, sums, bcc, weights_in, decays, mine(conv_x, 1)
+        place, slabs, blocks, sources, 5, 11, sums, bcc, weights_in, decays, mine(conv_x, 1)
     )
     before, before_decay, earlier = earlier_states(final)
     skip_lanes = jnp.repeat(mine(skip, 0), HEAD)[None, :]

time: 214 us -> 219 us (1.023)
  Pallas kernels: 65.3 us -> 83.1 us
  local copies, waits for them, and re-layouts: 29.5 us -> 15.2 us
    unnamed x61 -> x53, local copies, waits for them, and re-layouts: 23.7 us -> 6.55 us
    pallas_call x1, Pallas kernels: 14 us -> 20 us  [local_states(): pl.pallas_call(functools.partial(states_kernel, sources, done, count), gr...]
    ppermute x5, starting transfers between devices: 0.81 us -> 4.04 us  [swap_cores(): return lax.ppermute(a, 'core', [(0, 1), (1, 0)])]
    ppermute x20, starting transfers between devices: 31.1 us -> 28 us  [round_ring(): lax.ppermute(a, axis, [(i, (i + distance) % size) for i in range(size)])]
    pallas_call x1, Pallas kernels: 11.9 us -> 14.5 us  [prepared(): pl.pallas_call(prepare_kernel, grid_spec=pltpu.PrefetchScalarGridSpec(num...]
    ppermute x20, waiting for transfers between devices: 47.3 us -> 49.9 us  [round_ring(): lax.ppermute(a, axis, [(i, (i + distance) % size) for i in range(size)])]
    pallas_call x1, Pallas kernels: 6.85 us -> 9.04 us  [gate_outputs(): pl.pallas_call(gate_kernel, grid_spec=pltpu.PrefetchScalarGridSpec(num_sc...]
    slice x12 -> x13, local copies, waits for them, and re-layouts: 4.19 us -> 5.26 us  [the longest x2 1.95 us: travelling(): z_far = join(halves[2][block:], halves[3][block:])]
  transfers between devices with their start and end apart: 32 -> 32, of which waited for: 13 -> 17; matrix products, arithmetic and copies ran while one was open for 6% -> 7% of each run, Pallas kernels for 27% -> 32%
where the time goes in v7:
time: 219 us; the launch traced here: 218 us
  Pallas kernels  83.1 us (38%)
  waiting for transfers between devices  53.8 us (25%)
  starting transfers between devices  42.4 us (19%)
  local copies, waits for them, and re-layouts  15.2 us (7%)
  between operations  13.8 us (6%)
  other arithmetic  9.91 us (5%)
    ppermute x20, waiting for transfers between devices, round_ring(): lax.ppermute(a, axis, [(i, (i + distance) % size) for i in range(size)])  49.9 us
    ppermute x20, starting transfers between devices, round_ring(): lax.ppermute(a, axis, [(i, (i + distance) % size) for i in range(size)])  28 us
    pallas_call x1, Pallas kernels, local_states(): pl.pallas_call(functools.partial(states_kernel, sources, done, count), gr...  20 us
    pallas_call x1, Pallas kernels, prepared(): pl.pallas_call(prepare_kernel, grid_spec=pltpu.PrefetchScalarGridSpec(num...  14.5 us
    pallas_call x1, Pallas kernels, project_gate(): pl.pallas_call(z_kernel, grid_spec=pltpu.PrefetchScalarGridSpec(num_scala...  14.4 us
    pallas_call x1, Pallas kernels, first_products(): pl.pallas_call(functools.partial(first_kernel, sources, count), grid_spec...  10.2 us
    pallas_call x1, Pallas kernels, gate_outputs(): pl.pallas_call(gate_kernel, grid_spec=pltpu.PrefetchScalarGridSpec(num_sc...  9.04 us
    ppermute x3, starting transfers between devices, earlier_states(): lax.ppermute(total, 'z', [(i, i + distance) for i in range(rows - distanc...  9 us
  transfers between devices with their start and end apart: 32, of which 17 were waited for; matrix products, arithmetic and copies ran while one was open for 7% of the time, Pallas kernels for 32%

profile of v7, /device:TPU:6, one launch (start us, length us, event | category | flops | bytes accessed | tf_op | source)
XLA Modules:
  0.0 218.2 jit_solution(11147085165762576454)
XLA Ops:
  7.4 1.5 maximum_maximum_fusion
  10.2 1.5 collective-permute-done
  11.8 1.6 collective-permute-start.1
  13.4 1.7 collective-permute-start.2
  15.1 1.9 collective-permute-start.3
  17.0 2.1 collective-permute-start.4
  19.1 8.5 %collective-permute-done.1.refs_1_ = bf16[256,1024]{1,0:T(8,128)(2,1)S(1)} collective-permute-done((bf16[256,1024]{1,0:T(8,128)(2,1)S(1)}, bf16[256,1024]{1,0:T(8,128)(2,1)S(1)}, u32[]{:S(2)}, u32[]{:S(2)}) %collective-permute-start.1) | collective-permute-done | bytes 524320 | tf_op jit(solution)/shard_map/ppermute | solution.py:24
  27.7 4.3 %collective-permute-done.3.refs_3_ = bf16[256,1024]{1,0:T(8,128)(2,1)S(1)} collective-permute-done((bf16[256,1024]{1,0:T(8,128)(2,1)S(1)}, bf16[256,1024]{1,0:T(8,128)(2,1)S(1)}, u32[]{:S(2)}, u32[]{:S(2)}) %collective-permute-start.3) | collective-permute-done | bytes 524320 | tf_op jit(solution)/shard_map/ppermute | solution.py:24
  36.1 3.4 %collective-permute-start.10 = (bf16[384,1024]{1,0:T(8,128)(2,1)}, bf16[384,1024]{1,0:T(8,128)(2,1)}, u32[]{:S(2)}, u32[]{:S(2)}) collective-permute-start(bf16[384,1024]{1,0:T(8,128)(2,1)} %pad_maximum_fusion.3), channel_id=1, source_target_pairs={{0,96},{32,0},{64,32},{96,64},{1,97},{33,1},{65,33},{97,65},{2,98}... | collective-permute-start | bytes 2359304 | tf_op jit(solution)/shard_map/ppermute | solution.py:24
  39.6 3.4 %collective-permute-start.6 = (bf16[128,1024]{1,0:T(8,128)(2,1)S(1)}, bf16[128,1024]{1,0:T(8,128)(2,1)S(1)}, u32[]{:S(2)}, u32[]{:S(2)}) collective-permute-start(bf16[128,1024]{1,0:T(8,128)(2,1)S(1)} %constant_dynamic-slice_fusion.1), channel_id=1, source_target_pairs={{0,4},{4,0},{1,5},{5,1},{2,6},{6,2},{3,7},{7,3},{8,12},{12,8},{9,1... | collective-permute-start | bytes 786440 | tf_op jit(solution)/shard_map/ppermute | solution.py:19
  48.0 1.9 collective-permute-start.8
  51.6 10.2 %first_products.1 = (f32[1024,1024]{1,0:T(8,128)}, f32[16,1024]{1,0:T(8,128)}) custom-call(s32[17]{0:T(128)} %stack.68.place_ref, bf16[512,4096]{1,0:T(8,128)(2,1)} %own_ref.3, bf16[512,4096]{1,0:T(8,128)(2,1)} %collective-permute-done.5.other_ref, bf16[16,4096]{1,0:T(8,128)(2,1)} %add.201.before_ref, bf16[256,1024]{1,0:T(8,128)(2,1)} %copy-done.16, ...), custom_call_target="tpu_custom_call" | custom-call | flops 6000000000 | bytes 18874368 | tf_op jit(solution)/shard_map/first_products/pallas_call | solution.py:416
  62.4 9.0 %collective-permute-done.7.refs_0_ = bf16[384,1024]{1,0:T(8,128)(2,1)S(1)} collective-permute-done((bf16[384,1024]{1,0:T(8,128)(2,1)}, bf16[384,1024]{1,0:T(8,128)(2,1)S(1)}, u32[]{:S(2)}, u32[]{:S(2)}) %collective-permute-start.7) | collective-permute-done | bytes 786464 | tf_op jit(solution)/shard_map/ppermute | solution.py:24
  79.2 3.0 %collective-permute-start.14 = (bf16[256,1024]{1,0:T(8,128)(2,1)}, bf16[256,1024]{1,0:T(8,128)(2,1)}, u32[]{:S(2)}, u32[]{:S(2)}) collective-permute-start(bf16[256,1024]{1,0:T(8,128)(2,1)} %pad_maximum_fusion.6), channel_id=1, source_target_pairs={{0,24},{8,0},{16,8},{24,16},{1,25},{9,1},{17,9},{25,17},{2,26},{10... | collective-permute-start | bytes 1572872 | tf_op jit(solution)/shard_map/ppermute | solution.py:24
  82.2 14.5 %prepared.1 = (bf16[1024,256]{1,0:T(8,128)(2,1)}, f32[1024,128]{1,0:T(8,128)}, f32[1024,128]{1,0:T(8,128)}, f32[16,1024]{1,0:T(8,128)}, f32[16,1024]{1,0:T(8,128...) custom-call(s32[17]{0:T(128)} %stack.68.place_ref, bf16[512,4096]{1,0:T(8,128)(2,1)} %own_ref.3, ...), custom_call_target="tpu_custom_call" | custom-call | flops 4000000000 | bytes 14680064 | tf_op jit(solution)/shard_map/prepared/pallas_call | solution.py:393
  96.7 1.6 collective-permute-done.13.refs_4_
  101.0 5.9 %collective-permute-done.17.refs_8_ = bf16[128,1024]{1,0:T(8,128)(2,1)} collective-permute-done((bf16[128,1024]{1,0:T(8,128)(2,1)}, bf16[128,1024]{1,0:T(8,128)(2,1)}, u32[]{:S(2)}, u32[]{:S(2)}) %collective-permute-start.17) | collective-permute-done | bytes 262176 | tf_op jit(solution)/shard_map/ppermute | solution.py:24
  110.1 20.0 %states.1 = (bf16[1024,1024]{1,0:T(8,128)(2,1)}, bf16[4,128,1024]{2,1,0:T(8,128)(2,1)}, bf16[144,1024]{1,0:T(8,128)(2,1)S(1)}) custom-call(s32[17]{0:T(128)S(1)} %copy-done.4, bf16[512,4096]{1,0:T(8,128)(2,1)} %own_ref.3, bf16[512,4096]{1,0:T(8,128)(2,1)} %collective-permute-done.5.other_ref, bf16[16,4096]{1,0:T(8,128)(2,1)S(1)} %copy-done.3, ...), custom_call_target="tpu_custom_call" | custom-call | flops 11000000512 | bytes 18874368 | tf_op jit(solution)/shard_map/states/pallas_call | solution.py:439
  131.0 3.9 %collective-permute-start.20 = (bf16[144,1024]{1,0:T(8,128)(2,1)S(1)}, bf16[144,1024]{1,0:T(8,128)(2,1)S(1)}, u32[]{:S(2)}, u32[]{:S(2)}) collective-permute-start(bf16[144,1024]{1,0:T(8,128)(2,1)S(1)} %get-tuple-element.52.refs_0_), channel_id=1, source_target_pairs={{0,16},{8,24},{16,0},{24,8},{1,17},{9,25},{17,1},{25,9},{2,18},{10... | collective-permute-start | bytes 884744 | tf_op jit(solution)/shard_map/ppermute | solution.py:24
  136.1 8.9 %outputs.1.local_ref = bf16[1024,1024]{1,0:T(8,128)(2,1)} custom-call(bf16[1024,1024]{1,0:T(8,128)(2,1)} %get-tuple-element.46.xc_ref, bf16[1024,256]{1,0:T(8,128)(2,1)} %get-tuple-element.40.refs_12_.bcc_ref, f32[1024,128]{1,0:T(8,128)} %get-tuple-element.47.cum_ref, f32[16,1024]{1,0:T(8,128)} %get-tuple-element.48.cum_t_ref, ...), custom_call_target="tpu_custom_call" | custom-call | flops 10000000000 | bytes 10485760 | tf_op jit(solution)/shard_map/outputs/pallas_call | solution.py:471
  144.9 2.6 %collective-permute-done.19.refs_1_ = bf16[144,1024]{1,0:T(8,128)(2,1)S(1)} collective-permute-done((bf16[144,1024]{1,0:T(8,128)(2,1)S(1)}, bf16[144,1024]{1,0:T(8,128)(2,1)S(1)}, u32[]{:S(2)}, u32[]{:S(2)}) %collective-permute-start.19) | collective-permute-done | bytes 294944 | tf_op jit(solution)/shard_map/ppermute | solution.py:24
  147.6 10.8 %collective-permute-done.20.refs_2_ = bf16[144,1024]{1,0:T(8,128)(2,1)S(1)} collective-permute-done((bf16[144,1024]{1,0:T(8,128)(2,1)S(1)}, bf16[144,1024]{1,0:T(8,128)(2,1)S(1)}, u32[]{:S(2)}, u32[]{:S(2)}) %collective-permute-start.20) | collective-permute-done | bytes 294944 | tf_op jit(solution)/shard_map/ppermute | solution.py:24
  159.2 2.6 %row_states.1 = (bf16[144,1024]{1,0:T(8,128)(2,1)}, f32[128,1024]{1,0:T(8,128)}, f32[8,1024]{1,0:T(8,128)}) custom-call(s32[1]{0:T(128)} %bitcast.19.place_ref, bf16[144,1024]{1,0:T(8,128)(2,1)} %copy-done.2, bf16[144,1024]{1,0:T(8,128)(2,1)} %copy-done.17, bf16[144,1024]{1,0:T(8,128)(2,1)} %copy-done.18, bf16[144,1024]{1,0:T(8,128)(2,1)} %copy-done.19), custom_call_target="tpu_custom_call" | custom-call | flops 10000000 | bytes 2097152 | tf_op jit(solution)/shard_map/row_states/pallas_call | solution.py:557
  161.8 4.7 %collective-permute-start.22 = (bf16[144,1024]{1,0:T(8,128)(2,1)}, bf16[144,1024]{1,0:T(8,128)(2,1)S(1)}, u32[]{:S(2)}, u32[]{:S(2)}) collective-permute-start(bf16[144,1024]{1,0:T(8,128)(2,1)} %get-tuple-element.55), channel_id=1, source_target_pairs={{0,96},{1,97},{2,98},{3,99},{4,100},{5,101},{6,102},{7,103},{8,104... | collective-permute-start | bytes 884744 | tf_op jit(solution)/shard_map/ppermute | solution.py:571
  167.8 3.0 %collective-permute-start.24 = (bf16[144,1024]{1,0:T(8,128)(2,1)}, bf16[144,1024]{1,0:T(8,128)(2,1)S(1)}, u32[]{:S(2)}, u32[]{:S(2)}) collective-permute-start(bf16[144,1024]{1,0:T(8,128)(2,1)} %get-tuple-element.55), channel_id=1, source_target_pairs={{0,32},{32,64},{64,96},{1,33},{33,65},{65,97},{2,34},{34,66},{66,9... | collective-permute-start | bytes 884744 | tf_op jit(solution)/shard_map/ppermute | solution.py:571
  170.8 14.4 %project_gate.1.gate_ref = bf16[1024,1024]{1,0:T(8,128)(2,1)} custom-call(s32[17]{0:T(128)} %stack.68.place_ref, bf16[512,4096]{1,0:T(8,128)(2,1)} %own_ref.3, bf16[512,4096]{1,0:T(8,128)(2,1)} %collective-permute-done.5.other_ref, bf16[4096,1024]{1,0:T(8,128)(2,1)} %all-gather.3.cloned.1.call-done.weight_ref), custom_call_target="tpu_custom_call" | custom-call | flops 8999999488 | bytes 20971520 | tf_op jit(solution)/shard_map/project_gate/pallas_call | solution.py:492
  186.2 9.0 %gate.1 = (bf16[512,1024]{1,0:T(8,128)(2,1)}, bf16[512,1024]{1,0:T(8,128)(2,1)}, f32[1,1024]{1,0:T(1,128)}) custom-call(s32[1]{0:T(128)} %bitcast.core_ref, bf16[1024,1024]{1,0:T(8,128)(2,1)} %project_gate.1.gate_ref, bf16[1024,1024]{1,0:T(8,128)(2,1)} %outputs.1.local_ref, bf16[1024,256]{1,0:T(8,128)(2,1)} %get-tuple-element.40.refs_12_.bcc_ref, ...), custom_call_target="tpu_custom_call" | custom-call | flops 1000000000 | bytes 10485760 | tf_op jit(solution)/shard_map/gate/pallas_call | solution.py:510
  195.7 2.4 %collective-permute-done.26 = f32[1,1024]{1,0:T(1,128)S(1)} collective-permute-done((f32[1,1024]{1,0:T(1,128)}, f32[1,1024]{1,0:T(1,128)S(1)}, u32[]{:S(2)}, u32[]{:S(2)}) %collective-permute-start.26) | collective-permute-done | bytes 4128 | tf_op jit(solution)/shard_map/ppermute | solution.py:19
  199.2 2.4 %collective-permute-start.28 = (f32[1,512]{1,0:T(1,128)S(1)}, f32[1,512]{1,0:T(1,128)S(1)}, u32[]{:S(2)}, u32[]{:S(2)}) collective-permute-start(f32[1,512]{1,0:T(1,128)S(1)} %dynamic-slice_add_fusion), channel_id=1, source_target_pairs={{0,2},{1,3},{2,0},{3,1},{4,6},{5,7},{6,4},{7,5},{8,10},{9,11},{10,... | collective-permute-start | bytes 6152 | tf_op jit(solution)/shard_map/ppermute | solution.py:24
  202.4 1.9 collective-permute-done.28
  204.3 2.1 collective-permute-done.29
  207.9 3.5 %normalized.1 = bf16[512,2048]{1,0:T(8,128)(2,1)} custom-call(s32[1]{0:T(128)} %bitcast.core_ref, bf16[512,1024]{1,0:T(8,128)(2,1)} %get-tuple-element.56.mine_ref, bf16[512,1024]{1,0:T(8,128)(2,1)} %copy-done.13, f32[1,512]{1,0:T(1,128)} %add_multiply_fusion.squares_ref, f32[1,2048]{1,0:T(1,128)} %bitcast.23), custom_call_target="tpu_custom_call" | custom-call | flops 10000000 | bytes 4194304 | tf_op jit(solution)/shard_map/normalized/pallas_call | solution.py:528
  (133 shorter events, 36.3 us)
Async XLA Ops:
  6.5 75.6 %all-gather.5.cloned.1.call-start = ((), (), s32[]{:S(2)}) async-start(), calls=%async_computation.1 | async-start | bytes 3244032 | tf_op jit(solution)/shard_map/all_gather | solution.py:639
  9.0 161.9 %all-gather.3.cloned.1.call-start = ((), (), s32[]{:S(2)}) async-start(), calls=%async_computation | async-start | bytes 8912896 | tf_op jit(solution)/shard_map/all_gather | solution.py:660
  10.1 1.6 collective-permute-start
  11.8 15.8 %collective-permute-start.1 = (bf16[256,1024]{1,0:T(8,128)(2,1)S(1)}, bf16[256,1024]{1,0:T(8,128)(2,1)S(1)}, u32[]{:S(2)}, u32[]{:S(2)}) collective-permute-start(bf16[256,1024]{1,0:T(8,128)(2,1)S(1)} %pad_maximum_fusion.4.refs_0_), channel_id=1, source_target_pairs={{0,8},{8,16},{16,24},{24,0},{1,9},{9,17},{17,25},{25,1},{2,10},{10... | collective-permute-start | bytes 1572872 | tf_op jit(solution)/shard_map/ppermute | solution.py:24
  13.4 14.3 %collective-permute-start.2 = (bf16[256,1024]{1,0:T(8,128)(2,1)S(1)}, bf16[256,1024]{1,0:T(8,128)(2,1)S(1)}, u32[]{:S(2)}, u32[]{:S(2)}) collective-permute-start(bf16[256,1024]{1,0:T(8,128)(2,1)S(1)} %pad_maximum_fusion.4.refs_0_), channel_id=1, source_target_pairs={{0,24},{8,0},{16,8},{24,16},{1,25},{9,1},{17,9},{25,17},{2,26},{10... | collective-permute-start | bytes 1572872 | tf_op jit(solution)/shard_map/ppermute | solution.py:24
  15.1 16.9 %collective-permute-start.3 = (bf16[256,1024]{1,0:T(8,128)(2,1)S(1)}, bf16[256,1024]{1,0:T(8,128)(2,1)S(1)}, u32[]{:S(2)}, u32[]{:S(2)}) collective-permute-start(bf16[256,1024]{1,0:T(8,128)(2,1)S(1)} %pad_maximum_fusion.4.refs_0_), channel_id=1, source_target_pairs={{0,32},{32,64},{64,96},{96,0},{1,33},{33,65},{65,97},{97,1},{2,34}... | collective-permute-start | bytes 1572872 | tf_op jit(solution)/shard_map/ppermute | solution.py:24
  17.0 15.0 %collective-permute-start.4 = (bf16[256,1024]{1,0:T(8,128)(2,1)S(1)}, bf16[256,1024]{1,0:T(8,128)(2,1)S(1)}, u32[]{:S(2)}, u32[]{:S(2)}) collective-permute-start(bf16[256,1024]{1,0:T(8,128)(2,1)S(1)} %pad_maximum_fusion.4.refs_0_), channel_id=1, source_target_pairs={{0,96},{32,0},{64,32},{96,64},{1,97},{33,1},{65,33},{97,65},{2,98}... | collective-permute-start | bytes 1572872 | tf_op jit(solution)/shard_map/ppermute | solution.py:24
  32.0 19.6 %collective-permute-start.5 = (bf16[512,4096]{1,0:T(8,128)(2,1)}, bf16[512,4096]{1,0:T(8,128)(2,1)}, u32[]{:S(2)}, u32[]{:S(2)}) collective-permute-start(bf16[512,4096]{1,0:T(8,128)(2,1)} %own_ref.3), channel_id=1, source_target_pairs={{0,4},{4,0},{1,5},{5,1},{2,6},{6,2},{3,7},{7,3},{8,12},{12,8},{9,1... | collective-permute-start | bytes 12582920 | tf_op jit(solution)/shard_map/ppermute | solution.py:19
  33.8 13.0 %collective-permute-start.11 = (bf16[16,4096]{1,0:T(8,128)(2,1)S(1)}, bf16[16,4096]{1,0:T(8,128)(2,1)S(1)}, u32[]{:S(2)}, u32[]{:S(2)}) collective-permute-start(bf16[16,4096]{1,0:T(8,128)(2,1)S(1)} %slice.38), channel_id=1, source_target_pairs={{4,8},{12,16},{20,24},{28,32},{36,40},{44,48},{52,56},{60,64},{68,... | collective-permute-start | bytes 393224 | tf_op jit(solution)/shard_map/ppermute | solution.py:647
  34.4 13.6 %collective-permute-start.12 = (bf16[16,4096]{1,0:T(8,128)(2,1)S(1)}, bf16[16,4096]{1,0:T(8,128)(2,1)S(1)}, u32[]{:S(2)}, u32[]{:S(2)}) collective-permute-start(bf16[16,4096]{1,0:T(8,128)(2,1)S(1)} %slice.38), channel_id=1, source_target_pairs={{4,12},{12,20},{20,28},{28,36},{36,44},{44,52},{52,60},{60,68},{68... | collective-permute-start | bytes 393224 | tf_op jit(solution)/shard_map/ppermute | solution.py:647
  36.1 26.3 %collective-permute-start.10 = (bf16[384,1024]{1,0:T(8,128)(2,1)}, bf16[384,1024]{1,0:T(8,128)(2,1)}, u32[]{:S(2)}, u32[]{:S(2)}) collective-permute-start(bf16[384,1024]{1,0:T(8,128)(2,1)} %pad_maximum_fusion.3), channel_id=1, source_target_pairs={{0,96},{32,0},{64,32},{96,64},{1,97},{33,1},{65,33},{97,65},{2,98}... | collective-permute-start | bytes 2359304 | tf_op jit(solution)/shard_map/ppermute | solution.py:24
  39.6 11.1 %collective-permute-start.6 = (bf16[128,1024]{1,0:T(8,128)(2,1)S(1)}, bf16[128,1024]{1,0:T(8,128)(2,1)S(1)}, u32[]{:S(2)}, u32[]{:S(2)}) collective-permute-start(bf16[128,1024]{1,0:T(8,128)(2,1)S(1)} %constant_dynamic-slice_fusion.1), channel_id=1, source_target_pairs={{0,4},{4,0},{1,5},{5,1},{2,6},{6,2},{3,7},{7,3},{8,12},{12,8},{9,1... | collective-permute-start | bytes 786440 | tf_op jit(solution)/shard_map/ppermute | solution.py:19
  46.7 24.7 %collective-permute-start.7 = (bf16[384,1024]{1,0:T(8,128)(2,1)}, bf16[384,1024]{1,0:T(8,128)(2,1)S(1)}, u32[]{:S(2)}, u32[]{:S(2)}) collective-permute-start(bf16[384,1024]{1,0:T(8,128)(2,1)} %pad_maximum_fusion), channel_id=1, source_target_pairs={{0,8},{8,16},{16,24},{24,0},{1,9},{9,17},{17,25},{25,1},{2,10},{10... | collective-permute-start | bytes 2359304 | tf_op jit(solution)/shard_map/ppermute | solution.py:24
  48.0 23.4 %collective-permute-start.8 = (bf16[384,1024]{1,0:T(8,128)(2,1)}, bf16[384,1024]{1,0:T(8,128)(2,1)S(1)}, u32[]{:S(2)}, u32[]{:S(2)}) collective-permute-start(bf16[384,1024]{1,0:T(8,128)(2,1)} %pad_maximum_fusion.1), channel_id=1, source_target_pairs={{0,24},{8,0},{16,8},{24,16},{1,25},{9,1},{17,9},{25,17},{2,26},{10... | collective-permute-start | bytes 2359304 | tf_op jit(solution)/shard_map/ppermute | solution.py:24
  50.7 21.8 %collective-permute-start.9 = (bf16[384,1024]{1,0:T(8,128)(2,1)}, bf16[384,1024]{1,0:T(8,128)(2,1)}, u32[]{:S(2)}, u32[]{:S(2)}) collective-permute-start(bf16[384,1024]{1,0:T(8,128)(2,1)} %pad_maximum_fusion.2), channel_id=1, source_target_pairs={{0,32},{32,64},{64,96},{96,0},{1,33},{33,65},{65,97},{97,1},{2,34}... | collective-permute-start | bytes 2359304 | tf_op jit(solution)/shard_map/ppermute | solution.py:24
  75.3 21.3 %collective-permute-start.16 = (bf16[256,1024]{1,0:T(8,128)(2,1)}, bf16[256,1024]{1,0:T(8,128)(2,1)S(1)}, u32[]{:S(2)}, u32[]{:S(2)}) collective-permute-start(bf16[256,1024]{1,0:T(8,128)(2,1)} %pad_maximum_fusion.7), channel_id=1, source_target_pairs={{0,96},{32,0},{64,32},{96,64},{1,97},{33,1},{65,33},{97,65},{2,98}... | collective-permute-start | bytes 1572872 | tf_op jit(solution)/shard_map/ppermute | solution.py:24
  76.2 22.1 %collective-permute-start.13 = (bf16[256,1024]{1,0:T(8,128)(2,1)}, bf16[256,1024]{1,0:T(8,128)(2,1)S(1)}, u32[]{:S(2)}, u32[]{:S(2)}) collective-permute-start(bf16[256,1024]{1,0:T(8,128)(2,1)} %pad_maximum_fusion.6), channel_id=1, source_target_pairs={{0,8},{8,16},{16,24},{24,0},{1,9},{9,17},{17,25},{25,1},{2,10},{10... | collective-permute-start | bytes 1572872 | tf_op jit(solution)/shard_map/ppermute | solution.py:24
  78.1 22.9 %collective-permute-start.15 = (bf16[256,1024]{1,0:T(8,128)(2,1)}, bf16[256,1024]{1,0:T(8,128)(2,1)S(1)}, u32[]{:S(2)}, u32[]{:S(2)}) collective-permute-start(bf16[256,1024]{1,0:T(8,128)(2,1)} %pad_maximum_fusion.7), channel_id=1, source_target_pairs={{0,32},{32,64},{64,96},{96,0},{1,33},{33,65},{65,97},{97,1},{2,34}... | collective-permute-start | bytes 1572872 | tf_op jit(solution)/shard_map/ppermute | solution.py:24
  79.2 21.8 %collective-permute-start.14 = (bf16[256,1024]{1,0:T(8,128)(2,1)}, bf16[256,1024]{1,0:T(8,128)(2,1)}, u32[]{:S(2)}, u32[]{:S(2)}) collective-permute-start(bf16[256,1024]{1,0:T(8,128)(2,1)} %pad_maximum_fusion.6), channel_id=1, source_target_pairs={{0,24},{8,0},{16,8},{24,16},{1,25},{9,1},{17,9},{25,17},{2,26},{10... | collective-permute-start | bytes 1572872 | tf_op jit(solution)/shard_map/ppermute | solution.py:24
  99.0 7.9 %collective-permute-start.17 = (bf16[128,1024]{1,0:T(8,128)(2,1)}, bf16[128,1024]{1,0:T(8,128)(2,1)}, u32[]{:S(2)}, u32[]{:S(2)}) collective-permute-start(bf16[128,1024]{1,0:T(8,128)(2,1)} %slice.43), channel_id=1, source_target_pairs={{0,8},{8,16},{16,24},{24,0},{1,9},{9,17},{17,25},{25,1},{2,10},{10... | collective-permute-start | bytes 786440 | tf_op jit(solution)/shard_map/ppermute | solution.py:24
  99.7 7.4 %collective-permute-start.18 = (bf16[128,1024]{1,0:T(8,128)(2,1)}, bf16[128,1024]{1,0:T(8,128)(2,1)}, u32[]{:S(2)}, u32[]{:S(2)}) collective-permute-start(bf16[128,1024]{1,0:T(8,128)(2,1)} %slice.44), channel_id=1, source_target_pairs={{0,96},{32,0},{64,32},{96,64},{1,97},{33,1},{65,33},{97,65},{2,98}... | collective-permute-start | bytes 786440 | tf_op jit(solution)/shard_map/ppermute | solution.py:24
  130.2 17.4 %collective-permute-start.19 = (bf16[144,1024]{1,0:T(8,128)(2,1)S(1)}, bf16[144,1024]{1,0:T(8,128)(2,1)S(1)}, u32[]{:S(2)}, u32[]{:S(2)}) collective-permute-start(bf16[144,1024]{1,0:T(8,128)(2,1)S(1)} %get-tuple-element.52.refs_0_), channel_id=1, source_target_pairs={{0,8},{8,16},{16,24},{24,0},{1,9},{9,17},{17,25},{25,1},{2,10},{10... | collective-permute-start | bytes 884744 | tf_op jit(solution)/shard_map/ppermute | solution.py:24
  131.0 27.4 %collective-permute-start.20 = (bf16[144,1024]{1,0:T(8,128)(2,1)S(1)}, bf16[144,1024]{1,0:T(8,128)(2,1)S(1)}, u32[]{:S(2)}, u32[]{:S(2)}) collective-permute-start(bf16[144,1024]{1,0:T(8,128)(2,1)S(1)} %get-tuple-element.52.refs_0_), channel_id=1, source_target_pairs={{0,16},{8,24},{16,0},{24,8},{1,17},{9,25},{17,1},{25,9},{2,18},{10... | collective-permute-start | bytes 884744 | tf_op jit(solution)/shard_map/ppermute | solution.py:24
  134.9 23.5 %collective-permute-start.21 = (bf16[144,1024]{1,0:T(8,128)(2,1)S(1)}, bf16[144,1024]{1,0:T(8,128)(2,1)S(1)}, u32[]{:S(2)}, u32[]{:S(2)}) collective-permute-start(bf16[144,1024]{1,0:T(8,128)(2,1)S(1)} %get-tuple-element.52.refs_0_), channel_id=1, source_target_pairs={{0,24},{8,0},{16,8},{24,16},{1,25},{9,1},{17,9},{25,17},{2,26},{10... | collective-permute-start | bytes 884744 | tf_op jit(solution)/shard_map/ppermute | solution.py:24
  161.8 23.4 %collective-permute-start.22 = (bf16[144,1024]{1,0:T(8,128)(2,1)}, bf16[144,1024]{1,0:T(8,128)(2,1)S(1)}, u32[]{:S(2)}, u32[]{:S(2)}) collective-permute-start(bf16[144,1024]{1,0:T(8,128)(2,1)} %get-tuple-element.55), channel_id=1, source_target_pairs={{0,96},{1,97},{2,98},{3,99},{4,100},{5,101},{6,102},{7,103},{8,104... | collective-permute-start | bytes 884744 | tf_op jit(solution)/shard_map/ppermute | solution.py:571
  166.5 18.7 %collective-permute-start.23 = (bf16[144,1024]{1,0:T(8,128)(2,1)}, bf16[144,1024]{1,0:T(8,128)(2,1)S(1)}, u32[]{:S(2)}, u32[]{:S(2)}) collective-permute-start(bf16[144,1024]{1,0:T(8,128)(2,1)} %get-tuple-element.55), channel_id=1, source_target_pairs={{0,64},{32,96},{1,65},{33,97},{2,66},{34,98},{3,67},{35,99},{4,68}... | collective-permute-start | bytes 884744 | tf_op jit(solution)/shard_map/ppermute | solution.py:571
  167.8 17.4 %collective-permute-start.24 = (bf16[144,1024]{1,0:T(8,128)(2,1)}, bf16[144,1024]{1,0:T(8,128)(2,1)S(1)}, u32[]{:S(2)}, u32[]{:S(2)}) collective-permute-start(bf16[144,1024]{1,0:T(8,128)(2,1)} %get-tuple-element.55), channel_id=1, source_target_pairs={{0,32},{32,64},{64,96},{1,33},{33,65},{65,97},{2,34},{34,66},{66,9... | collective-permute-start | bytes 884744 | tf_op jit(solution)/shard_map/ppermute | solution.py:571
  195.2 11.7 %collective-permute-start.25 = (bf16[512,1024]{1,0:T(8,128)(2,1)}, bf16[512,1024]{1,0:T(8,128)(2,1)S(1)}, u32[]{:S(2)}, u32[]{:S(2)}) collective-permute-start(bf16[512,1024]{1,0:T(8,128)(2,1)} %get-tuple-element.57), channel_id=1, source_target_pairs={{0,4},{4,0},{1,5},{5,1},{2,6},{6,2},{3,7},{7,3},{8,12},{12,8},{9,1... | collective-permute-start | bytes 3145736 | tf_op jit(solution)/shard_map/ppermute | solution.py:19
  195.2 2.9 %collective-permute-start.26 = (f32[1,1024]{1,0:T(1,128)}, f32[1,1024]{1,0:T(1,128)S(1)}, u32[]{:S(2)}, u32[]{:S(2)}) collective-permute-start(f32[1,1024]{1,0:T(1,128)} %get-tuple-element.58), channel_id=1, source_target_pairs={{0,4},{4,0},{1,5},{5,1},{2,6},{6,2},{3,7},{7,3},{8,12},{12,8},{9,1... | collective-permute-start | bytes 12296 | tf_op jit(solution)/shard_map/ppermute | solution.py:19
  198.8 3.6 %collective-permute-start.27 = (f32[1,512]{1,0:T(1,128)S(1)}, f32[1,512]{1,0:T(1,128)S(1)}, u32[]{:S(2)}, u32[]{:S(2)}) collective-permute-start(f32[1,512]{1,0:T(1,128)S(1)} %dynamic-slice_add_fusion), channel_id=1, source_target_pairs={{0,1},{1,2},{2,3},{3,0},{4,5},{5,6},{6,7},{7,4},{8,9},{9,10},{10,1... | collective-permute-start | bytes 6152 | tf_op jit(solution)/shard_map/ppermute | solution.py:24
  199.2 5.1 %collective-permute-start.28 = (f32[1,512]{1,0:T(1,128)S(1)}, f32[1,512]{1,0:T(1,128)S(1)}, u32[]{:S(2)}, u32[]{:S(2)}) collective-permute-start(f32[1,512]{1,0:T(1,128)S(1)} %dynamic-slice_add_fusion), channel_id=1, source_target_pairs={{0,2},{1,3},{2,0},{3,1},{4,6},{5,7},{6,4},{7,5},{8,10},{9,11},{10,... | collective-permute-start | bytes 6152 | tf_op jit(solution)/shard_map/ppermute | solution.py:24
  201.6 4.8 %collective-permute-start.29 = (f32[1,512]{1,0:T(1,128)S(1)}, f32[1,512]{1,0:T(1,128)S(1)}, u32[]{:S(2)}, u32[]{:S(2)}) collective-permute-start(f32[1,512]{1,0:T(1,128)S(1)} %dynamic-slice_add_fusion), channel_id=1, source_target_pairs={{0,3},{1,0},{2,1},{3,2},{4,7},{5,4},{6,5},{7,6},{8,11},{9,8},{10,9... | collective-permute-start | bytes 6152 | tf_op jit(solution)/shard_map/ppermute | solution.py:24
  (28 other events, 342.6 us)
Sparse Core Ops, SparseCore 0:
  9.6 50.5 all-gather.4
  72.6 85.0 all-gather.2

commit v8 on v7

--- a/solution.py
+++ b/solution.py
@@ -357,7 +357,7 @@
     return pl.BlockSpec((GROUP, width), lambda i: (i, 0))
 
 
-def params(flops, megabytes, vmem=60):
+def params(flops, megabytes, vmem=32):
     return dict(
         compiler_params=pltpu.CompilerParams(vmem_limit_bytes=vmem * 2**20),
         cost_estimate=pl.CostEstimate(
@@ -403,7 +403,7 @@
         ),
         out_shape=outs,
         name="prepared",
-        **params(4e9, 14),
+        **params(4e9, 14, 48),
     )(place, *slabs, weight, conv_bc, bias, rate)
 
 
@@ -423,7 +423,7 @@
         ),
         out_shape=outs,
         name="first_products",
-        **params(6e9, 18),
+        **params(6e9, 18, 48),
     )(place, *slabs, *weights)
 
 
@@ -460,7 +460,7 @@
         ),
         out_shape=outs,
         name="states",
-        **params(11e9, 18, 48),
+        **params(11e9, 18, 40),
     )(place, *slabs, *weights, *sums, bcc, weights_in, decays, conv_x)
 
 
@@ -478,7 +478,7 @@
         out_specs=rows_of(width),
         out_shape=jax.ShapeDtypeStruct((rows, width), BF16),
         scratch_shapes=[pltpu.VMEM((GROUP, width), F32)],
-        compiler_params=pltpu.CompilerParams(vmem_limit_bytes=60 * 2**20),
+        compiler_params=pltpu.CompilerParams(vmem_limit_bytes=32 * 2**20),
         cost_estimate=pl.CostEstimate(flops=10**10, bytes_accessed=10 * 2**20, transcendentals=4 * 2**20),
         name="outputs",
     )(xc, bcc, cum, cum_t, step_t, entering, skip)
@@ -486,7 +486,7 @@
 
 def project_gate(place, slabs, weight):
     own, other, _ = slabs
-    rows, width, depth = 2 * own.shape[0], weight.shape[1], 1024
+    rows, width, depth = 2 * own.shape[0], weight.shape[1] // 2, 1024
     columns = pl.BlockSpec((own.shape[0], depth), lambda i, place: (0, i))
     out = jax.ShapeDtypeStruct((rows, width), BF16)
     return pl.pallas_call(
@@ -494,13 +494,13 @@
         grid_spec=pltpu.PrefetchScalarGridSpec(
             num_scalar_prefetch=1,
             grid=(weight.shape[0] // depth,),
-            in_specs=[columns, columns, pl.BlockSpec((depth, width), lambda i, place: (i, 0))],
+            in_specs=[columns, columns, pl.BlockSpec((depth, width), lambda i, place: (i, place[0]))],
             out_specs=fixed(out),
             scratch_shapes=[pltpu.VMEM((rows, width), F32)],
         ),
         out_shape=out,
         name="project_gate",
-        **params(9e9, 20),
+        **params(9e9, 20, 48),
     )(place, own, other, weight)
 
 
@@ -519,7 +519,7 @@
         ),
         out_shape=[half, half, jax.ShapeDtypeStruct((1, rows), F32)],
         name="gate",
-        **params(1e9, 10),
+        **params(1e9, 10, 60),
     )(core, gate, local, bcc, cum_slab, before, before_decay, *earlier)
 
 
@@ -539,7 +539,7 @@
             out_specs=pl.BlockSpec((rows, width), lambda j, core: (0, j)),
         ),
         out_shape=jax.ShapeDtypeStruct((rows, 2 * width), BF16),
-        compiler_params=pltpu.CompilerParams(vmem_limit_bytes=60 * 2**20),
+        compiler_params=pltpu.CompilerParams(vmem_limit_bytes=32 * 2**20),
         cost_estimate=pl.CostEstimate(flops=10**7, bytes_accessed=4 * 2**20, transcendentals=0),
         name="normalized",
     )(core.astype(jnp.int32)[None], gated, other, mean_squares, gain)
@@ -578,37 +578,31 @@
     return lax.optimization_barrier((*values, *to))[: len(values)]
 
 
-def travelling(own, after_first, before_third, before_last):
-    block = own.shape[0]
-    half = block // 2
+def travelling(own, after_first, before_last):
     y_less, y_more = round_ring(own, "y", 1), round_ring(own, "y", -1)
     z_less, z_more = round_ring(own, "z", 1), round_ring(own, "z", -1)
-    after_first([own, y_less, y_more, z_less, z_more])
-    join = lambda *parts: jnp.concatenate(parts, axis=0)
-    from_y_less = round_ring(join(z_less, y_less[:half]), "y", 1)
-    from_y_more = round_ring(join(z_more, y_more[half:]), "y", -1)
-    from_z_less = round_ring(join(y_more, z_less[:half]), "z", 1)
-    from_z_more = round_ring(join(y_less, z_more[half:]), "z", -1)
-    halves = tied((from_y_less, from_y_more, from_z_less, from_z_more), *before_third())
-    y_far = join(halves[0][block:], halves[1][block:])
-    z_far = join(halves[2][block:], halves[3][block:])
-    far_y_less, far_y_more = round_ring(z_far, "y", 1), round_ring(z_far, "y", -1)
-    far_z_less, far_z_more = round_ring(y_far, "z", 1), round_ring(y_far, "z", -1)
-    top, low = tied((far_y_less, far_z_more), *before_last(halves))
-    blocks = [
-        from_y_less, from_y_more, from_z_less, from_z_more,
-        far_y_less, far_y_more, far_z_less, far_z_more,
-        round_ring(top[:half], "y", 1), round_ring(low[half:], "z", -1),
+    after_first([y_less, y_more, z_less, z_more])
+    y_far, z_far = round_ring(y_less, "y", 1), round_ring(z_more, "z", -1)
+    more_more, more_less = round_ring(z_more, "y", -1), round_ring(y_more, "z", 1)
+    y_far, z_far = tied((y_far, z_far), more_more, more_less)
+    far = [
+        round_ring(z_far, "y", -1), round_ring(z_far, "y", 1),
+        round_ring(y_far, "z", 1), round_ring(y_far, "z", -1),
     ]
-    sources = [(i, 0, block) for i in range(4)] + [(i, block, half) for i in range(4)]
-    sources += [(i, 0, block) for i in range(4, 8)] + [(8, 0, half), (9, 0, half)]
-    return blocks, sources
+    early = [own, y_less, y_more, z_less, z_more, y_far, z_far, more_more, more_less]
+    held_z, held_y, last, *_ = tied((z_less, y_less, *far), *before_last(early))
+    less_less, less_more = round_ring(held_z, "y", 1), round_ring(held_y, "z", -1)
+    return [*far, less_less, less_more, round_ring(last, "y", -1)]
+
+
+def all_rows(blocks):
+    return [(index, 0, block.shape[0]) for index, block in enumerate(blocks)]
 
 
 def block_order():
     places = (
-        ((0, 0), (-1, 0), (1, 0), (0, -1), (0, 1), (-1, -1), (1, 1), (1, -1), (-1, 1), (2, 0), (0, 2))
-        + ((-1, 2), (1, 2), (2, -1), (2, 1), (2, 2))
+        ((0, 0), (-1, 0), (1, 0), (0, -1), (0, 1), (2, 0), (0, 2), (1, 1), (1, -1))
+        + ((1, 2), (-1, 2), (2, -1), (2, 1), (-1, -1), (-1, 1), (2, 2))
     )
     y, z = lax.axis_index("y"), lax.axis_index("z")
     return [(z + dz) % 4 * 4 + (y + dy) % 4 for dy, dz in places]
@@ -639,35 +633,29 @@
     narrow = lax.all_gather(narrow, ("z", "y", "core"), axis=0, tiled=True)
     own_block = jnp.concatenate([mine(x_weight, 1), swap_cores(others(x_weight, 1))], axis=0)
     place = jnp.stack([core, *block_order()]).astype(jnp.int32)
-    slabs, sums, early, z_blocks, z_wholes = [], [], [], [], []
+    slabs, sums = [], []
 
     def after_first(blocks):
-        rows, z_rows = tied((tokens, z_weight), *blocks[1:])
+        (rows,) = tied((tokens,), *blocks)
         chips = lax.axis_size("z") * lax.axis_size("y")
         to_next = lambda target: lax.ppermute(
             rows[-HALO:], ("z", "y", "core"),
             [(2 * i + 1, 2 * i + 2 + target) for i in range(chips - 1)],
         )
         slabs.extend((rows, swap_cores(rows), to_next(0) + to_next(1)))
-        z_blocks.append(
-            in_core_order(core, mine(z_rows, 1), swap_cores(others(z_rows, 1)), 0)
-        )
-        sources = [(i, 0, blocks[0].shape[0]) for i in range(5)]
-        sums.extend(first_products(place, slabs, blocks, sources, 5))
-
-    def before_last(second):
-        (z_block,) = tied((z_blocks[0],), *second)
-        z_wholes.append(lax.all_gather(z_block, ("z", "y"), axis=0, tiled=True))
-        early.extend(
-            prepared(place, slabs, narrow, conv_bc, per_lane(dt_bias), per_lane(decay_rate), heads)
-        )
-        return early[:1]
-
-    blocks, sources = travelling(own_block, after_first, lambda: sums[:1], before_last)
-    bcc, cum, cum_slab, cum_t, step_t, weights_in, decays = early
-    (z_whole,) = z_wholes
+
+    def before_last(blocks):
+        sums.extend(first_products(place, slabs, blocks, all_rows(blocks), len(blocks)))
+        return sums[:1]
+
+    blocks = travelling(own_block, after_first, before_last)
+    (z_rows,) = tied((z_weight,), own_block)
+    z_whole = lax.all_gather(z_rows, ("z", "y", "core"), axis=0, tiled=True)
+    bcc, cum, cum_slab, cum_t, step_t, weights_in, decays = prepared(
+        place, slabs, narrow, conv_bc, per_lane(dt_bias), per_lane(decay_rate), heads
+    )
     xc, entering, final = local_states(
-        place, slabs, blocks, sources, 5, 11, sums, bcc, weights_in, decays, mine(conv_x, 1)
+        place, slabs, blocks, all_rows(blocks), 9, 7, sums, bcc, weights_in, decays, mine(conv_x, 1)
     )
     before, before_decay, earlier = earlier_states(final)
     skip_lanes = jnp.repeat(mine(skip, 0), HEAD)[None, :]

time: 219 us -> 207 us (0.945)
  Pallas kernels: 83.1 us -> 70.7 us
  starting transfers between devices: 42.4 us -> 49.7 us
  other arithmetic: 9.91 us -> 3.16 us
    ppermute x20 -> x21, starting transfers between devices: 28 us -> 37.9 us  [round_ring(): lax.ppermute(a, axis, [(i, (i + distance) % size) for i in range(size)])]
    concatenate x7 -> x0, other arithmetic: 6.32 us -> none  [the longest x6 5.49 us: travelling(): join = lambda *parts: jnp.concatenate(parts, axis=0)]
    unnamed x53 -> x49, local copies, waits for them, and re-layouts: 6.55 us -> 12.2 us
    pallas_call x1, Pallas kernels: 20 us -> 15.4 us  [local_states(): pl.pallas_call(functools.partial(states_kernel, sources, done, count), gr...]
    slice x12 -> x0, local copies, waits for them, and re-layouts: 4.34 us -> none  [the longest x2 1.95 us: travelling(): z_far = join(halves[2][block:], halves[3][block:])]
    ppermute x5 -> x4, starting transfers between devices: 4.04 us -> 0.59 us  [swap_cores(): return lax.ppermute(a, 'core', [(0, 1), (1, 0)])]
    ppermute x20 -> x21, waiting for transfers between devices: 49.9 us -> 49.9 us  [round_ring(): lax.ppermute(a, axis, [(i, (i + distance) % size) for i in range(size)])]
  transfers between devices with their start and end apart: 32 -> 32, of which waited for: 17 -> 17; matrix products, arithmetic and copies ran while one was open for 7% -> 2% of each run, Pallas kernels for 32% -> 29%
where the time goes in v8:
time: 207 us; the launch traced here: 206 us
  Pallas kernels  70.7 us (34%)
  waiting for transfers between devices  53.9 us (26%)
  starting transfers between devices  49.7 us (24%)
  local copies, waits for them, and re-layouts  14.8 us (7%)
  between operations  13.7 us (7%)
  other arithmetic  3.16 us (2%)
    ppermute x21, waiting for transfers between devices, round_ring(): lax.ppermute(a, axis, [(i, (i + distance) % size) for i in range(size)])  49.9 us
    ppermute x21, starting transfers between devices, round_ring(): lax.ppermute(a, axis, [(i, (i + distance) % size) for i in range(size)])  37.9 us
    pallas_call x1, Pallas kernels, local_states(): pl.pallas_call(functools.partial(states_kernel, sources, done, count), gr...  15.4 us
    pallas_call x1, Pallas kernels, project_gate(): pl.pallas_call(z_kernel, grid_spec=pltpu.PrefetchScalarGridSpec(num_scala...  13 us
    pallas_call x1, Pallas kernels, prepared(): pl.pallas_call(prepare_kernel, grid_spec=pltpu.PrefetchScalarGridSpec(num...  12.7 us
    unnamed x49, local copies, waits for them, and re-layouts  12.2 us
    pallas_call x1, Pallas kernels, first_products(): pl.pallas_call(functools.partial(first_kernel, sources, count), grid_spec...  11.2 us
    ppermute x3, starting transfers between devices, earlier_states(): lax.ppermute(total, 'z', [(i, i + distance) for i in range(rows - distanc...  9.14 us
  transfers between devices with their start and end apart: 32, of which 17 were waited for; matrix products, arithmetic and copies ran while one was open for 2% of the time, Pallas kernels for 29%

profile of v8, /device:TPU:6, one launch (start us, length us, event | category | flops | bytes accessed | tf_op | source)
XLA Modules:
  0.0 205.9 jit_solution(9249637427018675177)
XLA Ops:
  13.4 1.7 collective-permute-start.2
  15.1 1.9 collective-permute-start.3
  17.0 2.1 %collective-permute-start.4 = (bf16[256,1024]{1,0:T(8,128)(2,1)S(1)}, bf16[256,1024]{1,0:T(8,128)(2,1)S(1)}, u32[]{:S(2)}, u32[]{:S(2)}) collective-permute-start(bf16[256,1024]{1,0:T(8,128)(2,1)S(1)} %pad_maximum_fusion.refs_0_), channel_id=1, source_target_pairs={{0,96},{32,0},{64,32},{96,64},{1,97},{33,1},{65,33},{97,65},{2,98}... | collective-permute-start | bytes 1572872 | tf_op jit(solution)/shard_map/ppermute | solution.py:24
  19.1 8.5 %collective-permute-done.1.refs_1_ = bf16[256,1024]{1,0:T(8,128)(2,1)S(1)} collective-permute-done((bf16[256,1024]{1,0:T(8,128)(2,1)S(1)}, bf16[256,1024]{1,0:T(8,128)(2,1)S(1)}, u32[]{:S(2)}, u32[]{:S(2)}) %collective-permute-start.1) | collective-permute-done | bytes 524320 | tf_op jit(solution)/shard_map/ppermute | solution.py:24
  27.7 4.3 %collective-permute-done.3.refs_3_ = bf16[256,1024]{1,0:T(8,128)(2,1)S(1)} collective-permute-done((bf16[256,1024]{1,0:T(8,128)(2,1)S(1)}, bf16[256,1024]{1,0:T(8,128)(2,1)S(1)}, u32[]{:S(2)}, u32[]{:S(2)}) %collective-permute-start.3) | collective-permute-done | bytes 524320 | tf_op jit(solution)/shard_map/ppermute | solution.py:24
  35.8 3.0 %collective-permute-start.9 = (bf16[256,1024]{1,0:T(8,128)(2,1)S(1)}, bf16[256,1024]{1,0:T(8,128)(2,1)}, u32[]{:S(2)}, u32[]{:S(2)}) collective-permute-start(bf16[256,1024]{1,0:T(8,128)(2,1)S(1)} %collective-permute-done.4.refs_4_), channel_id=1, source_target_pairs={{0,96},{32,0},{64,32},{96,64},{1,97},{33,1},{65,33},{97,65},{2,98}... | collective-permute-start | bytes 1572872 | tf_op jit(solution)/shard_map/ppermute | solution.py:24
  38.7 3.0 %collective-permute-start.10 = (bf16[256,1024]{1,0:T(8,128)(2,1)S(1)}, bf16[256,1024]{1,0:T(8,128)(2,1)}, u32[]{:S(2)}, u32[]{:S(2)}) collective-permute-start(bf16[256,1024]{1,0:T(8,128)(2,1)S(1)} %collective-permute-done.4.refs_4_), channel_id=1, source_target_pairs={{0,24},{8,0},{16,8},{24,16},{1,25},{9,1},{17,9},{25,17},{2,26},{10... | collective-permute-start | bytes 1572872 | tf_op jit(solution)/shard_map/ppermute | solution.py:24
  41.7 2.2 %collective-permute-start.11 = (bf16[256,1024]{1,0:T(8,128)(2,1)S(1)}, bf16[256,1024]{1,0:T(8,128)(2,1)}, u32[]{:S(2)}, u32[]{:S(2)}) collective-permute-start(bf16[256,1024]{1,0:T(8,128)(2,1)S(1)} %collective-permute-done.2.refs_2_), channel_id=1, source_target_pairs={{0,32},{32,64},{64,96},{96,0},{1,33},{33,65},{65,97},{97,1},{2,34}... | collective-permute-start | bytes 1572872 | tf_op jit(solution)/shard_map/ppermute | solution.py:24
  45.2 10.1 %collective-permute-done.8.refs_5_ = bf16[256,1024]{1,0:T(8,128)(2,1)S(1)} collective-permute-done((bf16[256,1024]{1,0:T(8,128)(2,1)S(1)}, bf16[256,1024]{1,0:T(8,128)(2,1)S(1)}, u32[]{:S(2)}, u32[]{:S(2)}) %collective-permute-start.8) | collective-permute-done | bytes 524320 | tf_op jit(solution)/shard_map/ppermute | solution.py:24
  55.3 3.9 %collective-permute-done.10.refs_7_ = bf16[256,1024]{1,0:T(8,128)(2,1)} collective-permute-done((bf16[256,1024]{1,0:T(8,128)(2,1)S(1)}, bf16[256,1024]{1,0:T(8,128)(2,1)}, u32[]{:S(2)}, u32[]{:S(2)}) %collective-permute-start.10) | collective-permute-done | bytes 524320 | tf_op jit(solution)/shard_map/ppermute | solution.py:24
  59.2 3.0 %collective-permute-done.11.refs_8_ = bf16[256,1024]{1,0:T(8,128)(2,1)} collective-permute-done((bf16[256,1024]{1,0:T(8,128)(2,1)S(1)}, bf16[256,1024]{1,0:T(8,128)(2,1)}, u32[]{:S(2)}, u32[]{:S(2)}) %collective-permute-start.11) | collective-permute-done | bytes 524320 | tf_op jit(solution)/shard_map/ppermute | solution.py:24
  63.0 1.7 collective-permute-start.13
  65.2 2.8 %collective-permute-start.15 = (bf16[256,1024]{1,0:T(8,128)(2,1)S(1)}, bf16[256,1024]{1,0:T(8,128)(2,1)S(1)}, u32[]{:S(2)}, u32[]{:S(2)}) collective-permute-start(bf16[256,1024]{1,0:T(8,128)(2,1)S(1)} %collective-permute-done.8.refs_5_), channel_id=1, source_target_pairs={{0,96},{32,0},{64,32},{96,64},{1,97},{33,1},{65,33},{97,65},{2,98}... | collective-permute-start | bytes 1572872 | tf_op jit(solution)/shard_map/ppermute | solution.py:24
  68.0 11.2 %first_products.1 = (f32[1024,1024]{1,0:T(8,128)}, f32[16,1024]{1,0:T(8,128)S(1)}) custom-call(s32[17]{0:T(128)S(1)} %stack.68.place_ref, bf16[512,4096]{1,0:T(8,128)(2,1)} %own_ref.3, bf16[512,4096]{1,0:T(8,128)(2,1)} %collective-permute-done.5.other_ref, bf16[16,4096]{1,0:T(8,128)(2,1)S(1)} %add.199.before_ref, ...), custom_call_target="tpu_custom_call" | custom-call | flops 6000000000 | bytes 18874368 | tf_op jit(solution)/shard_map/first_products/pallas_call | solution.py:416
  79.7 1.8 collective-permute-done.13.refs_1_
  86.1 2.9 %collective-permute-start.16 = (bf16[256,1024]{1,0:T(8,128)(2,1)S(1)}, bf16[256,1024]{1,0:T(8,128)(2,1)S(1)}, u32[]{:S(2)}, u32[]{:S(2)}) collective-permute-start(bf16[256,1024]{1,0:T(8,128)(2,1)S(1)} %collective-permute-done.3.refs_3_), channel_id=1, source_target_pairs={{0,8},{8,16},{16,24},{24,0},{1,9},{9,17},{17,25},{25,1},{2,10},{10... | collective-permute-start | bytes 1572872 | tf_op jit(solution)/shard_map/ppermute | solution.py:24
  89.0 3.7 %collective-permute-start.17 = (bf16[256,1024]{1,0:T(8,128)(2,1)S(1)}, bf16[256,1024]{1,0:T(8,128)(2,1)S(1)}, u32[]{:S(2)}, u32[]{:S(2)}) collective-permute-start(bf16[256,1024]{1,0:T(8,128)(2,1)S(1)} %collective-permute-done.1.refs_1_), channel_id=1, source_target_pairs={{0,96},{32,0},{64,32},{96,64},{1,97},{33,1},{65,33},{97,65},{2,98}... | collective-permute-start | bytes 1572872 | tf_op jit(solution)/shard_map/ppermute | solution.py:24
  93.3 1.9 copy-done.10
  95.2 12.7 %prepared.1 = (bf16[1024,256]{1,0:T(8,128)(2,1)S(1)}, f32[1024,128]{1,0:T(8,128)S(1)}, f32[1024,128]{1,0:T(8,128)S(1)}, f32[16,1024]{1,0:T(8,128)S(1)}, f32[16,1...) custom-call(s32[17]{0:T(128)S(1)} %stack.68.place_ref, bf16[512,4096]{1,0:T(8,128)(2,1)} %own_ref.3, ...), custom_call_target="tpu_custom_call" | custom-call | flops 4000000000 | bytes 14680064 | tf_op jit(solution)/shard_map/prepared/pallas_call | solution.py:393
  109.2 15.4 %states.1 = (bf16[1024,1024]{1,0:T(8,128)(2,1)S(1)}, bf16[4,128,1024]{2,1,0:T(8,128)(2,1)S(1)}, bf16[144,1024]{1,0:T(8,128)(2,1)S(1)}) custom-call(s32[17]{0:T(128)S(1)} %stack.68.place_ref, bf16[512,4096]{1,0:T(8,128)(2,1)S(1)} %copy-done.9, bf16[512,4096]{1,0:T(8,128)(2,1)} %collective-permute-done.5.other_ref, bf16[16,4096]{1,0:T(8,128)(2,1)S(1)} %add.199.before_ref, ...), custom_call_target="tpu_custom_call" | custom-call | flops 11000000512 | bytes 18874368 | tf_op jit(solution)/shard_map/states/pallas_call | solution.py:439
  125.8 4.2 %collective-permute-start.20 = (bf16[144,1024]{1,0:T(8,128)(2,1)S(1)}, bf16[144,1024]{1,0:T(8,128)(2,1)S(1)}, u32[]{:S(2)}, u32[]{:S(2)}) collective-permute-start(bf16[144,1024]{1,0:T(8,128)(2,1)S(1)} %get-tuple-element.48.refs_0_), channel_id=1, source_target_pairs={{0,16},{8,24},{16,0},{24,8},{1,17},{9,25},{17,1},{25,9},{2,18},{10... | collective-permute-start | bytes 884744 | tf_op jit(solution)/shard_map/ppermute | solution.py:24
  130.0 6.8 %outputs.1.local_ref = bf16[1024,1024]{1,0:T(8,128)(2,1)S(1)} custom-call(bf16[1024,1024]{1,0:T(8,128)(2,1)S(1)} %get-tuple-element.42.xc_ref, bf16[1024,256]{1,0:T(8,128)(2,1)S(1)} %get-tuple-element.39.refs_9_.bcc_ref, f32[1024,128]{1,0:T(8,128)S(1)} %get-tuple-element.43.cum_ref, f32[16,1024]{1,0:T(8,128)S(1)} %get-tuple-element.44.cum_t_ref, ...), custom_call_target="tpu_custom_call" | custom-call | flops 10000000000 | bytes 10485760 | tf_op jit(solution)/shard_map/outputs/pallas_call | solution.py:471
  138.2 4.6 %collective-permute-done.19.refs_1_ = bf16[144,1024]{1,0:T(8,128)(2,1)S(1)} collective-permute-done((bf16[144,1024]{1,0:T(8,128)(2,1)S(1)}, bf16[144,1024]{1,0:T(8,128)(2,1)S(1)}, u32[]{:S(2)}, u32[]{:S(2)}) %collective-permute-start.19) | collective-permute-done | bytes 294944 | tf_op jit(solution)/shard_map/ppermute | solution.py:24
  142.8 5.6 %collective-permute-done.20.refs_2_ = bf16[144,1024]{1,0:T(8,128)(2,1)S(1)} collective-permute-done((bf16[144,1024]{1,0:T(8,128)(2,1)S(1)}, bf16[144,1024]{1,0:T(8,128)(2,1)S(1)}, u32[]{:S(2)}, u32[]{:S(2)}) %collective-permute-start.20) | collective-permute-done | bytes 294944 | tf_op jit(solution)/shard_map/ppermute | solution.py:24
  150.4 4.8 %collective-permute-start.22 = (bf16[144,1024]{1,0:T(8,128)(2,1)S(1)}, bf16[144,1024]{1,0:T(8,128)(2,1)S(1)}, u32[]{:S(2)}, u32[]{:S(2)}) collective-permute-start(bf16[144,1024]{1,0:T(8,128)(2,1)S(1)} %get-tuple-element.51), channel_id=1, source_target_pairs={{0,96},{1,97},{2,98},{3,99},{4,100},{5,101},{6,102},{7,103},{8,104... | collective-permute-start | bytes 884744 | tf_op jit(solution)/shard_map/ppermute | solution.py:571
  156.6 3.0 %collective-permute-start.24 = (bf16[144,1024]{1,0:T(8,128)(2,1)S(1)}, bf16[144,1024]{1,0:T(8,128)(2,1)S(1)}, u32[]{:S(2)}, u32[]{:S(2)}) collective-permute-start(bf16[144,1024]{1,0:T(8,128)(2,1)S(1)} %get-tuple-element.51), channel_id=1, source_target_pairs={{0,32},{32,64},{64,96},{1,33},{33,65},{65,97},{2,34},{34,66},{66,9... | collective-permute-start | bytes 884744 | tf_op jit(solution)/shard_map/ppermute | solution.py:571
  159.6 13.0 %project_gate.1.gate_ref = bf16[1024,1024]{1,0:T(8,128)(2,1)S(1)} custom-call(s32[17]{0:T(128)S(1)} %stack.68.place_ref, bf16[512,4096]{1,0:T(8,128)(2,1)} %own_ref.3, bf16[512,4096]{1,0:T(8,128)(2,1)} %collective-permute-done.5.other_ref, bf16[4096,2048]{1,0:T(8,128)(2,1)} %all-gather.3.cloned.1.call-done.weight_ref), custom_call_target="tpu_custom_call" | custom-call | flops 8999999488 | bytes 20971520 | tf_op jit(solution)/shard_map/project_gate/pallas_call | solution.py:492
  174.9 9.1 %gate.1 = (bf16[512,1024]{1,0:T(8,128)(2,1)}, bf16[512,1024]{1,0:T(8,128)(2,1)}, f32[1,1024]{1,0:T(1,128)}) custom-call(s32[1]{0:T(128)} %bitcast.core_ref, bf16[1024,1024]{1,0:T(8,128)(2,1)} %copy-done.2, bf16[1024,1024]{1,0:T(8,128)(2,1)} %copy-done.1, bf16[1024,256]{1,0:T(8,128)(2,1)} %copy-done.4, f32[1024,128]{1,0:T(8,128)} %copy-done.5, ...), custom_call_target="tpu_custom_call" | custom-call | flops 1000000000 | bytes 10485760 | tf_op jit(solution)/shard_map/gate/pallas_call | solution.py:510
  184.5 2.4 %collective-permute-done.26 = f32[1,1024]{1,0:T(1,128)S(1)} collective-permute-done((f32[1,1024]{1,0:T(1,128)}, f32[1,1024]{1,0:T(1,128)S(1)}, u32[]{:S(2)}, u32[]{:S(2)}) %collective-permute-start.26) | collective-permute-done | bytes 4128 | tf_op jit(solution)/shard_map/ppermute | solution.py:19
  188.4 2.4 %collective-permute-start.27 = (f32[1,512]{1,0:T(1,128)S(1)}, f32[1,512]{1,0:T(1,128)S(1)}, u32[]{:S(2)}, u32[]{:S(2)}) collective-permute-start(f32[1,512]{1,0:T(1,128)S(1)} %dynamic-slice_add_fusion), channel_id=1, source_target_pairs={{0,1},{1,2},{2,3},{3,0},{4,5},{5,6},{6,7},{7,4},{8,9},{9,10},{10,1... | collective-permute-start | bytes 6152 | tf_op jit(solution)/shard_map/ppermute | solution.py:24
  192.4 3.5 %collective-permute-done.28 = f32[1,512]{1,0:T(1,128)S(1)} collective-permute-done((f32[1,512]{1,0:T(1,128)S(1)}, f32[1,512]{1,0:T(1,128)S(1)}, u32[]{:S(2)}, u32[]{:S(2)}) %collective-permute-start.28) | collective-permute-done | bytes 2080 | tf_op jit(solution)/shard_map/ppermute | solution.py:24
  197.2 1.9 normalized.1
  (108 shorter events, 33.0 us)
Async XLA Ops:
  6.5 86.7 %all-gather.5.cloned.1.call-start = ((), (), s32[]{:S(2)}) async-start(), calls=%async_computation.1 | async-start | bytes 3244032 | tf_op jit(solution)/shard_map/all_gather | solution.py:633
  9.0 150.6 %all-gather.3.cloned.1.call-start = ((), (), s32[]{:S(2)}) async-start(), calls=%async_computation | async-start | bytes 17301504 | tf_op jit(solution)/shard_map/all_gather | solution.py:653
  10.1 1.6 collective-permute-start
  11.8 15.8 %collective-permute-start.1 = (bf16[256,1024]{1,0:T(8,128)(2,1)S(1)}, bf16[256,1024]{1,0:T(8,128)(2,1)S(1)}, u32[]{:S(2)}, u32[]{:S(2)}) collective-permute-start(bf16[256,1024]{1,0:T(8,128)(2,1)S(1)} %pad_maximum_fusion.refs_0_), channel_id=1, source_target_pairs={{0,8},{8,16},{16,24},{24,0},{1,9},{9,17},{17,25},{25,1},{2,10},{10... | collective-permute-start | bytes 1572872 | tf_op jit(solution)/shard_map/ppermute | solution.py:24
  13.4 14.3 %collective-permute-start.2 = (bf16[256,1024]{1,0:T(8,128)(2,1)S(1)}, bf16[256,1024]{1,0:T(8,128)(2,1)S(1)}, u32[]{:S(2)}, u32[]{:S(2)}) collective-permute-start(bf16[256,1024]{1,0:T(8,128)(2,1)S(1)} %pad_maximum_fusion.refs_0_), channel_id=1, source_target_pairs={{0,24},{8,0},{16,8},{24,16},{1,25},{9,1},{17,9},{25,17},{2,26},{10... | collective-permute-start | bytes 1572872 | tf_op jit(solution)/shard_map/ppermute | solution.py:24
  15.1 16.9 %collective-permute-start.3 = (bf16[256,1024]{1,0:T(8,128)(2,1)S(1)}, bf16[256,1024]{1,0:T(8,128)(2,1)S(1)}, u32[]{:S(2)}, u32[]{:S(2)}) collective-permute-start(bf16[256,1024]{1,0:T(8,128)(2,1)S(1)} %pad_maximum_fusion.refs_0_), channel_id=1, source_target_pairs={{0,32},{32,64},{64,96},{96,0},{1,33},{33,65},{65,97},{97,1},{2,34}... | collective-permute-start | bytes 1572872 | tf_op jit(solution)/shard_map/ppermute | solution.py:24
  17.0 15.0 %collective-permute-start.4 = (bf16[256,1024]{1,0:T(8,128)(2,1)S(1)}, bf16[256,1024]{1,0:T(8,128)(2,1)S(1)}, u32[]{:S(2)}, u32[]{:S(2)}) collective-permute-start(bf16[256,1024]{1,0:T(8,128)(2,1)S(1)} %pad_maximum_fusion.refs_0_), channel_id=1, source_target_pairs={{0,96},{32,0},{64,32},{96,64},{1,97},{33,1},{65,33},{97,65},{2,98}... | collective-permute-start | bytes 1572872 | tf_op jit(solution)/shard_map/ppermute | solution.py:24
  32.0 36.0 %collective-permute-start.5 = (bf16[512,4096]{1,0:T(8,128)(2,1)}, bf16[512,4096]{1,0:T(8,128)(2,1)}, u32[]{:S(2)}, u32[]{:S(2)}) collective-permute-start(bf16[512,4096]{1,0:T(8,128)(2,1)} %own_ref.3), channel_id=1, source_target_pairs={{0,4},{4,0},{1,5},{5,1},{2,6},{6,2},{3,7},{7,3},{8,12},{12,8},{9,1... | collective-permute-start | bytes 12582920 | tf_op jit(solution)/shard_map/ppermute | solution.py:19
  32.9 5.8 %collective-permute-start.6 = (bf16[16,4096]{1,0:T(8,128)(2,1)S(1)}, bf16[16,4096]{1,0:T(8,128)(2,1)S(1)}, u32[]{:S(2)}, u32[]{:S(2)}) collective-permute-start(bf16[16,4096]{1,0:T(8,128)(2,1)S(1)} %slice.4), channel_id=1, source_target_pairs={{4,8},{12,16},{20,24},{28,32},{36,40},{44,48},{52,56},{60,64},{68,... | collective-permute-start | bytes 393224 | tf_op jit(solution)/shard_map/ppermute | solution.py:641
  33.6 8.2 %collective-permute-start.7 = (bf16[16,4096]{1,0:T(8,128)(2,1)S(1)}, bf16[16,4096]{1,0:T(8,128)(2,1)}, u32[]{:S(2)}, u32[]{:S(2)}) collective-permute-start(bf16[16,4096]{1,0:T(8,128)(2,1)S(1)} %slice.4), channel_id=1, source_target_pairs={{4,12},{12,20},{20,28},{28,36},{36,44},{44,52},{52,60},{60,68},{68... | collective-permute-start | bytes 393224 | tf_op jit(solution)/shard_map/ppermute | solution.py:641
  34.9 20.4 %collective-permute-start.8 = (bf16[256,1024]{1,0:T(8,128)(2,1)S(1)}, bf16[256,1024]{1,0:T(8,128)(2,1)S(1)}, u32[]{:S(2)}, u32[]{:S(2)}) collective-permute-start(bf16[256,1024]{1,0:T(8,128)(2,1)S(1)} %collective-permute-done.1.refs_1_), channel_id=1, source_target_pairs={{0,8},{8,16},{16,24},{24,0},{1,9},{9,17},{17,25},{25,1},{2,10},{10... | collective-permute-start | bytes 1572872 | tf_op jit(solution)/shard_map/ppermute | solution.py:24
  35.8 19.6 %collective-permute-start.9 = (bf16[256,1024]{1,0:T(8,128)(2,1)S(1)}, bf16[256,1024]{1,0:T(8,128)(2,1)}, u32[]{:S(2)}, u32[]{:S(2)}) collective-permute-start(bf16[256,1024]{1,0:T(8,128)(2,1)S(1)} %collective-permute-done.4.refs_4_), channel_id=1, source_target_pairs={{0,96},{32,0},{64,32},{96,64},{1,97},{33,1},{65,33},{97,65},{2,98}... | collective-permute-start | bytes 1572872 | tf_op jit(solution)/shard_map/ppermute | solution.py:24
  38.7 20.5 %collective-permute-start.10 = (bf16[256,1024]{1,0:T(8,128)(2,1)S(1)}, bf16[256,1024]{1,0:T(8,128)(2,1)}, u32[]{:S(2)}, u32[]{:S(2)}) collective-permute-start(bf16[256,1024]{1,0:T(8,128)(2,1)S(1)} %collective-permute-done.4.refs_4_), channel_id=1, source_target_pairs={{0,24},{8,0},{16,8},{24,16},{1,25},{9,1},{17,9},{25,17},{2,26},{10... | collective-permute-start | bytes 1572872 | tf_op jit(solution)/shard_map/ppermute | solution.py:24
  41.7 20.5 %collective-permute-start.11 = (bf16[256,1024]{1,0:T(8,128)(2,1)S(1)}, bf16[256,1024]{1,0:T(8,128)(2,1)}, u32[]{:S(2)}, u32[]{:S(2)}) collective-permute-start(bf16[256,1024]{1,0:T(8,128)(2,1)S(1)} %collective-permute-done.2.refs_2_), channel_id=1, source_target_pairs={{0,32},{32,64},{64,96},{96,0},{1,33},{33,65},{65,97},{97,1},{2,34}... | collective-permute-start | bytes 1572872 | tf_op jit(solution)/shard_map/ppermute | solution.py:24
  62.3 17.4 %collective-permute-start.12 = (bf16[256,1024]{1,0:T(8,128)(2,1)}, bf16[256,1024]{1,0:T(8,128)(2,1)}, u32[]{:S(2)}, u32[]{:S(2)}) collective-permute-start(bf16[256,1024]{1,0:T(8,128)(2,1)} %collective-permute-done.9.refs_6_), channel_id=1, source_target_pairs={{0,24},{8,0},{16,8},{24,16},{1,25},{9,1},{17,9},{25,17},{2,26},{10... | collective-permute-start | bytes 1572872 | tf_op jit(solution)/shard_map/ppermute | solution.py:24
  63.0 18.5 %collective-permute-start.13 = (bf16[256,1024]{1,0:T(8,128)(2,1)}, bf16[256,1024]{1,0:T(8,128)(2,1)S(1)}, u32[]{:S(2)}, u32[]{:S(2)}) collective-permute-start(bf16[256,1024]{1,0:T(8,128)(2,1)} %collective-permute-done.9.refs_6_), channel_id=1, source_target_pairs={{0,8},{8,16},{16,24},{24,0},{1,9},{9,17},{17,25},{25,1},{2,10},{10... | collective-permute-start | bytes 1572872 | tf_op jit(solution)/shard_map/ppermute | solution.py:24
  64.8 18.6 %collective-permute-start.14 = (bf16[256,1024]{1,0:T(8,128)(2,1)S(1)}, bf16[256,1024]{1,0:T(8,128)(2,1)S(1)}, u32[]{:S(2)}, u32[]{:S(2)}) collective-permute-start(bf16[256,1024]{1,0:T(8,128)(2,1)S(1)} %collective-permute-done.8.refs_5_), channel_id=1, source_target_pairs={{0,32},{32,64},{64,96},{96,0},{1,33},{33,65},{65,97},{97,1},{2,34}... | collective-permute-start | bytes 1572872 | tf_op jit(solution)/shard_map/ppermute | solution.py:24
  65.2 20.1 %collective-permute-start.15 = (bf16[256,1024]{1,0:T(8,128)(2,1)S(1)}, bf16[256,1024]{1,0:T(8,128)(2,1)S(1)}, u32[]{:S(2)}, u32[]{:S(2)}) collective-permute-start(bf16[256,1024]{1,0:T(8,128)(2,1)S(1)} %collective-permute-done.8.refs_5_), channel_id=1, source_target_pairs={{0,96},{32,0},{64,32},{96,64},{1,97},{33,1},{65,33},{97,65},{2,98}... | collective-permute-start | bytes 1572872 | tf_op jit(solution)/shard_map/ppermute | solution.py:24
  86.1 22.6 %collective-permute-start.16 = (bf16[256,1024]{1,0:T(8,128)(2,1)S(1)}, bf16[256,1024]{1,0:T(8,128)(2,1)S(1)}, u32[]{:S(2)}, u32[]{:S(2)}) collective-permute-start(bf16[256,1024]{1,0:T(8,128)(2,1)S(1)} %collective-permute-done.3.refs_3_), channel_id=1, source_target_pairs={{0,8},{8,16},{16,24},{24,0},{1,9},{9,17},{17,25},{25,1},{2,10},{10... | collective-permute-start | bytes 1572872 | tf_op jit(solution)/shard_map/ppermute | solution.py:24
  89.0 19.7 %collective-permute-start.17 = (bf16[256,1024]{1,0:T(8,128)(2,1)S(1)}, bf16[256,1024]{1,0:T(8,128)(2,1)S(1)}, u32[]{:S(2)}, u32[]{:S(2)}) collective-permute-start(bf16[256,1024]{1,0:T(8,128)(2,1)S(1)} %collective-permute-done.1.refs_1_), channel_id=1, source_target_pairs={{0,96},{32,0},{64,32},{96,64},{1,97},{33,1},{65,33},{97,65},{2,98}... | collective-permute-start | bytes 1572872 | tf_op jit(solution)/shard_map/ppermute | solution.py:24
  92.6 16.6 %collective-permute-start.18 = (bf16[256,1024]{1,0:T(8,128)(2,1)}, bf16[256,1024]{1,0:T(8,128)(2,1)S(1)}, u32[]{:S(2)}, u32[]{:S(2)}) collective-permute-start(bf16[256,1024]{1,0:T(8,128)(2,1)} %collective-permute-done.12.refs_0_), channel_id=1, source_target_pairs={{0,24},{8,0},{16,8},{24,16},{1,25},{9,1},{17,9},{25,17},{2,26},{10... | collective-permute-start | bytes 1572872 | tf_op jit(solution)/shard_map/ppermute | solution.py:24
  124.7 18.1 %collective-permute-start.19 = (bf16[144,1024]{1,0:T(8,128)(2,1)S(1)}, bf16[144,1024]{1,0:T(8,128)(2,1)S(1)}, u32[]{:S(2)}, u32[]{:S(2)}) collective-permute-start(bf16[144,1024]{1,0:T(8,128)(2,1)S(1)} %get-tuple-element.48.refs_0_), channel_id=1, source_target_pairs={{0,8},{8,16},{16,24},{24,0},{1,9},{9,17},{17,25},{25,1},{2,10},{10... | collective-permute-start | bytes 884744 | tf_op jit(solution)/shard_map/ppermute | solution.py:24
  125.8 22.5 %collective-permute-start.20 = (bf16[144,1024]{1,0:T(8,128)(2,1)S(1)}, bf16[144,1024]{1,0:T(8,128)(2,1)S(1)}, u32[]{:S(2)}, u32[]{:S(2)}) collective-permute-start(bf16[144,1024]{1,0:T(8,128)(2,1)S(1)} %get-tuple-element.48.refs_0_), channel_id=1, source_target_pairs={{0,16},{8,24},{16,0},{24,8},{1,17},{9,25},{17,1},{25,9},{2,18},{10... | collective-permute-start | bytes 884744 | tf_op jit(solution)/shard_map/ppermute | solution.py:24
  130.0 18.4 %collective-permute-start.21 = (bf16[144,1024]{1,0:T(8,128)(2,1)S(1)}, bf16[144,1024]{1,0:T(8,128)(2,1)S(1)}, u32[]{:S(2)}, u32[]{:S(2)}) collective-permute-start(bf16[144,1024]{1,0:T(8,128)(2,1)S(1)} %get-tuple-element.48.refs_0_), channel_id=1, source_target_pairs={{0,24},{8,0},{16,8},{24,16},{1,25},{9,1},{17,9},{25,17},{2,26},{10... | collective-permute-start | bytes 884744 | tf_op jit(solution)/shard_map/ppermute | solution.py:24
  150.4 23.5 %collective-permute-start.22 = (bf16[144,1024]{1,0:T(8,128)(2,1)S(1)}, bf16[144,1024]{1,0:T(8,128)(2,1)S(1)}, u32[]{:S(2)}, u32[]{:S(2)}) collective-permute-start(bf16[144,1024]{1,0:T(8,128)(2,1)S(1)} %get-tuple-element.51), channel_id=1, source_target_pairs={{0,96},{1,97},{2,98},{3,99},{4,100},{5,101},{6,102},{7,103},{8,104... | collective-permute-start | bytes 884744 | tf_op jit(solution)/shard_map/ppermute | solution.py:571
  155.3 18.7 %collective-permute-start.23 = (bf16[144,1024]{1,0:T(8,128)(2,1)S(1)}, bf16[144,1024]{1,0:T(8,128)(2,1)S(1)}, u32[]{:S(2)}, u32[]{:S(2)}) collective-permute-start(bf16[144,1024]{1,0:T(8,128)(2,1)S(1)} %get-tuple-element.51), channel_id=1, source_target_pairs={{0,64},{32,96},{1,65},{33,97},{2,66},{34,98},{3,67},{35,99},{4,68}... | collective-permute-start | bytes 884744 | tf_op jit(solution)/shard_map/ppermute | solution.py:571
  156.6 17.4 %collective-permute-start.24 = (bf16[144,1024]{1,0:T(8,128)(2,1)S(1)}, bf16[144,1024]{1,0:T(8,128)(2,1)S(1)}, u32[]{:S(2)}, u32[]{:S(2)}) collective-permute-start(bf16[144,1024]{1,0:T(8,128)(2,1)S(1)} %get-tuple-element.51), channel_id=1, source_target_pairs={{0,32},{32,64},{64,96},{1,33},{33,65},{65,97},{2,34},{34,66},{66,9... | collective-permute-start | bytes 884744 | tf_op jit(solution)/shard_map/ppermute | solution.py:571
  184.0 11.9 %collective-permute-start.25 = (bf16[512,1024]{1,0:T(8,128)(2,1)}, bf16[512,1024]{1,0:T(8,128)(2,1)S(1)}, u32[]{:S(2)}, u32[]{:S(2)}) collective-permute-start(bf16[512,1024]{1,0:T(8,128)(2,1)} %get-tuple-element.53), channel_id=1, source_target_pairs={{0,4},{4,0},{1,5},{5,1},{2,6},{6,2},{3,7},{7,3},{8,12},{12,8},{9,1... | collective-permute-start | bytes 3145736 | tf_op jit(solution)/shard_map/ppermute | solution.py:19
  184.0 2.9 %collective-permute-start.26 = (f32[1,1024]{1,0:T(1,128)}, f32[1,1024]{1,0:T(1,128)S(1)}, u32[]{:S(2)}, u32[]{:S(2)}) collective-permute-start(f32[1,1024]{1,0:T(1,128)} %get-tuple-element.54), channel_id=1, source_target_pairs={{0,4},{4,0},{1,5},{5,1},{2,6},{6,2},{3,7},{7,3},{8,12},{12,8},{9,1... | collective-permute-start | bytes 12296 | tf_op jit(solution)/shard_map/ppermute | solution.py:19
  187.6 4.8 %collective-permute-start.29 = (f32[1,512]{1,0:T(1,128)S(1)}, f32[1,512]{1,0:T(1,128)S(1)}, u32[]{:S(2)}, u32[]{:S(2)}) collective-permute-start(f32[1,512]{1,0:T(1,128)S(1)} %dynamic-slice_add_fusion), channel_id=1, source_target_pairs={{0,3},{1,0},{2,1},{3,2},{4,7},{5,4},{6,5},{7,6},{8,11},{9,8},{10,9... | collective-permute-start | bytes 6152 | tf_op jit(solution)/shard_map/ppermute | solution.py:24
  188.4 3.9 %collective-permute-start.27 = (f32[1,512]{1,0:T(1,128)S(1)}, f32[1,512]{1,0:T(1,128)S(1)}, u32[]{:S(2)}, u32[]{:S(2)}) collective-permute-start(f32[1,512]{1,0:T(1,128)S(1)} %dynamic-slice_add_fusion), channel_id=1, source_target_pairs={{0,1},{1,2},{2,3},{3,0},{4,5},{5,6},{6,7},{7,4},{8,9},{9,10},{10,1... | collective-permute-start | bytes 6152 | tf_op jit(solution)/shard_map/ppermute | solution.py:24
  190.8 5.1 %collective-permute-start.28 = (f32[1,512]{1,0:T(1,128)S(1)}, f32[1,512]{1,0:T(1,128)S(1)}, u32[]{:S(2)}, u32[]{:S(2)}) collective-permute-start(f32[1,512]{1,0:T(1,128)S(1)} %dynamic-slice_add_fusion), channel_id=1, source_target_pairs={{0,2},{1,3},{2,0},{3,1},{4,6},{5,7},{6,4},{7,5},{8,10},{9,11},{10,... | collective-permute-start | bytes 6152 | tf_op jit(solution)/shard_map/ppermute | solution.py:24
  (24 other events, 369.2 us)
Sparse Core Ops, SparseCore 0:
  9.6 50.7 all-gather.4
  62.6 85.9 all-gather.2

commit v9 on v8

--- a/solution.py
+++ b/solution.py
@@ -36,15 +36,20 @@
 
 
 def expand_heads(values, width):
-    high = values.astype(BF16)
-    rest = values - high.astype(F32)
-    middle = rest.astype(BF16)
-    low = (rest - middle.astype(F32)).astype(BF16)
+    heads = width // HEAD
+    high = values.astype(BF16).astype(F32)
+    rest = values - high
+    middle = rest.astype(BF16).astype(F32)
+    low = rest - middle
+    lane = lax.broadcasted_iota(jnp.int32, values.shape, 1)
+    parts = jnp.where(lane < heads, high, pltpu.roll(middle, heads, axis=1))
+    parts = jnp.where(lane < 2 * heads, parts, pltpu.roll(low, 2 * heads, axis=1))
+    parts = jnp.where(lane < 3 * heads, parts, 0.0).astype(BF16)
     row = lax.broadcasted_iota(jnp.int32, (LANES, width), 0)
     col = lax.broadcasted_iota(jnp.int32, (LANES, width), 1)
-    spread = ((col >= row * HEAD) & (col < row * HEAD + HEAD)).astype(BF16)
-    dot = lambda part: jnp.dot(part, spread, preferred_element_type=F32)
-    return dot(high) + dot(middle) + dot(low)
+    head = row % heads
+    spread = (col >= head * HEAD) & (col < head * HEAD + HEAD) & (row < 3 * heads)
+    return jnp.dot(parts, spread.astype(BF16), preferred_element_type=F32)
 
 
 def silu(a):
@@ -125,26 +130,33 @@
     return jnp.concatenate([refs[ref][first : first + size, :] for ref, first, size in sources], axis=0)
 
 
-def first_kernel(sources, count, place_ref, own_ref, other_ref, before_ref, *refs):
-    weights, (out_ref, out_before_ref) = refs[:-2], refs[-2:]
+def products_kernel(sources, done, count, started, place_ref, own_ref, other_ref, before_ref, *refs):
+    weights, sums, (out_ref, out_before_ref, wide) = refs[: -3 - 2 * started], refs[-3 - 2 * started : -3], refs[-3:]
     block = pl.program_id(0)
     is_own = block // 2 == place_ref[0]
 
     def product(ref):
-        columns = block_columns(ref, place_ref, 0, count)
-        return jnp.dot(columns, stacked(sources, weights), preferred_element_type=F32)
+        columns = block_columns(ref, place_ref, done, count)
+        return jnp.dot(columns, wide[...], preferred_element_type=F32)
 
     @pl.when(block == 0)
     def _():
-        out_before_ref[...] = product(before_ref)
+        row = 0
+        for ref, first, size in sources:
+            wide[row : row + size, :] = weights[ref][first : first + size, :]
+            row += size
+        added = product(before_ref)
+        out_before_ref[...] = sums[1][...] + added if started else added
 
     @pl.when(is_own)
     def _():
-        out_ref[...] = product(own_ref)
+        added = product(own_ref)
+        out_ref[...] = sums[0][...] + added if started else added
 
     @pl.when(jnp.logical_not(is_own))
     def _():
-        out_ref[...] = product(other_ref)
+        added = product(other_ref)
+        out_ref[...] = sums[0][...] + added if started else added
 
 
 def states_kernel(
@@ -407,24 +419,29 @@
     )(place, *slabs, weight, conv_bc, bias, rate)
 
 
-def first_products(place, slabs, weights, sources, count):
+def products(place, slabs, weights, done, sums=()):
     own, other, before = slabs
-    width = weights[0].shape[1]
+    width, count = weights[0].shape[1], len(weights)
     outs = [
         jax.ShapeDtypeStruct((2 * own.shape[0], width), F32), jax.ShapeDtypeStruct((HALO, width), F32),
     ]
+    specs = [row_block(width), fixed(outs[1])]
+    sources = all_rows(weights)
     return pl.pallas_call(
-        functools.partial(first_kernel, sources, count),
+        functools.partial(products_kernel, sources, done, count, len(sums) // 2),
         grid_spec=pltpu.PrefetchScalarGridSpec(
             num_scalar_prefetch=1,
             grid=(2 * own.shape[0] // GROUP,),
-            in_specs=slab_blocks(own.shape[1]) + [fixed(a) for a in (before, *weights)],
-            out_specs=[row_block(width), fixed(outs[1])],
+            in_specs=slab_blocks(own.shape[1])
+            + [fixed(a) for a in (before, *weights)]
+            + specs[: len(sums)],
+            out_specs=specs,
+            scratch_shapes=[pltpu.VMEM((sum(size for _, _, size in sources), width), BF16)],
         ),
         out_shape=outs,
-        name="first_products",
-        **params(6e9, 18, 48),
-    )(place, *slabs, *weights)
+        name="more_products" if sums else "first_products",
+        **params(5e9, 16, 48),
+    )(place, *slabs, *weights, *sums)
 
 
 def local_states(place, slabs, weights, sources, done, count, sums, bcc, weights_in, decays, conv_x):
@@ -578,21 +595,22 @@
     return lax.optimization_barrier((*values, *to))[: len(values)]
 
 
-def travelling(own, after_first, before_last):
+def travelling(own, before_third, before_last):
     y_less, y_more = round_ring(own, "y", 1), round_ring(own, "y", -1)
     z_less, z_more = round_ring(own, "z", 1), round_ring(own, "z", -1)
-    after_first([y_less, y_more, z_less, z_more])
-    y_far, z_far = round_ring(y_less, "y", 1), round_ring(z_more, "z", -1)
-    more_more, more_less = round_ring(z_more, "y", -1), round_ring(y_more, "z", 1)
-    y_far, z_far = tied((y_far, z_far), more_more, more_less)
+    nearest = [own, y_less, y_more, z_less, z_more]
+    second = [
+        round_ring(y_less, "y", 1), round_ring(z_more, "z", -1),
+        round_ring(z_more, "y", -1), round_ring(y_more, "z", 1),
+    ]
+    y_far, z_far, *_ = tied(second, *before_third(nearest))
     far = [
         round_ring(z_far, "y", -1), round_ring(z_far, "y", 1),
         round_ring(y_far, "z", 1), round_ring(y_far, "z", -1),
     ]
-    early = [own, y_less, y_more, z_less, z_more, y_far, z_far, more_more, more_less]
-    held_z, held_y, last, *_ = tied((z_less, y_less, *far), *before_last(early))
+    held_z, held_y, last, *_ = tied((z_less, y_less, *far), *before_last())
     less_less, less_more = round_ring(held_z, "y", 1), round_ring(held_y, "z", -1)
-    return [*far, less_less, less_more, round_ring(last, "y", -1)]
+    return nearest, second, [*far, less_less, less_more, round_ring(last, "y", -1)]
 
 
 def all_rows(blocks):
@@ -633,27 +651,30 @@
     narrow = lax.all_gather(narrow, ("z", "y", "core"), axis=0, tiled=True)
     own_block = jnp.concatenate([mine(x_weight, 1), swap_cores(others(x_weight, 1))], axis=0)
     place = jnp.stack([core, *block_order()]).astype(jnp.int32)
-    slabs, sums = [], []
-
-    def after_first(blocks):
-        (rows,) = tied((tokens,), *blocks)
+    slabs, sums, early = [], [], []
+
+    def before_third(blocks):
+        (rows,) = tied((tokens,), *blocks[1:])
         chips = lax.axis_size("z") * lax.axis_size("y")
         to_next = lambda target: lax.ppermute(
             rows[-HALO:], ("z", "y", "core"),
             [(2 * i + 1, 2 * i + 2 + target) for i in range(chips - 1)],
         )
         slabs.extend((rows, swap_cores(rows), to_next(0) + to_next(1)))
-
-    def before_last(blocks):
-        sums.extend(first_products(place, slabs, blocks, all_rows(blocks), len(blocks)))
+        sums.extend(products(place, slabs, blocks, 0))
         return sums[:1]
 
-    blocks = travelling(own_block, after_first, before_last)
+    def before_last():
+        early.extend(
+            prepared(place, slabs, narrow, conv_bc, per_lane(dt_bias), per_lane(decay_rate), heads)
+        )
+        return early[:1]
+
+    nearest, second, blocks = travelling(own_block, before_third, before_last)
     (z_rows,) = tied((z_weight,), own_block)
     z_whole = lax.all_gather(z_rows, ("z", "y", "core"), axis=0, tiled=True)
-    bcc, cum, cum_slab, cum_t, step_t, weights_in, decays = prepared(
-        place, slabs, narrow, conv_bc, per_lane(dt_bias), per_lane(decay_rate), heads
-    )
+    sums = products(place, slabs, second, len(nearest), sums)
+    bcc, cum, cum_slab, cum_t, step_t, weights_in, decays = early
     xc, entering, final = local_states(
         place, slabs, blocks, all_rows(blocks), 9, 7, sums, bcc, weights_in, decays, mine(conv_x, 1)
     )

time: 207 us -> 204 us (0.986)
  waiting for transfers between devices: 53.9 us -> 45.9 us
  Pallas kernels: 70.7 us -> 77.3 us
    ppermute x21, waiting for transfers between devices: 49.9 us -> 42 us  [round_ring(): lax.ppermute(a, axis, [(i, (i + distance) % size) for i in range(size)])]
    pallas_call x1 -> x2, Pallas kernels: 11.2 us -> 19.2 us  [products(): pl.pallas_call(functools.partial(products_kernel, sources, done, count, l...]
    unnamed x49 -> x45, local copies, waits for them, and re-layouts: 12.2 us -> 11.4 us
  transfers between devices with their start and end apart: 32 -> 32, of which waited for: 17 -> 14; matrix products, arithmetic and copies ran while one was open for 2% -> 3% of each run, Pallas kernels for 29% -> 33%
where the time goes in v9:
time: 204 us
  Pallas kernels  77.3 us (38%)
  starting transfers between devices  48.2 us (24%)
  waiting for transfers between devices  45.9 us (22%)
  local copies, waits for them, and re-layouts  15.2 us (7%)
  between operations  13.7 us (7%)
  other arithmetic  3.18 us (2%)
    ppermute x21, waiting for transfers between devices, round_ring(): lax.ppermute(a, axis, [(i, (i + distance) % size) for i in range(size)])  42 us
    ppermute x21, starting transfers between devices, round_ring(): lax.ppermute(a, axis, [(i, (i + distance) % size) for i in range(size)])  37.9 us
    pallas_call x2, Pallas kernels, products(): pl.pallas_call(functools.partial(products_kernel, sources, done, count, l...  19.2 us
    pallas_call x1, Pallas kernels, local_states(): pl.pallas_call(functools.partial(states_kernel, sources, done, count), gr...  15.4 us
    pallas_call x1, Pallas kernels, project_gate(): pl.pallas_call(z_kernel, grid_spec=pltpu.PrefetchScalarGridSpec(num_scala...  13 us
    pallas_call x1, Pallas kernels, prepared(): pl.pallas_call(prepare_kernel, grid_spec=pltpu.PrefetchScalarGridSpec(num...  12.2 us
    unnamed x45, local copies, waits for them, and re-layouts  11.4 us
    pallas_call x1, Pallas kernels, gate_outputs(): pl.pallas_call(gate_kernel, grid_spec=pltpu.PrefetchScalarGridSpec(num_sc...  8.02 us
  transfers between devices with their start and end apart: 32, of which 14 were waited for; matrix products, arithmetic and copies ran while one was open for 3% of the time, Pallas kernels for 33%

profile of v9, /device:TPU:6, one launch (start us, length us, event | category | flops | bytes accessed | tf_op | source)
XLA Modules:
  0.0 203.6 jit_solution(3211584789485280820)
XLA Ops:
  11.8 1.6 collective-permute-start.1
  13.4 1.7 collective-permute-start.2
  15.1 1.9 collective-permute-start.3
  17.0 2.1 %collective-permute-start.4 = (bf16[256,1024]{1,0:T(8,128)(2,1)S(1)}, bf16[256,1024]{1,0:T(8,128)(2,1)}, u32[]{:S(2)}, u32[]{:S(2)}) collective-permute-start(bf16[256,1024]{1,0:T(8,128)(2,1)S(1)} %pad_maximum_fusion.refs_0_), channel_id=1, source_target_pairs={{0,96},{32,0},{64,32},{96,64},{1,97},{33,1},{65,33},{97,65},{2,98}... | collective-permute-start | bytes 1572872 | tf_op jit(solution)/shard_map/ppermute | solution.py:24
  19.1 8.5 %collective-permute-done.1.refs_1_ = bf16[256,1024]{1,0:T(8,128)(2,1)S(1)} collective-permute-done((bf16[256,1024]{1,0:T(8,128)(2,1)S(1)}, bf16[256,1024]{1,0:T(8,128)(2,1)S(1)}, u32[]{:S(2)}, u32[]{:S(2)}) %collective-permute-start.1) | collective-permute-done | bytes 524320 | tf_op jit(solution)/shard_map/ppermute | solution.py:24
  27.8 4.2 %collective-permute-done.3.refs_3_ = bf16[256,1024]{1,0:T(8,128)(2,1)S(1)} collective-permute-done((bf16[256,1024]{1,0:T(8,128)(2,1)S(1)}, bf16[256,1024]{1,0:T(8,128)(2,1)S(1)}, u32[]{:S(2)}, u32[]{:S(2)}) %collective-permute-start.3) | collective-permute-done | bytes 524320 | tf_op jit(solution)/shard_map/ppermute | solution.py:24
  35.7 3.1 %collective-permute-start.9 = (bf16[256,1024]{1,0:T(8,128)(2,1)}, bf16[256,1024]{1,0:T(8,128)(2,1)S(1)}, u32[]{:S(2)}, u32[]{:S(2)}) collective-permute-start(bf16[256,1024]{1,0:T(8,128)(2,1)} %collective-permute-done.4.refs_4_), channel_id=1, source_target_pairs={{0,96},{32,0},{64,32},{96,64},{1,97},{33,1},{65,33},{97,65},{2,98}... | collective-permute-start | bytes 1572872 | tf_op jit(solution)/shard_map/ppermute | solution.py:24
  38.8 3.0 %collective-permute-start.10 = (bf16[256,1024]{1,0:T(8,128)(2,1)}, bf16[256,1024]{1,0:T(8,128)(2,1)S(1)}, u32[]{:S(2)}, u32[]{:S(2)}) collective-permute-start(bf16[256,1024]{1,0:T(8,128)(2,1)} %collective-permute-done.4.refs_4_), channel_id=1, source_target_pairs={{0,24},{8,0},{16,8},{24,16},{1,25},{9,1},{17,9},{25,17},{2,26},{10... | collective-permute-start | bytes 1572872 | tf_op jit(solution)/shard_map/ppermute | solution.py:24
  41.8 2.3 %collective-permute-start.11 = (bf16[256,1024]{1,0:T(8,128)(2,1)}, bf16[256,1024]{1,0:T(8,128)(2,1)}, u32[]{:S(2)}, u32[]{:S(2)}) collective-permute-start(bf16[256,1024]{1,0:T(8,128)(2,1)} %collective-permute-done.2.refs_2_), channel_id=1, source_target_pairs={{0,32},{32,64},{64,96},{96,0},{1,33},{33,65},{65,97},{97,1},{2,34}... | collective-permute-start | bytes 1572872 | tf_op jit(solution)/shard_map/ppermute | solution.py:24
  45.2 9.4 %first_products.1 = (f32[1024,1024]{1,0:T(8,128)}, f32[16,1024]{1,0:T(8,128)S(1)}) custom-call(s32[17]{0:T(128)S(1)} %stack.68.place_ref, bf16[512,4096]{1,0:T(8,128)(2,1)} %own_ref.4, bf16[512,4096]{1,0:T(8,128)(2,1)} %collective-permute-done.5.other_ref, bf16[16,4096]{1,0:T(8,128)(2,1)S(1)} %add.199.before_ref, ...), custom_call_target="tpu_custom_call" | custom-call | flops 5000000000 | bytes 16777216 | tf_op jit(solution)/shard_map/first_products/pallas_call | solution.py:430
  55.1 4.3 %collective-permute-done.10.refs_2_ = bf16[256,1024]{1,0:T(8,128)(2,1)S(1)} collective-permute-done((bf16[256,1024]{1,0:T(8,128)(2,1)}, bf16[256,1024]{1,0:T(8,128)(2,1)S(1)}, u32[]{:S(2)}, u32[]{:S(2)}) %collective-permute-start.10) | collective-permute-done | bytes 524320 | tf_op jit(solution)/shard_map/ppermute | solution.py:24
  59.3 2.9 %collective-permute-done.11.refs_3_ = bf16[256,1024]{1,0:T(8,128)(2,1)} collective-permute-done((bf16[256,1024]{1,0:T(8,128)(2,1)}, bf16[256,1024]{1,0:T(8,128)(2,1)}, u32[]{:S(2)}, u32[]{:S(2)}) %collective-permute-start.11) | collective-permute-done | bytes 524320 | tf_op jit(solution)/shard_map/ppermute | solution.py:24
  65.1 3.0 %collective-permute-start.15 = (bf16[256,1024]{1,0:T(8,128)(2,1)S(1)}, bf16[256,1024]{1,0:T(8,128)(2,1)}, u32[]{:S(2)}, u32[]{:S(2)}) collective-permute-start(bf16[256,1024]{1,0:T(8,128)(2,1)S(1)} %collective-permute-done.8.refs_0_), channel_id=1, source_target_pairs={{0,96},{32,0},{64,32},{96,64},{1,97},{33,1},{65,33},{97,65},{2,98}... | collective-permute-start | bytes 1572872 | tf_op jit(solution)/shard_map/ppermute | solution.py:24
  68.2 1.9 copy-done.10
  70.1 12.2 %prepared.1 = (bf16[1024,256]{1,0:T(8,128)(2,1)S(1)}, f32[1024,128]{1,0:T(8,128)S(1)}, f32[1024,128]{1,0:T(8,128)S(1)}, f32[16,1024]{1,0:T(8,128)S(1)}, f32[16,1...) custom-call(s32[17]{0:T(128)S(1)} %stack.68.place_ref, bf16[512,4096]{1,0:T(8,128)(2,1)} %own_ref.4, ...), custom_call_target="tpu_custom_call" | custom-call | flops 4000000000 | bytes 14680064 | tf_op jit(solution)/shard_map/prepared/pallas_call | solution.py:405
  85.6 2.5 %collective-permute-start.16 = (bf16[256,1024]{1,0:T(8,128)(2,1)S(1)}, bf16[256,1024]{1,0:T(8,128)(2,1)}, u32[]{:S(2)}, u32[]{:S(2)}) collective-permute-start(bf16[256,1024]{1,0:T(8,128)(2,1)S(1)} %collective-permute-done.3.refs_3_), channel_id=1, source_target_pairs={{0,8},{8,16},{16,24},{24,0},{1,9},{9,17},{17,25},{25,1},{2,10},{10... | collective-permute-start | bytes 1572872 | tf_op jit(solution)/shard_map/ppermute | solution.py:24
  88.0 3.8 %collective-permute-start.17 = (bf16[256,1024]{1,0:T(8,128)(2,1)S(1)}, bf16[256,1024]{1,0:T(8,128)(2,1)}, u32[]{:S(2)}, u32[]{:S(2)}) collective-permute-start(bf16[256,1024]{1,0:T(8,128)(2,1)S(1)} %collective-permute-done.1.refs_1_), channel_id=1, source_target_pairs={{0,96},{32,0},{64,32},{96,64},{1,97},{33,1},{65,33},{97,65},{2,98}... | collective-permute-start | bytes 1572872 | tf_op jit(solution)/shard_map/ppermute | solution.py:24
  94.1 9.7 %more_products.1 = (f32[1024,1024]{1,0:T(8,128)}, f32[16,1024]{1,0:T(8,128)S(1)}) custom-call(s32[17]{0:T(128)S(1)} %stack.68.place_ref, bf16[512,4096]{1,0:T(8,128)(2,1)} %own_ref.4, bf16[512,4096]{1,0:T(8,128)(2,1)} %collective-permute-done.5.other_ref, bf16[16,4096]{1,0:T(8,128)(2,1)S(1)} %add.199.before_ref, ...), custom_call_target="tpu_custom_call" | custom-call | flops 5000000000 | bytes 16777216 | tf_op jit(solution)/shard_map/more_products/pallas_call | solution.py:430
  103.9 3.9 %collective-permute-done.18.refs_6_ = bf16[256,1024]{1,0:T(8,128)(2,1)} collective-permute-done((bf16[256,1024]{1,0:T(8,128)(2,1)}, bf16[256,1024]{1,0:T(8,128)(2,1)}, u32[]{:S(2)}, u32[]{:S(2)}) %collective-permute-start.18) | collective-permute-done | bytes 524320 | tf_op jit(solution)/shard_map/ppermute | solution.py:24
  107.8 15.4 %states.1 = (bf16[1024,1024]{1,0:T(8,128)(2,1)S(1)}, bf16[4,128,1024]{2,1,0:T(8,128)(2,1)S(1)}, bf16[144,1024]{1,0:T(8,128)(2,1)S(1)}) custom-call(s32[17]{0:T(128)S(1)} %stack.68.place_ref, bf16[512,4096]{1,0:T(8,128)(2,1)S(1)} %copy-done.9, bf16[512,4096]{1,0:T(8,128)(2,1)} %collective-permute-done.5.other_ref, bf16[16,4096]{1,0:T(8,128)(2,1)S(1)} %add.199.before_ref, ...), custom_call_target="tpu_custom_call" | custom-call | flops 11000000512 | bytes 18874368 | tf_op jit(solution)/shard_map/states/pallas_call | solution.py:456
  123.3 5.0 %collective-permute-start.20 = (bf16[144,1024]{1,0:T(8,128)(2,1)S(1)}, bf16[144,1024]{1,0:T(8,128)(2,1)S(1)}, u32[]{:S(2)}, u32[]{:S(2)}) collective-permute-start(bf16[144,1024]{1,0:T(8,128)(2,1)S(1)} %get-tuple-element.52.refs_0_), channel_id=1, source_target_pairs={{0,16},{8,24},{16,0},{24,8},{1,17},{9,25},{17,1},{25,9},{2,18},{10... | collective-permute-start | bytes 884744 | tf_op jit(solution)/shard_map/ppermute | solution.py:24
  128.3 7.1 %outputs.1.local_ref = bf16[1024,1024]{1,0:T(8,128)(2,1)S(1)} custom-call(bf16[1024,1024]{1,0:T(8,128)(2,1)S(1)} %get-tuple-element.46.xc_ref, bf16[1024,256]{1,0:T(8,128)(2,1)S(1)} %get-tuple-element.37.refs_9_.bcc_ref, f32[1024,128]{1,0:T(8,128)S(1)} %copy-done.13, f32[16,1024]{1,0:T(8,128)S(1)} %get-tuple-element.48.cum_t_ref, ...), custom_call_target="tpu_custom_call" | custom-call | flops 10000000000 | bytes 10485760 | tf_op jit(solution)/shard_map/outputs/pallas_call | solution.py:488
  136.9 4.6 %collective-permute-done.19.refs_1_ = bf16[144,1024]{1,0:T(8,128)(2,1)S(1)} collective-permute-done((bf16[144,1024]{1,0:T(8,128)(2,1)S(1)}, bf16[144,1024]{1,0:T(8,128)(2,1)S(1)}, u32[]{:S(2)}, u32[]{:S(2)}) %collective-permute-start.19) | collective-permute-done | bytes 294944 | tf_op jit(solution)/shard_map/ppermute | solution.py:24
  141.4 7.2 %collective-permute-done.20.refs_2_ = bf16[144,1024]{1,0:T(8,128)(2,1)S(1)} collective-permute-done((bf16[144,1024]{1,0:T(8,128)(2,1)S(1)}, bf16[144,1024]{1,0:T(8,128)(2,1)S(1)}, u32[]{:S(2)}, u32[]{:S(2)}) %collective-permute-start.20) | collective-permute-done | bytes 294944 | tf_op jit(solution)/shard_map/ppermute | solution.py:24
  150.6 3.4 %collective-permute-start.22 = (bf16[144,1024]{1,0:T(8,128)(2,1)S(1)}, bf16[144,1024]{1,0:T(8,128)(2,1)S(1)}, u32[]{:S(2)}, u32[]{:S(2)}) collective-permute-start(bf16[144,1024]{1,0:T(8,128)(2,1)S(1)} %get-tuple-element.55), channel_id=1, source_target_pairs={{0,96},{1,97},{2,98},{3,99},{4,100},{5,101},{6,102},{7,103},{8,104... | collective-permute-start | bytes 884744 | tf_op jit(solution)/shard_map/ppermute | solution.py:588
  155.3 3.0 %collective-permute-start.24 = (bf16[144,1024]{1,0:T(8,128)(2,1)S(1)}, bf16[144,1024]{1,0:T(8,128)(2,1)S(1)}, u32[]{:S(2)}, u32[]{:S(2)}) collective-permute-start(bf16[144,1024]{1,0:T(8,128)(2,1)S(1)} %get-tuple-element.55), channel_id=1, source_target_pairs={{0,32},{32,64},{64,96},{1,33},{33,65},{65,97},{2,34},{34,66},{66,9... | collective-permute-start | bytes 884744 | tf_op jit(solution)/shard_map/ppermute | solution.py:588
  158.3 13.0 %project_gate.1.gate_ref = bf16[1024,1024]{1,0:T(8,128)(2,1)S(1)} custom-call(s32[17]{0:T(128)S(1)} %stack.68.place_ref, bf16[512,4096]{1,0:T(8,128)(2,1)} %own_ref.4, bf16[512,4096]{1,0:T(8,128)(2,1)} %collective-permute-done.5.other_ref, bf16[4096,2048]{1,0:T(8,128)(2,1)} %all-gather.3.cloned.1.call-done.weight_ref), custom_call_target="tpu_custom_call" | custom-call | flops 8999999488 | bytes 20971520 | tf_op jit(solution)/shard_map/project_gate/pallas_call | solution.py:509
  173.7 8.0 %gate.1 = (bf16[512,1024]{1,0:T(8,128)(2,1)}, bf16[512,1024]{1,0:T(8,128)(2,1)}, f32[1,1024]{1,0:T(1,128)}) custom-call(s32[1]{0:T(128)} %bitcast.core_ref, bf16[1024,1024]{1,0:T(8,128)(2,1)} %copy-done.2, bf16[1024,1024]{1,0:T(8,128)(2,1)} %copy-done.1, bf16[1024,256]{1,0:T(8,128)(2,1)} %copy-done.4, f32[1024,128]{1,0:T(8,128)} %copy-done.5, ...), custom_call_target="tpu_custom_call" | custom-call | flops 1000000000 | bytes 10485760 | tf_op jit(solution)/shard_map/gate/pallas_call | solution.py:527
  182.2 2.4 %collective-permute-done.26 = f32[1,1024]{1,0:T(1,128)S(1)} collective-permute-done((f32[1,1024]{1,0:T(1,128)}, f32[1,1024]{1,0:T(1,128)S(1)}, u32[]{:S(2)}, u32[]{:S(2)}) %collective-permute-start.26) | collective-permute-done | bytes 4128 | tf_op jit(solution)/shard_map/ppermute | solution.py:19
  186.2 2.3 %collective-permute-start.27 = (f32[1,512]{1,0:T(1,128)S(1)}, f32[1,512]{1,0:T(1,128)S(1)}, u32[]{:S(2)}, u32[]{:S(2)}) collective-permute-start(f32[1,512]{1,0:T(1,128)S(1)} %dynamic-slice_add_fusion), channel_id=1, source_target_pairs={{0,1},{1,2},{2,3},{3,0},{4,5},{5,6},{6,7},{7,4},{8,9},{9,10},{10,1... | collective-permute-start | bytes 6152 | tf_op jit(solution)/shard_map/ppermute | solution.py:24
  190.1 3.5 %collective-permute-done.28 = f32[1,512]{1,0:T(1,128)S(1)} collective-permute-done((f32[1,512]{1,0:T(1,128)S(1)}, f32[1,512]{1,0:T(1,128)S(1)}, u32[]{:S(2)}, u32[]{:S(2)}) %collective-permute-start.28) | collective-permute-done | bytes 2080 | tf_op jit(solution)/shard_map/ppermute | solution.py:24
  194.8 1.9 normalized.1
  (105 shorter events, 31.1 us)
Async XLA Ops:
  6.5 61.7 %all-gather.5.cloned.1.call-start = ((), (), s32[]{:S(2)}) async-start(), calls=%async_computation.1 | async-start | bytes 3244032 | tf_op jit(solution)/shard_map/all_gather | solution.py:651
  9.0 149.4 %all-gather.3.cloned.1.call-start = ((), (), s32[]{:S(2)}) async-start(), calls=%async_computation | async-start | bytes 17301504 | tf_op jit(solution)/shard_map/all_gather | solution.py:675
  10.1 1.6 collective-permute-start
  11.8 15.8 %collective-permute-start.1 = (bf16[256,1024]{1,0:T(8,128)(2,1)S(1)}, bf16[256,1024]{1,0:T(8,128)(2,1)S(1)}, u32[]{:S(2)}, u32[]{:S(2)}) collective-permute-start(bf16[256,1024]{1,0:T(8,128)(2,1)S(1)} %pad_maximum_fusion.refs_0_), channel_id=1, source_target_pairs={{0,8},{8,16},{16,24},{24,0},{1,9},{9,17},{17,25},{25,1},{2,10},{10... | collective-permute-start | bytes 1572872 | tf_op jit(solution)/shard_map/ppermute | solution.py:24
  13.4 14.3 %collective-permute-start.2 = (bf16[256,1024]{1,0:T(8,128)(2,1)S(1)}, bf16[256,1024]{1,0:T(8,128)(2,1)}, u32[]{:S(2)}, u32[]{:S(2)}) collective-permute-start(bf16[256,1024]{1,0:T(8,128)(2,1)S(1)} %pad_maximum_fusion.refs_0_), channel_id=1, source_target_pairs={{0,24},{8,0},{16,8},{24,16},{1,25},{9,1},{17,9},{25,17},{2,26},{10... | collective-permute-start | bytes 1572872 | tf_op jit(solution)/shard_map/ppermute | solution.py:24
  15.1 16.9 %collective-permute-start.3 = (bf16[256,1024]{1,0:T(8,128)(2,1)S(1)}, bf16[256,1024]{1,0:T(8,128)(2,1)S(1)}, u32[]{:S(2)}, u32[]{:S(2)}) collective-permute-start(bf16[256,1024]{1,0:T(8,128)(2,1)S(1)} %pad_maximum_fusion.refs_0_), channel_id=1, source_target_pairs={{0,32},{32,64},{64,96},{96,0},{1,33},{33,65},{65,97},{97,1},{2,34}... | collective-permute-start | bytes 1572872 | tf_op jit(solution)/shard_map/ppermute | solution.py:24
  17.0 15.0 %collective-permute-start.4 = (bf16[256,1024]{1,0:T(8,128)(2,1)S(1)}, bf16[256,1024]{1,0:T(8,128)(2,1)}, u32[]{:S(2)}, u32[]{:S(2)}) collective-permute-start(bf16[256,1024]{1,0:T(8,128)(2,1)S(1)} %pad_maximum_fusion.refs_0_), channel_id=1, source_target_pairs={{0,96},{32,0},{64,32},{96,64},{1,97},{33,1},{65,33},{97,65},{2,98}... | collective-permute-start | bytes 1572872 | tf_op jit(solution)/shard_map/ppermute | solution.py:24
  32.0 13.2 %collective-permute-start.5 = (bf16[512,4096]{1,0:T(8,128)(2,1)}, bf16[512,4096]{1,0:T(8,128)(2,1)}, u32[]{:S(2)}, u32[]{:S(2)}) collective-permute-start(bf16[512,4096]{1,0:T(8,128)(2,1)} %own_ref.4), channel_id=1, source_target_pairs={{0,4},{4,0},{1,5},{5,1},{2,6},{6,2},{3,7},{7,3},{8,12},{12,8},{9,1... | collective-permute-start | bytes 12582920 | tf_op jit(solution)/shard_map/ppermute | solution.py:19
  32.9 5.9 %collective-permute-start.6 = (bf16[16,4096]{1,0:T(8,128)(2,1)S(1)}, bf16[16,4096]{1,0:T(8,128)(2,1)S(1)}, u32[]{:S(2)}, u32[]{:S(2)}) collective-permute-start(bf16[16,4096]{1,0:T(8,128)(2,1)S(1)} %slice.4), channel_id=1, source_target_pairs={{4,8},{12,16},{20,24},{28,32},{36,40},{44,48},{52,56},{60,64},{68,... | collective-permute-start | bytes 393224 | tf_op jit(solution)/shard_map/ppermute | solution.py:659
  33.6 8.2 %collective-permute-start.7 = (bf16[16,4096]{1,0:T(8,128)(2,1)S(1)}, bf16[16,4096]{1,0:T(8,128)(2,1)}, u32[]{:S(2)}, u32[]{:S(2)}) collective-permute-start(bf16[16,4096]{1,0:T(8,128)(2,1)S(1)} %slice.4), channel_id=1, source_target_pairs={{4,12},{12,20},{20,28},{28,36},{36,44},{44,52},{52,60},{60,68},{68... | collective-permute-start | bytes 393224 | tf_op jit(solution)/shard_map/ppermute | solution.py:659
  34.9 20.2 %collective-permute-start.8 = (bf16[256,1024]{1,0:T(8,128)(2,1)S(1)}, bf16[256,1024]{1,0:T(8,128)(2,1)S(1)}, u32[]{:S(2)}, u32[]{:S(2)}) collective-permute-start(bf16[256,1024]{1,0:T(8,128)(2,1)S(1)} %collective-permute-done.1.refs_1_), channel_id=1, source_target_pairs={{0,8},{8,16},{16,24},{24,0},{1,9},{9,17},{17,25},{25,1},{2,10},{10... | collective-permute-start | bytes 1572872 | tf_op jit(solution)/shard_map/ppermute | solution.py:24
  35.7 19.3 %collective-permute-start.9 = (bf16[256,1024]{1,0:T(8,128)(2,1)}, bf16[256,1024]{1,0:T(8,128)(2,1)S(1)}, u32[]{:S(2)}, u32[]{:S(2)}) collective-permute-start(bf16[256,1024]{1,0:T(8,128)(2,1)} %collective-permute-done.4.refs_4_), channel_id=1, source_target_pairs={{0,96},{32,0},{64,32},{96,64},{1,97},{33,1},{65,33},{97,65},{2,98}... | collective-permute-start | bytes 1572872 | tf_op jit(solution)/shard_map/ppermute | solution.py:24
  38.8 20.5 %collective-permute-start.10 = (bf16[256,1024]{1,0:T(8,128)(2,1)}, bf16[256,1024]{1,0:T(8,128)(2,1)S(1)}, u32[]{:S(2)}, u32[]{:S(2)}) collective-permute-start(bf16[256,1024]{1,0:T(8,128)(2,1)} %collective-permute-done.4.refs_4_), channel_id=1, source_target_pairs={{0,24},{8,0},{16,8},{24,16},{1,25},{9,1},{17,9},{25,17},{2,26},{10... | collective-permute-start | bytes 1572872 | tf_op jit(solution)/shard_map/ppermute | solution.py:24
  41.8 20.5 %collective-permute-start.11 = (bf16[256,1024]{1,0:T(8,128)(2,1)}, bf16[256,1024]{1,0:T(8,128)(2,1)}, u32[]{:S(2)}, u32[]{:S(2)}) collective-permute-start(bf16[256,1024]{1,0:T(8,128)(2,1)} %collective-permute-done.2.refs_2_), channel_id=1, source_target_pairs={{0,32},{32,64},{64,96},{96,0},{1,33},{33,65},{65,97},{97,1},{2,34}... | collective-permute-start | bytes 1572872 | tf_op jit(solution)/shard_map/ppermute | solution.py:24
  62.3 22.4 %collective-permute-start.12 = (bf16[256,1024]{1,0:T(8,128)(2,1)S(1)}, bf16[256,1024]{1,0:T(8,128)(2,1)}, u32[]{:S(2)}, u32[]{:S(2)}) collective-permute-start(bf16[256,1024]{1,0:T(8,128)(2,1)S(1)} %collective-permute-done.9.refs_1_), channel_id=1, source_target_pairs={{0,24},{8,0},{16,8},{24,16},{1,25},{9,1},{17,9},{25,17},{2,26},{10... | collective-permute-start | bytes 1572872 | tf_op jit(solution)/shard_map/ppermute | solution.py:24
  63.3 21.4 %collective-permute-start.13 = (bf16[256,1024]{1,0:T(8,128)(2,1)S(1)}, bf16[256,1024]{1,0:T(8,128)(2,1)}, u32[]{:S(2)}, u32[]{:S(2)}) collective-permute-start(bf16[256,1024]{1,0:T(8,128)(2,1)S(1)} %collective-permute-done.9.refs_1_), channel_id=1, source_target_pairs={{0,8},{8,16},{16,24},{24,0},{1,9},{9,17},{17,25},{25,1},{2,10},{10... | collective-permute-start | bytes 1572872 | tf_op jit(solution)/shard_map/ppermute | solution.py:24
  64.8 19.9 %collective-permute-start.14 = (bf16[256,1024]{1,0:T(8,128)(2,1)S(1)}, bf16[256,1024]{1,0:T(8,128)(2,1)}, u32[]{:S(2)}, u32[]{:S(2)}) collective-permute-start(bf16[256,1024]{1,0:T(8,128)(2,1)S(1)} %collective-permute-done.8.refs_0_), channel_id=1, source_target_pairs={{0,32},{32,64},{64,96},{96,0},{1,33},{33,65},{65,97},{97,1},{2,34}... | collective-permute-start | bytes 1572872 | tf_op jit(solution)/shard_map/ppermute | solution.py:24
  65.1 20.5 %collective-permute-start.15 = (bf16[256,1024]{1,0:T(8,128)(2,1)S(1)}, bf16[256,1024]{1,0:T(8,128)(2,1)}, u32[]{:S(2)}, u32[]{:S(2)}) collective-permute-start(bf16[256,1024]{1,0:T(8,128)(2,1)S(1)} %collective-permute-done.8.refs_0_), channel_id=1, source_target_pairs={{0,96},{32,0},{64,32},{96,64},{1,97},{33,1},{65,33},{97,65},{2,98}... | collective-permute-start | bytes 1572872 | tf_op jit(solution)/shard_map/ppermute | solution.py:24
  85.6 18.3 %collective-permute-start.16 = (bf16[256,1024]{1,0:T(8,128)(2,1)S(1)}, bf16[256,1024]{1,0:T(8,128)(2,1)}, u32[]{:S(2)}, u32[]{:S(2)}) collective-permute-start(bf16[256,1024]{1,0:T(8,128)(2,1)S(1)} %collective-permute-done.3.refs_3_), channel_id=1, source_target_pairs={{0,8},{8,16},{16,24},{24,0},{1,9},{9,17},{17,25},{25,1},{2,10},{10... | collective-permute-start | bytes 1572872 | tf_op jit(solution)/shard_map/ppermute | solution.py:24
  88.0 15.8 %collective-permute-start.17 = (bf16[256,1024]{1,0:T(8,128)(2,1)S(1)}, bf16[256,1024]{1,0:T(8,128)(2,1)}, u32[]{:S(2)}, u32[]{:S(2)}) collective-permute-start(bf16[256,1024]{1,0:T(8,128)(2,1)S(1)} %collective-permute-done.1.refs_1_), channel_id=1, source_target_pairs={{0,96},{32,0},{64,32},{96,64},{1,97},{33,1},{65,33},{97,65},{2,98}... | collective-permute-start | bytes 1572872 | tf_op jit(solution)/shard_map/ppermute | solution.py:24
  91.8 16.0 %collective-permute-start.18 = (bf16[256,1024]{1,0:T(8,128)(2,1)}, bf16[256,1024]{1,0:T(8,128)(2,1)}, u32[]{:S(2)}, u32[]{:S(2)}) collective-permute-start(bf16[256,1024]{1,0:T(8,128)(2,1)} %collective-permute-done.12.refs_0_), channel_id=1, source_target_pairs={{0,24},{8,0},{16,8},{24,16},{1,25},{9,1},{17,9},{25,17},{2,26},{10... | collective-permute-start | bytes 1572872 | tf_op jit(solution)/shard_map/ppermute | solution.py:24
  123.2 18.2 %collective-permute-start.19 = (bf16[144,1024]{1,0:T(8,128)(2,1)S(1)}, bf16[144,1024]{1,0:T(8,128)(2,1)S(1)}, u32[]{:S(2)}, u32[]{:S(2)}) collective-permute-start(bf16[144,1024]{1,0:T(8,128)(2,1)S(1)} %get-tuple-element.52.refs_0_), channel_id=1, source_target_pairs={{0,8},{8,16},{16,24},{24,0},{1,9},{9,17},{17,25},{25,1},{2,10},{10... | collective-permute-start | bytes 884744 | tf_op jit(solution)/shard_map/ppermute | solution.py:24
  123.3 25.3 %collective-permute-start.20 = (bf16[144,1024]{1,0:T(8,128)(2,1)S(1)}, bf16[144,1024]{1,0:T(8,128)(2,1)S(1)}, u32[]{:S(2)}, u32[]{:S(2)}) collective-permute-start(bf16[144,1024]{1,0:T(8,128)(2,1)S(1)} %get-tuple-element.52.refs_0_), channel_id=1, source_target_pairs={{0,16},{8,24},{16,0},{24,8},{1,17},{9,25},{17,1},{25,9},{2,18},{10... | collective-permute-start | bytes 884744 | tf_op jit(solution)/shard_map/ppermute | solution.py:24
  128.3 20.3 %collective-permute-start.21 = (bf16[144,1024]{1,0:T(8,128)(2,1)S(1)}, bf16[144,1024]{1,0:T(8,128)(2,1)S(1)}, u32[]{:S(2)}, u32[]{:S(2)}) collective-permute-start(bf16[144,1024]{1,0:T(8,128)(2,1)S(1)} %get-tuple-element.52.refs_0_), channel_id=1, source_target_pairs={{0,24},{8,0},{16,8},{24,16},{1,25},{9,1},{17,9},{25,17},{2,26},{10... | collective-permute-start | bytes 884744 | tf_op jit(solution)/shard_map/ppermute | solution.py:24
  150.6 22.0 %collective-permute-start.22 = (bf16[144,1024]{1,0:T(8,128)(2,1)S(1)}, bf16[144,1024]{1,0:T(8,128)(2,1)S(1)}, u32[]{:S(2)}, u32[]{:S(2)}) collective-permute-start(bf16[144,1024]{1,0:T(8,128)(2,1)S(1)} %get-tuple-element.55), channel_id=1, source_target_pairs={{0,96},{1,97},{2,98},{3,99},{4,100},{5,101},{6,102},{7,103},{8,104... | collective-permute-start | bytes 884744 | tf_op jit(solution)/shard_map/ppermute | solution.py:588
  154.0 18.7 %collective-permute-start.23 = (bf16[144,1024]{1,0:T(8,128)(2,1)S(1)}, bf16[144,1024]{1,0:T(8,128)(2,1)S(1)}, u32[]{:S(2)}, u32[]{:S(2)}) collective-permute-start(bf16[144,1024]{1,0:T(8,128)(2,1)S(1)} %get-tuple-element.55), channel_id=1, source_target_pairs={{0,64},{32,96},{1,65},{33,97},{2,66},{34,98},{3,67},{35,99},{4,68}... | collective-permute-start | bytes 884744 | tf_op jit(solution)/shard_map/ppermute | solution.py:588
  155.3 17.4 %collective-permute-start.24 = (bf16[144,1024]{1,0:T(8,128)(2,1)S(1)}, bf16[144,1024]{1,0:T(8,128)(2,1)S(1)}, u32[]{:S(2)}, u32[]{:S(2)}) collective-permute-start(bf16[144,1024]{1,0:T(8,128)(2,1)S(1)} %get-tuple-element.55), channel_id=1, source_target_pairs={{0,32},{32,64},{64,96},{1,33},{33,65},{65,97},{2,34},{34,66},{66,9... | collective-permute-start | bytes 884744 | tf_op jit(solution)/shard_map/ppermute | solution.py:588
  181.7 11.9 %collective-permute-start.25 = (bf16[512,1024]{1,0:T(8,128)(2,1)}, bf16[512,1024]{1,0:T(8,128)(2,1)S(1)}, u32[]{:S(2)}, u32[]{:S(2)}) collective-permute-start(bf16[512,1024]{1,0:T(8,128)(2,1)} %get-tuple-element.57), channel_id=1, source_target_pairs={{0,4},{4,0},{1,5},{5,1},{2,6},{6,2},{3,7},{7,3},{8,12},{12,8},{9,1... | collective-permute-start | bytes 3145736 | tf_op jit(solution)/shard_map/ppermute | solution.py:19
  181.7 2.9 %collective-permute-start.26 = (f32[1,1024]{1,0:T(1,128)}, f32[1,1024]{1,0:T(1,128)S(1)}, u32[]{:S(2)}, u32[]{:S(2)}) collective-permute-start(f32[1,1024]{1,0:T(1,128)} %get-tuple-element.58), channel_id=1, source_target_pairs={{0,4},{4,0},{1,5},{5,1},{2,6},{6,2},{3,7},{7,3},{8,12},{12,8},{9,1... | collective-permute-start | bytes 12296 | tf_op jit(solution)/shard_map/ppermute | solution.py:19
  185.3 4.8 %collective-permute-start.29 = (f32[1,512]{1,0:T(1,128)S(1)}, f32[1,512]{1,0:T(1,128)S(1)}, u32[]{:S(2)}, u32[]{:S(2)}) collective-permute-start(f32[1,512]{1,0:T(1,128)S(1)} %dynamic-slice_add_fusion), channel_id=1, source_target_pairs={{0,3},{1,0},{2,1},{3,2},{4,7},{5,4},{6,5},{7,6},{8,11},{9,8},{10,9... | collective-permute-start | bytes 6152 | tf_op jit(solution)/shard_map/ppermute | solution.py:24
  186.2 3.9 %collective-permute-start.27 = (f32[1,512]{1,0:T(1,128)S(1)}, f32[1,512]{1,0:T(1,128)S(1)}, u32[]{:S(2)}, u32[]{:S(2)}) collective-permute-start(f32[1,512]{1,0:T(1,128)S(1)} %dynamic-slice_add_fusion), channel_id=1, source_target_pairs={{0,1},{1,2},{2,3},{3,0},{4,5},{5,6},{6,7},{7,4},{8,9},{9,10},{10,1... | collective-permute-start | bytes 6152 | tf_op jit(solution)/shard_map/ppermute | solution.py:24
  188.5 5.1 %collective-permute-start.28 = (f32[1,512]{1,0:T(1,128)S(1)}, f32[1,512]{1,0:T(1,128)S(1)}, u32[]{:S(2)}, u32[]{:S(2)}) collective-permute-start(f32[1,512]{1,0:T(1,128)S(1)} %dynamic-slice_add_fusion), channel_id=1, source_target_pairs={{0,2},{1,3},{2,0},{3,1},{4,6},{5,7},{6,4},{7,5},{8,10},{9,11},{10,... | collective-permute-start | bytes 6152 | tf_op jit(solution)/shard_map/ppermute | solution.py:24
  (22 other events, 302.2 us)
Sparse Core Ops, SparseCore 0:
  9.6 50.5 all-gather.4
  62.5 85.8 all-gather.2

commit v10 on v9

--- a/solution.py
+++ b/solution.py
@@ -415,7 +415,7 @@
         ),
         out_shape=outs,
         name="prepared",
-        **params(4e9, 14, 48),
+        **params(4e9, 14, 60),
     )(place, *slabs, weight, conv_bc, bias, rate)
 
 
@@ -603,13 +603,14 @@
         round_ring(y_less, "y", 1), round_ring(z_more, "z", -1),
         round_ring(z_more, "y", -1), round_ring(y_more, "z", 1),
     ]
-    y_far, z_far, *_ = tied(second, *before_third(nearest))
+    y_far, z_far, _, _, held_z, held_y = tied((*second, z_less, y_less), *before_third(nearest))
+    less_less = round_ring(held_z, "y", 1)
     far = [
         round_ring(z_far, "y", -1), round_ring(z_far, "y", 1),
         round_ring(y_far, "z", 1), round_ring(y_far, "z", -1),
     ]
-    held_z, held_y, last, *_ = tied((z_less, y_less, *far), *before_last())
-    less_less, less_more = round_ring(held_z, "y", 1), round_ring(held_y, "z", -1)
+    held_y, last, *_ = tied((held_y, *far), *before_last())
+    less_more = round_ring(held_y, "z", -1)
     return nearest, second, [*far, less_less, less_more, round_ring(last, "y", -1)]
 
 

time: 204 us -> 204 us (level)
  local copies, waits for them, and re-layouts: 15.2 us -> 10.2 us
  waiting for transfers between devices: 45.9 us -> 49.5 us
  Pallas kernels: 77.3 us -> 79.4 us
    unnamed x45 -> x49, local copies, waits for them, and re-layouts: 11.4 us -> 7.13 us
    ppermute x21, waiting for transfers between devices: 42 us -> 45.5 us  [round_ring(): lax.ppermute(a, axis, [(i, (i + distance) % size) for i in range(size)])]
    pallas_call x1, Pallas kernels: 12.2 us -> 14.5 us  [prepared(): pl.pallas_call(prepare_kernel, grid_spec=pltpu.PrefetchScalarGridSpec(num...]
  transfers between devices with their start and end apart: 32 -> 32, of which waited for: 14 -> 12; matrix products, arithmetic and copies ran while one was open for 3% -> 2% of each run, Pallas kernels for 33% -> 34%
where the time goes in v10:
time: 204 us
  Pallas kernels  79.4 us (39%)
  waiting for transfers between devices  49.5 us (24%)
  starting transfers between devices  48.4 us (24%)
  between operations  13.8 us (7%)
  local copies, waits for them, and re-layouts  10.2 us (5%)
  other arithmetic  2.25 us (1%)
    ppermute x21, waiting for transfers between devices, round_ring(): lax.ppermute(a, axis, [(i, (i + distance) % size) for i in range(size)])  45.5 us
    ppermute x21, starting transfers between devices, round_ring(): lax.ppermute(a, axis, [(i, (i + distance) % size) for i in range(size)])  39.6 us
    pallas_call x2, Pallas kernels, products(): pl.pallas_call(functools.partial(products_kernel, sources, done, count, l...  19.1 us
    pallas_call x1, Pallas kernels, local_states(): pl.pallas_call(functools.partial(states_kernel, sources, done, count), gr...  15 us
    pallas_call x1, Pallas kernels, prepared(): pl.pallas_call(prepare_kernel, grid_spec=pltpu.PrefetchScalarGridSpec(num...  14.5 us
    pallas_call x1, Pallas kernels, project_gate(): pl.pallas_call(z_kernel, grid_spec=pltpu.PrefetchScalarGridSpec(num_scala...  13 us
    pallas_call x1, Pallas kernels, gate_outputs(): pl.pallas_call(gate_kernel, grid_spec=pltpu.PrefetchScalarGridSpec(num_sc...  8.08 us
    pallas_call x1, Pallas kernels, local_outputs(): pl.pallas_call(outputs_kernel, grid=(rows // GROUP,), in_specs=[rows_of(w...  7.13 us
  transfers between devices with their start and end apart: 32, of which 12 were waited for; matrix products, arithmetic and copies ran while one was open for 2% of the time, Pallas kernels for 34%

profile of v10, /device:TPU:6, one launch (start us, length us, event | category | flops | bytes accessed | tf_op | source)
XLA Modules:
  0.0 203.5 jit_solution(2883244301596908503)
XLA Ops:
  11.8 1.6 collective-permute-start.1
  13.4 1.7 collective-permute-start.2
  15.1 1.9 collective-permute-start.3
  17.0 2.1 %collective-permute-start.4 = (bf16[256,1024]{1,0:T(8,128)(2,1)S(1)}, bf16[256,1024]{1,0:T(8,128)(2,1)}, u32[]{:S(2)}, u32[]{:S(2)}) collective-permute-start(bf16[256,1024]{1,0:T(8,128)(2,1)S(1)} %pad_maximum_fusion.refs_0_), channel_id=1, source_target_pairs={{0,96},{32,0},{64,32},{96,64},{1,97},{33,1},{65,33},{97,65},{2,98}... | collective-permute-start | bytes 1572872 | tf_op jit(solution)/shard_map/ppermute | solution.py:24
  19.1 8.5 %collective-permute-done.1.refs_1_ = bf16[256,1024]{1,0:T(8,128)(2,1)S(1)} collective-permute-done((bf16[256,1024]{1,0:T(8,128)(2,1)S(1)}, bf16[256,1024]{1,0:T(8,128)(2,1)S(1)}, u32[]{:S(2)}, u32[]{:S(2)}) %collective-permute-start.1) | collective-permute-done | bytes 524320 | tf_op jit(solution)/shard_map/ppermute | solution.py:24
  27.8 4.2 %collective-permute-done.3.refs_3_ = bf16[256,1024]{1,0:T(8,128)(2,1)S(1)} collective-permute-done((bf16[256,1024]{1,0:T(8,128)(2,1)S(1)}, bf16[256,1024]{1,0:T(8,128)(2,1)S(1)}, u32[]{:S(2)}, u32[]{:S(2)}) %collective-permute-start.3) | collective-permute-done | bytes 524320 | tf_op jit(solution)/shard_map/ppermute | solution.py:24
  35.2 3.1 %collective-permute-start.9 = (bf16[256,1024]{1,0:T(8,128)(2,1)}, bf16[256,1024]{1,0:T(8,128)(2,1)S(1)}, u32[]{:S(2)}, u32[]{:S(2)}) collective-permute-start(bf16[256,1024]{1,0:T(8,128)(2,1)} %collective-permute-done.4.refs_4_), channel_id=1, source_target_pairs={{0,96},{32,0},{64,32},{96,64},{1,97},{33,1},{65,33},{97,65},{2,98}... | collective-permute-start | bytes 1572872 | tf_op jit(solution)/shard_map/ppermute | solution.py:24
  38.2 3.3 %collective-permute-start.10 = (bf16[256,1024]{1,0:T(8,128)(2,1)}, bf16[256,1024]{1,0:T(8,128)(2,1)S(1)}, u32[]{:S(2)}, u32[]{:S(2)}) collective-permute-start(bf16[256,1024]{1,0:T(8,128)(2,1)} %collective-permute-done.4.refs_4_), channel_id=1, source_target_pairs={{0,24},{8,0},{16,8},{24,16},{1,25},{9,1},{17,9},{25,17},{2,26},{10... | collective-permute-start | bytes 1572872 | tf_op jit(solution)/shard_map/ppermute | solution.py:24
  41.6 2.5 %collective-permute-start.11 = (bf16[256,1024]{1,0:T(8,128)(2,1)}, bf16[256,1024]{1,0:T(8,128)(2,1)}, u32[]{:S(2)}, u32[]{:S(2)}) collective-permute-start(bf16[256,1024]{1,0:T(8,128)(2,1)} %collective-permute-done.2.refs_2_), channel_id=1, source_target_pairs={{0,32},{32,64},{64,96},{96,0},{1,33},{33,65},{65,97},{97,1},{2,34}... | collective-permute-start | bytes 1572872 | tf_op jit(solution)/shard_map/ppermute | solution.py:24
  44.2 9.5 %first_products.1 = (f32[1024,1024]{1,0:T(8,128)}, f32[16,1024]{1,0:T(8,128)S(1)}) custom-call(s32[17]{0:T(128)S(1)} %stack.68.place_ref, bf16[512,4096]{1,0:T(8,128)(2,1)} %own_ref.4, bf16[512,4096]{1,0:T(8,128)(2,1)} %collective-permute-done.5.other_ref, bf16[16,4096]{1,0:T(8,128)(2,1)S(1)} %add.199.before_ref, ...), custom_call_target="tpu_custom_call" | custom-call | flops 5000000000 | bytes 16777216 | tf_op jit(solution)/shard_map/first_products/pallas_call | solution.py:430
  53.8 5.5 %collective-permute-done.10.refs_2_ = bf16[256,1024]{1,0:T(8,128)(2,1)S(1)} collective-permute-done((bf16[256,1024]{1,0:T(8,128)(2,1)}, bf16[256,1024]{1,0:T(8,128)(2,1)S(1)}, u32[]{:S(2)}, u32[]{:S(2)}) %collective-permute-start.10) | collective-permute-done | bytes 524320 | tf_op jit(solution)/shard_map/ppermute | solution.py:24
  59.2 2.7 %collective-permute-done.11.refs_3_ = bf16[256,1024]{1,0:T(8,128)(2,1)} collective-permute-done((bf16[256,1024]{1,0:T(8,128)(2,1)}, bf16[256,1024]{1,0:T(8,128)(2,1)}, u32[]{:S(2)}, u32[]{:S(2)}) %collective-permute-start.11) | collective-permute-done | bytes 524320 | tf_op jit(solution)/shard_map/ppermute | solution.py:24
  65.1 3.0 %collective-permute-start.15 = (bf16[256,1024]{1,0:T(8,128)(2,1)S(1)}, bf16[256,1024]{1,0:T(8,128)(2,1)}, u32[]{:S(2)}, u32[]{:S(2)}) collective-permute-start(bf16[256,1024]{1,0:T(8,128)(2,1)S(1)} %collective-permute-done.8.refs_0_), channel_id=1, source_target_pairs={{0,96},{32,0},{64,32},{96,64},{1,97},{33,1},{65,33},{97,65},{2,98}... | collective-permute-start | bytes 1572872 | tf_op jit(solution)/shard_map/ppermute | solution.py:24
  68.8 2.0 collective-permute-start.16
  70.8 14.5 %prepared.1 = (bf16[1024,256]{1,0:T(8,128)(2,1)}, f32[1024,128]{1,0:T(8,128)}, f32[1024,128]{1,0:T(8,128)}, f32[16,1024]{1,0:T(8,128)}, f32[16,1024]{1,0:T(8,128...) custom-call(s32[17]{0:T(128)} %copy-done.11, bf16[512,4096]{1,0:T(8,128)(2,1)} %own_ref.4, ...), custom_call_target="tpu_custom_call" | custom-call | flops 4000000000 | bytes 14680064 | tf_op jit(solution)/shard_map/prepared/pallas_call | solution.py:405
  85.4 3.1 %collective-permute-start.17 = (bf16[256,1024]{1,0:T(8,128)(2,1)S(1)}, bf16[256,1024]{1,0:T(8,128)(2,1)}, u32[]{:S(2)}, u32[]{:S(2)}) collective-permute-start(bf16[256,1024]{1,0:T(8,128)(2,1)S(1)} %collective-permute-done.1.refs_1_), channel_id=1, source_target_pairs={{0,96},{32,0},{64,32},{96,64},{1,97},{33,1},{65,33},{97,65},{2,98}... | collective-permute-start | bytes 1572872 | tf_op jit(solution)/shard_map/ppermute | solution.py:24
  88.5 2.5 %collective-permute-start.18 = (bf16[256,1024]{1,0:T(8,128)(2,1)}, bf16[256,1024]{1,0:T(8,128)(2,1)}, u32[]{:S(2)}, u32[]{:S(2)}) collective-permute-start(bf16[256,1024]{1,0:T(8,128)(2,1)} %collective-permute-done.12.refs_0_), channel_id=1, source_target_pairs={{0,24},{8,0},{16,8},{24,16},{1,25},{9,1},{17,9},{25,17},{2,26},{10... | collective-permute-start | bytes 1572872 | tf_op jit(solution)/shard_map/ppermute | solution.py:24
  91.3 9.6 %more_products.1 = (f32[1024,1024]{1,0:T(8,128)}, f32[16,1024]{1,0:T(8,128)S(1)}) custom-call(s32[17]{0:T(128)S(1)} %copy-done.12, bf16[512,4096]{1,0:T(8,128)(2,1)} %own_ref.4, bf16[512,4096]{1,0:T(8,128)(2,1)} %collective-permute-done.5.other_ref, bf16[16,4096]{1,0:T(8,128)(2,1)S(1)} %copy-done.7, bf16[256,1024]{1,0:T(8,128)(2,1)S(1)} %collective-permute-done.8.refs_0_, ...), custom_call_target="tpu_custom_call" | custom-call | flops 5000000000 | bytes 16777216 | tf_op jit(solution)/shard_map/more_products/pallas_call | solution.py:430
  100.9 2.8 %collective-permute-done.18.refs_6_ = bf16[256,1024]{1,0:T(8,128)(2,1)} collective-permute-done((bf16[256,1024]{1,0:T(8,128)(2,1)}, bf16[256,1024]{1,0:T(8,128)(2,1)}, u32[]{:S(2)}, u32[]{:S(2)}) %collective-permute-start.18) | collective-permute-done | bytes 524320 | tf_op jit(solution)/shard_map/ppermute | solution.py:24
  103.8 15.0 %states.1 = (bf16[1024,1024]{1,0:T(8,128)(2,1)S(1)}, bf16[4,128,1024]{2,1,0:T(8,128)(2,1)S(1)}, bf16[144,1024]{1,0:T(8,128)(2,1)S(1)}) custom-call(s32[17]{0:T(128)S(1)} %copy-done.12, bf16[512,4096]{1,0:T(8,128)(2,1)S(1)} %copy-done.10, bf16[512,4096]{1,0:T(8,128)(2,1)} %collective-permute-done.5.other_ref, bf16[16,4096]{1,0:T(8,128)(2,1)S(1)} %copy-done.7, ...), custom_call_target="tpu_custom_call" | custom-call | flops 11000000512 | bytes 18874368 | tf_op jit(solution)/shard_map/states/pallas_call | solution.py:456
  118.9 5.2 %collective-permute-start.20 = (bf16[144,1024]{1,0:T(8,128)(2,1)S(1)}, bf16[144,1024]{1,0:T(8,128)(2,1)S(1)}, u32[]{:S(2)}, u32[]{:S(2)}) collective-permute-start(bf16[144,1024]{1,0:T(8,128)(2,1)S(1)} %get-tuple-element.54.refs_0_), channel_id=1, source_target_pairs={{0,16},{8,24},{16,0},{24,8},{1,17},{9,25},{17,1},{25,9},{2,18},{10... | collective-permute-start | bytes 884744 | tf_op jit(solution)/shard_map/ppermute | solution.py:24
  124.1 7.1 %outputs.1.local_ref = bf16[1024,1024]{1,0:T(8,128)(2,1)S(1)} custom-call(bf16[1024,1024]{1,0:T(8,128)(2,1)S(1)} %get-tuple-element.48.xc_ref, bf16[1024,256]{1,0:T(8,128)(2,1)S(1)} %copy-done.4, f32[1024,128]{1,0:T(8,128)S(1)} %copy-done.13, f32[16,1024]{1,0:T(8,128)S(1)} %copy-done.15, f32[16,1024]{1,0:T(8,128)S(1)} %copy-done.16, ...), custom_call_target="tpu_custom_call" | custom-call | flops 10000000000 | bytes 10485760 | tf_op jit(solution)/shard_map/outputs/pallas_call | solution.py:488
  132.6 3.9 %collective-permute-done.19.refs_1_ = bf16[144,1024]{1,0:T(8,128)(2,1)S(1)} collective-permute-done((bf16[144,1024]{1,0:T(8,128)(2,1)S(1)}, bf16[144,1024]{1,0:T(8,128)(2,1)S(1)}, u32[]{:S(2)}, u32[]{:S(2)}) %collective-permute-start.19) | collective-permute-done | bytes 294944 | tf_op jit(solution)/shard_map/ppermute | solution.py:24
  136.4 13.0 %collective-permute-done.20.refs_2_ = bf16[144,1024]{1,0:T(8,128)(2,1)S(1)} collective-permute-done((bf16[144,1024]{1,0:T(8,128)(2,1)S(1)}, bf16[144,1024]{1,0:T(8,128)(2,1)S(1)}, u32[]{:S(2)}, u32[]{:S(2)}) %collective-permute-start.20) | collective-permute-done | bytes 294944 | tf_op jit(solution)/shard_map/ppermute | solution.py:24
  151.4 2.5 %collective-permute-start.22 = (bf16[144,1024]{1,0:T(8,128)(2,1)S(1)}, bf16[144,1024]{1,0:T(8,128)(2,1)S(1)}, u32[]{:S(2)}, u32[]{:S(2)}) collective-permute-start(bf16[144,1024]{1,0:T(8,128)(2,1)S(1)} %get-tuple-element.57), channel_id=1, source_target_pairs={{0,96},{1,97},{2,98},{3,99},{4,100},{5,101},{6,102},{7,103},{8,104... | collective-permute-start | bytes 884744 | tf_op jit(solution)/shard_map/ppermute | solution.py:588
  155.2 3.0 %collective-permute-start.24 = (bf16[144,1024]{1,0:T(8,128)(2,1)S(1)}, bf16[144,1024]{1,0:T(8,128)(2,1)S(1)}, u32[]{:S(2)}, u32[]{:S(2)}) collective-permute-start(bf16[144,1024]{1,0:T(8,128)(2,1)S(1)} %get-tuple-element.57), channel_id=1, source_target_pairs={{0,32},{32,64},{64,96},{1,33},{33,65},{65,97},{2,34},{34,66},{66,9... | collective-permute-start | bytes 884744 | tf_op jit(solution)/shard_map/ppermute | solution.py:588
  158.3 13.0 %project_gate.1.gate_ref = bf16[1024,1024]{1,0:T(8,128)(2,1)S(1)} custom-call(s32[17]{0:T(128)S(1)} %copy-done.12, bf16[512,4096]{1,0:T(8,128)(2,1)} %own_ref.4, bf16[512,4096]{1,0:T(8,128)(2,1)} %collective-permute-done.5.other_ref, bf16[4096,2048]{1,0:T(8,128)(2,1)} %all-gather.3.cloned.1.call-done.weight_ref), custom_call_target="tpu_custom_call" | custom-call | flops 8999999488 | bytes 20971520 | tf_op jit(solution)/shard_map/project_gate/pallas_call | solution.py:509
  173.6 8.1 %gate.1 = (bf16[512,1024]{1,0:T(8,128)(2,1)}, bf16[512,1024]{1,0:T(8,128)(2,1)}, f32[1,1024]{1,0:T(1,128)}) custom-call(s32[1]{0:T(128)} %bitcast.core_ref, bf16[1024,1024]{1,0:T(8,128)(2,1)} %copy-done.2, bf16[1024,1024]{1,0:T(8,128)(2,1)} %copy-done.1, bf16[1024,256]{1,0:T(8,128)(2,1)} %get-tuple-element.40.refs_9_.bcc_ref, ...), custom_call_target="tpu_custom_call" | custom-call | flops 1000000000 | bytes 10485760 | tf_op jit(solution)/shard_map/gate/pallas_call | solution.py:527
  182.2 2.4 %collective-permute-done.26 = f32[1,1024]{1,0:T(1,128)S(1)} collective-permute-done((f32[1,1024]{1,0:T(1,128)}, f32[1,1024]{1,0:T(1,128)S(1)}, u32[]{:S(2)}, u32[]{:S(2)}) %collective-permute-start.26) | collective-permute-done | bytes 4128 | tf_op jit(solution)/shard_map/ppermute | solution.py:19
  186.1 2.4 %collective-permute-start.27 = (f32[1,512]{1,0:T(1,128)S(1)}, f32[1,512]{1,0:T(1,128)S(1)}, u32[]{:S(2)}, u32[]{:S(2)}) collective-permute-start(f32[1,512]{1,0:T(1,128)S(1)} %dynamic-slice_add_fusion), channel_id=1, source_target_pairs={{0,1},{1,2},{2,3},{3,0},{4,5},{5,6},{6,7},{7,4},{8,9},{9,10},{10,1... | collective-permute-start | bytes 6152 | tf_op jit(solution)/shard_map/ppermute | solution.py:24
  190.0 3.5 %collective-permute-done.28 = f32[1,512]{1,0:T(1,128)S(1)} collective-permute-done((f32[1,512]{1,0:T(1,128)S(1)}, f32[1,512]{1,0:T(1,128)S(1)}, u32[]{:S(2)}, u32[]{:S(2)}) %collective-permute-start.28) | collective-permute-done | bytes 2080 | tf_op jit(solution)/shard_map/ppermute | solution.py:24
  194.8 1.9 normalized.1
  (109 shorter events, 24.7 us)
Async XLA Ops:
  6.5 64.2 %all-gather.5.cloned.1.call-start = ((), (), s32[]{:S(2)}) async-start(), calls=%async_computation.1 | async-start | bytes 3244032 | tf_op jit(solution)/shard_map/all_gather | solution.py:652
  9.0 149.3 %all-gather.3.cloned.1.call-start = ((), (), s32[]{:S(2)}) async-start(), calls=%async_computation | async-start | bytes 17301504 | tf_op jit(solution)/shard_map/all_gather | solution.py:676
  10.1 1.6 collective-permute-start
  11.8 15.8 %collective-permute-start.1 = (bf16[256,1024]{1,0:T(8,128)(2,1)S(1)}, bf16[256,1024]{1,0:T(8,128)(2,1)S(1)}, u32[]{:S(2)}, u32[]{:S(2)}) collective-permute-start(bf16[256,1024]{1,0:T(8,128)(2,1)S(1)} %pad_maximum_fusion.refs_0_), channel_id=1, source_target_pairs={{0,8},{8,16},{16,24},{24,0},{1,9},{9,17},{17,25},{25,1},{2,10},{10... | collective-permute-start | bytes 1572872 | tf_op jit(solution)/shard_map/ppermute | solution.py:24
  13.4 14.3 %collective-permute-start.2 = (bf16[256,1024]{1,0:T(8,128)(2,1)S(1)}, bf16[256,1024]{1,0:T(8,128)(2,1)}, u32[]{:S(2)}, u32[]{:S(2)}) collective-permute-start(bf16[256,1024]{1,0:T(8,128)(2,1)S(1)} %pad_maximum_fusion.refs_0_), channel_id=1, source_target_pairs={{0,24},{8,0},{16,8},{24,16},{1,25},{9,1},{17,9},{25,17},{2,26},{10... | collective-permute-start | bytes 1572872 | tf_op jit(solution)/shard_map/ppermute | solution.py:24
  15.1 16.9 %collective-permute-start.3 = (bf16[256,1024]{1,0:T(8,128)(2,1)S(1)}, bf16[256,1024]{1,0:T(8,128)(2,1)S(1)}, u32[]{:S(2)}, u32[]{:S(2)}) collective-permute-start(bf16[256,1024]{1,0:T(8,128)(2,1)S(1)} %pad_maximum_fusion.refs_0_), channel_id=1, source_target_pairs={{0,32},{32,64},{64,96},{96,0},{1,33},{33,65},{65,97},{97,1},{2,34}... | collective-permute-start | bytes 1572872 | tf_op jit(solution)/shard_map/ppermute | solution.py:24
  17.0 15.0 %collective-permute-start.4 = (bf16[256,1024]{1,0:T(8,128)(2,1)S(1)}, bf16[256,1024]{1,0:T(8,128)(2,1)}, u32[]{:S(2)}, u32[]{:S(2)}) collective-permute-start(bf16[256,1024]{1,0:T(8,128)(2,1)S(1)} %pad_maximum_fusion.refs_0_), channel_id=1, source_target_pairs={{0,96},{32,0},{64,32},{96,64},{1,97},{33,1},{65,33},{97,65},{2,98}... | collective-permute-start | bytes 1572872 | tf_op jit(solution)/shard_map/ppermute | solution.py:24
  32.0 12.2 %collective-permute-start.5 = (bf16[512,4096]{1,0:T(8,128)(2,1)}, bf16[512,4096]{1,0:T(8,128)(2,1)}, u32[]{:S(2)}, u32[]{:S(2)}) collective-permute-start(bf16[512,4096]{1,0:T(8,128)(2,1)} %own_ref.4), channel_id=1, source_target_pairs={{0,4},{4,0},{1,5},{5,1},{2,6},{6,2},{3,7},{7,3},{8,12},{12,8},{9,1... | collective-permute-start | bytes 12582920 | tf_op jit(solution)/shard_map/ppermute | solution.py:19
  32.9 5.3 %collective-permute-start.6 = (bf16[16,4096]{1,0:T(8,128)(2,1)S(1)}, bf16[16,4096]{1,0:T(8,128)(2,1)S(1)}, u32[]{:S(2)}, u32[]{:S(2)}) collective-permute-start(bf16[16,4096]{1,0:T(8,128)(2,1)S(1)} %slice.4), channel_id=1, source_target_pairs={{4,8},{12,16},{20,24},{28,32},{36,40},{44,48},{52,56},{60,64},{68,... | collective-permute-start | bytes 393224 | tf_op jit(solution)/shard_map/ppermute | solution.py:660
  33.6 8.0 %collective-permute-start.7 = (bf16[16,4096]{1,0:T(8,128)(2,1)S(1)}, bf16[16,4096]{1,0:T(8,128)(2,1)S(1)}, u32[]{:S(2)}, u32[]{:S(2)}) collective-permute-start(bf16[16,4096]{1,0:T(8,128)(2,1)S(1)} %slice.4), channel_id=1, source_target_pairs={{4,12},{12,20},{20,28},{28,36},{36,44},{44,52},{52,60},{60,68},{68... | collective-permute-start | bytes 393224 | tf_op jit(solution)/shard_map/ppermute | solution.py:660
  34.3 19.5 %collective-permute-start.8 = (bf16[256,1024]{1,0:T(8,128)(2,1)S(1)}, bf16[256,1024]{1,0:T(8,128)(2,1)S(1)}, u32[]{:S(2)}, u32[]{:S(2)}) collective-permute-start(bf16[256,1024]{1,0:T(8,128)(2,1)S(1)} %collective-permute-done.1.refs_1_), channel_id=1, source_target_pairs={{0,8},{8,16},{16,24},{24,0},{1,9},{9,17},{17,25},{25,1},{2,10},{10... | collective-permute-start | bytes 1572872 | tf_op jit(solution)/shard_map/ppermute | solution.py:24
  35.2 18.6 %collective-permute-start.9 = (bf16[256,1024]{1,0:T(8,128)(2,1)}, bf16[256,1024]{1,0:T(8,128)(2,1)S(1)}, u32[]{:S(2)}, u32[]{:S(2)}) collective-permute-start(bf16[256,1024]{1,0:T(8,128)(2,1)} %collective-permute-done.4.refs_4_), channel_id=1, source_target_pairs={{0,96},{32,0},{64,32},{96,64},{1,97},{33,1},{65,33},{97,65},{2,98}... | collective-permute-start | bytes 1572872 | tf_op jit(solution)/shard_map/ppermute | solution.py:24
  38.2 21.0 %collective-permute-start.10 = (bf16[256,1024]{1,0:T(8,128)(2,1)}, bf16[256,1024]{1,0:T(8,128)(2,1)S(1)}, u32[]{:S(2)}, u32[]{:S(2)}) collective-permute-start(bf16[256,1024]{1,0:T(8,128)(2,1)} %collective-permute-done.4.refs_4_), channel_id=1, source_target_pairs={{0,24},{8,0},{16,8},{24,16},{1,25},{9,1},{17,9},{25,17},{2,26},{10... | collective-permute-start | bytes 1572872 | tf_op jit(solution)/shard_map/ppermute | solution.py:24
  41.6 20.4 %collective-permute-start.11 = (bf16[256,1024]{1,0:T(8,128)(2,1)}, bf16[256,1024]{1,0:T(8,128)(2,1)}, u32[]{:S(2)}, u32[]{:S(2)}) collective-permute-start(bf16[256,1024]{1,0:T(8,128)(2,1)} %collective-permute-done.2.refs_2_), channel_id=1, source_target_pairs={{0,32},{32,64},{64,96},{96,0},{1,33},{33,65},{65,97},{97,1},{2,34}... | collective-permute-start | bytes 1572872 | tf_op jit(solution)/shard_map/ppermute | solution.py:24
  61.9 23.4 %collective-permute-start.12 = (bf16[256,1024]{1,0:T(8,128)(2,1)S(1)}, bf16[256,1024]{1,0:T(8,128)(2,1)}, u32[]{:S(2)}, u32[]{:S(2)}) collective-permute-start(bf16[256,1024]{1,0:T(8,128)(2,1)S(1)} %collective-permute-done.9.refs_1_), channel_id=1, source_target_pairs={{0,24},{8,0},{16,8},{24,16},{1,25},{9,1},{17,9},{25,17},{2,26},{10... | collective-permute-start | bytes 1572872 | tf_op jit(solution)/shard_map/ppermute | solution.py:24
  63.2 22.2 %collective-permute-start.13 = (bf16[256,1024]{1,0:T(8,128)(2,1)S(1)}, bf16[256,1024]{1,0:T(8,128)(2,1)}, u32[]{:S(2)}, u32[]{:S(2)}) collective-permute-start(bf16[256,1024]{1,0:T(8,128)(2,1)S(1)} %collective-permute-done.9.refs_1_), channel_id=1, source_target_pairs={{0,8},{8,16},{16,24},{24,0},{1,9},{9,17},{17,25},{25,1},{2,10},{10... | collective-permute-start | bytes 1572872 | tf_op jit(solution)/shard_map/ppermute | solution.py:24
  64.8 20.6 %collective-permute-start.14 = (bf16[256,1024]{1,0:T(8,128)(2,1)S(1)}, bf16[256,1024]{1,0:T(8,128)(2,1)}, u32[]{:S(2)}, u32[]{:S(2)}) collective-permute-start(bf16[256,1024]{1,0:T(8,128)(2,1)S(1)} %collective-permute-done.8.refs_0_), channel_id=1, source_target_pairs={{0,32},{32,64},{64,96},{96,0},{1,33},{33,65},{65,97},{97,1},{2,34}... | collective-permute-start | bytes 1572872 | tf_op jit(solution)/shard_map/ppermute | solution.py:24
  65.1 20.3 %collective-permute-start.15 = (bf16[256,1024]{1,0:T(8,128)(2,1)S(1)}, bf16[256,1024]{1,0:T(8,128)(2,1)}, u32[]{:S(2)}, u32[]{:S(2)}) collective-permute-start(bf16[256,1024]{1,0:T(8,128)(2,1)S(1)} %collective-permute-done.8.refs_0_), channel_id=1, source_target_pairs={{0,96},{32,0},{64,32},{96,64},{1,97},{33,1},{65,33},{97,65},{2,98}... | collective-permute-start | bytes 1572872 | tf_op jit(solution)/shard_map/ppermute | solution.py:24
  68.8 32.2 %collective-permute-start.16 = (bf16[256,1024]{1,0:T(8,128)(2,1)S(1)}, bf16[256,1024]{1,0:T(8,128)(2,1)}, u32[]{:S(2)}, u32[]{:S(2)}) collective-permute-start(bf16[256,1024]{1,0:T(8,128)(2,1)S(1)} %collective-permute-done.3.refs_3_), channel_id=1, source_target_pairs={{0,8},{8,16},{16,24},{24,0},{1,9},{9,17},{17,25},{25,1},{2,10},{10... | collective-permute-start | bytes 1572872 | tf_op jit(solution)/shard_map/ppermute | solution.py:24
  85.4 15.5 %collective-permute-start.17 = (bf16[256,1024]{1,0:T(8,128)(2,1)S(1)}, bf16[256,1024]{1,0:T(8,128)(2,1)}, u32[]{:S(2)}, u32[]{:S(2)}) collective-permute-start(bf16[256,1024]{1,0:T(8,128)(2,1)S(1)} %collective-permute-done.1.refs_1_), channel_id=1, source_target_pairs={{0,96},{32,0},{64,32},{96,64},{1,97},{33,1},{65,33},{97,65},{2,98}... | collective-permute-start | bytes 1572872 | tf_op jit(solution)/shard_map/ppermute | solution.py:24
  88.5 15.3 %collective-permute-start.18 = (bf16[256,1024]{1,0:T(8,128)(2,1)}, bf16[256,1024]{1,0:T(8,128)(2,1)}, u32[]{:S(2)}, u32[]{:S(2)}) collective-permute-start(bf16[256,1024]{1,0:T(8,128)(2,1)} %collective-permute-done.12.refs_0_), channel_id=1, source_target_pairs={{0,24},{8,0},{16,8},{24,16},{1,25},{9,1},{17,9},{25,17},{2,26},{10... | collective-permute-start | bytes 1572872 | tf_op jit(solution)/shard_map/ppermute | solution.py:24
  118.8 17.7 %collective-permute-start.19 = (bf16[144,1024]{1,0:T(8,128)(2,1)S(1)}, bf16[144,1024]{1,0:T(8,128)(2,1)S(1)}, u32[]{:S(2)}, u32[]{:S(2)}) collective-permute-start(bf16[144,1024]{1,0:T(8,128)(2,1)S(1)} %get-tuple-element.54.refs_0_), channel_id=1, source_target_pairs={{0,8},{8,16},{16,24},{24,0},{1,9},{9,17},{17,25},{25,1},{2,10},{10... | collective-permute-start | bytes 884744 | tf_op jit(solution)/shard_map/ppermute | solution.py:24
  118.9 30.5 %collective-permute-start.20 = (bf16[144,1024]{1,0:T(8,128)(2,1)S(1)}, bf16[144,1024]{1,0:T(8,128)(2,1)S(1)}, u32[]{:S(2)}, u32[]{:S(2)}) collective-permute-start(bf16[144,1024]{1,0:T(8,128)(2,1)S(1)} %get-tuple-element.54.refs_0_), channel_id=1, source_target_pairs={{0,16},{8,24},{16,0},{24,8},{1,17},{9,25},{17,1},{25,9},{2,18},{10... | collective-permute-start | bytes 884744 | tf_op jit(solution)/shard_map/ppermute | solution.py:24
  124.0 25.3 %collective-permute-start.21 = (bf16[144,1024]{1,0:T(8,128)(2,1)S(1)}, bf16[144,1024]{1,0:T(8,128)(2,1)S(1)}, u32[]{:S(2)}, u32[]{:S(2)}) collective-permute-start(bf16[144,1024]{1,0:T(8,128)(2,1)S(1)} %get-tuple-element.54.refs_0_), channel_id=1, source_target_pairs={{0,24},{8,0},{16,8},{24,16},{1,25},{9,1},{17,9},{25,17},{2,26},{10... | collective-permute-start | bytes 884744 | tf_op jit(solution)/shard_map/ppermute | solution.py:24
  151.4 21.2 %collective-permute-start.22 = (bf16[144,1024]{1,0:T(8,128)(2,1)S(1)}, bf16[144,1024]{1,0:T(8,128)(2,1)S(1)}, u32[]{:S(2)}, u32[]{:S(2)}) collective-permute-start(bf16[144,1024]{1,0:T(8,128)(2,1)S(1)} %get-tuple-element.57), channel_id=1, source_target_pairs={{0,96},{1,97},{2,98},{3,99},{4,100},{5,101},{6,102},{7,103},{8,104... | collective-permute-start | bytes 884744 | tf_op jit(solution)/shard_map/ppermute | solution.py:588
  153.9 18.7 %collective-permute-start.23 = (bf16[144,1024]{1,0:T(8,128)(2,1)S(1)}, bf16[144,1024]{1,0:T(8,128)(2,1)S(1)}, u32[]{:S(2)}, u32[]{:S(2)}) collective-permute-start(bf16[144,1024]{1,0:T(8,128)(2,1)S(1)} %get-tuple-element.57), channel_id=1, source_target_pairs={{0,64},{32,96},{1,65},{33,97},{2,66},{34,98},{3,67},{35,99},{4,68}... | collective-permute-start | bytes 884744 | tf_op jit(solution)/shard_map/ppermute | solution.py:588
  155.2 17.4 %collective-permute-start.24 = (bf16[144,1024]{1,0:T(8,128)(2,1)S(1)}, bf16[144,1024]{1,0:T(8,128)(2,1)S(1)}, u32[]{:S(2)}, u32[]{:S(2)}) collective-permute-start(bf16[144,1024]{1,0:T(8,128)(2,1)S(1)} %get-tuple-element.57), channel_id=1, source_target_pairs={{0,32},{32,64},{64,96},{1,33},{33,65},{65,97},{2,34},{34,66},{66,9... | collective-permute-start | bytes 884744 | tf_op jit(solution)/shard_map/ppermute | solution.py:588
  181.7 11.9 %collective-permute-start.25 = (bf16[512,1024]{1,0:T(8,128)(2,1)}, bf16[512,1024]{1,0:T(8,128)(2,1)S(1)}, u32[]{:S(2)}, u32[]{:S(2)}) collective-permute-start(bf16[512,1024]{1,0:T(8,128)(2,1)} %get-tuple-element.59), channel_id=1, source_target_pairs={{0,4},{4,0},{1,5},{5,1},{2,6},{6,2},{3,7},{7,3},{8,12},{12,8},{9,1... | collective-permute-start | bytes 3145736 | tf_op jit(solution)/shard_map/ppermute | solution.py:19
  181.7 2.9 %collective-permute-start.26 = (f32[1,1024]{1,0:T(1,128)}, f32[1,1024]{1,0:T(1,128)S(1)}, u32[]{:S(2)}, u32[]{:S(2)}) collective-permute-start(f32[1,1024]{1,0:T(1,128)} %get-tuple-element.60), channel_id=1, source_target_pairs={{0,4},{4,0},{1,5},{5,1},{2,6},{6,2},{3,7},{7,3},{8,12},{12,8},{9,1... | collective-permute-start | bytes 12296 | tf_op jit(solution)/shard_map/ppermute | solution.py:19
  185.2 4.8 %collective-permute-start.29 = (f32[1,512]{1,0:T(1,128)S(1)}, f32[1,512]{1,0:T(1,128)S(1)}, u32[]{:S(2)}, u32[]{:S(2)}) collective-permute-start(f32[1,512]{1,0:T(1,128)S(1)} %dynamic-slice_add_fusion), channel_id=1, source_target_pairs={{0,3},{1,0},{2,1},{3,2},{4,7},{5,4},{6,5},{7,6},{8,11},{9,8},{10,9... | collective-permute-start | bytes 6152 | tf_op jit(solution)/shard_map/ppermute | solution.py:24
  186.1 3.9 %collective-permute-start.27 = (f32[1,512]{1,0:T(1,128)S(1)}, f32[1,512]{1,0:T(1,128)S(1)}, u32[]{:S(2)}, u32[]{:S(2)}) collective-permute-start(f32[1,512]{1,0:T(1,128)S(1)} %dynamic-slice_add_fusion), channel_id=1, source_target_pairs={{0,1},{1,2},{2,3},{3,0},{4,5},{5,6},{6,7},{7,4},{8,9},{9,10},{10,1... | collective-permute-start | bytes 6152 | tf_op jit(solution)/shard_map/ppermute | solution.py:24
  188.5 5.1 %collective-permute-start.28 = (f32[1,512]{1,0:T(1,128)S(1)}, f32[1,512]{1,0:T(1,128)S(1)}, u32[]{:S(2)}, u32[]{:S(2)}) collective-permute-start(f32[1,512]{1,0:T(1,128)S(1)} %dynamic-slice_add_fusion), channel_id=1, source_target_pairs={{0,2},{1,3},{2,0},{3,1},{4,6},{5,7},{6,4},{7,5},{8,10},{9,11},{10,... | collective-permute-start | bytes 6152 | tf_op jit(solution)/shard_map/ppermute | solution.py:24
  (24 other events, 352.2 us)
Sparse Core Ops, SparseCore 0:
  9.6 50.6 all-gather.4
  62.6 89.5 all-gather.2

commit v11 on v10

--- a/solution.py
+++ b/solution.py
@@ -503,7 +503,7 @@
 
 def project_gate(place, slabs, weight):
     own, other, _ = slabs
-    rows, width, depth = 2 * own.shape[0], weight.shape[1] // 2, 1024
+    rows, width, depth = 2 * own.shape[0], weight.shape[1], 1024
     columns = pl.BlockSpec((own.shape[0], depth), lambda i, place: (0, i))
     out = jax.ShapeDtypeStruct((rows, width), BF16)
     return pl.pallas_call(
@@ -511,7 +511,7 @@
         grid_spec=pltpu.PrefetchScalarGridSpec(
             num_scalar_prefetch=1,
             grid=(weight.shape[0] // depth,),
-            in_specs=[columns, columns, pl.BlockSpec((depth, width), lambda i, place: (i, place[0]))],
+            in_specs=[columns, columns, pl.BlockSpec((depth, width), lambda i, place: (i, 0))],
             out_specs=fixed(out),
             scratch_shapes=[pltpu.VMEM((rows, width), F32)],
         ),
@@ -673,7 +673,8 @@
 
     nearest, second, blocks = travelling(own_block, before_third, before_last)
     (z_rows,) = tied((z_weight,), own_block)
-    z_whole = lax.all_gather(z_rows, ("z", "y", "core"), axis=0, tiled=True)
+    z_block = in_core_order(core, mine(z_rows, 1), swap_cores(others(z_rows, 1)), 0)
+    z_whole = lax.all_gather(z_block, ("z", "y"), axis=0, tiled=True)
     sums = products(place, slabs, second, len(nearest), sums)
     bcc, cum, cum_slab, cum_t, step_t, weights_in, decays = early
     xc, entering, final = local_states(

time: 204 us -> 207 us (1.015)
  starting transfers between devices: 48.4 us -> 45.8 us
    ppermute x21, starting transfers between devices: 39.6 us -> 35.6 us  [round_ring(): lax.ppermute(a, axis, [(i, (i + distance) % size) for i in range(size)])]
    ppermute x4 -> x5, waiting for transfers between devices: 3.89 us -> 5.29 us  [swap_cores(): return lax.ppermute(a, 'core', [(0, 1), (1, 0)])]
  transfers between devices with their start and end apart: 32 -> 33, of which waited for: 12 -> 19; matrix products, arithmetic and copies ran while one was open for 2% -> 3% of each run, Pallas kernels for 34% -> 34%
where the time goes in v11:
time: 207 us; the launch traced here: 206 us
  Pallas kernels  79.8 us (39%)
  waiting for transfers between devices  51.2 us (25%)
  starting transfers between devices  45.8 us (22%)
  between operations  13.8 us (7%)
  local copies, waits for them, and re-layouts  11.1 us (5%)
  other arithmetic  4.15 us (2%)
    ppermute x21, waiting for transfers between devices, round_ring(): lax.ppermute(a, axis, [(i, (i + distance) % size) for i in range(size)])  45.9 us
    ppermute x21, starting transfers between devices, round_ring(): lax.ppermute(a, axis, [(i, (i + distance) % size) for i in range(size)])  35.6 us
    pallas_call x2, Pallas kernels, products(): pl.pallas_call(functools.partial(products_kernel, sources, done, count, l...  19.4 us
    pallas_call x1, Pallas kernels, local_states(): pl.pallas_call(functools.partial(states_kernel, sources, done, count), gr...  15.2 us
    pallas_call x1, Pallas kernels, prepared(): pl.pallas_call(prepare_kernel, grid_spec=pltpu.PrefetchScalarGridSpec(num...  14.5 us
    pallas_call x1, Pallas kernels, project_gate(): pl.pallas_call(z_kernel, grid_spec=pltpu.PrefetchScalarGridSpec(num_scala...  13 us
    pallas_call x1, Pallas kernels, gate_outputs(): pl.pallas_call(gate_kernel, grid_spec=pltpu.PrefetchScalarGridSpec(num_sc...  8.07 us
    ppermute x3, starting transfers between devices, earlier_states(): lax.ppermute(total, 'z', [(i, i + distance) for i in range(rows - distanc...  8.04 us
  transfers between devices with their start and end apart: 33, of which 19 were waited for; matrix products, arithmetic and copies ran while one was open for 3% of the time, Pallas kernels for 34%

profile of v11, /device:TPU:6, one launch (start us, length us, event | category | flops | bytes accessed | tf_op | source)
XLA Modules:
  0.0 205.8 jit_solution(13028609524726107133)
XLA Ops:
  16.3 1.6 collective-permute-start.1
  17.9 4.0 %collective-permute-start.4 = (bf16[256,1024]{1,0:T(8,128)(2,1)S(1)}, bf16[256,1024]{1,0:T(8,128)(2,1)}, u32[]{:S(2)}, u32[]{:S(2)}) collective-permute-start(bf16[256,1024]{1,0:T(8,128)(2,1)S(1)} %pad_maximum_fusion.refs_0_), channel_id=1, source_target_pairs={{0,96},{32,0},{64,32},{96,64},{1,97},{33,1},{65,33},{97,65},{2,98}... | collective-permute-start | bytes 1572872 | tf_op jit(solution)/shard_map/ppermute | solution.py:24
  22.0 1.7 collective-permute-start.2
  23.6 9.2 %collective-permute-done.1.refs_1_ = bf16[256,1024]{1,0:T(8,128)(2,1)S(1)} collective-permute-done((bf16[256,1024]{1,0:T(8,128)(2,1)S(1)}, bf16[256,1024]{1,0:T(8,128)(2,1)S(1)}, u32[]{:S(2)}, u32[]{:S(2)}) %collective-permute-start.1) | collective-permute-done | bytes 524320 | tf_op jit(solution)/shard_map/ppermute | solution.py:24
  32.8 1.9 collective-permute-done.4.refs_4_
  34.7 2.3 %collective-permute-done.2.refs_2_ = bf16[256,1024]{1,0:T(8,128)(2,1)} collective-permute-done((bf16[256,1024]{1,0:T(8,128)(2,1)S(1)}, bf16[256,1024]{1,0:T(8,128)(2,1)}, u32[]{:S(2)}, u32[]{:S(2)}) %collective-permute-start.2) | collective-permute-done | bytes 524320 | tf_op jit(solution)/shard_map/ppermute | solution.py:24
  37.1 2.1 %collective-permute-done.3.refs_3_ = bf16[256,1024]{1,0:T(8,128)(2,1)S(1)} collective-permute-done((bf16[256,1024]{1,0:T(8,128)(2,1)S(1)}, bf16[256,1024]{1,0:T(8,128)(2,1)S(1)}, u32[]{:S(2)}, u32[]{:S(2)}) %collective-permute-start.3) | collective-permute-done | bytes 524320 | tf_op jit(solution)/shard_map/ppermute | solution.py:24
  41.8 2.6 %collective-permute-start.11 = (bf16[256,1024]{1,0:T(8,128)(2,1)}, bf16[256,1024]{1,0:T(8,128)(2,1)S(1)}, u32[]{:S(2)}, u32[]{:S(2)}) collective-permute-start(bf16[256,1024]{1,0:T(8,128)(2,1)} %collective-permute-done.4.refs_4_), channel_id=1, source_target_pairs={{0,24},{8,0},{16,8},{24,16},{1,25},{9,1},{17,9},{25,17},{2,26},{10... | collective-permute-start | bytes 1572872 | tf_op jit(solution)/shard_map/ppermute | solution.py:24
  44.4 4.0 %collective-permute-start.9 = (bf16[256,1024]{1,0:T(8,128)(2,1)S(1)}, bf16[256,1024]{1,0:T(8,128)(2,1)S(1)}, u32[]{:S(2)}, u32[]{:S(2)}) collective-permute-start(bf16[256,1024]{1,0:T(8,128)(2,1)S(1)} %collective-permute-done.1.refs_1_), channel_id=1, source_target_pairs={{0,8},{8,16},{16,24},{24,0},{1,9},{9,17},{17,25},{25,1},{2,10},{10... | collective-permute-start | bytes 1572872 | tf_op jit(solution)/shard_map/ppermute | solution.py:24
  49.4 9.6 %first_products.1 = (f32[1024,1024]{1,0:T(8,128)}, f32[16,1024]{1,0:T(8,128)S(1)}) custom-call(s32[17]{0:T(128)S(1)} %stack.68.place_ref, bf16[512,4096]{1,0:T(8,128)(2,1)} %own_ref.4, bf16[512,4096]{1,0:T(8,128)(2,1)} %collective-permute-done.5.other_ref, bf16[16,4096]{1,0:T(8,128)(2,1)S(1)} %add.201.before_ref, ...), custom_call_target="tpu_custom_call" | custom-call | flops 5000000000 | bytes 16777216 | tf_op jit(solution)/shard_map/first_products/pallas_call | solution.py:430
  60.1 5.2 %collective-permute-done.9.refs_0_ = bf16[256,1024]{1,0:T(8,128)(2,1)S(1)} collective-permute-done((bf16[256,1024]{1,0:T(8,128)(2,1)S(1)}, bf16[256,1024]{1,0:T(8,128)(2,1)S(1)}, u32[]{:S(2)}, u32[]{:S(2)}) %collective-permute-start.9) | collective-permute-done | bytes 524320 | tf_op jit(solution)/shard_map/ppermute | solution.py:24
  68.7 3.0 %collective-permute-start.16 = (bf16[256,1024]{1,0:T(8,128)(2,1)S(1)}, bf16[256,1024]{1,0:T(8,128)(2,1)}, u32[]{:S(2)}, u32[]{:S(2)}) collective-permute-start(bf16[256,1024]{1,0:T(8,128)(2,1)S(1)} %collective-permute-done.9.refs_0_), channel_id=1, source_target_pairs={{0,96},{32,0},{64,32},{96,64},{1,97},{33,1},{65,33},{97,65},{2,98}... | collective-permute-start | bytes 1572872 | tf_op jit(solution)/shard_map/ppermute | solution.py:24
  73.7 14.5 %prepared.1 = (bf16[1024,256]{1,0:T(8,128)(2,1)}, f32[1024,128]{1,0:T(8,128)}, f32[1024,128]{1,0:T(8,128)}, f32[16,1024]{1,0:T(8,128)}, f32[16,1024]{1,0:T(8,128...) custom-call(s32[17]{0:T(128)} %copy-done.11, bf16[512,4096]{1,0:T(8,128)(2,1)} %own_ref.4, ...), custom_call_target="tpu_custom_call" | custom-call | flops 4000000000 | bytes 14680064 | tf_op jit(solution)/shard_map/prepared/pallas_call | solution.py:405
  88.2 2.8 %collective-permute-done.14.refs_1_ = bf16[256,1024]{1,0:T(8,128)(2,1)} collective-permute-done((bf16[256,1024]{1,0:T(8,128)(2,1)S(1)}, bf16[256,1024]{1,0:T(8,128)(2,1)}, u32[]{:S(2)}, u32[]{:S(2)}) %collective-permute-start.14) | collective-permute-done | bytes 524320 | tf_op jit(solution)/shard_map/ppermute | solution.py:24
  91.0 3.3 %collective-permute-start.18 = (bf16[256,1024]{1,0:T(8,128)(2,1)S(1)}, bf16[256,1024]{1,0:T(8,128)(2,1)}, u32[]{:S(2)}, u32[]{:S(2)}) collective-permute-start(bf16[256,1024]{1,0:T(8,128)(2,1)S(1)} %collective-permute-done.1.refs_1_), channel_id=1, source_target_pairs={{0,96},{32,0},{64,32},{96,64},{1,97},{33,1},{65,33},{97,65},{2,98}... | collective-permute-start | bytes 1572872 | tf_op jit(solution)/shard_map/ppermute | solution.py:24
  94.3 2.6 %collective-permute-start.19 = (bf16[256,1024]{1,0:T(8,128)(2,1)}, bf16[256,1024]{1,0:T(8,128)(2,1)}, u32[]{:S(2)}, u32[]{:S(2)}) collective-permute-start(bf16[256,1024]{1,0:T(8,128)(2,1)} %collective-permute-done.13.refs_0_), channel_id=1, source_target_pairs={{0,24},{8,0},{16,8},{24,16},{1,25},{9,1},{17,9},{25,17},{2,26},{10... | collective-permute-start | bytes 1572872 | tf_op jit(solution)/shard_map/ppermute | solution.py:24
  97.2 9.9 %more_products.1 = (f32[1024,1024]{1,0:T(8,128)}, f32[16,1024]{1,0:T(8,128)S(1)}) custom-call(s32[17]{0:T(128)S(1)} %copy-done.12, bf16[512,4096]{1,0:T(8,128)(2,1)} %own_ref.4, bf16[512,4096]{1,0:T(8,128)(2,1)} %collective-permute-done.5.other_ref, bf16[16,4096]{1,0:T(8,128)(2,1)S(1)} %copy-done.7, bf16[256,1024]{1,0:T(8,128)(2,1)S(1)} %collective-permute-done.9.refs_0_, ...), custom_call_target="tpu_custom_call" | custom-call | flops 5000000000 | bytes 16777216 | tf_op jit(solution)/shard_map/more_products/pallas_call | solution.py:430
  107.0 7.5 %collective-permute-done.19.refs_6_ = bf16[256,1024]{1,0:T(8,128)(2,1)} collective-permute-done((bf16[256,1024]{1,0:T(8,128)(2,1)}, bf16[256,1024]{1,0:T(8,128)(2,1)}, u32[]{:S(2)}, u32[]{:S(2)}) %collective-permute-start.19) | collective-permute-done | bytes 524320 | tf_op jit(solution)/shard_map/ppermute | solution.py:24
  114.6 15.2 %states.1 = (bf16[1024,1024]{1,0:T(8,128)(2,1)S(1)}, bf16[4,128,1024]{2,1,0:T(8,128)(2,1)S(1)}, bf16[144,1024]{1,0:T(8,128)(2,1)S(1)}) custom-call(s32[17]{0:T(128)S(1)} %copy-done.12, bf16[512,4096]{1,0:T(8,128)(2,1)S(1)} %copy-done.10, bf16[512,4096]{1,0:T(8,128)(2,1)} %collective-permute-done.5.other_ref, bf16[16,4096]{1,0:T(8,128)(2,1)S(1)} %copy-done.7, ...), custom_call_target="tpu_custom_call" | custom-call | flops 11000000512 | bytes 18874368 | tf_op jit(solution)/shard_map/states/pallas_call | solution.py:456
  129.9 5.1 %collective-permute-start.21 = (bf16[144,1024]{1,0:T(8,128)(2,1)S(1)}, bf16[144,1024]{1,0:T(8,128)(2,1)S(1)}, u32[]{:S(2)}, u32[]{:S(2)}) collective-permute-start(bf16[144,1024]{1,0:T(8,128)(2,1)S(1)} %get-tuple-element.54.refs_0_), channel_id=1, source_target_pairs={{0,16},{8,24},{16,0},{24,8},{1,17},{9,25},{17,1},{25,9},{2,18},{10... | collective-permute-start | bytes 884744 | tf_op jit(solution)/shard_map/ppermute | solution.py:24
  135.0 7.1 %outputs.1.local_ref = bf16[1024,1024]{1,0:T(8,128)(2,1)S(1)} custom-call(bf16[1024,1024]{1,0:T(8,128)(2,1)S(1)} %get-tuple-element.48.xc_ref, bf16[1024,256]{1,0:T(8,128)(2,1)S(1)} %copy-done.4, f32[1024,128]{1,0:T(8,128)S(1)} %copy-done.13, f32[16,1024]{1,0:T(8,128)S(1)} %copy-done.15, f32[16,1024]{1,0:T(8,128)S(1)} %copy-done.16, ...), custom_call_target="tpu_custom_call" | custom-call | flops 10000000000 | bytes 10485760 | tf_op jit(solution)/shard_map/outputs/pallas_call | solution.py:488
  143.5 3.2 %collective-permute-done.20.refs_1_ = bf16[144,1024]{1,0:T(8,128)(2,1)S(1)} collective-permute-done((bf16[144,1024]{1,0:T(8,128)(2,1)S(1)}, bf16[144,1024]{1,0:T(8,128)(2,1)S(1)}, u32[]{:S(2)}, u32[]{:S(2)}) %collective-permute-start.20) | collective-permute-done | bytes 294944 | tf_op jit(solution)/shard_map/ppermute | solution.py:24
  146.6 3.4 %collective-permute-done.21.refs_2_ = bf16[144,1024]{1,0:T(8,128)(2,1)S(1)} collective-permute-done((bf16[144,1024]{1,0:T(8,128)(2,1)S(1)}, bf16[144,1024]{1,0:T(8,128)(2,1)S(1)}, u32[]{:S(2)}, u32[]{:S(2)}) %collective-permute-start.21) | collective-permute-done | bytes 294944 | tf_op jit(solution)/shard_map/ppermute | solution.py:24
  153.2 3.7 %collective-permute-start.23 = (bf16[144,1024]{1,0:T(8,128)(2,1)S(1)}, bf16[144,1024]{1,0:T(8,128)(2,1)S(1)}, u32[]{:S(2)}, u32[]{:S(2)}) collective-permute-start(bf16[144,1024]{1,0:T(8,128)(2,1)S(1)} %get-tuple-element.57), channel_id=1, source_target_pairs={{0,96},{1,97},{2,98},{3,99},{4,100},{5,101},{6,102},{7,103},{8,104... | collective-permute-start | bytes 884744 | tf_op jit(solution)/shard_map/ppermute | solution.py:588
  158.3 3.0 %collective-permute-start.25 = (bf16[144,1024]{1,0:T(8,128)(2,1)S(1)}, bf16[144,1024]{1,0:T(8,128)(2,1)S(1)}, u32[]{:S(2)}, u32[]{:S(2)}) collective-permute-start(bf16[144,1024]{1,0:T(8,128)(2,1)S(1)} %get-tuple-element.57), channel_id=1, source_target_pairs={{0,32},{32,64},{64,96},{1,33},{33,65},{65,97},{2,34},{34,66},{66,9... | collective-permute-start | bytes 884744 | tf_op jit(solution)/shard_map/ppermute | solution.py:588
  161.3 13.0 %project_gate.1.gate_ref = bf16[1024,1024]{1,0:T(8,128)(2,1)S(1)} custom-call(s32[17]{0:T(128)S(1)} %copy-done.12, bf16[512,4096]{1,0:T(8,128)(2,1)} %own_ref.4, bf16[512,4096]{1,0:T(8,128)(2,1)} %collective-permute-done.5.other_ref, bf16[4096,1024]{1,0:T(8,128)(2,1)} %all-gather.3.cloned.1.call-done.weight_ref), custom_call_target="tpu_custom_call" | custom-call | flops 8999999488 | bytes 20971520 | tf_op jit(solution)/shard_map/project_gate/pallas_call | solution.py:509
  176.5 8.1 %gate.1 = (bf16[512,1024]{1,0:T(8,128)(2,1)}, bf16[512,1024]{1,0:T(8,128)(2,1)}, f32[1,1024]{1,0:T(1,128)}) custom-call(s32[1]{0:T(128)} %bitcast.core_ref, bf16[1024,1024]{1,0:T(8,128)(2,1)} %copy-done.2, bf16[1024,1024]{1,0:T(8,128)(2,1)} %copy-done.1, bf16[1024,256]{1,0:T(8,128)(2,1)} %get-tuple-element.40.refs_9_.bcc_ref, ...), custom_call_target="tpu_custom_call" | custom-call | flops 1000000000 | bytes 10485760 | tf_op jit(solution)/shard_map/gate/pallas_call | solution.py:527
  185.1 2.4 %collective-permute-done.27 = f32[1,1024]{1,0:T(1,128)S(1)} collective-permute-done((f32[1,1024]{1,0:T(1,128)}, f32[1,1024]{1,0:T(1,128)S(1)}, u32[]{:S(2)}, u32[]{:S(2)}) %collective-permute-start.27) | collective-permute-done | bytes 4128 | tf_op jit(solution)/shard_map/ppermute | solution.py:19
  188.7 2.4 %collective-permute-start.29 = (f32[1,512]{1,0:T(1,128)S(1)}, f32[1,512]{1,0:T(1,128)S(1)}, u32[]{:S(2)}, u32[]{:S(2)}) collective-permute-start(f32[1,512]{1,0:T(1,128)S(1)} %dynamic-slice_add_fusion), channel_id=1, source_target_pairs={{0,2},{1,3},{2,0},{3,1},{4,6},{5,7},{6,4},{7,5},{8,10},{9,11},{10,... | collective-permute-start | bytes 6152 | tf_op jit(solution)/shard_map/ppermute | solution.py:24
  191.7 2.1 collective-permute-done.29
  193.8 2.1 %collective-permute-done.30 = f32[1,512]{1,0:T(1,128)S(1)} collective-permute-done((f32[1,512]{1,0:T(1,128)S(1)}, f32[1,512]{1,0:T(1,128)S(1)}, u32[]{:S(2)}, u32[]{:S(2)}) %collective-permute-start.30) | collective-permute-done | bytes 2080 | tf_op jit(solution)/shard_map/ppermute | solution.py:24
  197.1 1.9 normalized.1
  (114 shorter events, 31.7 us)
Async XLA Ops:
  6.5 67.1 %all-gather.5.cloned.1.call-start = ((), (), s32[]{:S(2)}) async-start(), calls=%async_computation.1 | async-start | bytes 3244032 | tf_op jit(solution)/shard_map/all_gather | solution.py:652
  9.0 152.3 %all-gather.3.cloned.1.call-start = ((), (), s32[]{:S(2)}) async-start(), calls=%async_computation | async-start | bytes 8912896 | tf_op jit(solution)/shard_map/all_gather | solution.py:677
  12.7 1.6 collective-permute-start.6
  16.3 16.6 %collective-permute-start.1 = (bf16[256,1024]{1,0:T(8,128)(2,1)S(1)}, bf16[256,1024]{1,0:T(8,128)(2,1)S(1)}, u32[]{:S(2)}, u32[]{:S(2)}) collective-permute-start(bf16[256,1024]{1,0:T(8,128)(2,1)S(1)} %pad_maximum_fusion.refs_0_), channel_id=1, source_target_pairs={{0,8},{8,16},{16,24},{24,0},{1,9},{9,17},{17,25},{25,1},{2,10},{10... | collective-permute-start | bytes 1572872 | tf_op jit(solution)/shard_map/ppermute | solution.py:24
  17.9 16.8 %collective-permute-start.4 = (bf16[256,1024]{1,0:T(8,128)(2,1)S(1)}, bf16[256,1024]{1,0:T(8,128)(2,1)}, u32[]{:S(2)}, u32[]{:S(2)}) collective-permute-start(bf16[256,1024]{1,0:T(8,128)(2,1)S(1)} %pad_maximum_fusion.refs_0_), channel_id=1, source_target_pairs={{0,96},{32,0},{64,32},{96,64},{1,97},{33,1},{65,33},{97,65},{2,98}... | collective-permute-start | bytes 1572872 | tf_op jit(solution)/shard_map/ppermute | solution.py:24
  22.0 15.1 %collective-permute-start.2 = (bf16[256,1024]{1,0:T(8,128)(2,1)S(1)}, bf16[256,1024]{1,0:T(8,128)(2,1)}, u32[]{:S(2)}, u32[]{:S(2)}) collective-permute-start(bf16[256,1024]{1,0:T(8,128)(2,1)S(1)} %pad_maximum_fusion.refs_0_), channel_id=1, source_target_pairs={{0,24},{8,0},{16,8},{24,16},{1,25},{9,1},{17,9},{25,17},{2,26},{10... | collective-permute-start | bytes 1572872 | tf_op jit(solution)/shard_map/ppermute | solution.py:24
  23.6 15.5 %collective-permute-start.3 = (bf16[256,1024]{1,0:T(8,128)(2,1)S(1)}, bf16[256,1024]{1,0:T(8,128)(2,1)S(1)}, u32[]{:S(2)}, u32[]{:S(2)}) collective-permute-start(bf16[256,1024]{1,0:T(8,128)(2,1)S(1)} %pad_maximum_fusion.refs_0_), channel_id=1, source_target_pairs={{0,32},{32,64},{64,96},{96,0},{1,33},{33,65},{65,97},{97,1},{2,34}... | collective-permute-start | bytes 1572872 | tf_op jit(solution)/shard_map/ppermute | solution.py:24
  39.2 10.2 %collective-permute-start.5 = (bf16[512,4096]{1,0:T(8,128)(2,1)}, bf16[512,4096]{1,0:T(8,128)(2,1)}, u32[]{:S(2)}, u32[]{:S(2)}) collective-permute-start(bf16[512,4096]{1,0:T(8,128)(2,1)} %own_ref.4), channel_id=1, source_target_pairs={{0,4},{4,0},{1,5},{5,1},{2,6},{6,2},{3,7},{7,3},{8,12},{12,8},{9,1... | collective-permute-start | bytes 12582920 | tf_op jit(solution)/shard_map/ppermute | solution.py:19
  40.1 4.3 %collective-permute-start.7 = (bf16[16,4096]{1,0:T(8,128)(2,1)S(1)}, bf16[16,4096]{1,0:T(8,128)(2,1)S(1)}, u32[]{:S(2)}, u32[]{:S(2)}) collective-permute-start(bf16[16,4096]{1,0:T(8,128)(2,1)S(1)} %slice.4), channel_id=1, source_target_pairs={{4,8},{12,16},{20,24},{28,32},{36,40},{44,48},{52,56},{60,64},{68,... | collective-permute-start | bytes 393224 | tf_op jit(solution)/shard_map/ppermute | solution.py:660
  40.7 7.7 %collective-permute-start.8 = (bf16[16,4096]{1,0:T(8,128)(2,1)S(1)}, bf16[16,4096]{1,0:T(8,128)(2,1)S(1)}, u32[]{:S(2)}, u32[]{:S(2)}) collective-permute-start(bf16[16,4096]{1,0:T(8,128)(2,1)S(1)} %slice.4), channel_id=1, source_target_pairs={{4,12},{12,20},{20,28},{28,36},{36,44},{44,52},{52,60},{60,68},{68... | collective-permute-start | bytes 393224 | tf_op jit(solution)/shard_map/ppermute | solution.py:660
  41.4 18.6 %collective-permute-start.10 = (bf16[256,1024]{1,0:T(8,128)(2,1)}, bf16[256,1024]{1,0:T(8,128)(2,1)S(1)}, u32[]{:S(2)}, u32[]{:S(2)}) collective-permute-start(bf16[256,1024]{1,0:T(8,128)(2,1)} %collective-permute-done.4.refs_4_), channel_id=1, source_target_pairs={{0,96},{32,0},{64,32},{96,64},{1,97},{33,1},{65,33},{97,65},{2,98}... | collective-permute-start | bytes 1572872 | tf_op jit(solution)/shard_map/ppermute | solution.py:24
  41.8 18.2 %collective-permute-start.11 = (bf16[256,1024]{1,0:T(8,128)(2,1)}, bf16[256,1024]{1,0:T(8,128)(2,1)S(1)}, u32[]{:S(2)}, u32[]{:S(2)}) collective-permute-start(bf16[256,1024]{1,0:T(8,128)(2,1)} %collective-permute-done.4.refs_4_), channel_id=1, source_target_pairs={{0,24},{8,0},{16,8},{24,16},{1,25},{9,1},{17,9},{25,17},{2,26},{10... | collective-permute-start | bytes 1572872 | tf_op jit(solution)/shard_map/ppermute | solution.py:24
  44.4 20.9 %collective-permute-start.9 = (bf16[256,1024]{1,0:T(8,128)(2,1)S(1)}, bf16[256,1024]{1,0:T(8,128)(2,1)S(1)}, u32[]{:S(2)}, u32[]{:S(2)}) collective-permute-start(bf16[256,1024]{1,0:T(8,128)(2,1)S(1)} %collective-permute-done.1.refs_1_), channel_id=1, source_target_pairs={{0,8},{8,16},{16,24},{24,0},{1,9},{9,17},{17,25},{25,1},{2,10},{10... | collective-permute-start | bytes 1572872 | tf_op jit(solution)/shard_map/ppermute | solution.py:24
  48.4 18.0 %collective-permute-start.12 = (bf16[256,1024]{1,0:T(8,128)(2,1)}, bf16[256,1024]{1,0:T(8,128)(2,1)}, u32[]{:S(2)}, u32[]{:S(2)}) collective-permute-start(bf16[256,1024]{1,0:T(8,128)(2,1)} %collective-permute-done.2.refs_2_), channel_id=1, source_target_pairs={{0,32},{32,64},{64,96},{96,0},{1,33},{33,65},{65,97},{97,1},{2,34}... | collective-permute-start | bytes 1572872 | tf_op jit(solution)/shard_map/ppermute | solution.py:24
  66.4 21.8 %collective-permute-start.13 = (bf16[256,1024]{1,0:T(8,128)(2,1)S(1)}, bf16[256,1024]{1,0:T(8,128)(2,1)}, u32[]{:S(2)}, u32[]{:S(2)}) collective-permute-start(bf16[256,1024]{1,0:T(8,128)(2,1)S(1)} %collective-permute-done.10.refs_1_), channel_id=1, source_target_pairs={{0,24},{8,0},{16,8},{24,16},{1,25},{9,1},{17,9},{25,17},{2,26},{10... | collective-permute-start | bytes 1572872 | tf_op jit(solution)/shard_map/ppermute | solution.py:24
  67.4 23.6 %collective-permute-start.14 = (bf16[256,1024]{1,0:T(8,128)(2,1)S(1)}, bf16[256,1024]{1,0:T(8,128)(2,1)}, u32[]{:S(2)}, u32[]{:S(2)}) collective-permute-start(bf16[256,1024]{1,0:T(8,128)(2,1)S(1)} %collective-permute-done.10.refs_1_), channel_id=1, source_target_pairs={{0,8},{8,16},{16,24},{24,0},{1,9},{9,17},{17,25},{25,1},{2,10},{10... | collective-permute-start | bytes 1572872 | tf_op jit(solution)/shard_map/ppermute | solution.py:24
  68.4 22.6 %collective-permute-start.15 = (bf16[256,1024]{1,0:T(8,128)(2,1)S(1)}, bf16[256,1024]{1,0:T(8,128)(2,1)}, u32[]{:S(2)}, u32[]{:S(2)}) collective-permute-start(bf16[256,1024]{1,0:T(8,128)(2,1)S(1)} %collective-permute-done.9.refs_0_), channel_id=1, source_target_pairs={{0,32},{32,64},{64,96},{96,0},{1,33},{33,65},{65,97},{97,1},{2,34}... | collective-permute-start | bytes 1572872 | tf_op jit(solution)/shard_map/ppermute | solution.py:24
  68.7 22.3 %collective-permute-start.16 = (bf16[256,1024]{1,0:T(8,128)(2,1)S(1)}, bf16[256,1024]{1,0:T(8,128)(2,1)}, u32[]{:S(2)}, u32[]{:S(2)}) collective-permute-start(bf16[256,1024]{1,0:T(8,128)(2,1)S(1)} %collective-permute-done.9.refs_0_), channel_id=1, source_target_pairs={{0,96},{32,0},{64,32},{96,64},{1,97},{33,1},{65,33},{97,65},{2,98}... | collective-permute-start | bytes 1572872 | tf_op jit(solution)/shard_map/ppermute | solution.py:24
  72.3 34.7 %collective-permute-start.17 = (bf16[256,1024]{1,0:T(8,128)(2,1)S(1)}, bf16[256,1024]{1,0:T(8,128)(2,1)}, u32[]{:S(2)}, u32[]{:S(2)}) collective-permute-start(bf16[256,1024]{1,0:T(8,128)(2,1)S(1)} %collective-permute-done.3.refs_3_), channel_id=1, source_target_pairs={{0,8},{8,16},{16,24},{24,0},{1,9},{9,17},{17,25},{25,1},{2,10},{10... | collective-permute-start | bytes 1572872 | tf_op jit(solution)/shard_map/ppermute | solution.py:24
  91.0 16.0 %collective-permute-start.18 = (bf16[256,1024]{1,0:T(8,128)(2,1)S(1)}, bf16[256,1024]{1,0:T(8,128)(2,1)}, u32[]{:S(2)}, u32[]{:S(2)}) collective-permute-start(bf16[256,1024]{1,0:T(8,128)(2,1)S(1)} %collective-permute-done.1.refs_1_), channel_id=1, source_target_pairs={{0,96},{32,0},{64,32},{96,64},{1,97},{33,1},{65,33},{97,65},{2,98}... | collective-permute-start | bytes 1572872 | tf_op jit(solution)/shard_map/ppermute | solution.py:24
  94.3 20.3 %collective-permute-start.19 = (bf16[256,1024]{1,0:T(8,128)(2,1)}, bf16[256,1024]{1,0:T(8,128)(2,1)}, u32[]{:S(2)}, u32[]{:S(2)}) collective-permute-start(bf16[256,1024]{1,0:T(8,128)(2,1)} %collective-permute-done.13.refs_0_), channel_id=1, source_target_pairs={{0,24},{8,0},{16,8},{24,16},{1,25},{9,1},{17,9},{25,17},{2,26},{10... | collective-permute-start | bytes 1572872 | tf_op jit(solution)/shard_map/ppermute | solution.py:24
  129.8 16.8 %collective-permute-start.20 = (bf16[144,1024]{1,0:T(8,128)(2,1)S(1)}, bf16[144,1024]{1,0:T(8,128)(2,1)S(1)}, u32[]{:S(2)}, u32[]{:S(2)}) collective-permute-start(bf16[144,1024]{1,0:T(8,128)(2,1)S(1)} %get-tuple-element.54.refs_0_), channel_id=1, source_target_pairs={{0,8},{8,16},{16,24},{24,0},{1,9},{9,17},{17,25},{25,1},{2,10},{10... | collective-permute-start | bytes 884744 | tf_op jit(solution)/shard_map/ppermute | solution.py:24
  129.9 20.2 %collective-permute-start.21 = (bf16[144,1024]{1,0:T(8,128)(2,1)S(1)}, bf16[144,1024]{1,0:T(8,128)(2,1)S(1)}, u32[]{:S(2)}, u32[]{:S(2)}) collective-permute-start(bf16[144,1024]{1,0:T(8,128)(2,1)S(1)} %get-tuple-element.54.refs_0_), channel_id=1, source_target_pairs={{0,16},{8,24},{16,0},{24,8},{1,17},{9,25},{17,1},{25,9},{2,18},{10... | collective-permute-start | bytes 884744 | tf_op jit(solution)/shard_map/ppermute | solution.py:24
  135.0 16.2 %collective-permute-start.22 = (bf16[144,1024]{1,0:T(8,128)(2,1)S(1)}, bf16[144,1024]{1,0:T(8,128)(2,1)S(1)}, u32[]{:S(2)}, u32[]{:S(2)}) collective-permute-start(bf16[144,1024]{1,0:T(8,128)(2,1)S(1)} %get-tuple-element.54.refs_0_), channel_id=1, source_target_pairs={{0,24},{8,0},{16,8},{24,16},{1,25},{9,1},{17,9},{25,17},{2,26},{10... | collective-permute-start | bytes 884744 | tf_op jit(solution)/shard_map/ppermute | solution.py:24
  153.2 22.4 %collective-permute-start.23 = (bf16[144,1024]{1,0:T(8,128)(2,1)S(1)}, bf16[144,1024]{1,0:T(8,128)(2,1)S(1)}, u32[]{:S(2)}, u32[]{:S(2)}) collective-permute-start(bf16[144,1024]{1,0:T(8,128)(2,1)S(1)} %get-tuple-element.57), channel_id=1, source_target_pairs={{0,96},{1,97},{2,98},{3,99},{4,100},{5,101},{6,102},{7,103},{8,104... | collective-permute-start | bytes 884744 | tf_op jit(solution)/shard_map/ppermute | solution.py:588
  157.0 18.6 %collective-permute-start.24 = (bf16[144,1024]{1,0:T(8,128)(2,1)S(1)}, bf16[144,1024]{1,0:T(8,128)(2,1)S(1)}, u32[]{:S(2)}, u32[]{:S(2)}) collective-permute-start(bf16[144,1024]{1,0:T(8,128)(2,1)S(1)} %get-tuple-element.57), channel_id=1, source_target_pairs={{0,64},{32,96},{1,65},{33,97},{2,66},{34,98},{3,67},{35,99},{4,68}... | collective-permute-start | bytes 884744 | tf_op jit(solution)/shard_map/ppermute | solution.py:588
  158.3 17.3 %collective-permute-start.25 = (bf16[144,1024]{1,0:T(8,128)(2,1)S(1)}, bf16[144,1024]{1,0:T(8,128)(2,1)S(1)}, u32[]{:S(2)}, u32[]{:S(2)}) collective-permute-start(bf16[144,1024]{1,0:T(8,128)(2,1)S(1)} %get-tuple-element.57), channel_id=1, source_target_pairs={{0,32},{32,64},{64,96},{1,33},{33,65},{65,97},{2,34},{34,66},{66,9... | collective-permute-start | bytes 884744 | tf_op jit(solution)/shard_map/ppermute | solution.py:588
  184.6 11.3 %collective-permute-start.26 = (bf16[512,1024]{1,0:T(8,128)(2,1)}, bf16[512,1024]{1,0:T(8,128)(2,1)S(1)}, u32[]{:S(2)}, u32[]{:S(2)}) collective-permute-start(bf16[512,1024]{1,0:T(8,128)(2,1)} %get-tuple-element.59), channel_id=1, source_target_pairs={{0,4},{4,0},{1,5},{5,1},{2,6},{6,2},{3,7},{7,3},{8,12},{12,8},{9,1... | collective-permute-start | bytes 3145736 | tf_op jit(solution)/shard_map/ppermute | solution.py:19
  184.6 2.9 %collective-permute-start.27 = (f32[1,1024]{1,0:T(1,128)}, f32[1,1024]{1,0:T(1,128)S(1)}, u32[]{:S(2)}, u32[]{:S(2)}) collective-permute-start(f32[1,1024]{1,0:T(1,128)} %get-tuple-element.60), channel_id=1, source_target_pairs={{0,4},{4,0},{1,5},{5,1},{2,6},{6,2},{3,7},{7,3},{8,12},{12,8},{9,1... | collective-permute-start | bytes 12296 | tf_op jit(solution)/shard_map/ppermute | solution.py:19
  188.1 3.6 %collective-permute-start.28 = (f32[1,512]{1,0:T(1,128)S(1)}, f32[1,512]{1,0:T(1,128)S(1)}, u32[]{:S(2)}, u32[]{:S(2)}) collective-permute-start(f32[1,512]{1,0:T(1,128)S(1)} %dynamic-slice_add_fusion), channel_id=1, source_target_pairs={{0,1},{1,2},{2,3},{3,0},{4,5},{5,6},{6,7},{7,4},{8,9},{9,10},{10,1... | collective-permute-start | bytes 6152 | tf_op jit(solution)/shard_map/ppermute | solution.py:24
  188.7 5.1 %collective-permute-start.29 = (f32[1,512]{1,0:T(1,128)S(1)}, f32[1,512]{1,0:T(1,128)S(1)}, u32[]{:S(2)}, u32[]{:S(2)}) collective-permute-start(f32[1,512]{1,0:T(1,128)S(1)} %dynamic-slice_add_fusion), channel_id=1, source_target_pairs={{0,2},{1,3},{2,0},{3,1},{4,6},{5,7},{6,4},{7,5},{8,10},{9,11},{10,... | collective-permute-start | bytes 6152 | tf_op jit(solution)/shard_map/ppermute | solution.py:24
  191.0 4.8 %collective-permute-start.30 = (f32[1,512]{1,0:T(1,128)S(1)}, f32[1,512]{1,0:T(1,128)S(1)}, u32[]{:S(2)}, u32[]{:S(2)}) collective-permute-start(f32[1,512]{1,0:T(1,128)S(1)} %dynamic-slice_add_fusion), channel_id=1, source_target_pairs={{0,3},{1,0},{2,1},{3,2},{4,7},{5,4},{6,5},{7,6},{8,11},{9,8},{10,9... | collective-permute-start | bytes 6152 | tf_op jit(solution)/shard_map/ppermute | solution.py:24
  (25 other events, 385.0 us)
Sparse Core Ops, SparseCore 0:
  9.6 50.7 all-gather.4
  62.6 89.2 all-gather.2

commit v12 on v10

--- a/solution.py
+++ b/solution.py
@@ -564,7 +564,10 @@
 
 def earlier_states(final):
     size = lax.axis_size("y")
-    parts = [final] + [round_ring(final, "y", distance) for distance in range(1, size)]
+    less, more = round_ring(final, "y", 1), round_ring(final, "y", size - 1)
+    cut = final.shape[0] // 2 // HALO * HALO
+    opposite = [round_ring(less[:cut], "y", 1), round_ring(more[cut:], "y", size - 1)]
+    parts = [final, less, jnp.concatenate(opposite, axis=0), more]
     width = final.shape[1]
     outs = [
         jax.ShapeDtypeStruct(final.shape, BF16),

time: 204 us -> 205 us (level)
  waiting for transfers between devices: 49.5 us -> 45 us
  local copies, waits for them, and re-layouts: 10.2 us -> 14 us
    ppermute x21 -> x22, waiting for transfers between devices: 45.5 us -> 41 us  [round_ring(): lax.ppermute(a, axis, [(i, (i + distance) % size) for i in range(size)])]
    unnamed x49 -> x57, local copies, waits for them, and re-layouts: 7.13 us -> 10.9 us
    ppermute x21 -> x22, starting transfers between devices: 39.6 us -> 41.1 us  [round_ring(): lax.ppermute(a, axis, [(i, (i + distance) % size) for i in range(size)])]
  transfers between devices with their start and end apart: 32 -> 33, of which waited for: 12 -> 11; matrix products, arithmetic and copies ran while one was open for 2% -> 2% of each run, Pallas kernels for 34% -> 34%
where the time goes in v12:
time: 205 us; the launch traced here: 204 us
  Pallas kernels  79 us (39%)
  starting transfers between devices  49.8 us (24%)
  waiting for transfers between devices  45 us (22%)
  local copies, waits for them, and re-layouts  14 us (7%)
  between operations  13.9 us (7%)
  other arithmetic  2.27 us (1%)
    ppermute x22, starting transfers between devices, round_ring(): lax.ppermute(a, axis, [(i, (i + distance) % size) for i in range(size)])  41.1 us
    ppermute x22, waiting for transfers between devices, round_ring(): lax.ppermute(a, axis, [(i, (i + distance) % size) for i in range(size)])  41 us
    pallas_call x2, Pallas kernels, products(): pl.pallas_call(functools.partial(products_kernel, sources, done, count, l...  19.1 us
    pallas_call x1, Pallas kernels, local_states(): pl.pallas_call(functools.partial(states_kernel, sources, done, count), gr...  14.5 us
    pallas_call x1, Pallas kernels, prepared(): pl.pallas_call(prepare_kernel, grid_spec=pltpu.PrefetchScalarGridSpec(num...  14.5 us
    pallas_call x1, Pallas kernels, project_gate(): pl.pallas_call(z_kernel, grid_spec=pltpu.PrefetchScalarGridSpec(num_scala...  13 us
    unnamed x57, local copies, waits for them, and re-layouts  10.9 us
    pallas_call x1, Pallas kernels, gate_outputs(): pl.pallas_call(gate_kernel, grid_spec=pltpu.PrefetchScalarGridSpec(num_sc...  8.09 us
  transfers between devices with their start and end apart: 33, of which 11 were waited for; matrix products, arithmetic and copies ran while one was open for 2% of the time, Pallas kernels for 34%

profile of v12, /device:TPU:6, one launch (start us, length us, event | category | flops | bytes accessed | tf_op | source)
XLA Modules:
  0.0 203.9 jit_solution(14768942766670746049)
XLA Ops:
  11.8 1.6 collective-permute-start.1
  13.4 1.7 collective-permute-start.2
  15.1 1.9 collective-permute-start.3
  17.0 2.1 %collective-permute-start.4 = (bf16[256,1024]{1,0:T(8,128)(2,1)S(1)}, bf16[256,1024]{1,0:T(8,128)(2,1)}, u32[]{:S(2)}, u32[]{:S(2)}) collective-permute-start(bf16[256,1024]{1,0:T(8,128)(2,1)S(1)} %pad_maximum_fusion.refs_0_), channel_id=1, source_target_pairs={{0,96},{32,0},{64,32},{96,64},{1,97},{33,1},{65,33},{97,65},{2,98}... | collective-permute-start | bytes 1572872 | tf_op jit(solution)/shard_map/ppermute | solution.py:24
  19.1 8.5 %collective-permute-done.1.refs_1_ = bf16[256,1024]{1,0:T(8,128)(2,1)S(1)} collective-permute-done((bf16[256,1024]{1,0:T(8,128)(2,1)S(1)}, bf16[256,1024]{1,0:T(8,128)(2,1)S(1)}, u32[]{:S(2)}, u32[]{:S(2)}) %collective-permute-start.1) | collective-permute-done | bytes 524320 | tf_op jit(solution)/shard_map/ppermute | solution.py:24
  27.8 4.2 %collective-permute-done.3.refs_3_ = bf16[256,1024]{1,0:T(8,128)(2,1)S(1)} collective-permute-done((bf16[256,1024]{1,0:T(8,128)(2,1)S(1)}, bf16[256,1024]{1,0:T(8,128)(2,1)S(1)}, u32[]{:S(2)}, u32[]{:S(2)}) %collective-permute-start.3) | collective-permute-done | bytes 524320 | tf_op jit(solution)/shard_map/ppermute | solution.py:24
  35.2 3.1 %collective-permute-start.9 = (bf16[256,1024]{1,0:T(8,128)(2,1)}, bf16[256,1024]{1,0:T(8,128)(2,1)S(1)}, u32[]{:S(2)}, u32[]{:S(2)}) collective-permute-start(bf16[256,1024]{1,0:T(8,128)(2,1)} %collective-permute-done.4.refs_4_), channel_id=1, source_target_pairs={{0,96},{32,0},{64,32},{96,64},{1,97},{33,1},{65,33},{97,65},{2,98}... | collective-permute-start | bytes 1572872 | tf_op jit(solution)/shard_map/ppermute | solution.py:24
  38.2 3.3 %collective-permute-start.10 = (bf16[256,1024]{1,0:T(8,128)(2,1)}, bf16[256,1024]{1,0:T(8,128)(2,1)S(1)}, u32[]{:S(2)}, u32[]{:S(2)}) collective-permute-start(bf16[256,1024]{1,0:T(8,128)(2,1)} %collective-permute-done.4.refs_4_), channel_id=1, source_target_pairs={{0,24},{8,0},{16,8},{24,16},{1,25},{9,1},{17,9},{25,17},{2,26},{10... | collective-permute-start | bytes 1572872 | tf_op jit(solution)/shard_map/ppermute | solution.py:24
  41.6 2.5 %collective-permute-start.11 = (bf16[256,1024]{1,0:T(8,128)(2,1)}, bf16[256,1024]{1,0:T(8,128)(2,1)}, u32[]{:S(2)}, u32[]{:S(2)}) collective-permute-start(bf16[256,1024]{1,0:T(8,128)(2,1)} %collective-permute-done.2.refs_2_), channel_id=1, source_target_pairs={{0,32},{32,64},{64,96},{96,0},{1,33},{33,65},{65,97},{97,1},{2,34}... | collective-permute-start | bytes 1572872 | tf_op jit(solution)/shard_map/ppermute | solution.py:24
  44.2 9.5 %first_products.1 = (f32[1024,1024]{1,0:T(8,128)}, f32[16,1024]{1,0:T(8,128)S(1)}) custom-call(s32[17]{0:T(128)S(1)} %stack.68.place_ref, bf16[512,4096]{1,0:T(8,128)(2,1)} %own_ref.4, bf16[512,4096]{1,0:T(8,128)(2,1)} %collective-permute-done.5.other_ref, bf16[16,4096]{1,0:T(8,128)(2,1)S(1)} %add.199.before_ref, ...), custom_call_target="tpu_custom_call" | custom-call | flops 5000000000 | bytes 16777216 | tf_op jit(solution)/shard_map/first_products/pallas_call | solution.py:430
  53.7 5.5 %collective-permute-done.10.refs_2_ = bf16[256,1024]{1,0:T(8,128)(2,1)S(1)} collective-permute-done((bf16[256,1024]{1,0:T(8,128)(2,1)}, bf16[256,1024]{1,0:T(8,128)(2,1)S(1)}, u32[]{:S(2)}, u32[]{:S(2)}) %collective-permute-start.10) | collective-permute-done | bytes 524320 | tf_op jit(solution)/shard_map/ppermute | solution.py:24
  59.2 2.7 %collective-permute-done.11.refs_3_ = bf16[256,1024]{1,0:T(8,128)(2,1)} collective-permute-done((bf16[256,1024]{1,0:T(8,128)(2,1)}, bf16[256,1024]{1,0:T(8,128)(2,1)}, u32[]{:S(2)}, u32[]{:S(2)}) %collective-permute-start.11) | collective-permute-done | bytes 524320 | tf_op jit(solution)/shard_map/ppermute | solution.py:24
  65.1 3.0 %collective-permute-start.15 = (bf16[256,1024]{1,0:T(8,128)(2,1)S(1)}, bf16[256,1024]{1,0:T(8,128)(2,1)}, u32[]{:S(2)}, u32[]{:S(2)}) collective-permute-start(bf16[256,1024]{1,0:T(8,128)(2,1)S(1)} %collective-permute-done.8.refs_0_), channel_id=1, source_target_pairs={{0,96},{32,0},{64,32},{96,64},{1,97},{33,1},{65,33},{97,65},{2,98}... | collective-permute-start | bytes 1572872 | tf_op jit(solution)/shard_map/ppermute | solution.py:24
  68.7 2.0 collective-permute-start.16
  70.7 14.5 %prepared.1 = (bf16[1024,256]{1,0:T(8,128)(2,1)}, f32[1024,128]{1,0:T(8,128)}, f32[1024,128]{1,0:T(8,128)}, f32[16,1024]{1,0:T(8,128)}, f32[16,1024]{1,0:T(8,128...) custom-call(s32[17]{0:T(128)} %copy-done.11, bf16[512,4096]{1,0:T(8,128)(2,1)} %own_ref.4, ...), custom_call_target="tpu_custom_call" | custom-call | flops 4000000000 | bytes 14680064 | tf_op jit(solution)/shard_map/prepared/pallas_call | solution.py:405
  86.1 2.4 %collective-permute-start.17 = (bf16[256,1024]{1,0:T(8,128)(2,1)S(1)}, bf16[256,1024]{1,0:T(8,128)(2,1)S(1)}, u32[]{:S(2)}, u32[]{:S(2)}) collective-permute-start(bf16[256,1024]{1,0:T(8,128)(2,1)S(1)} %collective-permute-done.1.refs_1_), channel_id=1, source_target_pairs={{0,96},{32,0},{64,32},{96,64},{1,97},{33,1},{65,33},{97,65},{2,98}... | collective-permute-start | bytes 1572872 | tf_op jit(solution)/shard_map/ppermute | solution.py:24
  88.5 2.5 %collective-permute-start.18 = (bf16[256,1024]{1,0:T(8,128)(2,1)}, bf16[256,1024]{1,0:T(8,128)(2,1)S(1)}, u32[]{:S(2)}, u32[]{:S(2)}) collective-permute-start(bf16[256,1024]{1,0:T(8,128)(2,1)} %collective-permute-done.12.refs_0_), channel_id=1, source_target_pairs={{0,24},{8,0},{16,8},{24,16},{1,25},{9,1},{17,9},{25,17},{2,26},{10... | collective-permute-start | bytes 1572872 | tf_op jit(solution)/shard_map/ppermute | solution.py:24
  91.1 9.6 %more_products.1 = (f32[1024,1024]{1,0:T(8,128)}, f32[16,1024]{1,0:T(8,128)S(1)}) custom-call(s32[17]{0:T(128)S(1)} %copy-done.12, bf16[512,4096]{1,0:T(8,128)(2,1)} %own_ref.4, bf16[512,4096]{1,0:T(8,128)(2,1)} %collective-permute-done.5.other_ref, bf16[16,4096]{1,0:T(8,128)(2,1)S(1)} %copy-done.7, bf16[256,1024]{1,0:T(8,128)(2,1)S(1)} %collective-permute-done.8.refs_0_, ...), custom_call_target="tpu_custom_call" | custom-call | flops 5000000000 | bytes 16777216 | tf_op jit(solution)/shard_map/more_products/pallas_call | solution.py:430
  100.7 3.0 %collective-permute-done.18.refs_6_ = bf16[256,1024]{1,0:T(8,128)(2,1)S(1)} collective-permute-done((bf16[256,1024]{1,0:T(8,128)(2,1)}, bf16[256,1024]{1,0:T(8,128)(2,1)S(1)}, u32[]{:S(2)}, u32[]{:S(2)}) %collective-permute-start.18) | collective-permute-done | bytes 524320 | tf_op jit(solution)/shard_map/ppermute | solution.py:24
  103.8 14.5 %states.1 = (bf16[1024,1024]{1,0:T(8,128)(2,1)S(1)}, bf16[4,128,1024]{2,1,0:T(8,128)(2,1)S(1)}, bf16[144,1024]{1,0:T(8,128)(2,1)S(1)}) custom-call(s32[17]{0:T(128)S(1)} %copy-done.12, bf16[512,4096]{1,0:T(8,128)(2,1)S(1)} %copy-done.10, bf16[512,4096]{1,0:T(8,128)(2,1)} %collective-permute-done.5.other_ref, bf16[16,4096]{1,0:T(8,128)(2,1)S(1)} %copy-done.7, ...), custom_call_target="tpu_custom_call" | custom-call | flops 11000000512 | bytes 18874368 | tf_op jit(solution)/shard_map/states/pallas_call | solution.py:456
  119.7 3.6 %collective-permute-start.21 = (bf16[144,1024]{1,0:T(8,128)(2,1)S(1)}, bf16[144,1024]{1,0:T(8,128)(2,1)S(1)}, u32[]{:S(2)}, u32[]{:S(2)}) collective-permute-start(bf16[144,1024]{1,0:T(8,128)(2,1)S(1)} %get-tuple-element.54.refs_0_), channel_id=1, source_target_pairs={{0,24},{8,0},{16,8},{24,16},{1,25},{9,1},{17,9},{25,17},{2,26},{10... | collective-permute-start | bytes 884744 | tf_op jit(solution)/shard_map/ppermute | solution.py:24
  123.5 12.1 %collective-permute-done.21.refs_3_ = bf16[144,1024]{1,0:T(8,128)(2,1)S(1)} collective-permute-done((bf16[144,1024]{1,0:T(8,128)(2,1)S(1)}, bf16[144,1024]{1,0:T(8,128)(2,1)S(1)}, u32[]{:S(2)}, u32[]{:S(2)}) %collective-permute-start.21) | collective-permute-done | bytes 294944 | tf_op jit(solution)/shard_map/ppermute | solution.py:24
  135.6 3.8 %collective-permute-start.22 = (bf16[80,1024]{1,0:T(8,128)(2,1)S(1)}, bf16[80,1024]{1,0:T(8,128)(2,1)S(1)}, u32[]{:S(2)}, u32[]{:S(2)}) collective-permute-start(bf16[80,1024]{1,0:T(8,128)(2,1)S(1)} %slice.14), channel_id=1, source_target_pairs={{0,24},{8,0},{16,8},{24,16},{1,25},{9,1},{17,9},{25,17},{2,26},{10... | collective-permute-start | bytes 491528 | tf_op jit(solution)/shard_map/ppermute | solution.py:24
  141.1 7.3 %outputs.1.local_ref = bf16[1024,1024]{1,0:T(8,128)(2,1)S(1)} custom-call(bf16[1024,1024]{1,0:T(8,128)(2,1)S(1)} %copy-done.20, bf16[1024,256]{1,0:T(8,128)(2,1)S(1)} %copy-done.4, f32[1024,128]{1,0:T(8,128)S(1)} %copy-done.15, f32[16,1024]{1,0:T(8,128)S(1)} %copy-done.17, f32[16,1024]{1,0:T(8,128)S(1)} %copy-done.18, ...), custom_call_target="tpu_custom_call" | custom-call | flops 10000000000 | bytes 10485760 | tf_op jit(solution)/shard_map/outputs/pallas_call | solution.py:488
  151.8 2.5 %collective-permute-start.23 = (bf16[144,1024]{1,0:T(8,128)(2,1)S(1)}, bf16[144,1024]{1,0:T(8,128)(2,1)S(1)}, u32[]{:S(2)}, u32[]{:S(2)}) collective-permute-start(bf16[144,1024]{1,0:T(8,128)(2,1)S(1)} %get-tuple-element.57), channel_id=1, source_target_pairs={{0,96},{1,97},{2,98},{3,99},{4,100},{5,101},{6,102},{7,103},{8,104... | collective-permute-start | bytes 884744 | tf_op jit(solution)/shard_map/ppermute | solution.py:591
  155.6 3.0 %collective-permute-start.25 = (bf16[144,1024]{1,0:T(8,128)(2,1)S(1)}, bf16[144,1024]{1,0:T(8,128)(2,1)S(1)}, u32[]{:S(2)}, u32[]{:S(2)}) collective-permute-start(bf16[144,1024]{1,0:T(8,128)(2,1)S(1)} %get-tuple-element.57), channel_id=1, source_target_pairs={{0,32},{32,64},{64,96},{1,33},{33,65},{65,97},{2,34},{34,66},{66,9... | collective-permute-start | bytes 884744 | tf_op jit(solution)/shard_map/ppermute | solution.py:591
  158.6 13.0 %project_gate.1.gate_ref = bf16[1024,1024]{1,0:T(8,128)(2,1)S(1)} custom-call(s32[17]{0:T(128)S(1)} %copy-done.12, bf16[512,4096]{1,0:T(8,128)(2,1)} %own_ref.4, bf16[512,4096]{1,0:T(8,128)(2,1)} %collective-permute-done.5.other_ref, bf16[4096,2048]{1,0:T(8,128)(2,1)} %all-gather.3.cloned.1.call-done.weight_ref), custom_call_target="tpu_custom_call" | custom-call | flops 8999999488 | bytes 20971520 | tf_op jit(solution)/shard_map/project_gate/pallas_call | solution.py:509
  174.0 8.1 %gate.1 = (bf16[512,1024]{1,0:T(8,128)(2,1)}, bf16[512,1024]{1,0:T(8,128)(2,1)}, f32[1,1024]{1,0:T(1,128)}) custom-call(s32[1]{0:T(128)} %bitcast.core_ref, bf16[1024,1024]{1,0:T(8,128)(2,1)} %copy-done.2, bf16[1024,1024]{1,0:T(8,128)(2,1)} %copy-done.1, bf16[1024,256]{1,0:T(8,128)(2,1)} %get-tuple-element.40.refs_9_.bcc_ref, ...), custom_call_target="tpu_custom_call" | custom-call | flops 1000000000 | bytes 10485760 | tf_op jit(solution)/shard_map/gate/pallas_call | solution.py:527
  182.6 2.4 %collective-permute-done.27 = f32[1,1024]{1,0:T(1,128)S(1)} collective-permute-done((f32[1,1024]{1,0:T(1,128)}, f32[1,1024]{1,0:T(1,128)S(1)}, u32[]{:S(2)}, u32[]{:S(2)}) %collective-permute-start.27) | collective-permute-done | bytes 4128 | tf_op jit(solution)/shard_map/ppermute | solution.py:19
  186.5 2.4 %collective-permute-start.28 = (f32[1,512]{1,0:T(1,128)S(1)}, f32[1,512]{1,0:T(1,128)S(1)}, u32[]{:S(2)}, u32[]{:S(2)}) collective-permute-start(f32[1,512]{1,0:T(1,128)S(1)} %dynamic-slice_add_fusion), channel_id=1, source_target_pairs={{0,1},{1,2},{2,3},{3,0},{4,5},{5,6},{6,7},{7,4},{8,9},{9,10},{10,1... | collective-permute-start | bytes 6152 | tf_op jit(solution)/shard_map/ppermute | solution.py:24
  190.4 3.5 %collective-permute-done.29 = f32[1,512]{1,0:T(1,128)S(1)} collective-permute-done((f32[1,512]{1,0:T(1,128)S(1)}, f32[1,512]{1,0:T(1,128)S(1)}, u32[]{:S(2)}, u32[]{:S(2)}) %collective-permute-start.29) | collective-permute-done | bytes 2080 | tf_op jit(solution)/shard_map/ppermute | solution.py:24
  195.2 1.9 normalized.1
  (122 shorter events, 28.4 us)
Async XLA Ops:
  6.5 64.2 %all-gather.5.cloned.1.call-start = ((), (), s32[]{:S(2)}) async-start(), calls=%async_computation.1 | async-start | bytes 3244032 | tf_op jit(solution)/shard_map/all_gather | solution.py:655
  9.0 149.7 %all-gather.3.cloned.1.call-start = ((), (), s32[]{:S(2)}) async-start(), calls=%async_computation | async-start | bytes 17301504 | tf_op jit(solution)/shard_map/all_gather | solution.py:679
  11.8 15.8 %collective-permute-start.1 = (bf16[256,1024]{1,0:T(8,128)(2,1)S(1)}, bf16[256,1024]{1,0:T(8,128)(2,1)S(1)}, u32[]{:S(2)}, u32[]{:S(2)}) collective-permute-start(bf16[256,1024]{1,0:T(8,128)(2,1)S(1)} %pad_maximum_fusion.refs_0_), channel_id=1, source_target_pairs={{0,8},{8,16},{16,24},{24,0},{1,9},{9,17},{17,25},{25,1},{2,10},{10... | collective-permute-start | bytes 1572872 | tf_op jit(solution)/shard_map/ppermute | solution.py:24
  13.4 14.3 %collective-permute-start.2 = (bf16[256,1024]{1,0:T(8,128)(2,1)S(1)}, bf16[256,1024]{1,0:T(8,128)(2,1)}, u32[]{:S(2)}, u32[]{:S(2)}) collective-permute-start(bf16[256,1024]{1,0:T(8,128)(2,1)S(1)} %pad_maximum_fusion.refs_0_), channel_id=1, source_target_pairs={{0,24},{8,0},{16,8},{24,16},{1,25},{9,1},{17,9},{25,17},{2,26},{10... | collective-permute-start | bytes 1572872 | tf_op jit(solution)/shard_map/ppermute | solution.py:24
  15.1 16.9 %collective-permute-start.3 = (bf16[256,1024]{1,0:T(8,128)(2,1)S(1)}, bf16[256,1024]{1,0:T(8,128)(2,1)S(1)}, u32[]{:S(2)}, u32[]{:S(2)}) collective-permute-start(bf16[256,1024]{1,0:T(8,128)(2,1)S(1)} %pad_maximum_fusion.refs_0_), channel_id=1, source_target_pairs={{0,32},{32,64},{64,96},{96,0},{1,33},{33,65},{65,97},{97,1},{2,34}... | collective-permute-start | bytes 1572872 | tf_op jit(solution)/shard_map/ppermute | solution.py:24
  17.0 15.0 %collective-permute-start.4 = (bf16[256,1024]{1,0:T(8,128)(2,1)S(1)}, bf16[256,1024]{1,0:T(8,128)(2,1)}, u32[]{:S(2)}, u32[]{:S(2)}) collective-permute-start(bf16[256,1024]{1,0:T(8,128)(2,1)S(1)} %pad_maximum_fusion.refs_0_), channel_id=1, source_target_pairs={{0,96},{32,0},{64,32},{96,64},{1,97},{33,1},{65,33},{97,65},{2,98}... | collective-permute-start | bytes 1572872 | tf_op jit(solution)/shard_map/ppermute | solution.py:24
  32.0 12.2 %collective-permute-start.5 = (bf16[512,4096]{1,0:T(8,128)(2,1)}, bf16[512,4096]{1,0:T(8,128)(2,1)}, u32[]{:S(2)}, u32[]{:S(2)}) collective-permute-start(bf16[512,4096]{1,0:T(8,128)(2,1)} %own_ref.4), channel_id=1, source_target_pairs={{0,4},{4,0},{1,5},{5,1},{2,6},{6,2},{3,7},{7,3},{8,12},{12,8},{9,1... | collective-permute-start | bytes 12582920 | tf_op jit(solution)/shard_map/ppermute | solution.py:19
  32.9 5.3 %collective-permute-start.6 = (bf16[16,4096]{1,0:T(8,128)(2,1)S(1)}, bf16[16,4096]{1,0:T(8,128)(2,1)S(1)}, u32[]{:S(2)}, u32[]{:S(2)}) collective-permute-start(bf16[16,4096]{1,0:T(8,128)(2,1)S(1)} %slice.10), channel_id=1, source_target_pairs={{4,8},{12,16},{20,24},{28,32},{36,40},{44,48},{52,56},{60,64},{68,... | collective-permute-start | bytes 393224 | tf_op jit(solution)/shard_map/ppermute | solution.py:663
  33.6 8.0 %collective-permute-start.7 = (bf16[16,4096]{1,0:T(8,128)(2,1)S(1)}, bf16[16,4096]{1,0:T(8,128)(2,1)S(1)}, u32[]{:S(2)}, u32[]{:S(2)}) collective-permute-start(bf16[16,4096]{1,0:T(8,128)(2,1)S(1)} %slice.10), channel_id=1, source_target_pairs={{4,12},{12,20},{20,28},{28,36},{36,44},{44,52},{52,60},{60,68},{68... | collective-permute-start | bytes 393224 | tf_op jit(solution)/shard_map/ppermute | solution.py:663
  34.3 19.5 %collective-permute-start.8 = (bf16[256,1024]{1,0:T(8,128)(2,1)S(1)}, bf16[256,1024]{1,0:T(8,128)(2,1)S(1)}, u32[]{:S(2)}, u32[]{:S(2)}) collective-permute-start(bf16[256,1024]{1,0:T(8,128)(2,1)S(1)} %collective-permute-done.1.refs_1_), channel_id=1, source_target_pairs={{0,8},{8,16},{16,24},{24,0},{1,9},{9,17},{17,25},{25,1},{2,10},{10... | collective-permute-start | bytes 1572872 | tf_op jit(solution)/shard_map/ppermute | solution.py:24
  35.2 18.5 %collective-permute-start.9 = (bf16[256,1024]{1,0:T(8,128)(2,1)}, bf16[256,1024]{1,0:T(8,128)(2,1)S(1)}, u32[]{:S(2)}, u32[]{:S(2)}) collective-permute-start(bf16[256,1024]{1,0:T(8,128)(2,1)} %collective-permute-done.4.refs_4_), channel_id=1, source_target_pairs={{0,96},{32,0},{64,32},{96,64},{1,97},{33,1},{65,33},{97,65},{2,98}... | collective-permute-start | bytes 1572872 | tf_op jit(solution)/shard_map/ppermute | solution.py:24
  38.2 21.0 %collective-permute-start.10 = (bf16[256,1024]{1,0:T(8,128)(2,1)}, bf16[256,1024]{1,0:T(8,128)(2,1)S(1)}, u32[]{:S(2)}, u32[]{:S(2)}) collective-permute-start(bf16[256,1024]{1,0:T(8,128)(2,1)} %collective-permute-done.4.refs_4_), channel_id=1, source_target_pairs={{0,24},{8,0},{16,8},{24,16},{1,25},{9,1},{17,9},{25,17},{2,26},{10... | collective-permute-start | bytes 1572872 | tf_op jit(solution)/shard_map/ppermute | solution.py:24
  41.6 20.4 %collective-permute-start.11 = (bf16[256,1024]{1,0:T(8,128)(2,1)}, bf16[256,1024]{1,0:T(8,128)(2,1)}, u32[]{:S(2)}, u32[]{:S(2)}) collective-permute-start(bf16[256,1024]{1,0:T(8,128)(2,1)} %collective-permute-done.2.refs_2_), channel_id=1, source_target_pairs={{0,32},{32,64},{64,96},{96,0},{1,33},{33,65},{65,97},{97,1},{2,34}... | collective-permute-start | bytes 1572872 | tf_op jit(solution)/shard_map/ppermute | solution.py:24
  61.9 23.4 %collective-permute-start.12 = (bf16[256,1024]{1,0:T(8,128)(2,1)S(1)}, bf16[256,1024]{1,0:T(8,128)(2,1)}, u32[]{:S(2)}, u32[]{:S(2)}) collective-permute-start(bf16[256,1024]{1,0:T(8,128)(2,1)S(1)} %collective-permute-done.9.refs_1_), channel_id=1, source_target_pairs={{0,24},{8,0},{16,8},{24,16},{1,25},{9,1},{17,9},{25,17},{2,26},{10... | collective-permute-start | bytes 1572872 | tf_op jit(solution)/shard_map/ppermute | solution.py:24
  63.2 22.1 %collective-permute-start.13 = (bf16[256,1024]{1,0:T(8,128)(2,1)S(1)}, bf16[256,1024]{1,0:T(8,128)(2,1)S(1)}, u32[]{:S(2)}, u32[]{:S(2)}) collective-permute-start(bf16[256,1024]{1,0:T(8,128)(2,1)S(1)} %collective-permute-done.9.refs_1_), channel_id=1, source_target_pairs={{0,8},{8,16},{16,24},{24,0},{1,9},{9,17},{17,25},{25,1},{2,10},{10... | collective-permute-start | bytes 1572872 | tf_op jit(solution)/shard_map/ppermute | solution.py:24
  64.8 21.3 %collective-permute-start.14 = (bf16[256,1024]{1,0:T(8,128)(2,1)S(1)}, bf16[256,1024]{1,0:T(8,128)(2,1)}, u32[]{:S(2)}, u32[]{:S(2)}) collective-permute-start(bf16[256,1024]{1,0:T(8,128)(2,1)S(1)} %collective-permute-done.8.refs_0_), channel_id=1, source_target_pairs={{0,32},{32,64},{64,96},{96,0},{1,33},{33,65},{65,97},{97,1},{2,34}... | collective-permute-start | bytes 1572872 | tf_op jit(solution)/shard_map/ppermute | solution.py:24
  65.1 21.0 %collective-permute-start.15 = (bf16[256,1024]{1,0:T(8,128)(2,1)S(1)}, bf16[256,1024]{1,0:T(8,128)(2,1)}, u32[]{:S(2)}, u32[]{:S(2)}) collective-permute-start(bf16[256,1024]{1,0:T(8,128)(2,1)S(1)} %collective-permute-done.8.refs_0_), channel_id=1, source_target_pairs={{0,96},{32,0},{64,32},{96,64},{1,97},{33,1},{65,33},{97,65},{2,98}... | collective-permute-start | bytes 1572872 | tf_op jit(solution)/shard_map/ppermute | solution.py:24
  68.7 32.0 %collective-permute-start.16 = (bf16[256,1024]{1,0:T(8,128)(2,1)S(1)}, bf16[256,1024]{1,0:T(8,128)(2,1)}, u32[]{:S(2)}, u32[]{:S(2)}) collective-permute-start(bf16[256,1024]{1,0:T(8,128)(2,1)S(1)} %collective-permute-done.3.refs_3_), channel_id=1, source_target_pairs={{0,8},{8,16},{16,24},{24,0},{1,9},{9,17},{17,25},{25,1},{2,10},{10... | collective-permute-start | bytes 1572872 | tf_op jit(solution)/shard_map/ppermute | solution.py:24
  86.1 14.6 %collective-permute-start.17 = (bf16[256,1024]{1,0:T(8,128)(2,1)S(1)}, bf16[256,1024]{1,0:T(8,128)(2,1)S(1)}, u32[]{:S(2)}, u32[]{:S(2)}) collective-permute-start(bf16[256,1024]{1,0:T(8,128)(2,1)S(1)} %collective-permute-done.1.refs_1_), channel_id=1, source_target_pairs={{0,96},{32,0},{64,32},{96,64},{1,97},{33,1},{65,33},{97,65},{2,98}... | collective-permute-start | bytes 1572872 | tf_op jit(solution)/shard_map/ppermute | solution.py:24
  88.5 15.3 %collective-permute-start.18 = (bf16[256,1024]{1,0:T(8,128)(2,1)}, bf16[256,1024]{1,0:T(8,128)(2,1)S(1)}, u32[]{:S(2)}, u32[]{:S(2)}) collective-permute-start(bf16[256,1024]{1,0:T(8,128)(2,1)} %collective-permute-done.12.refs_0_), channel_id=1, source_target_pairs={{0,24},{8,0},{16,8},{24,16},{1,25},{9,1},{17,9},{25,17},{2,26},{10... | collective-permute-start | bytes 1572872 | tf_op jit(solution)/shard_map/ppermute | solution.py:24
  119.7 15.9 %collective-permute-start.21 = (bf16[144,1024]{1,0:T(8,128)(2,1)S(1)}, bf16[144,1024]{1,0:T(8,128)(2,1)S(1)}, u32[]{:S(2)}, u32[]{:S(2)}) collective-permute-start(bf16[144,1024]{1,0:T(8,128)(2,1)S(1)} %get-tuple-element.54.refs_0_), channel_id=1, source_target_pairs={{0,24},{8,0},{16,8},{24,16},{1,25},{9,1},{17,9},{25,17},{2,26},{10... | collective-permute-start | bytes 884744 | tf_op jit(solution)/shard_map/ppermute | solution.py:24
  123.3 16.1 %collective-permute-start.19 = (bf16[144,1024]{1,0:T(8,128)(2,1)S(1)}, bf16[144,1024]{1,0:T(8,128)(2,1)S(1)}, u32[]{:S(2)}, u32[]{:S(2)}) collective-permute-start(bf16[144,1024]{1,0:T(8,128)(2,1)S(1)} %get-tuple-element.54.refs_0_), channel_id=1, source_target_pairs={{0,8},{8,16},{16,24},{24,0},{1,9},{9,17},{17,25},{25,1},{2,10},{10... | collective-permute-start | bytes 884744 | tf_op jit(solution)/shard_map/ppermute | solution.py:24
  135.6 14.2 %collective-permute-start.22 = (bf16[80,1024]{1,0:T(8,128)(2,1)S(1)}, bf16[80,1024]{1,0:T(8,128)(2,1)S(1)}, u32[]{:S(2)}, u32[]{:S(2)}) collective-permute-start(bf16[80,1024]{1,0:T(8,128)(2,1)S(1)} %slice.14), channel_id=1, source_target_pairs={{0,24},{8,0},{16,8},{24,16},{1,25},{9,1},{17,9},{25,17},{2,26},{10... | collective-permute-start | bytes 491528 | tf_op jit(solution)/shard_map/ppermute | solution.py:24
  139.4 10.4 %collective-permute-start.20 = (bf16[64,1024]{1,0:T(8,128)(2,1)S(1)}, bf16[64,1024]{1,0:T(8,128)(2,1)S(1)}, u32[]{:S(2)}, u32[]{:S(2)}) collective-permute-start(bf16[64,1024]{1,0:T(8,128)(2,1)S(1)} %slice.13), channel_id=1, source_target_pairs={{0,8},{8,16},{16,24},{24,0},{1,9},{9,17},{17,25},{25,1},{2,10},{10... | collective-permute-start | bytes 393224 | tf_op jit(solution)/shard_map/ppermute | solution.py:24
  151.8 21.1 %collective-permute-start.23 = (bf16[144,1024]{1,0:T(8,128)(2,1)S(1)}, bf16[144,1024]{1,0:T(8,128)(2,1)S(1)}, u32[]{:S(2)}, u32[]{:S(2)}) collective-permute-start(bf16[144,1024]{1,0:T(8,128)(2,1)S(1)} %get-tuple-element.57), channel_id=1, source_target_pairs={{0,96},{1,97},{2,98},{3,99},{4,100},{5,101},{6,102},{7,103},{8,104... | collective-permute-start | bytes 884744 | tf_op jit(solution)/shard_map/ppermute | solution.py:591
  154.3 18.7 %collective-permute-start.24 = (bf16[144,1024]{1,0:T(8,128)(2,1)S(1)}, bf16[144,1024]{1,0:T(8,128)(2,1)S(1)}, u32[]{:S(2)}, u32[]{:S(2)}) collective-permute-start(bf16[144,1024]{1,0:T(8,128)(2,1)S(1)} %get-tuple-element.57), channel_id=1, source_target_pairs={{0,64},{32,96},{1,65},{33,97},{2,66},{34,98},{3,67},{35,99},{4,68}... | collective-permute-start | bytes 884744 | tf_op jit(solution)/shard_map/ppermute | solution.py:591
  155.6 17.4 %collective-permute-start.25 = (bf16[144,1024]{1,0:T(8,128)(2,1)S(1)}, bf16[144,1024]{1,0:T(8,128)(2,1)S(1)}, u32[]{:S(2)}, u32[]{:S(2)}) collective-permute-start(bf16[144,1024]{1,0:T(8,128)(2,1)S(1)} %get-tuple-element.57), channel_id=1, source_target_pairs={{0,32},{32,64},{64,96},{1,33},{33,65},{65,97},{2,34},{34,66},{66,9... | collective-permute-start | bytes 884744 | tf_op jit(solution)/shard_map/ppermute | solution.py:591
  182.1 11.9 %collective-permute-start.26 = (bf16[512,1024]{1,0:T(8,128)(2,1)}, bf16[512,1024]{1,0:T(8,128)(2,1)S(1)}, u32[]{:S(2)}, u32[]{:S(2)}) collective-permute-start(bf16[512,1024]{1,0:T(8,128)(2,1)} %get-tuple-element.59), channel_id=1, source_target_pairs={{0,4},{4,0},{1,5},{5,1},{2,6},{6,2},{3,7},{7,3},{8,12},{12,8},{9,1... | collective-permute-start | bytes 3145736 | tf_op jit(solution)/shard_map/ppermute | solution.py:19
  182.1 2.9 %collective-permute-start.27 = (f32[1,1024]{1,0:T(1,128)}, f32[1,1024]{1,0:T(1,128)S(1)}, u32[]{:S(2)}, u32[]{:S(2)}) collective-permute-start(f32[1,1024]{1,0:T(1,128)} %get-tuple-element.60), channel_id=1, source_target_pairs={{0,4},{4,0},{1,5},{5,1},{2,6},{6,2},{3,7},{7,3},{8,12},{12,8},{9,1... | collective-permute-start | bytes 12296 | tf_op jit(solution)/shard_map/ppermute | solution.py:19
  185.6 4.8 %collective-permute-start.30 = (f32[1,512]{1,0:T(1,128)S(1)}, f32[1,512]{1,0:T(1,128)S(1)}, u32[]{:S(2)}, u32[]{:S(2)}) collective-permute-start(f32[1,512]{1,0:T(1,128)S(1)} %dynamic-slice_add_fusion), channel_id=1, source_target_pairs={{0,3},{1,0},{2,1},{3,2},{4,7},{5,4},{6,5},{7,6},{8,11},{9,8},{10,9... | collective-permute-start | bytes 6152 | tf_op jit(solution)/shard_map/ppermute | solution.py:24
  186.5 4.0 %collective-permute-start.28 = (f32[1,512]{1,0:T(1,128)S(1)}, f32[1,512]{1,0:T(1,128)S(1)}, u32[]{:S(2)}, u32[]{:S(2)}) collective-permute-start(f32[1,512]{1,0:T(1,128)S(1)} %dynamic-slice_add_fusion), channel_id=1, source_target_pairs={{0,1},{1,2},{2,3},{3,0},{4,5},{5,6},{6,7},{7,4},{8,9},{9,10},{10,1... | collective-permute-start | bytes 6152 | tf_op jit(solution)/shard_map/ppermute | solution.py:24
  188.9 5.1 %collective-permute-start.29 = (f32[1,512]{1,0:T(1,128)S(1)}, f32[1,512]{1,0:T(1,128)S(1)}, u32[]{:S(2)}, u32[]{:S(2)}) collective-permute-start(f32[1,512]{1,0:T(1,128)S(1)} %dynamic-slice_add_fusion), channel_id=1, source_target_pairs={{0,2},{1,3},{2,0},{3,1},{4,6},{5,7},{6,4},{7,5},{8,10},{9,11},{10,... | collective-permute-start | bytes 6152 | tf_op jit(solution)/shard_map/ppermute | solution.py:24
  (29 other events, 416.2 us)
Sparse Core Ops, SparseCore 0:
  9.6 50.6 all-gather.4
  62.6 85.3 all-gather.2

commit v13 on v10

--- a/solution.py
+++ b/solution.py
@@ -646,11 +646,13 @@
     def per_lane(a):
         return jnp.pad(mine(a, 0), (0, LANES - heads))[None, :]
 
+    send = others(x_weight, 1)
+    bc_weight, dt_weight = tied((bc_weight, dt_weight), send)
     narrow = jnp.concatenate(
         [bc_weight, dt_weight, jnp.zeros((bc_weight.shape[0], LANES - 2 * heads), BF16)], axis=1
     )
     narrow = lax.all_gather(narrow, ("z", "y", "core"), axis=0, tiled=True)
-    own_block = jnp.concatenate([mine(x_weight, 1), swap_cores(others(x_weight, 1))], axis=0)
+    own_block = jnp.concatenate([mine(x_weight, 1), swap_cores(send)], axis=0)
     place = jnp.stack([core, *block_order()]).astype(jnp.int32)
     slabs, sums, early = [], [], []
 

time: 204 us -> 204 us (level)
    unnamed x49 -> x48, local copies, waits for them, and re-layouts: 7.13 us -> 6.31 us
  transfers between devices with their start and end apart: 32 -> 32, of which waited for: 12 -> 12; matrix products, arithmetic and copies ran while one was open for 2% -> 1% of each run, Pallas kernels for 34% -> 34%
where the time goes in v13:
time: 204 us
  Pallas kernels  79.4 us (39%)
  waiting for transfers between devices  49.5 us (24%)
  starting transfers between devices  48.6 us (24%)
  between operations  13.8 us (7%)
  local copies, waits for them, and re-layouts  10.2 us (5%)
  other arithmetic  2.25 us (1%)
    ppermute x21, waiting for transfers between devices, round_ring(): lax.ppermute(a, axis, [(i, (i + distance) % size) for i in range(size)])  45.5 us
    ppermute x21, starting transfers between devices, round_ring(): lax.ppermute(a, axis, [(i, (i + distance) % size) for i in range(size)])  39.4 us
    pallas_call x2, Pallas kernels, products(): pl.pallas_call(functools.partial(products_kernel, sources, done, count, l...  19.1 us
    pallas_call x1, Pallas kernels, local_states(): pl.pallas_call(functools.partial(states_kernel, sources, done, count), gr...  15 us
    pallas_call x1, Pallas kernels, prepared(): pl.pallas_call(prepare_kernel, grid_spec=pltpu.PrefetchScalarGridSpec(num...  14.5 us
    pallas_call x1, Pallas kernels, project_gate(): pl.pallas_call(z_kernel, grid_spec=pltpu.PrefetchScalarGridSpec(num_scala...  13 us
    pallas_call x1, Pallas kernels, gate_outputs(): pl.pallas_call(gate_kernel, grid_spec=pltpu.PrefetchScalarGridSpec(num_sc...  8.08 us
    ppermute x3, starting transfers between devices, earlier_states(): lax.ppermute(total, 'z', [(i, i + distance) for i in range(rows - distanc...  7.19 us
  transfers between devices with their start and end apart: 32, of which 12 were waited for; matrix products, arithmetic and copies ran while one was open for 1% of the time, Pallas kernels for 34%

profile of v13, /device:TPU:6, one launch (start us, length us, event | category | flops | bytes accessed | tf_op | source)
XLA Modules:
  0.0 203.7 jit_solution(2729764644833400307)
XLA Ops:
  13.4 1.7 collective-permute-start.2
  15.1 1.9 collective-permute-start.3
  17.0 2.1 %collective-permute-start.4 = (bf16[256,1024]{1,0:T(8,128)(2,1)S(1)}, bf16[256,1024]{1,0:T(8,128)(2,1)}, u32[]{:S(2)}, u32[]{:S(2)}) collective-permute-start(bf16[256,1024]{1,0:T(8,128)(2,1)S(1)} %pad_maximum_fusion.refs_0_), channel_id=1, source_target_pairs={{0,96},{32,0},{64,32},{96,64},{1,97},{33,1},{65,33},{97,65},{2,98}... | collective-permute-start | bytes 1572872 | tf_op jit(solution)/shard_map/ppermute | solution.py:24
  19.1 8.5 %collective-permute-done.1.refs_1_ = bf16[256,1024]{1,0:T(8,128)(2,1)S(1)} collective-permute-done((bf16[256,1024]{1,0:T(8,128)(2,1)S(1)}, bf16[256,1024]{1,0:T(8,128)(2,1)S(1)}, u32[]{:S(2)}, u32[]{:S(2)}) %collective-permute-start.1) | collective-permute-done | bytes 524320 | tf_op jit(solution)/shard_map/ppermute | solution.py:24
  27.7 4.0 %collective-permute-done.3.refs_3_ = bf16[256,1024]{1,0:T(8,128)(2,1)S(1)} collective-permute-done((bf16[256,1024]{1,0:T(8,128)(2,1)S(1)}, bf16[256,1024]{1,0:T(8,128)(2,1)S(1)}, u32[]{:S(2)}, u32[]{:S(2)}) %collective-permute-start.3) | collective-permute-done | bytes 524320 | tf_op jit(solution)/shard_map/ppermute | solution.py:24
  34.9 3.4 %collective-permute-start.9 = (bf16[256,1024]{1,0:T(8,128)(2,1)}, bf16[256,1024]{1,0:T(8,128)(2,1)S(1)}, u32[]{:S(2)}, u32[]{:S(2)}) collective-permute-start(bf16[256,1024]{1,0:T(8,128)(2,1)} %collective-permute-done.4.refs_4_), channel_id=1, source_target_pairs={{0,96},{32,0},{64,32},{96,64},{1,97},{33,1},{65,33},{97,65},{2,98}... | collective-permute-start | bytes 1572872 | tf_op jit(solution)/shard_map/ppermute | solution.py:24
  38.2 3.3 %collective-permute-start.10 = (bf16[256,1024]{1,0:T(8,128)(2,1)}, bf16[256,1024]{1,0:T(8,128)(2,1)S(1)}, u32[]{:S(2)}, u32[]{:S(2)}) collective-permute-start(bf16[256,1024]{1,0:T(8,128)(2,1)} %collective-permute-done.4.refs_4_), channel_id=1, source_target_pairs={{0,24},{8,0},{16,8},{24,16},{1,25},{9,1},{17,9},{25,17},{2,26},{10... | collective-permute-start | bytes 1572872 | tf_op jit(solution)/shard_map/ppermute | solution.py:24
  41.6 2.5 %collective-permute-start.11 = (bf16[256,1024]{1,0:T(8,128)(2,1)}, bf16[256,1024]{1,0:T(8,128)(2,1)}, u32[]{:S(2)}, u32[]{:S(2)}) collective-permute-start(bf16[256,1024]{1,0:T(8,128)(2,1)} %collective-permute-done.2.refs_2_), channel_id=1, source_target_pairs={{0,32},{32,64},{64,96},{96,0},{1,33},{33,65},{65,97},{97,1},{2,34}... | collective-permute-start | bytes 1572872 | tf_op jit(solution)/shard_map/ppermute | solution.py:24
  44.2 9.5 %first_products.1 = (f32[1024,1024]{1,0:T(8,128)}, f32[16,1024]{1,0:T(8,128)S(1)}) custom-call(s32[17]{0:T(128)S(1)} %stack.68.place_ref, bf16[512,4096]{1,0:T(8,128)(2,1)} %own_ref.4, bf16[512,4096]{1,0:T(8,128)(2,1)} %collective-permute-done.5.other_ref, bf16[16,4096]{1,0:T(8,128)(2,1)S(1)} %add.199.before_ref, ...), custom_call_target="tpu_custom_call" | custom-call | flops 5000000000 | bytes 16777216 | tf_op jit(solution)/shard_map/first_products/pallas_call | solution.py:430
  53.8 5.8 %collective-permute-done.10.refs_2_ = bf16[256,1024]{1,0:T(8,128)(2,1)S(1)} collective-permute-done((bf16[256,1024]{1,0:T(8,128)(2,1)}, bf16[256,1024]{1,0:T(8,128)(2,1)S(1)}, u32[]{:S(2)}, u32[]{:S(2)}) %collective-permute-start.10) | collective-permute-done | bytes 524320 | tf_op jit(solution)/shard_map/ppermute | solution.py:24
  59.5 2.6 %collective-permute-done.11.refs_3_ = bf16[256,1024]{1,0:T(8,128)(2,1)} collective-permute-done((bf16[256,1024]{1,0:T(8,128)(2,1)}, bf16[256,1024]{1,0:T(8,128)(2,1)}, u32[]{:S(2)}, u32[]{:S(2)}) %collective-permute-start.11) | collective-permute-done | bytes 524320 | tf_op jit(solution)/shard_map/ppermute | solution.py:24
  63.1 1.9 collective-permute-start.13
  65.3 3.0 %collective-permute-start.15 = (bf16[256,1024]{1,0:T(8,128)(2,1)S(1)}, bf16[256,1024]{1,0:T(8,128)(2,1)}, u32[]{:S(2)}, u32[]{:S(2)}) collective-permute-start(bf16[256,1024]{1,0:T(8,128)(2,1)S(1)} %collective-permute-done.8.refs_0_), channel_id=1, source_target_pairs={{0,96},{32,0},{64,32},{96,64},{1,97},{33,1},{65,33},{97,65},{2,98}... | collective-permute-start | bytes 1572872 | tf_op jit(solution)/shard_map/ppermute | solution.py:24
  69.0 2.0 collective-permute-start.16
  71.0 14.5 %prepared.1 = (bf16[1024,256]{1,0:T(8,128)(2,1)}, f32[1024,128]{1,0:T(8,128)}, f32[1024,128]{1,0:T(8,128)}, f32[16,1024]{1,0:T(8,128)}, f32[16,1024]{1,0:T(8,128...) custom-call(s32[17]{0:T(128)} %copy-done.11, bf16[512,4096]{1,0:T(8,128)(2,1)} %own_ref.4, ...), custom_call_target="tpu_custom_call" | custom-call | flops 4000000000 | bytes 14680064 | tf_op jit(solution)/shard_map/prepared/pallas_call | solution.py:405
  85.6 3.1 %collective-permute-start.17 = (bf16[256,1024]{1,0:T(8,128)(2,1)S(1)}, bf16[256,1024]{1,0:T(8,128)(2,1)}, u32[]{:S(2)}, u32[]{:S(2)}) collective-permute-start(bf16[256,1024]{1,0:T(8,128)(2,1)S(1)} %collective-permute-done.1.refs_1_), channel_id=1, source_target_pairs={{0,96},{32,0},{64,32},{96,64},{1,97},{33,1},{65,33},{97,65},{2,98}... | collective-permute-start | bytes 1572872 | tf_op jit(solution)/shard_map/ppermute | solution.py:24
  88.7 2.2 %collective-permute-start.18 = (bf16[256,1024]{1,0:T(8,128)(2,1)}, bf16[256,1024]{1,0:T(8,128)(2,1)}, u32[]{:S(2)}, u32[]{:S(2)}) collective-permute-start(bf16[256,1024]{1,0:T(8,128)(2,1)} %collective-permute-done.12.refs_0_), channel_id=1, source_target_pairs={{0,24},{8,0},{16,8},{24,16},{1,25},{9,1},{17,9},{25,17},{2,26},{10... | collective-permute-start | bytes 1572872 | tf_op jit(solution)/shard_map/ppermute | solution.py:24
  91.1 9.6 %more_products.1 = (f32[1024,1024]{1,0:T(8,128)}, f32[16,1024]{1,0:T(8,128)S(1)}) custom-call(s32[17]{0:T(128)S(1)} %copy-done.12, bf16[512,4096]{1,0:T(8,128)(2,1)} %own_ref.4, bf16[512,4096]{1,0:T(8,128)(2,1)} %collective-permute-done.5.other_ref, bf16[16,4096]{1,0:T(8,128)(2,1)S(1)} %copy-done.7, bf16[256,1024]{1,0:T(8,128)(2,1)S(1)} %collective-permute-done.8.refs_0_, ...), custom_call_target="tpu_custom_call" | custom-call | flops 5000000000 | bytes 16777216 | tf_op jit(solution)/shard_map/more_products/pallas_call | solution.py:430
  100.7 2.6 %collective-permute-done.18.refs_6_ = bf16[256,1024]{1,0:T(8,128)(2,1)} collective-permute-done((bf16[256,1024]{1,0:T(8,128)(2,1)}, bf16[256,1024]{1,0:T(8,128)(2,1)}, u32[]{:S(2)}, u32[]{:S(2)}) %collective-permute-start.18) | collective-permute-done | bytes 524320 | tf_op jit(solution)/shard_map/ppermute | solution.py:24
  103.4 15.0 %states.1 = (bf16[1024,1024]{1,0:T(8,128)(2,1)S(1)}, bf16[4,128,1024]{2,1,0:T(8,128)(2,1)S(1)}, bf16[144,1024]{1,0:T(8,128)(2,1)S(1)}) custom-call(s32[17]{0:T(128)S(1)} %copy-done.12, bf16[512,4096]{1,0:T(8,128)(2,1)S(1)} %copy-done.10, bf16[512,4096]{1,0:T(8,128)(2,1)} %collective-permute-done.5.other_ref, bf16[16,4096]{1,0:T(8,128)(2,1)S(1)} %copy-done.7, ...), custom_call_target="tpu_custom_call" | custom-call | flops 11000000512 | bytes 18874368 | tf_op jit(solution)/shard_map/states/pallas_call | solution.py:456
  118.5 5.2 %collective-permute-start.20 = (bf16[144,1024]{1,0:T(8,128)(2,1)S(1)}, bf16[144,1024]{1,0:T(8,128)(2,1)S(1)}, u32[]{:S(2)}, u32[]{:S(2)}) collective-permute-start(bf16[144,1024]{1,0:T(8,128)(2,1)S(1)} %get-tuple-element.58.refs_0_), channel_id=1, source_target_pairs={{0,16},{8,24},{16,0},{24,8},{1,17},{9,25},{17,1},{25,9},{2,18},{10... | collective-permute-start | bytes 884744 | tf_op jit(solution)/shard_map/ppermute | solution.py:24
  123.7 7.1 %outputs.1.local_ref = bf16[1024,1024]{1,0:T(8,128)(2,1)S(1)} custom-call(bf16[1024,1024]{1,0:T(8,128)(2,1)S(1)} %get-tuple-element.52.xc_ref, bf16[1024,256]{1,0:T(8,128)(2,1)S(1)} %copy-done.4, f32[1024,128]{1,0:T(8,128)S(1)} %copy-done.13, f32[16,1024]{1,0:T(8,128)S(1)} %copy-done.15, f32[16,1024]{1,0:T(8,128)S(1)} %copy-done.16, ...), custom_call_target="tpu_custom_call" | custom-call | flops 10000000000 | bytes 10485760 | tf_op jit(solution)/shard_map/outputs/pallas_call | solution.py:488
  132.2 3.8 %collective-permute-done.19.refs_1_ = bf16[144,1024]{1,0:T(8,128)(2,1)S(1)} collective-permute-done((bf16[144,1024]{1,0:T(8,128)(2,1)S(1)}, bf16[144,1024]{1,0:T(8,128)(2,1)S(1)}, u32[]{:S(2)}, u32[]{:S(2)}) %collective-permute-start.19) | collective-permute-done | bytes 294944 | tf_op jit(solution)/shard_map/ppermute | solution.py:24
  136.0 13.2 %collective-permute-done.20.refs_2_ = bf16[144,1024]{1,0:T(8,128)(2,1)S(1)} collective-permute-done((bf16[144,1024]{1,0:T(8,128)(2,1)S(1)}, bf16[144,1024]{1,0:T(8,128)(2,1)S(1)}, u32[]{:S(2)}, u32[]{:S(2)}) %collective-permute-start.20) | collective-permute-done | bytes 294944 | tf_op jit(solution)/shard_map/ppermute | solution.py:24
  151.2 2.9 %collective-permute-start.22 = (bf16[144,1024]{1,0:T(8,128)(2,1)S(1)}, bf16[144,1024]{1,0:T(8,128)(2,1)S(1)}, u32[]{:S(2)}, u32[]{:S(2)}) collective-permute-start(bf16[144,1024]{1,0:T(8,128)(2,1)S(1)} %get-tuple-element.61), channel_id=1, source_target_pairs={{0,96},{1,97},{2,98},{3,99},{4,100},{5,101},{6,102},{7,103},{8,104... | collective-permute-start | bytes 884744 | tf_op jit(solution)/shard_map/ppermute | solution.py:588
  155.4 3.0 %collective-permute-start.24 = (bf16[144,1024]{1,0:T(8,128)(2,1)S(1)}, bf16[144,1024]{1,0:T(8,128)(2,1)S(1)}, u32[]{:S(2)}, u32[]{:S(2)}) collective-permute-start(bf16[144,1024]{1,0:T(8,128)(2,1)S(1)} %get-tuple-element.61), channel_id=1, source_target_pairs={{0,32},{32,64},{64,96},{1,33},{33,65},{65,97},{2,34},{34,66},{66,9... | collective-permute-start | bytes 884744 | tf_op jit(solution)/shard_map/ppermute | solution.py:588
  158.5 13.0 %project_gate.1.gate_ref = bf16[1024,1024]{1,0:T(8,128)(2,1)S(1)} custom-call(s32[17]{0:T(128)S(1)} %copy-done.12, bf16[512,4096]{1,0:T(8,128)(2,1)} %own_ref.4, bf16[512,4096]{1,0:T(8,128)(2,1)} %collective-permute-done.5.other_ref, bf16[4096,2048]{1,0:T(8,128)(2,1)} %all-gather.3.cloned.1.call-done.weight_ref), custom_call_target="tpu_custom_call" | custom-call | flops 8999999488 | bytes 20971520 | tf_op jit(solution)/shard_map/project_gate/pallas_call | solution.py:509
  173.8 8.1 %gate.1 = (bf16[512,1024]{1,0:T(8,128)(2,1)}, bf16[512,1024]{1,0:T(8,128)(2,1)}, f32[1,1024]{1,0:T(1,128)}) custom-call(s32[1]{0:T(128)} %bitcast.core_ref, bf16[1024,1024]{1,0:T(8,128)(2,1)} %copy-done.2, bf16[1024,1024]{1,0:T(8,128)(2,1)} %copy-done.1, bf16[1024,256]{1,0:T(8,128)(2,1)} %get-tuple-element.44.refs_9_.bcc_ref, ...), custom_call_target="tpu_custom_call" | custom-call | flops 1000000000 | bytes 10485760 | tf_op jit(solution)/shard_map/gate/pallas_call | solution.py:527
  182.4 2.4 %collective-permute-done.26 = f32[1,1024]{1,0:T(1,128)S(1)} collective-permute-done((f32[1,1024]{1,0:T(1,128)}, f32[1,1024]{1,0:T(1,128)S(1)}, u32[]{:S(2)}, u32[]{:S(2)}) %collective-permute-start.26) | collective-permute-done | bytes 4128 | tf_op jit(solution)/shard_map/ppermute | solution.py:19
  186.3 2.4 %collective-permute-start.27 = (f32[1,512]{1,0:T(1,128)S(1)}, f32[1,512]{1,0:T(1,128)S(1)}, u32[]{:S(2)}, u32[]{:S(2)}) collective-permute-start(f32[1,512]{1,0:T(1,128)S(1)} %dynamic-slice_add_fusion), channel_id=1, source_target_pairs={{0,1},{1,2},{2,3},{3,0},{4,5},{5,6},{6,7},{7,4},{8,9},{9,10},{10,1... | collective-permute-start | bytes 6152 | tf_op jit(solution)/shard_map/ppermute | solution.py:24
  190.2 3.5 %collective-permute-done.28 = f32[1,512]{1,0:T(1,128)S(1)} collective-permute-done((f32[1,512]{1,0:T(1,128)S(1)}, f32[1,512]{1,0:T(1,128)S(1)}, u32[]{:S(2)}, u32[]{:S(2)}) %collective-permute-start.28) | collective-permute-done | bytes 2080 | tf_op jit(solution)/shard_map/ppermute | solution.py:24
  195.0 1.9 normalized.1
  (109 shorter events, 24.4 us)
Async XLA Ops:
  6.5 64.4 %all-gather.5.cloned.1.call-start = ((), (), s32[]{:S(2)}) async-start(), calls=%async_computation.1 | async-start | bytes 3244032 | tf_op jit(solution)/shard_map/all_gather | solution.py:654
  10.0 148.4 %all-gather.3.cloned.1.call-start = ((), (), s32[]{:S(2)}) async-start(), calls=%async_computation | async-start | bytes 17301504 | tf_op jit(solution)/shard_map/all_gather | solution.py:678
  10.1 1.6 collective-permute-start
  11.8 15.8 %collective-permute-start.1 = (bf16[256,1024]{1,0:T(8,128)(2,1)S(1)}, bf16[256,1024]{1,0:T(8,128)(2,1)S(1)}, u32[]{:S(2)}, u32[]{:S(2)}) collective-permute-start(bf16[256,1024]{1,0:T(8,128)(2,1)S(1)} %pad_maximum_fusion.refs_0_), channel_id=1, source_target_pairs={{0,8},{8,16},{16,24},{24,0},{1,9},{9,17},{17,25},{25,1},{2,10},{10... | collective-permute-start | bytes 1572872 | tf_op jit(solution)/shard_map/ppermute | solution.py:24
  13.4 14.3 %collective-permute-start.2 = (bf16[256,1024]{1,0:T(8,128)(2,1)S(1)}, bf16[256,1024]{1,0:T(8,128)(2,1)}, u32[]{:S(2)}, u32[]{:S(2)}) collective-permute-start(bf16[256,1024]{1,0:T(8,128)(2,1)S(1)} %pad_maximum_fusion.refs_0_), channel_id=1, source_target_pairs={{0,24},{8,0},{16,8},{24,16},{1,25},{9,1},{17,9},{25,17},{2,26},{10... | collective-permute-start | bytes 1572872 | tf_op jit(solution)/shard_map/ppermute | solution.py:24
  15.1 16.7 %collective-permute-start.3 = (bf16[256,1024]{1,0:T(8,128)(2,1)S(1)}, bf16[256,1024]{1,0:T(8,128)(2,1)S(1)}, u32[]{:S(2)}, u32[]{:S(2)}) collective-permute-start(bf16[256,1024]{1,0:T(8,128)(2,1)S(1)} %pad_maximum_fusion.refs_0_), channel_id=1, source_target_pairs={{0,32},{32,64},{64,96},{96,0},{1,33},{33,65},{65,97},{97,1},{2,34}... | collective-permute-start | bytes 1572872 | tf_op jit(solution)/shard_map/ppermute | solution.py:24
  17.0 14.8 %collective-permute-start.4 = (bf16[256,1024]{1,0:T(8,128)(2,1)S(1)}, bf16[256,1024]{1,0:T(8,128)(2,1)}, u32[]{:S(2)}, u32[]{:S(2)}) collective-permute-start(bf16[256,1024]{1,0:T(8,128)(2,1)S(1)} %pad_maximum_fusion.refs_0_), channel_id=1, source_target_pairs={{0,96},{32,0},{64,32},{96,64},{1,97},{33,1},{65,33},{97,65},{2,98}... | collective-permute-start | bytes 1572872 | tf_op jit(solution)/shard_map/ppermute | solution.py:24
  31.8 12.5 %collective-permute-start.5 = (bf16[512,4096]{1,0:T(8,128)(2,1)}, bf16[512,4096]{1,0:T(8,128)(2,1)}, u32[]{:S(2)}, u32[]{:S(2)}) collective-permute-start(bf16[512,4096]{1,0:T(8,128)(2,1)} %own_ref.4), channel_id=1, source_target_pairs={{0,4},{4,0},{1,5},{5,1},{2,6},{6,2},{3,7},{7,3},{8,12},{12,8},{9,1... | collective-permute-start | bytes 12582920 | tf_op jit(solution)/shard_map/ppermute | solution.py:19
  32.7 5.5 %collective-permute-start.6 = (bf16[16,4096]{1,0:T(8,128)(2,1)S(1)}, bf16[16,4096]{1,0:T(8,128)(2,1)S(1)}, u32[]{:S(2)}, u32[]{:S(2)}) collective-permute-start(bf16[16,4096]{1,0:T(8,128)(2,1)S(1)} %slice.4), channel_id=1, source_target_pairs={{4,8},{12,16},{20,24},{28,32},{36,40},{44,48},{52,56},{60,64},{68,... | collective-permute-start | bytes 393224 | tf_op jit(solution)/shard_map/ppermute | solution.py:662
  33.4 8.2 %collective-permute-start.7 = (bf16[16,4096]{1,0:T(8,128)(2,1)S(1)}, bf16[16,4096]{1,0:T(8,128)(2,1)S(1)}, u32[]{:S(2)}, u32[]{:S(2)}) collective-permute-start(bf16[16,4096]{1,0:T(8,128)(2,1)S(1)} %slice.4), channel_id=1, source_target_pairs={{4,12},{12,20},{20,28},{28,36},{36,44},{44,52},{52,60},{60,68},{68... | collective-permute-start | bytes 393224 | tf_op jit(solution)/shard_map/ppermute | solution.py:662
  34.0 19.7 %collective-permute-start.8 = (bf16[256,1024]{1,0:T(8,128)(2,1)S(1)}, bf16[256,1024]{1,0:T(8,128)(2,1)S(1)}, u32[]{:S(2)}, u32[]{:S(2)}) collective-permute-start(bf16[256,1024]{1,0:T(8,128)(2,1)S(1)} %collective-permute-done.1.refs_1_), channel_id=1, source_target_pairs={{0,8},{8,16},{16,24},{24,0},{1,9},{9,17},{17,25},{25,1},{2,10},{10... | collective-permute-start | bytes 1572872 | tf_op jit(solution)/shard_map/ppermute | solution.py:24
  34.9 18.9 %collective-permute-start.9 = (bf16[256,1024]{1,0:T(8,128)(2,1)}, bf16[256,1024]{1,0:T(8,128)(2,1)S(1)}, u32[]{:S(2)}, u32[]{:S(2)}) collective-permute-start(bf16[256,1024]{1,0:T(8,128)(2,1)} %collective-permute-done.4.refs_4_), channel_id=1, source_target_pairs={{0,96},{32,0},{64,32},{96,64},{1,97},{33,1},{65,33},{97,65},{2,98}... | collective-permute-start | bytes 1572872 | tf_op jit(solution)/shard_map/ppermute | solution.py:24
  38.2 21.3 %collective-permute-start.10 = (bf16[256,1024]{1,0:T(8,128)(2,1)}, bf16[256,1024]{1,0:T(8,128)(2,1)S(1)}, u32[]{:S(2)}, u32[]{:S(2)}) collective-permute-start(bf16[256,1024]{1,0:T(8,128)(2,1)} %collective-permute-done.4.refs_4_), channel_id=1, source_target_pairs={{0,24},{8,0},{16,8},{24,16},{1,25},{9,1},{17,9},{25,17},{2,26},{10... | collective-permute-start | bytes 1572872 | tf_op jit(solution)/shard_map/ppermute | solution.py:24
  41.6 20.6 %collective-permute-start.11 = (bf16[256,1024]{1,0:T(8,128)(2,1)}, bf16[256,1024]{1,0:T(8,128)(2,1)}, u32[]{:S(2)}, u32[]{:S(2)}) collective-permute-start(bf16[256,1024]{1,0:T(8,128)(2,1)} %collective-permute-done.2.refs_2_), channel_id=1, source_target_pairs={{0,32},{32,64},{64,96},{96,0},{1,33},{33,65},{65,97},{97,1},{2,34}... | collective-permute-start | bytes 1572872 | tf_op jit(solution)/shard_map/ppermute | solution.py:24
  62.2 23.4 %collective-permute-start.12 = (bf16[256,1024]{1,0:T(8,128)(2,1)S(1)}, bf16[256,1024]{1,0:T(8,128)(2,1)}, u32[]{:S(2)}, u32[]{:S(2)}) collective-permute-start(bf16[256,1024]{1,0:T(8,128)(2,1)S(1)} %collective-permute-done.9.refs_1_), channel_id=1, source_target_pairs={{0,24},{8,0},{16,8},{24,16},{1,25},{9,1},{17,9},{25,17},{2,26},{10... | collective-permute-start | bytes 1572872 | tf_op jit(solution)/shard_map/ppermute | solution.py:24
  63.1 22.4 %collective-permute-start.13 = (bf16[256,1024]{1,0:T(8,128)(2,1)S(1)}, bf16[256,1024]{1,0:T(8,128)(2,1)}, u32[]{:S(2)}, u32[]{:S(2)}) collective-permute-start(bf16[256,1024]{1,0:T(8,128)(2,1)S(1)} %collective-permute-done.9.refs_1_), channel_id=1, source_target_pairs={{0,8},{8,16},{16,24},{24,0},{1,9},{9,17},{17,25},{25,1},{2,10},{10... | collective-permute-start | bytes 1572872 | tf_op jit(solution)/shard_map/ppermute | solution.py:24
  65.0 20.6 %collective-permute-start.14 = (bf16[256,1024]{1,0:T(8,128)(2,1)S(1)}, bf16[256,1024]{1,0:T(8,128)(2,1)}, u32[]{:S(2)}, u32[]{:S(2)}) collective-permute-start(bf16[256,1024]{1,0:T(8,128)(2,1)S(1)} %collective-permute-done.8.refs_0_), channel_id=1, source_target_pairs={{0,32},{32,64},{64,96},{96,0},{1,33},{33,65},{65,97},{97,1},{2,34}... | collective-permute-start | bytes 1572872 | tf_op jit(solution)/shard_map/ppermute | solution.py:24
  65.3 20.3 %collective-permute-start.15 = (bf16[256,1024]{1,0:T(8,128)(2,1)S(1)}, bf16[256,1024]{1,0:T(8,128)(2,1)}, u32[]{:S(2)}, u32[]{:S(2)}) collective-permute-start(bf16[256,1024]{1,0:T(8,128)(2,1)S(1)} %collective-permute-done.8.refs_0_), channel_id=1, source_target_pairs={{0,96},{32,0},{64,32},{96,64},{1,97},{33,1},{65,33},{97,65},{2,98}... | collective-permute-start | bytes 1572872 | tf_op jit(solution)/shard_map/ppermute | solution.py:24
  69.0 31.8 %collective-permute-start.16 = (bf16[256,1024]{1,0:T(8,128)(2,1)S(1)}, bf16[256,1024]{1,0:T(8,128)(2,1)}, u32[]{:S(2)}, u32[]{:S(2)}) collective-permute-start(bf16[256,1024]{1,0:T(8,128)(2,1)S(1)} %collective-permute-done.3.refs_3_), channel_id=1, source_target_pairs={{0,8},{8,16},{16,24},{24,0},{1,9},{9,17},{17,25},{25,1},{2,10},{10... | collective-permute-start | bytes 1572872 | tf_op jit(solution)/shard_map/ppermute | solution.py:24
  85.6 15.2 %collective-permute-start.17 = (bf16[256,1024]{1,0:T(8,128)(2,1)S(1)}, bf16[256,1024]{1,0:T(8,128)(2,1)}, u32[]{:S(2)}, u32[]{:S(2)}) collective-permute-start(bf16[256,1024]{1,0:T(8,128)(2,1)S(1)} %collective-permute-done.1.refs_1_), channel_id=1, source_target_pairs={{0,96},{32,0},{64,32},{96,64},{1,97},{33,1},{65,33},{97,65},{2,98}... | collective-permute-start | bytes 1572872 | tf_op jit(solution)/shard_map/ppermute | solution.py:24
  88.7 14.7 %collective-permute-start.18 = (bf16[256,1024]{1,0:T(8,128)(2,1)}, bf16[256,1024]{1,0:T(8,128)(2,1)}, u32[]{:S(2)}, u32[]{:S(2)}) collective-permute-start(bf16[256,1024]{1,0:T(8,128)(2,1)} %collective-permute-done.12.refs_0_), channel_id=1, source_target_pairs={{0,24},{8,0},{16,8},{24,16},{1,25},{9,1},{17,9},{25,17},{2,26},{10... | collective-permute-start | bytes 1572872 | tf_op jit(solution)/shard_map/ppermute | solution.py:24
  118.4 17.6 %collective-permute-start.19 = (bf16[144,1024]{1,0:T(8,128)(2,1)S(1)}, bf16[144,1024]{1,0:T(8,128)(2,1)S(1)}, u32[]{:S(2)}, u32[]{:S(2)}) collective-permute-start(bf16[144,1024]{1,0:T(8,128)(2,1)S(1)} %get-tuple-element.58.refs_0_), channel_id=1, source_target_pairs={{0,8},{8,16},{16,24},{24,0},{1,9},{9,17},{17,25},{25,1},{2,10},{10... | collective-permute-start | bytes 884744 | tf_op jit(solution)/shard_map/ppermute | solution.py:24
  118.5 30.7 %collective-permute-start.20 = (bf16[144,1024]{1,0:T(8,128)(2,1)S(1)}, bf16[144,1024]{1,0:T(8,128)(2,1)S(1)}, u32[]{:S(2)}, u32[]{:S(2)}) collective-permute-start(bf16[144,1024]{1,0:T(8,128)(2,1)S(1)} %get-tuple-element.58.refs_0_), channel_id=1, source_target_pairs={{0,16},{8,24},{16,0},{24,8},{1,17},{9,25},{17,1},{25,9},{2,18},{10... | collective-permute-start | bytes 884744 | tf_op jit(solution)/shard_map/ppermute | solution.py:24
  123.6 25.5 %collective-permute-start.21 = (bf16[144,1024]{1,0:T(8,128)(2,1)S(1)}, bf16[144,1024]{1,0:T(8,128)(2,1)S(1)}, u32[]{:S(2)}, u32[]{:S(2)}) collective-permute-start(bf16[144,1024]{1,0:T(8,128)(2,1)S(1)} %get-tuple-element.58.refs_0_), channel_id=1, source_target_pairs={{0,24},{8,0},{16,8},{24,16},{1,25},{9,1},{17,9},{25,17},{2,26},{10... | collective-permute-start | bytes 884744 | tf_op jit(solution)/shard_map/ppermute | solution.py:24
  151.2 21.6 %collective-permute-start.22 = (bf16[144,1024]{1,0:T(8,128)(2,1)S(1)}, bf16[144,1024]{1,0:T(8,128)(2,1)S(1)}, u32[]{:S(2)}, u32[]{:S(2)}) collective-permute-start(bf16[144,1024]{1,0:T(8,128)(2,1)S(1)} %get-tuple-element.61), channel_id=1, source_target_pairs={{0,96},{1,97},{2,98},{3,99},{4,100},{5,101},{6,102},{7,103},{8,104... | collective-permute-start | bytes 884744 | tf_op jit(solution)/shard_map/ppermute | solution.py:588
  154.1 18.7 %collective-permute-start.23 = (bf16[144,1024]{1,0:T(8,128)(2,1)S(1)}, bf16[144,1024]{1,0:T(8,128)(2,1)S(1)}, u32[]{:S(2)}, u32[]{:S(2)}) collective-permute-start(bf16[144,1024]{1,0:T(8,128)(2,1)S(1)} %get-tuple-element.61), channel_id=1, source_target_pairs={{0,64},{32,96},{1,65},{33,97},{2,66},{34,98},{3,67},{35,99},{4,68}... | collective-permute-start | bytes 884744 | tf_op jit(solution)/shard_map/ppermute | solution.py:588
  155.4 17.4 %collective-permute-start.24 = (bf16[144,1024]{1,0:T(8,128)(2,1)S(1)}, bf16[144,1024]{1,0:T(8,128)(2,1)S(1)}, u32[]{:S(2)}, u32[]{:S(2)}) collective-permute-start(bf16[144,1024]{1,0:T(8,128)(2,1)S(1)} %get-tuple-element.61), channel_id=1, source_target_pairs={{0,32},{32,64},{64,96},{1,33},{33,65},{65,97},{2,34},{34,66},{66,9... | collective-permute-start | bytes 884744 | tf_op jit(solution)/shard_map/ppermute | solution.py:588
  181.9 11.9 %collective-permute-start.25 = (bf16[512,1024]{1,0:T(8,128)(2,1)}, bf16[512,1024]{1,0:T(8,128)(2,1)S(1)}, u32[]{:S(2)}, u32[]{:S(2)}) collective-permute-start(bf16[512,1024]{1,0:T(8,128)(2,1)} %get-tuple-element.63), channel_id=1, source_target_pairs={{0,4},{4,0},{1,5},{5,1},{2,6},{6,2},{3,7},{7,3},{8,12},{12,8},{9,1... | collective-permute-start | bytes 3145736 | tf_op jit(solution)/shard_map/ppermute | solution.py:19
  181.9 2.9 %collective-permute-start.26 = (f32[1,1024]{1,0:T(1,128)}, f32[1,1024]{1,0:T(1,128)S(1)}, u32[]{:S(2)}, u32[]{:S(2)}) collective-permute-start(f32[1,1024]{1,0:T(1,128)} %get-tuple-element.64), channel_id=1, source_target_pairs={{0,4},{4,0},{1,5},{5,1},{2,6},{6,2},{3,7},{7,3},{8,12},{12,8},{9,1... | collective-permute-start | bytes 12296 | tf_op jit(solution)/shard_map/ppermute | solution.py:19
  185.4 4.8 %collective-permute-start.29 = (f32[1,512]{1,0:T(1,128)S(1)}, f32[1,512]{1,0:T(1,128)S(1)}, u32[]{:S(2)}, u32[]{:S(2)}) collective-permute-start(f32[1,512]{1,0:T(1,128)S(1)} %dynamic-slice_add_fusion), channel_id=1, source_target_pairs={{0,3},{1,0},{2,1},{3,2},{4,7},{5,4},{6,5},{7,6},{8,11},{9,8},{10,9... | collective-permute-start | bytes 6152 | tf_op jit(solution)/shard_map/ppermute | solution.py:24
  186.3 4.0 %collective-permute-start.27 = (f32[1,512]{1,0:T(1,128)S(1)}, f32[1,512]{1,0:T(1,128)S(1)}, u32[]{:S(2)}, u32[]{:S(2)}) collective-permute-start(f32[1,512]{1,0:T(1,128)S(1)} %dynamic-slice_add_fusion), channel_id=1, source_target_pairs={{0,1},{1,2},{2,3},{3,0},{4,5},{5,6},{6,7},{7,4},{8,9},{9,10},{10,1... | collective-permute-start | bytes 6152 | tf_op jit(solution)/shard_map/ppermute | solution.py:24
  188.7 5.1 %collective-permute-start.28 = (f32[1,512]{1,0:T(1,128)S(1)}, f32[1,512]{1,0:T(1,128)S(1)}, u32[]{:S(2)}, u32[]{:S(2)}) collective-permute-start(f32[1,512]{1,0:T(1,128)S(1)} %dynamic-slice_add_fusion), channel_id=1, source_target_pairs={{0,2},{1,3},{2,0},{3,1},{4,6},{5,7},{6,4},{7,5},{8,10},{9,11},{10,... | collective-permute-start | bytes 6152 | tf_op jit(solution)/shard_map/ppermute | solution.py:24
  (24 other events, 350.3 us)
Sparse Core Ops, SparseCore 0:
  10.2 50.3 all-gather.4
  62.8 89.5 all-gather.2
